TPU v7x, 32 devices: a whole 2x2x4 slice. The times are simulated.
32 devices in a mesh: dp: 8 (over z, x), seq: 4 (over y, core).
Axes of the slice: x: 2, y: 2, z: 4, core: 2. Of those that a mesh axis runs over, the one named last changes fastest.
Arguments:
- xbc: bfloat16 [8, 1024, 2816], P('dp', 'seq'), may hold values from -6 to 6
- gate_input: bfloat16 [8, 1024, 2560], P('dp', 'seq'), may hold values from -6 to 6
- dt_raw: bfloat16 [8, 1024, 40], P('dp', 'seq'), may hold values from -3 to 3
- conv_weight: float32 [4, 2816], replicated, may hold values from -3 to 3
- conv_bias: float32 [2816], replicated, may hold values from -3 to 3
- dt_bias: float32 [40], replicated, may hold values from -0.5 to 0.5
- a_rate: float32 [40], replicated, may hold values from 0.0001953125 to 0.05
- d_skip: float32 [40], replicated, may hold values from 0.5 to 1.5
- norm_gain: float32 [2560], replicated, may hold values from 0.25 to 1.75
- labels: int32 [8], P('dp'), may hold values from 0 to 1, as said below
- readout: int32 [8, 4], P('dp'), may hold values from 0 to 1023
Outputs:
- layer_out: bfloat16 [8, 1024, 2560], P('dp', 'seq')
- steering: float32 [2560, 128], P(('dp', 'seq'))
Inputs may be any that keep to these rules, and one draw needn't show every extreme that they name: `labels`: every label is 0 or 1, and both classes occur.
All inputs are finite; a program needn't handle non-finite values.
Results may differ from a plain program's by a relative error of at most 0.0034.
Values may be sent and summed in bfloat16 or wider, within the bound.
No kernel may reach another device: no remote copies, remote signals or barrier semaphores. Data moves between devices by JAX's collectives and lax.ppermute only.
A program may use at most 64 MiB of HBM per device.

v0:
```python
import jax
import jax.numpy as jnp
from jax import lax
from jax.sharding import PartitionSpec as P

H = 40
P_SIZE = 64
N = 128
KW = 4
R = 4


group_heads = 8
highest = lax.Precision.HIGHEST


def from_behind(block, axis, distance):
    devices = range(lax.axis_size(axis))
    route = [(i - distance, i) for i in devices if i - distance in devices]
    return lax.ppermute(block, axis, route)


def local_terms(x_vals, b_vals, c_vals, dt_vals, cumulative, points, offset):
    row_count = x_vals.shape[0]
    x_wide = x_vals.astype(jnp.float32).reshape(row_count, H, P_SIZE)
    b_wide = b_vals.astype(jnp.float32)
    c_wide = c_vals.astype(jnp.float32)
    scores = lax.dot_general(
        c_vals, b_vals, (((1,), (1,)), ((), ())), preferred_element_type=jnp.float32
    )
    positions = jnp.arange(row_count, dtype=jnp.int32)
    causal = positions[:, None] >= positions[None, :]
    cum_heads = cumulative.T
    dt_heads = dt_vals.T

    def group_step(group_index, buffer):
        head_start = group_index * group_heads
        cum_group = lax.dynamic_slice_in_dim(cum_heads, head_start, group_heads, 0)
        dt_group = lax.dynamic_slice_in_dim(dt_heads, head_start, group_heads, 0)
        x_group = lax.dynamic_slice_in_dim(x_wide, head_start, group_heads, 1)
        spread = jnp.where(causal[None], cum_group[:, :, None] - cum_group[:, None, :], -1e30)
        weight = jnp.exp(spread) * dt_group[:, None, :] * scores[None]
        partial_value = jnp.einsum("hts,shp->thp", weight, x_group, precision=highest)
        return lax.dynamic_update_slice_in_dim(buffer, partial_value, head_start, 1)

    diagonal_part = lax.fori_loop(
        0, H // group_heads, group_step, jnp.zeros((row_count, H, P_SIZE), jnp.float32)
    )
    final_log = cumulative[row_count - 1]
    to_end = jnp.exp(final_log[None, :] - cumulative) * dt_vals
    decay_total = jnp.exp(final_log)
    local_state = jnp.einsum(
        "sk,sn->kn",
        (to_end[:, :, None] * x_wide).reshape(row_count, H * P_SIZE),
        b_wide,
        precision=highest,
    ).reshape(H, P_SIZE, N)
    local_index = points - offset
    owned_flag = ((local_index >= 0) & (local_index < row_count)).astype(jnp.float32)
    one_hot = (positions[None, :] == local_index[:, None]).astype(jnp.float32)
    cum_at = jnp.dot(one_hot, cumulative, precision=highest)
    before = positions[None, :] <= local_index[:, None]
    spread = jnp.where(before[:, :, None], cum_at[:, None, :] - cumulative[None], -1e30)
    read_weight = jnp.sum(owned_flag[:, None, None] * jnp.exp(spread), axis=0) * dt_vals / R
    carry_weight = jnp.sum(owned_flag[:, None] * jnp.exp(cum_at), axis=0) / R
    read_local = jnp.einsum(
        "sk,sn->kn",
        (read_weight[:, :, None] * x_wide).reshape(row_count, H * P_SIZE),
        b_wide,
        precision=highest,
    ).reshape(H, P_SIZE, N)
    return (diagonal_part, x_wide, c_wide, local_state, decay_total, read_local, carry_weight)


def finish_block(diagonal_part, x_wide, c_wide, cumulative, h_in, gate_rows, d_skip, norm_gain):
    row_count = x_wide.shape[0]
    incoming = jnp.einsum("tn,hpn->thp", c_wide, h_in, precision=highest)
    ssm_out = (
        diagonal_part + jnp.exp(cumulative)[:, :, None] * incoming + d_skip[None, :, None] * x_wide
    )
    gated_out = ssm_out.reshape(row_count, H * P_SIZE) * jax.nn.silu(gate_rows.astype(jnp.float32))
    inv_rms = lax.rsqrt(jnp.mean(gated_out * gated_out, axis=-1, keepdims=True) + 1e-05)
    return (gated_out * inv_rms * norm_gain).astype(jnp.bfloat16)


def on_device(
    xbc,
    gate_input,
    dt_raw,
    conv_weight,
    conv_bias,
    dt_bias,
    a_rate,
    d_skip,
    norm_gain,
    labels,
    readout,
):
    row_count = xbc.shape[1]
    n_one = lax.psum(jnp.sum(labels.astype(jnp.float32)), "dp")
    edge_rows = from_behind(xbc[:, row_count - (KW - 1) :, :], "seq", 1)
    padded = jnp.concatenate([edge_rows, xbc], axis=1)[0].astype(jnp.float32)
    conv_sum = conv_bias
    for tap_index in range(KW):
        conv_sum = conv_sum + conv_weight[tap_index] * padded[tap_index : tap_index + row_count]
    activated = jax.nn.silu(conv_sum).astype(jnp.bfloat16)
    dt_vals = jax.nn.softplus(dt_raw[0].astype(jnp.float32) + dt_bias)
    cumulative = jnp.cumsum(-a_rate * dt_vals, axis=0)
    offset = lax.axis_index("seq") * row_count
    diagonal_part, x_wide, c_wide, local_state, decay_total, read_local, carry_weight = local_terms(
        activated[:, : H * P_SIZE],
        activated[:, H * P_SIZE : H * P_SIZE + N],
        activated[:, H * P_SIZE + N :],
        dt_vals,
        cumulative,
        readout[0],
        offset,
    )
    h_in = jnp.zeros((H, P_SIZE, N), jnp.float32)
    for step_index in range(lax.axis_size("seq") - 1):
        h_in = from_behind(decay_total[:, None, None] * h_in + local_state, "seq", 1)
    layer_out = finish_block(
        diagonal_part, x_wide, c_wide, cumulative, h_in, gate_input[0], d_skip, norm_gain
    )
    mean_state = carry_weight[:, None, None] * h_in + read_local
    batch_count = lax.axis_size("dp")
    class_value = labels[0].astype(jnp.float32)
    class_weight = class_value / n_one - (1.0 - class_value) / (batch_count - n_one)
    partial_value = (class_weight * mean_state).reshape(H * P_SIZE, N)
    steering = lax.psum_scatter(partial_value, ("dp", "seq"), scatter_dimension=0, tiled=True)
    return (layer_out[None], steering)


def solution(mesh):
    return jax.shard_map(
        on_device,
        mesh=mesh,
        in_specs=(
            P("dp", "seq", None),
            P("dp", "seq", None),
            P("dp", "seq", None),
            P(),
            P(),
            P(),
            P(),
            P(),
            P(),
            P("dp"),
            P("dp", None),
        ),
        out_specs=(P("dp", "seq", None), P(("dp", "seq"), None)),
        check_vma=False,
    )
```

profile of v0, /device:TPU:0, one launch (start us, length us, event | category | flops | bytes accessed | tf_op | source)
XLA Modules:
  0.0 260.8 jit_solution(6513268378914063251)
XLA Ops:
  8.0 2.4 collective-permute-start
  16.0 1.7 mul.260
  17.7 3.2 %copy.36 = f32[256,2560]{1,0:T(8,128)} copy(f32[256,2560]{0,1:T(8,128)} %bitcast.120) | data formatting | bytes 5242880 | tf_op jit(solution)/shard_map/mul | solution.py:54
  21.0 1.7 mul.286
  22.7 3.4 %copy.40 = f32[256,2560]{1,0:T(8,128)} copy(f32[256,2560]{0,1:T(8,128)} %bitcast.121) | data formatting | bytes 5242880 | tf_op jit(solution)/shard_map/mul | solution.py:68
  26.7 1.9 multiply_convert_fusion
  29.3 3.0 %multiply_bitcast_fusion = (f32[2560,256]{0,1:T(8,128)}, f32[2560,256]{0,1:T(8,128)}) fusion(f32[256,2560]{1,0:T(8,128)S(1)} %copy-done.1, bf16[256,2816]{1,0:T(8,128)(2,1)S(1)} %multiply_convert_fusion, f32[256,2560]{1,0:T(8,128)S(1)} %copy-done), kind=kLoop, calls=%fused_computation.34 | loop fusion | flops 1966080 | bytes 11796480 | tf_op jit(solution)/shard_map/sk,sn->kn/dot_general | solution.py:66
  32.2 3.2 %copy.37 = f32[2560,256]{1,0:T(8,128)} copy(f32[2560,256]{0,1:T(8,128)} %get-tuple-element.168) | data formatting | bytes 5242880 | tf_op jit(solution)/shard_map/sk,sn->kn/dot_general | solution.py:52
  35.5 3.0 %broadcast_add_fusion = (f32[40,64,128]{2,1,0:T(8,128)S(1)}, f32[40,64,128]{2,1,0:T(8,128)S(1)}) fusion(f32[40]{0:T(128)S(1)} %get-tuple-element.176, f32[40,64,256]{2,1,0:T(8,128)} %bitcast.119, bf16[256,2816]{1,0:T(8,128)(2,1)S(1)} %multiply_convert_fusion), kind=kOutput, calls=%fused_computation.44 | convolution fusion | flops 1006960640 | bytes 5308928 | tf_op jit(solution)/shard_map/sk,sn->kn/dot_general | solution.py:52
  38.5 4.6 %collective-permute-start.1 = (f32[40,64,128]{2,1,0:T(8,128)S(1)}, f32[40,64,128]{2,1,0:T(8,128)S(1)}, u32[]{:S(2)}, u32[]{:S(2)}) collective-permute-start(f32[40,64,128]{2,1,0:T(8,128)S(1)} %get-tuple-element.177), channel_id=1, source_target_pairs={{0,1},{1,2},{2,3},{4,5},{5,6},{6,7},{8,9},{9,10},{10,11},{12,13},{... | collective-permute-start | bytes 3932168 | tf_op jit(solution)/shard_map/ppermute | solution.py:20
  43.1 2.6 collective-permute-done.1
  45.9 14.0 %collective-permute-start.2 = (f32[40,64,128]{2,1,0:T(8,128)S(1)}, f32[40,64,128]{2,1,0:T(8,128)S(1)}, u32[]{:S(2)}, u32[]{:S(2)}) collective-permute-start(f32[40,64,128]{2,1,0:T(8,128)S(1)} %multiply_add_fusion.2), channel_id=1, source_target_pairs={{0,1},{1,2},{2,3},{4,5},{5,6},{6,7},{8,9},{9,10},{10,11},{12,13},{... | collective-permute-start | bytes 3932168 | tf_op jit(solution)/shard_map/ppermute | solution.py:20
  59.9 2.6 collective-permute-done.2
  62.5 1.2 multiply_add_fusion.1
  63.7 17.3 %collective-permute-start.3 = (f32[40,64,128]{2,1,0:T(8,128)}, f32[40,64,128]{2,1,0:T(8,128)}, u32[]{:S(2)}, u32[]{:S(2)}) collective-permute-start(f32[40,64,128]{2,1,0:T(8,128)} %multiply_add_fusion.1), channel_id=1, source_target_pairs={{0,1},{1,2},{2,3},{4,5},{5,6},{6,7},{8,9},{9,10},{10,11},{12,13},{... | collective-permute-start | bytes 3932168 | tf_op jit(solution)/shard_map/ppermute | solution.py:20
  81.7 23.0 %psum.7 = f32[]{:T(128)} all-reduce(f32[]{:T(128)} %bitcast.16), channel_id=1, replica_groups=mesh['dp'=8,'seq'=4] {'dp'}, use_global_device_ids=true, to_apply=%region_5.6 | all-reduce | flops 1 | bytes 8 | tf_op jit(solution)/shard_map/psum | solution.py:100
  106.2 1.9 copy.39
  108.1 3.2 %copy.41 = f32[2560,256]{1,0:T(8,128)} copy(f32[2560,256]{0,1:T(8,128)} %get-tuple-element.167) | data formatting | bytes 5242880 | tf_op jit(solution)/shard_map/sk,sn->kn/dot_general | solution.py:66
  111.4 1.9 slice_convert_fusion
  113.2 3.3 %copy.33 = f32[256,2560]{0,1:T(8,128)} copy(f32[256,2560]{1,0:T(8,128)} %slice_convert_fusion) | data formatting | bytes 5242880 | tf_op jit(solution)/shard_map/convert_element_type | solution.py:25
  116.7 4.5 %add_multiply_fusion = f32[40,64,128]{2,1,0:T(8,128)} fusion(f32[40,64,128]{2,1,0:T(8,128)} %collective-permute-done.3, f32[40]{0:T(128)S(1)} %broadcast_multiply_fusion, f32[]{:T(128)S(6)} %sub.87, f32[40,64,256]{2,1,0:T(8,128)} %bitcast.118, bf16[256,2816]{1,0:T(8,128)(2,1)S(1)} %multiply_convert_fusion), kind=kOutput, calls=%fused_computation.41 | convolution fusion | flops 1007616000 | bytes 5308932 | tf_op jit(solution)/shard_map/sk,sn->kn/dot_general | solution.py:66
  121.2 1.9 broadcast_in_dim.82
  123.1 22.0 %while.14 = (s32[]{:T(128)}, f32[256,40,64]{0,2,1:T(8,128)}, f32[256,40,64]{0,2,1:T(8,128)}, f32[40,256]{1,0:T(8,128)S(1)}, f32[40,256]{1,0:T(8,128)S(1)}, /*ind...) while((s32[]{:T(128)}, f32[256,40,64]{0,2,1:T(8,128)}, ...), condition=%wide.region_3.4_spmd.clone, body=%wide.region_2.3_spmd.clone.sunk | while | flops 404815872 | bytes 1500311 | solution.py:46
  123.1 4.4 %fusion.63 = f32[256,40,64]{0,2,1:T(8,128)} fusion(f32[256,40,64]{0,2,1:T(8,128)} %get-tuple-element.235, s32[]{:T(128)S(6)} %select_n.56, f32[256,256]{1,0:T(8,128)S(1)} %get-tuple-element.249, f32[8,256]{1,0:T(8,128)S(1)} %get-tuple-element.222, f32[8,256]{1,0:T(8,128)S(1)} %get-tuple-element.223, pred[256,256]{1,0:T(8,128)(4,1)S(1)} %iota_compare_fusion.5, ...), kind=kOutput, calls=%fused_computation.8.clone.1 | convolution fusion | flops 404750336 | bytes 1401856 | tf_op jit(solution)/shard_map/while/body/eval_jaxpr/hts,shp->thp/dot_general | solution.py:43
  127.5 4.4 %fusion.63 = f32[256,40,64]{0,2,1:T(8,128)} fusion(f32[256,40,64]{0,2,1:T(8,128)} %get-tuple-element.235, s32[]{:T(128)S(6)} %select_n.56, f32[256,256]{1,0:T(8,128)S(1)} %get-tuple-element.249, f32[8,256]{1,0:T(8,128)S(1)} %get-tuple-element.222, f32[8,256]{1,0:T(8,128)S(1)} %get-tuple-element.223, pred[256,256]{1,0:T(8,128)(4,1)S(1)} %iota_compare_fusion.5, ...), kind=kOutput, calls=%fused_computation.8.clone.1 | convolution fusion | flops 404750336 | bytes 1401856 | tf_op jit(solution)/shard_map/while/body/eval_jaxpr/hts,shp->thp/dot_general | solution.py:43
  131.9 4.4 %fusion.63 = f32[256,40,64]{0,2,1:T(8,128)} fusion(f32[256,40,64]{0,2,1:T(8,128)} %get-tuple-element.235, s32[]{:T(128)S(6)} %select_n.56, f32[256,256]{1,0:T(8,128)S(1)} %get-tuple-element.249, f32[8,256]{1,0:T(8,128)S(1)} %get-tuple-element.222, f32[8,256]{1,0:T(8,128)S(1)} %get-tuple-element.223, pred[256,256]{1,0:T(8,128)(4,1)S(1)} %iota_compare_fusion.5, ...), kind=kOutput, calls=%fused_computation.8.clone.1 | convolution fusion | flops 404750336 | bytes 1401856 | tf_op jit(solution)/shard_map/while/body/eval_jaxpr/hts,shp->thp/dot_general | solution.py:43
  136.4 4.3 %fusion.63 = f32[256,40,64]{0,2,1:T(8,128)} fusion(f32[256,40,64]{0,2,1:T(8,128)} %get-tuple-element.235, s32[]{:T(128)S(6)} %select_n.56, f32[256,256]{1,0:T(8,128)S(1)} %get-tuple-element.249, f32[8,256]{1,0:T(8,128)S(1)} %get-tuple-element.222, f32[8,256]{1,0:T(8,128)S(1)} %get-tuple-element.223, pred[256,256]{1,0:T(8,128)(4,1)S(1)} %iota_compare_fusion.5, ...), kind=kOutput, calls=%fused_computation.8.clone.1 | convolution fusion | flops 404750336 | bytes 1401856 | tf_op jit(solution)/shard_map/while/body/eval_jaxpr/hts,shp->thp/dot_general | solution.py:43
  140.7 4.3 %fusion.63 = f32[256,40,64]{0,2,1:T(8,128)} fusion(f32[256,40,64]{0,2,1:T(8,128)} %get-tuple-element.235, s32[]{:T(128)S(6)} %select_n.56, f32[256,256]{1,0:T(8,128)S(1)} %get-tuple-element.249, f32[8,256]{1,0:T(8,128)S(1)} %get-tuple-element.222, f32[8,256]{1,0:T(8,128)S(1)} %get-tuple-element.223, pred[256,256]{1,0:T(8,128)(4,1)S(1)} %iota_compare_fusion.5, ...), kind=kOutput, calls=%fused_computation.8.clone.1 | convolution fusion | flops 404750336 | bytes 1401856 | tf_op jit(solution)/shard_map/while/body/eval_jaxpr/hts,shp->thp/dot_general | solution.py:43
  145.1 7.0 %multiply_reduce_fusion = (f32[256]{0:T(256)S(1)}, f32[256,40,64]{0,2,1:T(8,128)}) fusion(f32[256,40,64]{0,2,1:T(8,128)} %bitcast.125, f32[256,40,64]{0,2,1:T(8,128)} %get-tuple-element.257, f32[40]{0:T(128)S(1)} %copy-done.6, f32[256,40,64]{0,2,1:T(8,128)} %get-tuple-element.126, f32[40,64,128]{2,1,0:T(8,128)} %collective-permute-done.3, ...), kind=kOutput, calls=%fused_computation.36 | convolution fusion | flops 1013841664 | bytes 11904512 | tf_op jit(solution)/shard_map/tn,hpn->thp/dot_general | solution.py:77
  152.1 3.2 %copy.38 = f32[1,256,2560]{2,1,0:T(8,128)} copy(f32[1,256,2560]{1,2,0:T(8,128)} %bitcast.124) | data formatting | bytes 5242880 | tf_op jit(solution)/shard_map/reshape | solution.py:81
  155.3 3.8 %multiply_convert_fusion.1 = bf16[1,256,2560]{2,1,0:T(8,128)(2,1)} fusion(f32[1,256,2560]{2,1,0:T(8,128)} %copy.38, f32[2560]{0:T(1024)S(1)} %copy-done.4, f32[256]{0:T(256)S(1)} %add_rsqrt_fusion, bf16[1,256,2560]{2,1,0:T(8,128)(2,1)S(1)} %copy-done.2), kind=kLoop, calls=%fused_computation.35 | loop fusion | flops 5898240 | bytes 5254144 | tf_op jit(solution)/shard_map/convert_element_type | solution.py:83
  159.2 94.8 %reduce-scatter.2.cloned.1.call-done = f32[80,128]{1,0:T(8,128)} async-done(((f32[2560,128]{1,0:T(8,128)}), f32[80,128]{1,0:T(8,128)}) %reduce-scatter.2.cloned.1.call-update) | async-done | bytes 40976 | tf_op jit(solution)/shard_map/reduce_scatter | solution.py:130
  (49 shorter events, 8.3 us)
Async XLA Ops:
  7.2 246.8 %reduce-scatter.2.cloned.1.call-start = ((), (), s32[]{:S(2)}) async-start(), calls=%async_computation.1 | async-start | bytes 1351680 | tf_op jit(solution)/shard_map/reduce_scatter | solution.py:130
  8.0 18.0 %collective-permute-start = (bf16[1,3,2816]{2,1,0:T(4,128)(2,1)S(1)}, bf16[1,3,2816]{2,1,0:T(4,128)(2,1)S(1)}, u32[]{:S(2)}, u32[]{:S(2)}) collective-permute-start(bf16[1,3,2816]{2,1,0:T(4,128)(2,1)S(1)} %slice.58), channel_id=1, source_target_pairs={{0,1},{1,2},{2,3},{4,5},{5,6},{6,7},{8,9},{9,10},{10,11},{12,13},{... | collective-permute-start | bytes 50696 | tf_op jit(solution)/shard_map/ppermute | solution.py:20
  22.7 3.4 %copy-start.3 = (bf16[1,256,2816]{2,1,0:T(8,128)(2,1)S(1)}, bf16[1,256,2816]{2,1,0:T(8,128)(2,1)}, u32[]{:S(2)}) copy-start(bf16[1,256,2816]{2,1,0:T(8,128)(2,1)} %param.13) | copy-start | bytes 4325380
  26.0 0.7 copy-start.5
  26.7 1.9 copy-start
  26.7 2.5 copy-start.1
  38.5 7.2 %collective-permute-start.1 = (f32[40,64,128]{2,1,0:T(8,128)S(1)}, f32[40,64,128]{2,1,0:T(8,128)S(1)}, u32[]{:S(2)}, u32[]{:S(2)}) collective-permute-start(f32[40,64,128]{2,1,0:T(8,128)S(1)} %get-tuple-element.177), channel_id=1, source_target_pairs={{0,1},{1,2},{2,3},{4,5},{5,6},{6,7},{8,9},{9,10},{10,11},{12,13},{... | collective-permute-start | bytes 3932168 | tf_op jit(solution)/shard_map/ppermute | solution.py:20
  45.9 60.3 %copy-start.2 = (bf16[1,256,2560]{2,1,0:T(8,128)(2,1)S(1)}, bf16[1,256,2560]{2,1,0:T(8,128)(2,1)}, u32[]{:S(2)}) copy-start(bf16[1,256,2560]{2,1,0:T(8,128)(2,1)} %param.14) | copy-start | bytes 3932164
  45.9 16.6 %collective-permute-start.2 = (f32[40,64,128]{2,1,0:T(8,128)S(1)}, f32[40,64,128]{2,1,0:T(8,128)S(1)}, u32[]{:S(2)}, u32[]{:S(2)}) collective-permute-start(f32[40,64,128]{2,1,0:T(8,128)S(1)} %multiply_add_fusion.2), channel_id=1, source_target_pairs={{0,1},{1,2},{2,3},{4,5},{5,6},{6,7},{8,9},{9,10},{10,11},{12,13},{... | collective-permute-start | bytes 3932168 | tf_op jit(solution)/shard_map/ppermute | solution.py:20
  63.7 52.9 %collective-permute-start.3 = (f32[40,64,128]{2,1,0:T(8,128)}, f32[40,64,128]{2,1,0:T(8,128)}, u32[]{:S(2)}, u32[]{:S(2)}) collective-permute-start(f32[40,64,128]{2,1,0:T(8,128)} %multiply_add_fusion.1), channel_id=1, source_target_pairs={{0,1},{1,2},{2,3},{4,5},{5,6},{6,7},{8,9},{9,10},{10,11},{12,13},{... | collective-permute-start | bytes 3932168 | tf_op jit(solution)/shard_map/ppermute | solution.py:20
  123.1 22.0 %copy-start.6 = (f32[40]{0:T(128)S(1)}, f32[40]{0:T(128)}, u32[]{:S(2)}) copy-start(f32[40]{0:T(128)} %param.20) | copy-start | bytes 484
  152.1 3.2 %copy-start.4 = (f32[2560]{0:T(1024)S(1)}, f32[2560]{0:T(1024)}, u32[]{:S(2)}) copy-start(f32[2560]{0:T(1024)} %param.21) | copy-start | bytes 30724
Sparse Core Ops, SparseCore 0:
  121.3 132.5 reduce-scatter.1
where the time goes:
time: 262 us; the launch traced here: 261 us
  waiting for transfers between devices  99.9 us (38%)
  starting transfers between devices  38.4 us (15%)
  matrix products  36.8 us (14%)
  local copies, waits for them, and re-layouts  30 us (11%)
  blocking collectives  23 us (9%)
  other arithmetic  16.3 us (6%)
  between operations  16.3 us (6%)
    reduce_scatter x1, waiting for transfers between devices, on_device(): lax.psum_scatter(partial_value, ('dp', 'seq'), scatter_dimension=0, tiled...  94.8 us
    ppermute x4, starting transfers between devices, from_behind(): return lax.ppermute(block, axis, route)  38.3 us
    psum x1, blocking collectives, on_device(): n_one = lax.psum(jnp.sum(labels.astype(jnp.float32)), 'dp')  23 us
    dot_general x5, matrix products, group_step(): jnp.einsum('hts,shp->thp', weight, x_group, precision=highest)  21.8 us
    dot_general x1, matrix products, finish_block(): incoming = jnp.einsum('tn,hpn->thp', c_wide, h_in, precision=highest)  7.01 us
  transfers between devices with their start and end apart: 5, of which 3 were waited for; matrix products, arithmetic and copies ran while one was open for 25% of the time, Pallas kernels for 0%

commit v1 on v0

v1 whole, which is shorter than its diff:
```python
import functools

import jax
import jax.numpy as jnp
from jax import lax
from jax.experimental import pallas as pl
from jax.experimental.pallas import tpu as pltpu
from jax.sharding import PartitionSpec as P

H = 40
P_SIZE = 64
N = 128
KW = 4
R = 4
D = H * P_SIZE
HALF = D // 2
BC = 2 * N
SIDE = HALF + BC
CHUNK = 256
EDGE = 16
F32 = jnp.float32
BF16 = jnp.bfloat16
VMEM = pl.BlockSpec(memory_space=pltpu.VMEM)
SMEM = pl.BlockSpec(memory_space=pltpu.SMEM)
ANY = pl.BlockSpec(memory_space=pl.ANY)
MIB = 1024 * 1024


def params(mib):
    return pltpu.CompilerParams(vmem_limit_bytes=mib * MIB)


def cost(flops, read):
    return pl.CostEstimate(flops=flops, bytes_accessed=read, transcendentals=0)


def dot(a, b):
    return jnp.dot(a, b, preferred_element_type=F32)


def pack(w):
    high = w.astype(BF16).astype(F32)
    gap = jnp.zeros((w.shape[0], 64 - H), F32)
    return jnp.concatenate([high, gap, w - high, gap], axis=1).astype(BF16)


def spread_matrix(first_head):
    row = lax.broadcasted_iota(jnp.int32, (128, CHUNK), 0)
    lane = lax.broadcasted_iota(jnp.int32, (128, CHUNK), 1)
    hit = (row & 63) == first_head + lane // P_SIZE
    return jnp.where(hit, 1.0, 0.0).astype(BF16)


def silu(v):
    half = 0.5 * v
    return half + half * jnp.tanh(half)


def steps_kernel(own_ref, other_ref, bias_ref, rate_ref, skip_ref, points_ref, ws_ref, wr_ref, e_ref, eg_ref, rows_ref, small_ref):
    place = lax.axis_index("seq")
    core = lax.rem(place, 2)
    n = own_ref.shape[0]
    base = (place - core) * n
    own = own_ref[...].astype(F32)
    other = other_ref[...].astype(F32)
    first = core == 0
    row = lax.broadcasted_iota(jnp.int32, (n, n), 0)
    lane = lax.broadcasted_iota(jnp.int32, (n, n), 1)
    lower = jnp.where(row >= lane, 1.0, 0.0).astype(BF16)
    dts, cums = [], []
    for block in range(2):
        raw = jnp.where(first == (block == 0), own, other) + bias_ref[...]
        dt = jnp.maximum(raw, 0.0) + jnp.log1p(jnp.exp(-jnp.abs(raw)))
        step = -rate_ref[...] * dt
        high = step.astype(BF16)
        rest = step - high.astype(F32)
        middle = rest.astype(BF16)
        low = (rest - middle.astype(F32)).astype(BF16)
        dts.append(dt)
        cums.append(dot(lower, high) + (dot(lower, middle) + dot(lower, low)))
    ends = [cum[n - 1 : n] for cum in cums]
    for block in range(2):
        ws_ref[block * n : (block + 1) * n] = pack(dts[block] * jnp.exp(ends[block] - cums[block]))
    total = [cums[0], ends[0] + cums[1]]
    index = lax.broadcasted_iota(jnp.int32, (n, H), 0)
    weight = [jnp.zeros((n, H), F32), jnp.zeros((n, H), F32)]
    carry = jnp.zeros((1, H), F32)
    for r in range(R):
        at = points_ref[0, r] - base
        inside = jnp.where((at >= 0) & (at < 2 * n), 1.0, 0.0)
        level = jnp.zeros((1, H), F32)
        for block in range(2):
            level += jnp.sum(jnp.where(index + block * n == at, total[block], 0.0), axis=0, keepdims=True)
        for block in range(2):
            seen = jnp.where(index + block * n <= at, jnp.exp(jnp.minimum(level - total[block], 0.0)), 0.0)
            weight[block] += inside * seen
        carry += inside * jnp.exp(level)
    for block in range(2):
        wr_ref[block * n : (block + 1) * n] = pack(weight[block] * dts[block] * (1.0 / R))
    cum = jnp.where(first, cums[0], cums[1])
    e_ref[...] = pack(jnp.exp(cum))
    eg_ref[...] = pack(jnp.exp(cum - jnp.where(first, ends[0], ends[1])))
    decay = [jnp.exp(ends[0]), jnp.exp(ends[1])]
    zero = jnp.zeros((1, H), F32)
    table = [decay[0], decay[1], skip_ref[...], zero, zero, zero, zero, zero]
    rows_ref[...] = pack(jnp.concatenate(table + table, axis=0))
    whole = [carry * (1.0 / R), jnp.exp(ends[0] + ends[1])] + [zero] * 6
    small_ref[...] = jnp.concatenate(whole, axis=0)


def state_kernel(
    own_ref, other_ref, edge_a_ref, edge_b_ref, ws_ref, wr_ref, rows_ref, later_ref, conv_w_ref, conv_b_ref, ones_ref, label_ref,
    state_ref, early_ref, keep_ref, send_ref, act_own_ref, act_other_ref, bc_ref,
    x_ref, act_ref, taps_ref, bias_ref, read_ref, sems,
    *, sequences, split,
):
    place = lax.axis_index("seq")
    core = lax.rem(place, 2)
    n = own_ref.shape[1]
    col = pl.multiple_of(core * HALF, 128)
    copies = []
    for i, (source, to) in enumerate(((own_ref, core), (other_ref, 1 - core))):
        rows = pl.ds(pl.multiple_of(EDGE + to * n, 16), n)
        copies.append(pltpu.make_async_copy(source.at[0, :, pl.ds(D, BC)], x_ref.at[rows, pl.ds(HALF, BC)], sems.at[2 * i]))
        copies.append(pltpu.make_async_copy(source.at[0, :, pl.ds(col, HALF)], x_ref.at[rows, pl.ds(0, HALF)], sems.at[2 * i + 1]))
    for copy in (copies[0], copies[2], copies[1], copies[3]):
        copy.start()
    started = jnp.where(place >= 2, 1.0, 0.0)
    edge = jnp.where(core == 0, edge_a_ref[0].astype(F32), edge_b_ref[0].astype(F32)) * started
    taps_ref[:, :HALF] = conv_w_ref[:, pl.ds(col, HALF)]
    taps_ref[:, HALF:] = conv_w_ref[:, D:]
    bias_ref[:, :HALF] = conv_b_ref[:, pl.ds(col, HALF)]
    bias_ref[:, HALF:] = conv_b_ref[:, D:]
    x_ref[0:EDGE, HALF:] = edge[:, D:].astype(BF16)

    @pl.when(core == 0)
    def _():
        x_ref[0:EDGE, :HALF] = edge[:, :HALF].astype(BF16)

    @pl.when(core == 1)
    def _():
        x_ref[0:EDGE, :HALF] = edge[:, HALF:D].astype(BF16)

    tile = 128

    def convolve(at):
        cols = pl.ds(at, CHUNK)
        taps = taps_ref[:, cols]
        bias = bias_ref[:, cols]
        for t in range(2 * n // tile):
            seen = x_ref[t * tile : (t + 1) * tile + EDGE, cols].astype(F32)
            total = bias + taps[KW - 1 : KW] * seen[EDGE:]
            for back in range(1, KW):
                total += taps[KW - 1 - back : KW - back] * pltpu.roll(seen, back, 0)[EDGE:]
            act_ref[t * tile : (t + 1) * tile, cols] = silu(total).astype(BF16)

    copies[0].wait()
    copies[2].wait()
    convolve(HALF)
    b_turned = act_ref[:, HALF : HALF + N].astype(F32).T.astype(BF16)
    ones = ones_ref[0]
    label = label_ref[0].astype(F32)
    class_weight = label / ones - (1.0 - label) / (sequences - ones)
    after = jnp.where(place < lax.axis_size("seq") - 2, later_ref[0:1], 0.0)
    after = pack(jnp.concatenate([after] * 16, axis=0))
    copies[1].wait()
    copies[3].wait()

    @pl.loop(0, HALF // CHUNK)
    def _(j):
        at = pl.multiple_of(j * CHUNK, CHUNK)
        cols = pl.ds(at, CHUNK)
        convolve(at)
        spread = spread_matrix(core * (H // 2) + j * (CHUNK // P_SIZE))
        table = dot(rows_ref[...], spread)
        ahead = dot(after, spread)[0:1]
        act = act_ref[:, cols].astype(F32)
        weighted = (act * dot(ws_ref[...], spread)).astype(BF16)
        early = dot(b_turned[:, :n], weighted[:n])
        late = dot(b_turned[:, n:], weighted[n:])
        state = table[1:2] * early + late
        early_ref[:, cols] = early.astype(BF16)
        state_ref[:, cols] = state.astype(BF16)
        read = act * dot(wr_ref[...], spread)
        high = read.astype(BF16)
        low = (read - high.astype(F32)).astype(BF16)
        seen = dot(b_turned, high) + dot(b_turned, low) + ahead * state
        read_ref[pl.ds(at, CHUNK)] = (class_weight * seen).T

    if split:
        x_bit = lax.rem(lax.axis_index("dp"), 2)
        part = D // 8
        for q in range(2):
            keep_ref[q * part : (q + 1) * part] = read_ref[pl.ds(pl.multiple_of((2 * q + x_bit) * part, 8), part)]
            send_ref[q * part : (q + 1) * part] = read_ref[pl.ds(pl.multiple_of((2 * q + 1 - x_bit) * part, 8), part)]
    else:
        keep_ref[...] = read_ref[...]
        send_ref[...] = jnp.zeros_like(send_ref)
    mine = pl.ds(pl.multiple_of(core * n, 16), n)
    act_own_ref[...] = act_ref[mine, :HALF]
    bc_ref[...] = act_ref[mine, HALF:]
    act_other_ref[...] = act_ref[pl.ds(pl.multiple_of((1 - core) * n, 16), n), :HALF]


def diagonal_kernel(act_own_ref, act_other_ref, bc_ref, ws_ref, e_ref, eg_ref, rows_ref, gate_ref, near_ref, far_ref):
    core = lax.rem(lax.axis_index("seq"), 2)
    n = act_own_ref.shape[0]
    scores = lax.dot_general(bc_ref[:, N:], bc_ref[:, :N], (((1,), (1,)), ((), ())), preferred_element_type=F32)
    row = lax.broadcasted_iota(jnp.int32, (n, n), 0)
    lane = lax.broadcasted_iota(jnp.int32, (n, n), 1)
    masked = jnp.where(row >= lane, scores, 0.0).astype(BF16)
    ws = ws_ref[pl.ds(pl.multiple_of(core * n, 16), n)]
    for side, source in enumerate((act_own_ref, act_other_ref)):
        half = core if side == 0 else 1 - core

        @pl.loop(0, HALF // CHUNK)
        def _(j):
            at = pl.multiple_of(j * CHUNK, CHUNK)
            cols = pl.ds(at, CHUNK)
            spread = spread_matrix(half * (H // 2) + j * (CHUNK // P_SIZE))
            act = source[:, cols].astype(F32)
            weighted = (act * dot(ws, spread)).astype(BF16)
            value = dot(eg_ref[...], spread) * dot(masked, weighted)
            value += dot(rows_ref[...], spread)[2:3] * act
            gate = silu(gate_ref[0, :, pl.ds(pl.multiple_of(half * HALF + at, CHUNK), CHUNK)].astype(F32))
            near_ref[side, :, cols] = value * gate
            far_ref[side, :, cols] = dot(e_ref[...], spread) * gate


def finish_kernel(near_ref, far_ref, bc_ref, h_own_ref, h_other_ref, early_own_ref, early_other_ref, rows_ref, gain_ref, out_ref, g_ref):
    place = lax.axis_index("seq")
    core = lax.rem(place, 2)
    n = bc_ref.shape[0]
    second = core == 1
    started = place >= 2
    squares = jnp.zeros((n, CHUNK), F32)
    c_vals = bc_ref[:, N:]
    for side in range(2):
        half = core if side == 0 else 1 - core
        h_ref = (h_own_ref, h_other_ref)[side]
        early_ref = (early_own_ref, early_other_ref)[side]
        for j in range(HALF // CHUNK):
            cols = pl.ds(j * CHUNK, CHUNK)
            spread = spread_matrix(half * (H // 2) + j * (CHUNK // P_SIZE))
            decay = jnp.where(second, dot(rows_ref[...], spread)[0:1], 1.0)
            h = jnp.where(started, h_ref[:, cols].astype(F32), 0.0) * decay
            h += jnp.where(second, early_ref[:, cols].astype(F32), 0.0)
            g = near_ref[side, :, cols] + far_ref[side, :, cols] * dot(c_vals, h.astype(BF16))
            g_ref[side, :, cols] = g
            squares += g * g
    scale = lax.rsqrt(jnp.sum(squares, axis=-1, keepdims=True) * (1.0 / D) + 1e-05)
    for side in range(2):
        half = core if side == 0 else 1 - core
        for j in range(HALF // CHUNK):
            cols = pl.ds(pl.multiple_of(half * HALF + j * CHUNK, CHUNK), CHUNK)
            g = g_ref[side, :, pl.ds(j * CHUNK, CHUNK)]
            out_ref[0, :, cols] = (g * scale * gain_ref[:, cols]).astype(BF16)


def halve_kernel(kept_ref, came_ref, keep_ref, send_ref, *, axis, divide):
    bit = lax.rem(lax.axis_index(axis) // divide, 2)
    part = keep_ref.shape[0]
    mine = pl.ds(pl.multiple_of(bit * part, 8), part)
    yours = pl.ds(pl.multiple_of((1 - bit) * part, 8), part)
    send_ref[...] = kept_ref[yours] + came_ref[yours]
    keep_ref[...] = kept_ref[mine] + came_ref[mine]


def halve(kept, came, axis, divide):
    part = jax.ShapeDtypeStruct((kept.shape[0] // 2, N), F32)
    return pl.pallas_call(
        functools.partial(halve_kernel, axis=axis, divide=divide),
        out_shape=(part, part),
        in_specs=[VMEM] * 2,
        out_specs=(VMEM, VMEM),
        compiler_params=params(8),
        cost_estimate=cost(kept.size, kept.size * 12),
        name="halve",
    )(kept, came)


def last_kernel(kept_ref, came_ref, first_ref, second_ref, third_ref):
    part = first_ref.shape[0]
    z_bit = lax.rem(lax.axis_index("dp") // 4, 2)
    core = lax.rem(lax.axis_index("seq"), 2)
    zero = kept_ref[0:part] + came_ref[0:part]
    one = kept_ref[part:] + came_ref[part:]
    ring_one = z_bit == 0
    first_ref[...] = jnp.where(ring_one, one, zero)
    cross_one = core == 0
    second_ref[...] = jnp.where(cross_one, one, zero)
    third_ref[...] = jnp.where(core == 0, zero, one)


def last_sum_kernel(own_ref, ring_ref, cross_ref, out_ref):
    z_bit = lax.rem(lax.axis_index("dp") // 4, 2)
    core = lax.rem(lax.axis_index("seq"), 2)
    same = z_bit == core
    out_ref[...] = ring_ref[...] + jnp.where(same, own_ref[...], cross_ref[...])


def steering_sum(keep, send):
    swap = lambda k: [(i, i ^ k) for i in range(8)]
    came = lax.ppermute(send, "dp", swap(1))
    keep, send = halve(keep, came, "dp", 2)
    came = lax.ppermute(send, "dp", swap(2))
    keep, send = halve(keep, came, "seq", 2)
    came = lax.ppermute(send, "seq", [(i, i ^ 2) for i in range(4)])
    part = jax.ShapeDtypeStruct((keep.shape[0] // 2, N), F32)
    first, second, third = pl.pallas_call(
        last_kernel, out_shape=(part,) * 3, in_specs=[VMEM] * 2, out_specs=(VMEM,) * 3, compiler_params=params(8), name="last_parts"
    )(keep, came)
    ring, cross = [], []
    for dp in range(8):
        for seq in range(4):
            z, core = dp // 4, seq % 2
            place = lambda z_to, core_to: (dp % 4 + 4 * z_to) * 4 + seq - core + core_to
            ring.append((dp * 4 + seq, place(core, 1 if z == 0 else 0)))
            cross.append((dp * 4 + seq, place(core, 1 - core) if z != core else dp * 4 + seq))
    ring = lax.ppermute(first, ("dp", "seq"), ring)
    cross = lax.ppermute(second, ("dp", "seq"), cross)
    return pl.pallas_call(
        last_sum_kernel, out_shape=part, in_specs=[VMEM] * 3, out_specs=VMEM, compiler_params=params(8), name="last_sum"
    )(third, ring, cross)


def on_device(xbc, gate_input, dt_raw, conv_weight, conv_bias, dt_bias, a_rate, d_skip, norm_gain, labels, readout):
    n = xbc.shape[1]
    places = lax.axis_size("seq")
    sequences = lax.axis_size("dp")
    chips = places // 2
    place = lax.axis_index("seq")
    core = place % 2
    split = sequences == 8 and places == 4
    pair = [(i, i ^ 1) for i in range(places)]
    shape = jax.ShapeDtypeStruct

    dt_other = lax.ppermute(dt_raw[0], "seq", pair)
    xbc_other = lax.ppermute(xbc, "seq", pair)
    tail = xbc[:, n - EDGE :, :]
    edge_a = lax.ppermute(tail, "seq", [(i, (i + 1) % places) for i in range(places)])
    edge_b = lax.ppermute(tail, "seq", [(i, (i + 2) % places) for i in range(places)])

    ws, wr, e, eg, rows, small = pl.pallas_call(
        steps_kernel,
        out_shape=(
            shape((2 * n, 128), BF16), shape((2 * n, 128), BF16), shape((n, 128), BF16), shape((n, 128), BF16),
            shape((16, 128), BF16), shape((8, H), F32),
        ),
        in_specs=[VMEM] * 5 + [SMEM],
        out_specs=(VMEM,) * 6,
        compiler_params=params(16),
        cost_estimate=cost(2 * 6 * n * n * 128, 8 * n * 256),
        name="steps",
    )(dt_raw[0], dt_other, dt_bias[None], a_rate[None], d_skip[None], readout)

    later = jnp.zeros_like(small)
    for step in range(chips - 1):
        out = small if step == 0 else small.at[0:1].add(small[1:2] * later[0:1])
        later = lax.ppermute(out, "seq", [(i, (i - 2) % places) for i in range(places)])
        if chips > 2:
            later = jnp.where(place < places - 2, later, 0.0)

    ones = labels.astype(F32)
    reach = 1
    while reach < sequences:
        ones = ones + lax.ppermute(ones, "dp", [(i, i ^ reach) for i in range(sequences)])
        reach *= 2

    read_rows = HALF // 2 if split else HALF
    state, early, keep, send, act_own, act_other, bc = pl.pallas_call(
        functools.partial(state_kernel, sequences=float(sequences), split=split),
        out_shape=(
            shape((N, HALF), BF16), shape((N, HALF), BF16), shape((read_rows, N), F32),
            shape((read_rows if split else 8, N), F32),
            shape((n, HALF), BF16), shape((n, HALF), BF16), shape((n, BC), BF16),
        ),
        in_specs=[ANY, ANY] + [VMEM] * 8 + [SMEM, SMEM],
        out_specs=(VMEM,) * 7,
        scratch_shapes=[
            pltpu.VMEM((EDGE + 2 * n, SIDE), BF16),
            pltpu.VMEM((2 * n, SIDE), BF16),
            pltpu.VMEM((KW, SIDE), F32),
            pltpu.VMEM((1, SIDE), F32),
            pltpu.VMEM((HALF, N), F32),
            pltpu.SemaphoreType.DMA((4,)),
        ],
        compiler_params=params(24),
        cost_estimate=cost(10 * 2 * n * N * HALF, 4 * 2 * n * SIDE),
        name="states",
    )(xbc, xbc_other, edge_a, edge_b, ws, wr, rows, later, conv_weight, conv_bias[None], ones, labels)

    h = state
    for step in range(chips - 1):
        if step:
            scale = jnp.repeat(lax.dynamic_slice_in_dim(small[1], core * (H // 2), H // 2), P_SIZE)
            h = (h.astype(F32) * scale + state.astype(F32)).astype(BF16)
        h = lax.ppermute(h, "seq", [(i, (i + 2) % places) for i in range(places)])
        if chips > 2:
            h = jnp.where(place >= 2, h, jnp.zeros_like(h))
    act_in = lax.ppermute(act_other, "seq", pair)
    early_in = lax.ppermute(early, "seq", pair)

    if split:
        steering = steering_sum(keep, send)
    else:
        whole = lax.dynamic_update_slice_in_dim(jnp.zeros((D, N), F32), keep, core * HALF, 0)
        steering = lax.psum_scatter(whole, ("dp", "seq"), scatter_dimension=0, tiled=True)

    near, far = pl.pallas_call(
        diagonal_kernel,
        out_shape=(shape((2, n, HALF), F32), shape((2, n, HALF), F32)),
        in_specs=[VMEM] * 8,
        out_specs=(VMEM, VMEM),
        compiler_params=params(24),
        cost_estimate=cost(8 * n * n * D, 4 * n * D),
        name="diagonal",
    )(act_own, act_in, bc, ws, e, eg, rows, gate_input)
    h_other = lax.ppermute(h, "seq", pair)
    layer_out = pl.pallas_call(
        finish_kernel,
        out_shape=shape((1, n, D), BF16),
        in_specs=[VMEM] * 9,
        out_specs=VMEM,
        scratch_shapes=[pltpu.VMEM((2, n, HALF), F32)],
        compiler_params=params(24),
        cost_estimate=cost(2 * n * N * D, 12 * n * D),
        name="finish",
    )(near, far, bc, h, h_other, early, early_in, rows, norm_gain[None])
    return (layer_out, steering)


def solution(mesh):
    return jax.shard_map(
        on_device,
        mesh=mesh,
        in_specs=(
            P("dp", "seq", None),
            P("dp", "seq", None),
            P("dp", "seq", None),
            P(),
            P(),
            P(),
            P(),
            P(),
            P(),
            P("dp"),
            P("dp", None),
        ),
        out_specs=(P("dp", "seq", None), P(("dp", "seq"), None)),
        check_vma=False,
    )
```

time: 262 us -> 70.7 us (0.27)
  the two profiles are of different devices: /device:TPU:0 before, /device:TPU:1 now
where the time goes in v1:
time: 70.7 us; the launch traced here: 70.3 us
  starting transfers between devices  27.8 us (39%)
  Pallas kernels  16.3 us (23%)
  waiting for transfers between devices  15.8 us (22%)
  local copies, waits for them, and re-layouts  7.23 us (10%)
  between operations  3.28 us (5%)
    ppermute x1, waiting for transfers between devices, steering_sum(): came = lax.ppermute(send, 'dp', swap(1))  7.35 us
    ppermute x3, starting transfers between devices, on_device(): lax.ppermute(ones, 'dp', [(i, i ^ reach) for i in range(sequences)])  7.18 us
    pallas_call x1, Pallas kernels, on_device(): pl.pallas_call(functools.partial(state_kernel, sequences=float(sequences)...  6.31 us
    unnamed x17, local copies, waits for them, and re-layouts  5.61 us
    ppermute x1, starting transfers between devices, steering_sum(): cross = lax.ppermute(second, ('dp', 'seq'), cross)  5.01 us
    pallas_call x1, Pallas kernels, on_device(): pl.pallas_call(diagonal_kernel, out_shape=(shape((2, n, HALF), F32), shap...  4.62 us
    ppermute x1, starting transfers between devices, on_device(): act_in = lax.ppermute(act_other, 'seq', pair)  3.35 us
    pallas_call x1, Pallas kernels, on_device(): pl.pallas_call(finish_kernel, out_shape=shape((1, n, D), BF16), in_specs=...  2.93 us
  transfers between devices with their start and end apart: 17, of which 7 were waited for; matrix products, arithmetic and copies ran while one was open for 4% of the time, Pallas kernels for 10%

profile of v1, /device:TPU:1, one launch (start us, length us, event | category | flops | bytes accessed | tf_op | source)
XLA Modules:
  0.0 70.3 jit_solution(17542496071219578288)
XLA Ops:
  0.8 0.9 %slice.3 = bf16[1,16,2816]{2,1,0:T(8,128)(2,1)S(1)} slice(bf16[1,256,2816]{2,1,0:T(8,128)(2,1)} %own_ref.1), slice={[0:1], [240:256], [0:2816]} | slice | bytes 180224 | tf_op jit(solution)/shard_map/slice | solution.py:340
  1.6 2.6 %collective-permute-start.1 = (bf16[1,16,2816]{2,1,0:T(8,128)(2,1)S(1)}, bf16[1,16,2816]{2,1,0:T(8,128)(2,1)S(1)}, u32[]{:S(2)}, u32[]{:S(2)}) collective-permute-start(bf16[1,16,2816]{2,1,0:T(8,128)(2,1)S(1)} %slice.3), channel_id=1, source_target_pairs={{0,1},{1,2},{2,3},{3,0},{4,5},{5,6},{6,7},{7,4},{8,9},{9,10},{10,1... | collective-permute-start | bytes 270344 | tf_op jit(solution)/shard_map/ppermute | solution.py:341
  4.4 0.8 %copy.13 = bf16[1,256,40]{2,1,0:T(8,128)(2,1)S(1)} copy(bf16[1,256,40]{1,2,0:T(8,128)(2,1)} %param.13) | data formatting | bytes 40960 | tf_op args[2]
  5.2 0.8 %collective-permute-start.3 = (bf16[256,40]{1,0:T(8,128)(2,1)S(1)}, bf16[256,40]{1,0:T(8,128)(2,1)S(1)}, u32[]{:S(2)}, u32[]{:S(2)}) collective-permute-start(bf16[256,40]{1,0:T(8,128)(2,1)S(1)} %bitcast.4), channel_id=1, source_target_pairs={{0,1},{1,0},{2,3},{3,2},{4,5},{5,4},{6,7},{7,6},{8,9},{9,8},{10,11... | collective-permute-start | bytes 61448 | tf_op jit(solution)/shard_map/ppermute | solution.py:338
  6.0 0.9 %collective-permute-done.3.other_ref = bf16[256,40]{1,0:T(8,128)(2,1)S(1)} collective-permute-done((bf16[256,40]{1,0:T(8,128)(2,1)S(1)}, bf16[256,40]{1,0:T(8,128)(2,1)S(1)}, u32[]{:S(2)}, u32[]{:S(2)}) %collective-permute-start.3) | collective-permute-done | bytes 20512 | tf_op jit(solution)/shard_map/ppermute | solution.py:338
  6.9 0.7 copy-done.3
  7.6 0.7 copy-done.4
  8.2 0.7 copy-done.5
  8.9 0.7 copy-done.6
  9.6 1.7 %steps.1 = (bf16[512,128]{1,0:T(8,128)(2,1)S(1)}, bf16[512,128]{1,0:T(8,128)(2,1)S(1)}, bf16[256,128]{1,0:T(8,128)(2,1)S(1)}, bf16[256,128]{1,0:T(8,128)(2,1)S(1...) custom-call(bf16[256,40]{1,0:T(8,128)(2,1)S(1)} %bitcast.5, bf16[256,40]{1,0:T(8,128)(2,1)S(1)} %collective-permute-done.3.other_ref, ...), custom_call_target="tpu_custom_call" | custom-call | flops 100663296 | bytes 524288 | tf_op jit(solution)/shard_map/steps/pallas_call | solution.py:344
  11.3 1.0 %collective-permute-start.4 = (f32[8,40]{1,0:T(8,128)S(1)}, f32[8,40]{1,0:T(8,128)S(1)}, u32[]{:S(2)}, u32[]{:S(2)}) collective-permute-start(f32[8,40]{1,0:T(8,128)S(1)} %get-tuple-element.27), channel_id=1, source_target_pairs={{0,2},{1,3},{2,0},{3,1},{4,6},{5,7},{6,4},{7,5},{8,10},{9,11},{10,... | collective-permute-start | bytes 3848 | tf_op jit(solution)/shard_map/ppermute | solution.py:360
  12.9 2.0 %collective-permute-start.5 = (f32[1]{0:T(128)}, f32[1]{0:T(128)}, u32[]{:S(2)}, u32[]{:S(2)}) collective-permute-start(f32[1]{0:T(128)} %convert_element_type.3), channel_id=1, source_target_pairs={{0,4},{4,0},{8,12},{12,8},{16,20},{20,16},{24,28},{28,24},{1,5},{5... | collective-permute-start | bytes 20 | tf_op jit(solution)/shard_map/ppermute | solution.py:367
  14.9 0.7 %broadcast_in_dim.18.conv_b_ref = f32[1,2816]{1,0:T(1,128)S(1)} reshape(f32[2816]{0:T(1024)} %param.15) | data formatting | bytes 22528 | tf_op jit(solution)/shard_map/broadcast_in_dim | solution.py:391
  16.2 2.1 %collective-permute-start.6 = (f32[1]{0:T(128)}, f32[1]{0:T(128)}, u32[]{:S(2)}, u32[]{:S(2)}) collective-permute-start(f32[1]{0:T(128)} %add.9), channel_id=1, source_target_pairs={{0,8},{4,12},{8,0},{12,4},{16,24},{20,28},{24,16},{28,20},{1,9},{5... | collective-permute-start | bytes 20 | tf_op jit(solution)/shard_map/ppermute | solution.py:367
  19.4 3.1 %collective-permute-start.7 = (f32[1]{0:T(128)}, f32[1]{0:T(128)}, u32[]{:S(2)}, u32[]{:S(2)}) collective-permute-start(f32[1]{0:T(128)} %add.10), channel_id=1, source_target_pairs={{0,16},{4,20},{8,24},{12,28},{16,0},{20,4},{24,8},{28,12},{1,17},{... | collective-permute-start | bytes 20 | tf_op jit(solution)/shard_map/ppermute | solution.py:367
  23.5 1.4 %copy-done = bf16[1,256,2816]{2,1,0:T(8,128)(2,1)S(1)} copy-done((bf16[1,256,2816]{2,1,0:T(8,128)(2,1)S(1)}, bf16[1,256,2816]{2,1,0:T(8,128)(2,1)}, u32[]{:S(2)}) %copy-start) | copy-done | bytes 1441816
  24.9 0.8 %copy-done.1 = f32[4,2816]{1,0:T(4,128)S(1)} copy-done((f32[4,2816]{1,0:T(4,128)S(1)}, f32[4,2816]{1,0:T(4,128)}, u32[]{:S(2)}) %copy-start.1) | copy-done | bytes 45080
  25.7 6.3 %states.1 = (bf16[128,1280]{1,0:T(8,128)(2,1)S(1)}, bf16[128,1280]{1,0:T(8,128)(2,1)S(1)}, f32[640,128]{1,0:T(8,128)S(1)}, f32[640,128]{1,0:T(8,128)S(1)}, bf16[...) custom-call(bf16[1,256,2816]{2,1,0:T(8,128)(2,1)S(1)} %copy-done, ...), custom_call_target="tpu_custom_call" | custom-call | flops 838860800 | bytes 3145728 | tf_op jit(solution)/shard_map/states/pallas_call | solution.py:371
  32.0 3.4 %collective-permute-start.8 = (bf16[256,1280]{1,0:T(8,128)(2,1)S(1)}, bf16[256,1280]{1,0:T(8,128)(2,1)S(1)}, u32[]{:S(2)}, u32[]{:S(2)}) collective-permute-start(bf16[256,1280]{1,0:T(8,128)(2,1)S(1)} %get-tuple-element.29), channel_id=1, source_target_pairs={{0,1},{1,0},{2,3},{3,2},{4,5},{5,4},{6,7},{7,6},{8,9},{9,8},{10,11... | collective-permute-start | bytes 1966088 | tf_op jit(solution)/shard_map/ppermute | solution.py:401
  35.4 1.2 %collective-permute-start.12 = (f32[640,128]{1,0:T(8,128)S(1)}, f32[640,128]{1,0:T(8,128)S(1)}, u32[]{:S(2)}, u32[]{:S(2)}) collective-permute-start(f32[640,128]{1,0:T(8,128)S(1)} %get-tuple-element.38), channel_id=1, source_target_pairs={{0,4},{4,0},{8,12},{12,8},{16,20},{20,16},{24,28},{28,24},{1,5},{5... | collective-permute-start | bytes 983048 | tf_op jit(solution)/shard_map/ppermute | solution.py:304
  36.6 0.7 %collective-permute-start.9 = (bf16[128,1280]{1,0:T(8,128)(2,1)S(1)}, bf16[128,1280]{1,0:T(8,128)(2,1)S(1)}, u32[]{:S(2)}, u32[]{:S(2)}) collective-permute-start(bf16[128,1280]{1,0:T(8,128)(2,1)S(1)} %get-tuple-element.35), channel_id=1, source_target_pairs={{0,2},{1,3},{2,0},{3,1},{4,6},{5,7},{6,4},{7,5},{8,10},{9,11},{10,... | collective-permute-start | bytes 983048 | tf_op jit(solution)/shard_map/ppermute | solution.py:398
  37.3 7.4 %collective-permute-done.12.came_ref = f32[640,128]{1,0:T(8,128)S(1)} collective-permute-done((f32[640,128]{1,0:T(8,128)S(1)}, f32[640,128]{1,0:T(8,128)S(1)}, u32[]{:S(2)}, u32[]{:S(2)}) %collective-permute-start.12) | collective-permute-done | bytes 327712 | tf_op jit(solution)/shard_map/ppermute | solution.py:304
  44.7 1.4 %collective-permute-start.13 = (f32[320,128]{1,0:T(8,128)S(1)}, f32[320,128]{1,0:T(8,128)S(1)}, u32[]{:S(2)}, u32[]{:S(2)}) collective-permute-start(f32[320,128]{1,0:T(8,128)S(1)} %get-tuple-element.40), channel_id=1, source_target_pairs={{0,8},{4,12},{8,0},{12,4},{16,24},{20,28},{24,16},{28,20},{1,9},{5... | collective-permute-start | bytes 491528 | tf_op jit(solution)/shard_map/ppermute | solution.py:306
  46.0 1.1 %collective-permute-start.11 = (bf16[128,1280]{1,0:T(8,128)(2,1)S(1)}, bf16[128,1280]{1,0:T(8,128)(2,1)S(1)}, u32[]{:S(2)}, u32[]{:S(2)}) collective-permute-start(bf16[128,1280]{1,0:T(8,128)(2,1)S(1)} %get-tuple-element.36.early_own_ref), channel_id=1, source_target_pairs={{0,1},{1,0},{2,3},{3,2},{4,5},{5,4},{6,7},{7,6},{8,9},{9,8},{10,11... | collective-permute-start | bytes 983048 | tf_op jit(solution)/shard_map/ppermute | solution.py:402
  47.2 2.4 %collective-permute-done.13.came_ref = f32[320,128]{1,0:T(8,128)S(1)} collective-permute-done((f32[320,128]{1,0:T(8,128)S(1)}, f32[320,128]{1,0:T(8,128)S(1)}, u32[]{:S(2)}, u32[]{:S(2)}) %collective-permute-start.13) | collective-permute-done | bytes 163872 | tf_op jit(solution)/shard_map/ppermute | solution.py:306
  49.6 0.8 %collective-permute-start.14 = (f32[160,128]{1,0:T(8,128)S(1)}, f32[160,128]{1,0:T(8,128)S(1)}, u32[]{:S(2)}, u32[]{:S(2)}) collective-permute-start(f32[160,128]{1,0:T(8,128)S(1)} %get-tuple-element.42), channel_id=1, source_target_pairs={{0,2},{1,3},{2,0},{3,1},{4,6},{5,7},{6,4},{7,5},{8,10},{9,11},{10,... | collective-permute-start | bytes 245768 | tf_op jit(solution)/shard_map/ppermute | solution.py:308
  50.4 2.6 %collective-permute-done.14.came_ref = f32[160,128]{1,0:T(8,128)S(1)} collective-permute-done((f32[160,128]{1,0:T(8,128)S(1)}, f32[160,128]{1,0:T(8,128)S(1)}, u32[]{:S(2)}, u32[]{:S(2)}) %collective-permute-start.14) | collective-permute-done | bytes 81952 | tf_op jit(solution)/shard_map/ppermute | solution.py:308
  53.0 2.4 %collective-permute-start.15 = (f32[80,128]{1,0:T(8,128)S(1)}, f32[80,128]{1,0:T(8,128)S(1)}, u32[]{:S(2)}, u32[]{:S(2)}) collective-permute-start(f32[80,128]{1,0:T(8,128)S(1)} %get-tuple-element.44), channel_id=1, source_target_pairs={{0,1},{1,17},{2,3},{3,19},{4,5},{5,21},{6,7},{7,23},{8,9},{9,25},{... | collective-permute-start | bytes 122888 | tf_op jit(solution)/shard_map/ppermute | solution.py:320
  55.4 5.0 %collective-permute-start.16 = (f32[80,128]{1,0:T(8,128)S(1)}, f32[80,128]{1,0:T(8,128)S(1)}, u32[]{:S(2)}, u32[]{:S(2)}) collective-permute-start(f32[80,128]{1,0:T(8,128)S(1)} %get-tuple-element.45), channel_id=1, source_target_pairs={{0,0},{1,16},{2,2},{3,18},{4,4},{5,20},{6,6},{7,22},{8,8},{9,24},{... | collective-permute-start | bytes 122888 | tf_op jit(solution)/shard_map/ppermute | solution.py:321
  60.5 1.6 %collective-permute-done.16.cross_ref = f32[80,128]{1,0:T(8,128)S(1)} collective-permute-done((f32[80,128]{1,0:T(8,128)S(1)}, f32[80,128]{1,0:T(8,128)S(1)}, u32[]{:S(2)}, u32[]{:S(2)}) %collective-permute-start.16) | collective-permute-done | bytes 40992 | tf_op jit(solution)/shard_map/ppermute | solution.py:321
  62.7 4.6 %diagonal.1 = (f32[2,256,1280]{2,1,0:T(8,128)S(1)}, f32[2,256,1280]{2,1,0:T(8,128)S(1)}) custom-call(bf16[256,1280]{1,0:T(8,128)(2,1)S(1)} %get-tuple-element.28.act_own_ref, bf16[256,1280]{1,0:T(8,128)(2,1)S(1)} %collective-permute-done.8.act_other_ref, bf16[256,256]{1,0:T(8,128)(2,1)S(1)} %get-tuple-element.30.bc_ref, ...), custom_call_target="tpu_custom_call" | custom-call | flops 1342177280 | bytes 2621440 | tf_op jit(solution)/shard_map/diagonal/pallas_call | solution.py:410
  67.4 2.9 %finish.1 = bf16[1,256,2560]{2,1,0:T(8,128)(2,1)} custom-call(f32[2,256,1280]{2,1,0:T(8,128)S(1)} %get-tuple-element.33.near_ref, f32[2,256,1280]{2,1,0:T(8,128)S(1)} %get-tuple-element.34.far_ref, bf16[256,256]{1,0:T(8,128)(2,1)S(1)} %get-tuple-element.30.bc_ref, bf16[128,1280]{1,0:T(8,128)(2,1)S(1)} %collective-permute-done.9.h_own_ref, ...), custom_call_target="tpu_custom_call" | custom-call | flops 167772160 | bytes 7864320 | tf_op jit(solution)/shard_map/finish/pallas_call | solution.py:420
  (30 shorter events, 1.9 us)
Async XLA Ops:
  0.6 22.9 %collective-permute-start = (bf16[1,256,2816]{2,1,0:T(8,128)(2,1)}, bf16[1,256,2816]{2,1,0:T(8,128)(2,1)S(1)}, u32[]{:S(2)}, u32[]{:S(2)}) collective-permute-start(bf16[1,256,2816]{2,1,0:T(8,128)(2,1)} %own_ref.1), channel_id=1, source_target_pairs={{0,1},{1,0},{2,3},{3,2},{4,5},{5,4},{6,7},{7,6},{8,9},{9,8},{10,11... | collective-permute-start | bytes 4325384 | tf_op jit(solution)/shard_map/ppermute | solution.py:339
  1.6 21.9 %collective-permute-start.1 = (bf16[1,16,2816]{2,1,0:T(8,128)(2,1)S(1)}, bf16[1,16,2816]{2,1,0:T(8,128)(2,1)S(1)}, u32[]{:S(2)}, u32[]{:S(2)}) collective-permute-start(bf16[1,16,2816]{2,1,0:T(8,128)(2,1)S(1)} %slice.3), channel_id=1, source_target_pairs={{0,1},{1,2},{2,3},{3,0},{4,5},{5,6},{6,7},{7,4},{8,9},{9,10},{10,1... | collective-permute-start | bytes 270344 | tf_op jit(solution)/shard_map/ppermute | solution.py:341
  4.2 19.3 %collective-permute-start.2 = (bf16[1,16,2816]{2,1,0:T(8,128)(2,1)S(1)}, bf16[1,16,2816]{2,1,0:T(8,128)(2,1)S(1)}, u32[]{:S(2)}, u32[]{:S(2)}) collective-permute-start(bf16[1,16,2816]{2,1,0:T(8,128)(2,1)S(1)} %slice.3), channel_id=1, source_target_pairs={{0,2},{1,3},{2,0},{3,1},{4,6},{5,7},{6,4},{7,5},{8,10},{9,11},{10,... | collective-permute-start | bytes 270344 | tf_op jit(solution)/shard_map/ppermute | solution.py:342
  5.2 1.7 %collective-permute-start.3 = (bf16[256,40]{1,0:T(8,128)(2,1)S(1)}, bf16[256,40]{1,0:T(8,128)(2,1)S(1)}, u32[]{:S(2)}, u32[]{:S(2)}) collective-permute-start(bf16[256,40]{1,0:T(8,128)(2,1)S(1)} %bitcast.4), channel_id=1, source_target_pairs={{0,1},{1,0},{2,3},{3,2},{4,5},{5,4},{6,7},{7,6},{8,9},{9,8},{10,11... | collective-permute-start | bytes 61448 | tf_op jit(solution)/shard_map/ppermute | solution.py:338
  6.9 0.7 copy-start.3
  7.6 0.7 copy-start.4
  8.2 0.7 copy-start.5
  8.9 0.7 copy-start.6
  11.3 12.2 %collective-permute-start.4 = (f32[8,40]{1,0:T(8,128)S(1)}, f32[8,40]{1,0:T(8,128)S(1)}, u32[]{:S(2)}, u32[]{:S(2)}) collective-permute-start(f32[8,40]{1,0:T(8,128)S(1)} %get-tuple-element.27), channel_id=1, source_target_pairs={{0,2},{1,3},{2,0},{3,1},{4,6},{5,7},{6,4},{7,5},{8,10},{9,11},{10,... | collective-permute-start | bytes 3848 | tf_op jit(solution)/shard_map/ppermute | solution.py:360
  12.9 2.7 %collective-permute-start.5 = (f32[1]{0:T(128)}, f32[1]{0:T(128)}, u32[]{:S(2)}, u32[]{:S(2)}) collective-permute-start(f32[1]{0:T(128)} %convert_element_type.3), channel_id=1, source_target_pairs={{0,4},{4,0},{8,12},{12,8},{16,20},{20,16},{24,28},{28,24},{1,5},{5... | collective-permute-start | bytes 20 | tf_op jit(solution)/shard_map/ppermute | solution.py:367
  16.2 2.6 %collective-permute-start.6 = (f32[1]{0:T(128)}, f32[1]{0:T(128)}, u32[]{:S(2)}, u32[]{:S(2)}) collective-permute-start(f32[1]{0:T(128)} %add.9), channel_id=1, source_target_pairs={{0,8},{4,12},{8,0},{12,4},{16,24},{20,28},{24,16},{28,20},{1,9},{5... | collective-permute-start | bytes 20 | tf_op jit(solution)/shard_map/ppermute | solution.py:367
  19.4 3.5 %collective-permute-start.7 = (f32[1]{0:T(128)}, f32[1]{0:T(128)}, u32[]{:S(2)}, u32[]{:S(2)}) collective-permute-start(f32[1]{0:T(128)} %add.10), channel_id=1, source_target_pairs={{0,16},{4,20},{8,24},{12,28},{16,0},{20,4},{24,8},{28,12},{1,17},{... | collective-permute-start | bytes 20 | tf_op jit(solution)/shard_map/ppermute | solution.py:367
  23.5 1.4 %copy-start = (bf16[1,256,2816]{2,1,0:T(8,128)(2,1)S(1)}, bf16[1,256,2816]{2,1,0:T(8,128)(2,1)}, u32[]{:S(2)}) copy-start(bf16[1,256,2816]{2,1,0:T(8,128)(2,1)} %own_ref.1) | copy-start | bytes 4325380
  24.9 0.8 %copy-start.1 = (f32[4,2816]{1,0:T(4,128)S(1)}, f32[4,2816]{1,0:T(4,128)}, u32[]{:S(2)}) copy-start(f32[4,2816]{1,0:T(4,128)} %conv_w_ref.1) | copy-start | bytes 135172
  25.7 34.7 %copy-start.7 = (f32[2560]{0:T(1024)S(1)}, f32[2560]{0:T(1024)}, u32[]{:S(2)}) copy-start(f32[2560]{0:T(1024)} %param.19) | copy-start | bytes 30724
  25.7 37.0 %copy-start.2 = (bf16[1,256,2560]{2,1,0:T(8,128)(2,1)S(1)}, bf16[1,256,2560]{2,1,0:T(8,128)(2,1)}, u32[]{:S(2)}) copy-start(bf16[1,256,2560]{2,1,0:T(8,128)(2,1)} %gate_ref.1) | copy-start | bytes 3932164
  32.0 30.7 %collective-permute-start.8 = (bf16[256,1280]{1,0:T(8,128)(2,1)S(1)}, bf16[256,1280]{1,0:T(8,128)(2,1)S(1)}, u32[]{:S(2)}, u32[]{:S(2)}) collective-permute-start(bf16[256,1280]{1,0:T(8,128)(2,1)S(1)} %get-tuple-element.29), channel_id=1, source_target_pairs={{0,1},{1,0},{2,3},{3,2},{4,5},{5,4},{6,7},{7,6},{8,9},{9,8},{10,11... | collective-permute-start | bytes 1966088 | tf_op jit(solution)/shard_map/ppermute | solution.py:401
  35.4 9.3 %collective-permute-start.12 = (f32[640,128]{1,0:T(8,128)S(1)}, f32[640,128]{1,0:T(8,128)S(1)}, u32[]{:S(2)}, u32[]{:S(2)}) collective-permute-start(f32[640,128]{1,0:T(8,128)S(1)} %get-tuple-element.38), channel_id=1, source_target_pairs={{0,4},{4,0},{8,12},{12,8},{16,20},{20,16},{24,28},{28,24},{1,5},{5... | collective-permute-start | bytes 983048 | tf_op jit(solution)/shard_map/ppermute | solution.py:304
  36.6 10.6 %collective-permute-start.9 = (bf16[128,1280]{1,0:T(8,128)(2,1)S(1)}, bf16[128,1280]{1,0:T(8,128)(2,1)S(1)}, u32[]{:S(2)}, u32[]{:S(2)}) collective-permute-start(bf16[128,1280]{1,0:T(8,128)(2,1)S(1)} %get-tuple-element.35), channel_id=1, source_target_pairs={{0,2},{1,3},{2,0},{3,1},{4,6},{5,7},{6,4},{7,5},{8,10},{9,11},{10,... | collective-permute-start | bytes 983048 | tf_op jit(solution)/shard_map/ppermute | solution.py:398
  44.7 4.9 %collective-permute-start.13 = (f32[320,128]{1,0:T(8,128)S(1)}, f32[320,128]{1,0:T(8,128)S(1)}, u32[]{:S(2)}, u32[]{:S(2)}) collective-permute-start(f32[320,128]{1,0:T(8,128)S(1)} %get-tuple-element.40), channel_id=1, source_target_pairs={{0,8},{4,12},{8,0},{12,4},{16,24},{20,28},{24,16},{28,20},{1,9},{5... | collective-permute-start | bytes 491528 | tf_op jit(solution)/shard_map/ppermute | solution.py:306
  46.0 21.3 %collective-permute-start.11 = (bf16[128,1280]{1,0:T(8,128)(2,1)S(1)}, bf16[128,1280]{1,0:T(8,128)(2,1)S(1)}, u32[]{:S(2)}, u32[]{:S(2)}) collective-permute-start(bf16[128,1280]{1,0:T(8,128)(2,1)S(1)} %get-tuple-element.36.early_own_ref), channel_id=1, source_target_pairs={{0,1},{1,0},{2,3},{3,2},{4,5},{5,4},{6,7},{7,6},{8,9},{9,8},{10,11... | collective-permute-start | bytes 983048 | tf_op jit(solution)/shard_map/ppermute | solution.py:402
  47.2 20.2 %collective-permute-start.10 = (bf16[128,1280]{1,0:T(8,128)(2,1)S(1)}, bf16[128,1280]{1,0:T(8,128)(2,1)S(1)}, u32[]{:S(2)}, u32[]{:S(2)}) collective-permute-start(bf16[128,1280]{1,0:T(8,128)(2,1)S(1)} %collective-permute-done.9.h_own_ref), channel_id=1, source_target_pairs={{0,1},{1,0},{2,3},{3,2},{4,5},{5,4},{6,7},{7,6},{8,9},{9,8},{10,11... | collective-permute-start | bytes 983048 | tf_op jit(solution)/shard_map/ppermute | solution.py:419
  49.6 3.4 %collective-permute-start.14 = (f32[160,128]{1,0:T(8,128)S(1)}, f32[160,128]{1,0:T(8,128)S(1)}, u32[]{:S(2)}, u32[]{:S(2)}) collective-permute-start(f32[160,128]{1,0:T(8,128)S(1)} %get-tuple-element.42), channel_id=1, source_target_pairs={{0,2},{1,3},{2,0},{3,1},{4,6},{5,7},{6,4},{7,5},{8,10},{9,11},{10,... | collective-permute-start | bytes 245768 | tf_op jit(solution)/shard_map/ppermute | solution.py:308
  53.0 7.4 %collective-permute-start.15 = (f32[80,128]{1,0:T(8,128)S(1)}, f32[80,128]{1,0:T(8,128)S(1)}, u32[]{:S(2)}, u32[]{:S(2)}) collective-permute-start(f32[80,128]{1,0:T(8,128)S(1)} %get-tuple-element.44), channel_id=1, source_target_pairs={{0,1},{1,17},{2,3},{3,19},{4,5},{5,21},{6,7},{7,23},{8,9},{9,25},{... | collective-permute-start | bytes 122888 | tf_op jit(solution)/shard_map/ppermute | solution.py:320
  55.4 6.7 %collective-permute-start.16 = (f32[80,128]{1,0:T(8,128)S(1)}, f32[80,128]{1,0:T(8,128)S(1)}, u32[]{:S(2)}, u32[]{:S(2)}) collective-permute-start(f32[80,128]{1,0:T(8,128)S(1)} %get-tuple-element.45), channel_id=1, source_target_pairs={{0,0},{1,16},{2,2},{3,18},{4,4},{5,20},{6,6},{7,22},{8,8},{9,24},{... | collective-permute-start | bytes 122888 | tf_op jit(solution)/shard_map/ppermute | solution.py:321

commit v2 on v1

v2 whole, which is shorter than its diff:
```python
import functools

import jax
import jax.numpy as jnp
from jax import lax
from jax.experimental import pallas as pl
from jax.experimental.pallas import tpu as pltpu
from jax.sharding import PartitionSpec as P

H = 40
P_SIZE = 64
N = 128
KW = 4
R = 4
D = H * P_SIZE
HALF = D // 2
BC = 2 * N
SIDE = HALF + BC
CH = D + BC
CHUNK = 256
EDGE = 16
F32 = jnp.float32
BF16 = jnp.bfloat16
VMEM = pl.BlockSpec(memory_space=pltpu.VMEM)
SMEM = pl.BlockSpec(memory_space=pltpu.SMEM)
ANY = pl.BlockSpec(memory_space=pl.ANY)
HBM = pl.BlockSpec(memory_space=pltpu.HBM)
MIB = 1024 * 1024


def params(mib):
    return pltpu.CompilerParams(vmem_limit_bytes=mib * MIB)


def cost(flops, read):
    return pl.CostEstimate(flops=flops, bytes_accessed=read, transcendentals=0)


def in_hbm(x):
    return pltpu.with_memory_space_constraint(x, pltpu.HBM)


def tied(x, *others):
    return lax.optimization_barrier((x,) + others)[0]


def dot(a, b):
    return jnp.dot(a, b, preferred_element_type=F32)


def pack(w):
    high = w.astype(BF16).astype(F32)
    gap = jnp.zeros((64 - H, w.shape[1]), F32)
    return jnp.concatenate([high, gap, w - high, gap], axis=0).T.astype(BF16)


def beside(columns):
    lane = lax.broadcasted_iota(jnp.int32, (H, 128), 1)
    table = jnp.zeros((H, 128), F32)
    for i, column in enumerate(columns):
        table = jnp.where(lane == i, column, table)
    return table


def turned(rows):
    table = jnp.concatenate(list(rows) + [jnp.zeros((8 - len(rows), H), F32)], axis=0)
    return jnp.concatenate([table, jnp.zeros((8, 128 - H), F32)], axis=1).T[:H]


def spread_matrix(first_head):
    row = lax.broadcasted_iota(jnp.int32, (128, CHUNK), 0)
    lane = lax.broadcasted_iota(jnp.int32, (128, CHUNK), 1)
    hit = (row & 63) == first_head + lane // P_SIZE
    return jnp.where(hit, 1.0, 0.0).astype(BF16)


def silu(v):
    half = 0.5 * v
    return half + half * jnp.tanh(half)


def fetch(pairs, sems):
    copies = [pltpu.make_async_copy(source, to, sems.at[i]) for i, (source, to) in enumerate(pairs)]
    for copy in copies:
        copy.start()
    for copy in copies:
        copy.wait()


def step_sizes(raw, bias):
    raw = raw + bias
    return jnp.maximum(raw, 0.0) + jnp.log1p(jnp.exp(-jnp.abs(raw)))


def running_sums(steps):
    n = steps[0].shape[1]
    row = lax.broadcasted_iota(jnp.int32, (n, n), 0)
    lane = lax.broadcasted_iota(jnp.int32, (n, n), 1)
    upper = jnp.where(row <= lane, 1.0, 0.0).astype(BF16)
    parts = []
    for step in steps:
        high = step.astype(BF16).astype(F32)
        middle = (step - high).astype(BF16).astype(F32)
        parts += [high, middle, step - high - middle]
    sums = dot(jnp.concatenate(parts, axis=0).astype(BF16), upper)
    return [sums[i : i + H] + (sums[i + H : i + 2 * H] + sums[i + 2 * H : i + 3 * H]) for i in range(0, 3 * H * len(steps), 3 * H)]


def read_levels(points, base, total):
    n = total[0].shape[1]
    index = lax.broadcasted_iota(jnp.int32, (H, n), 1)
    found = []
    for r in range(R):
        at = points[r : r + 1, 0:1] - base
        inside = jnp.where((at >= 0) & (at < 2 * n), 1.0, 0.0)
        level = jnp.zeros((H, n), F32)
        for block in range(2):
            level += jnp.where(index + block * n == at, total[block], 0.0)
        found.append((at, inside, jnp.sum(level, axis=1, keepdims=True)))
    return found


def carry_of(found):
    carry = jnp.zeros((H, 1), F32)
    for _, inside, level in found:
        carry += inside * jnp.exp(level)
    return carry * (1.0 / R)


def tail_kernel(
    xbc_hbm, dt_hbm, bias_hbm, rate_hbm, skip_hbm, points_hbm, label_hbm, out_ref, mark_ref, dt_ref, columns_ref, points_ref,
    bias_ref, rate_ref, skip_ref, spot_ref, label_ref, sems,
):
    n = xbc_hbm.shape[1]
    width = xbc_hbm.shape[2]
    rows = xbc_hbm.at[0, pl.ds(n - EDGE, EDGE)]
    fetch(
        (
            (dt_hbm, dt_ref), (rows, out_ref.at[:, pl.ds(0, width)]), (label_hbm, label_ref), (points_hbm, spot_ref),
            (bias_hbm, bias_ref.at[0]), (rate_hbm, rate_ref.at[0]), (skip_hbm, skip_ref.at[0]),
        ),
        sems,
    )
    mark_ref[...] = jnp.zeros(mark_ref.shape, F32) + label_ref[0].astype(F32)
    steps = jnp.concatenate([dt_ref[0].astype(F32), jnp.zeros((-H % EDGE, n), F32)], axis=0).astype(BF16)
    for i in range(-(-H // EDGE)):
        out_ref[:, width + i * n : width + (i + 1) * n] = steps[i * EDGE : (i + 1) * EDGE]
    columns_ref[...] = turned((bias_ref[...], rate_ref[...], skip_ref[...]))
    spot = lax.broadcasted_iota(jnp.int32, points_ref.shape, 0)
    points = jnp.zeros(points_ref.shape, jnp.int32)
    for r in range(R):
        points = jnp.where(spot == r, spot_ref[0, r], points)
    points_ref[...] = points


def steps_kernel(own_ref, other_ref, columns_ref, points_ref, ws_ref, wr_ref, e_ref, rows_ref, small_ref):
    place = lax.axis_index("seq")
    core = lax.rem(place, 2)
    n = own_ref.shape[2]
    own = own_ref[0].astype(F32)
    other = other_ref[0].astype(F32)
    bias, rate, skip = columns_ref[:, 0:1], columns_ref[:, 1:2], columns_ref[:, 2:3]
    first = core == 0
    dts = [step_sizes(jnp.where(first == (block == 0), own, other), bias) for block in range(2)]
    cums = running_sums([-rate * dt for dt in dts])
    ends = [cum[:, n - 1 : n] for cum in cums]
    for block in range(2):
        ws_ref[block * n : (block + 1) * n] = pack(dts[block] * jnp.exp(ends[block] - cums[block]))
    total = [cums[0], ends[0] + cums[1]]
    index = lax.broadcasted_iota(jnp.int32, (H, n), 1)
    weight = [jnp.zeros((H, n), F32), jnp.zeros((H, n), F32)]
    found = read_levels(points_ref[...], (place - core) * n, total)
    for at, inside, level in found:
        for block in range(2):
            seen = jnp.where(index + block * n <= at, jnp.exp(jnp.minimum(level - total[block], 0.0)), 0.0)
            weight[block] += inside * seen
    for block in range(2):
        wr_ref[block * n : (block + 1) * n] = pack(weight[block] * dts[block] * (1.0 / R))
    e_ref[...] = pack(jnp.exp(jnp.where(first, cums[0], cums[1])))
    decay = [jnp.exp(end) for end in ends]
    back = jnp.exp(-jnp.where(first, ends[0], ends[1]))
    rows_ref[...] = pack(beside((decay[0], decay[1], skip, back)))[0:16]
    whole = beside((carry_of(found), jnp.exp(ends[0] + ends[1])))
    small_ref[...] = jnp.concatenate([whole, jnp.zeros((128 - H, 128), F32)], axis=0).T[0:8]


def later_kernel(same_ref, cross_ref, columns_ref, points_ref, later_ref):
    place = lax.axis_index("seq")
    core = lax.rem(place, 2)
    slabs = -(-H // EDGE)
    n = (same_ref.shape[1] - CH) // slabs

    def steps_of(ref):
        slab = [ref[:, CH + i * n : CH + (i + 1) * n].astype(F32) for i in range(slabs)]
        return jnp.concatenate(slab, axis=0)[:H]

    same, cross = steps_of(same_ref), steps_of(cross_ref)
    bias, rate = columns_ref[:, 0:1], columns_ref[:, 1:2]
    raws = [jnp.where((core == 0) == (block == 0), same, cross) for block in range(2)]
    cums = running_sums([-rate * step_sizes(raw, bias) for raw in raws])
    total = [cums[0], cums[0][:, n - 1 : n] + cums[1]]
    carry = carry_of(read_levels(points_ref[...], 2 * n, total))
    later_ref[...] = pack(beside((jnp.where(place < 2, carry, 0.0),)))[0:16]


def state_kernel(
    own_ref, other_ref, edge_a_ref, edge_b_ref, ws_ref, wr_ref, rows_ref, later_ref, conv_w_ref, conv_b_ref,
    state_ref, early_ref, act_own_ref, act_other_ref, bc_ref, *rest,
    split,
):
    reads = rest[:-6]
    x_ref, act_ref, taps_ref, bias_ref, read_ref, sems = rest[-6:]
    place = lax.axis_index("seq")
    core = lax.rem(place, 2)
    n = own_ref.shape[1]
    col = pl.multiple_of(core * HALF, 128)
    copies = []
    for i, (source, to) in enumerate(((own_ref, core), (other_ref, 1 - core))):
        rows = pl.ds(pl.multiple_of(EDGE + to * n, 16), n)
        copies.append(pltpu.make_async_copy(source.at[0, :, pl.ds(D, BC)], x_ref.at[rows, pl.ds(HALF, BC)], sems.at[2 * i]))
        copies.append(pltpu.make_async_copy(source.at[0, :, pl.ds(col, HALF)], x_ref.at[rows, pl.ds(0, HALF)], sems.at[2 * i + 1]))
    for i, (source, from_at, to_at, width) in enumerate(((conv_w_ref, D, HALF, BC), (conv_w_ref, col, 0, HALF))):
        copies.append(pltpu.make_async_copy(source.at[:, pl.ds(from_at, width)], taps_ref.at[:, pl.ds(to_at, width)], sems.at[4 + i]))
    for i, (from_at, to_at, width) in enumerate(((D, HALF, BC), (col, 0, HALF))):
        copies.append(pltpu.make_async_copy(conv_b_ref.at[pl.ds(from_at, width)], bias_ref.at[0, pl.ds(to_at, width)], sems.at[6 + i]))
    for i in (0, 2, 4, 6, 1, 3, 5, 7):
        copies[i].start()
    started = jnp.where(place >= 2, 1.0, 0.0)
    edge = jnp.where(core == 0, edge_a_ref[:, :CH].astype(F32), edge_b_ref[:, :CH].astype(F32)) * started
    x_ref[0:EDGE, HALF:] = edge[:, D:].astype(BF16)

    @pl.when(core == 0)
    def _():
        x_ref[0:EDGE, :HALF] = edge[:, :HALF].astype(BF16)

    @pl.when(core == 1)
    def _():
        x_ref[0:EDGE, :HALF] = edge[:, HALF:D].astype(BF16)

    tile = 128

    def convolve(at):
        cols = pl.ds(at, CHUNK)
        taps = taps_ref[:, cols]
        bias = bias_ref[:, cols]
        for t in range(2 * n // tile):
            seen = x_ref[t * tile : (t + 1) * tile + EDGE, cols].astype(F32)
            before = pltpu.roll(seen, 1, 0)
            pair = taps[1:2] * seen + taps[0:1] * before
            total = bias + taps[3:4] * seen[EDGE:] + taps[2:3] * before[EDGE:]
            total += pltpu.roll(pair, 2, 0)[EDGE:]
            act_ref[t * tile : (t + 1) * tile, cols] = silu(total).astype(BF16)

    for i in (0, 2, 4, 6):
        copies[i].wait()
    convolve(HALF)
    b_turned = act_ref[:, HALF : HALF + N].astype(F32).T.astype(BF16)
    for i in (1, 3, 5, 7):
        copies[i].wait()

    @pl.loop(0, HALF // CHUNK)
    def _(j):
        at = pl.multiple_of(j * CHUNK, CHUNK)
        cols = pl.ds(at, CHUNK)
        convolve(at)
        spread = spread_matrix(core * (H // 2) + j * (CHUNK // P_SIZE))
        table = dot(rows_ref[...], spread)
        ahead = dot(later_ref[...], spread)[0:1]
        act = act_ref[:, cols].astype(F32)
        weighted = (act * dot(ws_ref[...], spread)).astype(BF16)
        early = dot(b_turned[:, :n], weighted[:n])
        late = dot(b_turned[:, n:], weighted[n:])
        state = table[1:2] * early + late
        early_ref[:, cols] = early.astype(BF16)
        state_ref[:, cols] = state.astype(BF16)
        read = act * dot(wr_ref[...], spread)
        high = read.astype(BF16)
        low = (read - high.astype(F32)).astype(BF16)
        seen = dot(b_turned, high) + dot(b_turned, low) + ahead * state
        read_ref[pl.ds(at, CHUNK)] = seen.T

    if split:
        part = D // 16
        x_bit = lax.rem(lax.axis_index("dp"), 2)
        z_bit = lax.rem(lax.axis_index("dp") // 2, 2)

        def rows(z, x, y):
            return read_ref[pl.ds(pl.multiple_of((4 * z + 2 * x + y) * part, 8), part)]

        for q in range(2):
            here = slice(q * part, (q + 1) * part)
            reads[0][here] = rows(q, x_bit, 0)
            reads[1][here] = rows(q, 1 - x_bit, 0)
            reads[2][here] = rows(z_bit, q, 1)
            reads[3][here] = rows(1 - z_bit, q, 1)
    else:
        reads[0][...] = read_ref[...]
    mine = pl.ds(pl.multiple_of(core * n, 16), n)
    act_own_ref[...] = act_ref[mine, :HALF]
    bc_ref[...] = act_ref[mine, HALF:]
    act_other_ref[...] = act_ref[pl.ds(pl.multiple_of((1 - core) * n, 16), n), :HALF]


def diagonal_kernel(act_own_ref, act_other_ref, bc_ref, ws_ref, e_ref, rows_ref, gate_ref, near_ref, far_ref):
    core = lax.rem(lax.axis_index("seq"), 2)
    n = act_own_ref.shape[0]
    scores = lax.dot_general(bc_ref[:, N:], bc_ref[:, :N], (((1,), (1,)), ((), ())), preferred_element_type=F32)
    row = lax.broadcasted_iota(jnp.int32, (n, n), 0)
    lane = lax.broadcasted_iota(jnp.int32, (n, n), 1)
    masked = jnp.where(row >= lane, scores, 0.0).astype(BF16)
    ws = ws_ref[pl.ds(pl.multiple_of(core * n, 16), n)]
    for side, source in enumerate((act_own_ref, act_other_ref)):
        half = core if side == 0 else 1 - core

        @pl.loop(0, HALF // CHUNK)
        def _(j):
            at = pl.multiple_of(j * CHUNK, CHUNK)
            cols = pl.ds(at, CHUNK)
            spread = spread_matrix(half * (H // 2) + j * (CHUNK // P_SIZE))
            act = source[:, cols].astype(F32)
            weighted = (act * dot(ws, spread)).astype(BF16)
            table = dot(rows_ref[...], spread)
            decay = dot(e_ref[...], spread)
            value = decay * (table[3:4] * dot(masked, weighted)) + table[2:3] * act
            gate = silu(gate_ref[0, :, pl.ds(pl.multiple_of(half * HALF + at, CHUNK), CHUNK)].astype(F32))
            near_ref[side, :, cols] = value * gate
            far_ref[side, :, cols] = decay * gate


def finish_kernel(near_ref, far_ref, bc_ref, h_own_ref, h_other_ref, early_own_ref, early_other_ref, rows_ref, gain_hbm, out_ref, g_ref, gain_ref, sem):
    place = lax.axis_index("seq")
    core = lax.rem(place, 2)
    n = bc_ref.shape[0]
    second = core == 1
    started = place >= 2
    gain = pltpu.make_async_copy(gain_hbm, gain_ref.at[0], sem)
    gain.start()
    squares = jnp.zeros((n, CHUNK), F32)
    c_vals = bc_ref[:, N:]
    for side in range(2):
        half = core if side == 0 else 1 - core
        h_ref = (h_own_ref, h_other_ref)[side]
        early_ref = (early_own_ref, early_other_ref)[side]
        for j in range(HALF // CHUNK):
            cols = pl.ds(j * CHUNK, CHUNK)
            spread = spread_matrix(half * (H // 2) + j * (CHUNK // P_SIZE))
            decay = jnp.where(second, dot(rows_ref[...], spread)[0:1], 1.0)
            h = jnp.where(started, h_ref[:, cols].astype(F32), 0.0) * decay
            h += jnp.where(second, early_ref[:, cols].astype(F32), 0.0)
            g = near_ref[side, :, cols] + far_ref[side, :, cols] * dot(c_vals, h.astype(BF16))
            g_ref[side, :, cols] = g
            squares += g * g
    gain.wait()
    scale = lax.rsqrt(jnp.sum(squares, axis=-1, keepdims=True) * (1.0 / D) + 1e-05)
    for side in range(2):
        half = core if side == 0 else 1 - core
        for j in range(HALF // CHUNK):
            cols = pl.ds(pl.multiple_of(half * HALF + j * CHUNK, CHUNK), CHUNK)
            g = g_ref[side, :, pl.ds(j * CHUNK, CHUNK)]
            out_ref[0, :, cols] = (g * scale * gain_ref[:, cols]).astype(BF16)


def join_kernel(mark_ref, a_ref, b_ref, out_ref):
    row = lax.broadcasted_iota(jnp.int32, out_ref.shape, 0)
    out_ref[...] = jnp.where(row == 0, a_ref[...] + b_ref[...], mark_ref[...])


def join(mark, a, b):
    out = jax.ShapeDtypeStruct(a.shape, a.dtype)
    return pl.pallas_call(
        join_kernel, out_shape=out, in_specs=[VMEM] * 3, out_specs=VMEM, compiler_params=params(8), name="join"
    )(mark, a, b)


def halves_kernel(
    kept_x_ref, came_x_ref, kept_z_ref, came_z_ref, mark_ref, x_mark_ref, z_mark_ref, sum_ref,
    keep_a_ref, send_a_ref, keep_b_ref, send_b_ref,
    *, sequences,
):
    ones = sum_ref[0:1] + x_mark_ref[0:1]

    def weight(mark):
        return mark / ones - (1.0 - mark) / (sequences - ones)

    own = weight(mark_ref[1:2])
    part = keep_a_ref.shape[0]
    place = lax.axis_index("dp")
    x_bit = lax.rem(place, 2)
    z_bit = lax.rem(place // 2, 2)
    work = (
        (kept_x_ref, came_x_ref, x_mark_ref, z_bit, keep_a_ref, send_a_ref),
        (kept_z_ref, came_z_ref, z_mark_ref, x_bit, keep_b_ref, send_b_ref),
    )
    for kept, came, other_mark, bit, keep, send in work:
        other = weight(other_mark[1:2])
        mine = pl.ds(pl.multiple_of(bit * part, 8), part)
        yours = pl.ds(pl.multiple_of((1 - bit) * part, 8), part)
        send[...] = own * kept[yours] + other * came[yours]
        keep[...] = own * kept[mine] + other * came[mine]


def join_y_kernel(keep_a_ref, came_a_ref, keep_b_ref, came_b_ref, keep_ref, send_ref):
    first = lax.rem(lax.axis_index("seq") // 2, 2) == 0
    a = keep_a_ref[...] + came_a_ref[...]
    b = keep_b_ref[...] + came_b_ref[...]
    keep_ref[...] = jnp.where(first, a, b)
    send_ref[...] = jnp.where(first, b, a)


def last_kernel(kept_ref, came_ref, sum_ref):
    sum_ref[...] = kept_ref[...] + came_ref[...]


def core_kernel(kept_ref, came_ref, own_ref, send_ref):
    part = own_ref.shape[0]
    zero = kept_ref[0:part] + came_ref[0:part]
    one = kept_ref[part:] + came_ref[part:]
    first = lax.rem(lax.axis_index("seq"), 2) == 0
    own_ref[...] = jnp.where(first, zero, one)
    send_ref[...] = jnp.where(first, one, zero)


def owner_kernel(own_ref, came_ref, out_ref):
    z_bit = lax.rem(lax.axis_index("dp") // 4, 2)
    out_ref[...] = jnp.where(z_bit == lax.rem(lax.axis_index("seq"), 2), own_ref[...], came_ref[...])


def swap(k):
    return [(i, i ^ k) for i in range(8)]


def small_call(kernel, name, count, rows, *args):
    part = jax.ShapeDtypeStruct((rows, N), F32)
    return pl.pallas_call(
        kernel, out_shape=(part,) * count, in_specs=[VMEM] * len(args), out_specs=(VMEM,) * count, compiler_params=params(8), name=name
    )(*args)


def on_device(xbc, gate_input, dt_raw, conv_weight, conv_bias, dt_bias, a_rate, d_skip, norm_gain, labels, readout):
    n = xbc.shape[1]
    places = lax.axis_size("seq")
    sequences = lax.axis_size("dp")
    chips = places // 2
    place = lax.axis_index("seq")
    core = place % 2
    split = sequences == 8 and places == 4
    pair = [(i, i ^ 1) for i in range(places)]
    shape = jax.ShapeDtypeStruct

    one_back = [(i, i ^ 3) for i in range(4)] if chips == 2 else [(i, (i + 1) % places) for i in range(places)]
    two_back = [(i, (i + 2) % places) for i in range(places)]
    dt_turned = jnp.swapaxes(dt_raw, 1, 2)
    dt_other = lax.ppermute(dt_turned, "seq", pair)
    xbc_other = lax.ppermute(xbc, "seq", pair)
    xbc_here = in_hbm(xbc)
    tail, mark, dt_own, columns, points = pl.pallas_call(
        tail_kernel,
        out_shape=(
            shape((EDGE, CH + -(-H // EDGE) * n), BF16), shape((8, N), F32), shape((1, H, n), BF16),
            shape((H, 8), F32), shape((8, 128), jnp.int32),
        ),
        in_specs=[HBM] * 7,
        out_specs=(VMEM,) * 5,
        scratch_shapes=[pltpu.VMEM((1, H), F32)] * 3
        + [pltpu.SMEM((1, R), jnp.int32), pltpu.SMEM((1,), jnp.int32), pltpu.SemaphoreType.DMA((7,))],
        compiler_params=params(8),
        name="tail",
    )(xbc_here, in_hbm(dt_turned), in_hbm(dt_bias), in_hbm(a_rate), in_hbm(d_skip), in_hbm(readout), labels)
    edge_a = lax.ppermute(tail, "seq", one_back)
    edge_b = lax.ppermute(tail, "seq", two_back)

    ws, wr, e, rows, small = pl.pallas_call(
        steps_kernel,
        out_shape=(
            shape((2 * n, 128), BF16), shape((2 * n, 128), BF16), shape((n, 128), BF16), shape((16, 128), BF16), shape((8, 128), F32),
        ),
        in_specs=[VMEM] * 4,
        out_specs=(VMEM,) * 5,
        compiler_params=params(16),
        cost_estimate=cost(2 * 6 * n * n * 128, 8 * n * 256),
        name="steps",
    )(dt_own, dt_other, columns, points)

    if chips == 2:
        later = pl.pallas_call(
            later_kernel,
            out_shape=shape((16, 128), BF16),
            in_specs=[VMEM] * 4,
            out_specs=VMEM,
            compiler_params=params(16),
            cost_estimate=cost(2 * 6 * n * n * 128, 8 * n * 256),
            name="later",
        )(edge_b, edge_a, columns, points)
    else:
        later = jnp.zeros_like(small)
        for step in range(chips - 1):
            out = small.at[0:1].add(small[1:2] * later[0:1])
            later = lax.ppermute(out, "seq", [(i, (i - 2) % places) for i in range(places)])
            later = jnp.where(place < places - 2, later, 0.0)
        later = pack(jnp.broadcast_to(later[0, :H, None], (H, 16)))

    if split:
        z_mark = lax.ppermute(mark, "dp", swap(2))
        half = join(tied(mark, ws), mark, z_mark)
        quarter = join(tied(mark, later), half, lax.ppermute(half, "dp", swap(4)))
        later = tied(later, quarter)

    read_rows = D // 8 if split else HALF
    state, early, act_own, act_other, bc, *reads = pl.pallas_call(
        functools.partial(state_kernel, split=split),
        out_shape=(
            shape((N, HALF), BF16), shape((N, HALF), BF16),
            shape((n, HALF), BF16), shape((n, HALF), BF16), shape((n, BC), BF16),
        ) + (shape((read_rows, N), F32),) * (4 if split else 1),
        in_specs=[HBM, ANY] + [VMEM] * 6 + [HBM, HBM],
        out_specs=(VMEM,) * (9 if split else 6),
        scratch_shapes=[
            pltpu.VMEM((EDGE + 2 * n, SIDE), BF16),
            pltpu.VMEM((2 * n, SIDE), BF16),
            pltpu.VMEM((KW, SIDE), F32),
            pltpu.VMEM((1, SIDE), F32),
            pltpu.VMEM((HALF, N), F32),
            pltpu.SemaphoreType.DMA((8,)),
        ],
        compiler_params=params(24),
        cost_estimate=cost(50 * n * n * D, 4 * 2 * n * SIDE),
        name="states",
    )(xbc_here, xbc_other, edge_a, edge_b, ws, wr, rows, later, in_hbm(conv_weight), in_hbm(conv_bias))

    h = state
    for step in range(chips - 1):
        if step:
            scale = jnp.repeat(lax.dynamic_slice_in_dim(small[1, :H], core * (H // 2), H // 2), P_SIZE)
            h = (h.astype(F32) * scale + state.astype(F32)).astype(BF16)
        h = lax.ppermute(h, "seq", two_back)
        if chips > 2:
            h = jnp.where(place >= 2, h, jnp.zeros_like(h))
    act_in = lax.ppermute(act_other, "seq", pair)
    early_in = lax.ppermute(early, "seq", pair)
    if split:
        keep_x, send_x, keep_z, send_z = reads
        x_mark = lax.ppermute(tied(quarter, send_x), "dp", swap(1))
        came_x = lax.ppermute(send_x, "dp", swap(1))
        came_z = lax.ppermute(send_z, "dp", swap(2))

    near, reach = pl.pallas_call(
        diagonal_kernel,
        out_shape=(shape((2, n, HALF), F32), shape((2, n, HALF), F32)),
        in_specs=[VMEM] * 7,
        out_specs=(VMEM, VMEM),
        compiler_params=params(24),
        cost_estimate=cost(28 * n * n * D, 4 * n * D),
        name="diagonal",
    )(act_own, act_in, bc, ws, e, rows, gate_input)
    if split:
        keep_x, near, reach = lax.optimization_barrier((keep_x, near, reach))
        keep_a, send_a, keep_b, send_b = small_call(
            functools.partial(halves_kernel, sequences=float(sequences)), "halves", 4, D // 16,
            keep_x, came_x, keep_z, came_z, mark, x_mark, z_mark, quarter,
        )
        came_a = lax.ppermute(send_a, "dp", swap(2))
        came_b = lax.ppermute(send_b, "dp", swap(1))
        keep, send = small_call(join_y_kernel, "join_y", 2, D // 16, keep_a, came_a, keep_b, came_b)
        came = lax.ppermute(send, "seq", [(i, i ^ 2) for i in range(places)])
    h = tied(h, keep) if split else h
    h_other = lax.ppermute(h, "seq", pair)
    layer_out = pl.pallas_call(
        finish_kernel,
        out_shape=shape((1, n, D), BF16),
        in_specs=[VMEM] * 8 + [ANY],
        out_specs=VMEM,
        scratch_shapes=[pltpu.VMEM((2, n, HALF), F32), pltpu.VMEM((1, D), F32), pltpu.SemaphoreType.DMA(())],
        compiler_params=params(24),
        cost_estimate=cost(20 * n * n * D, 12 * n * D),
        name="finish",
    )(near, reach, bc, h, h_other, early, early_in, rows, norm_gain)
    if split:
        (total,) = small_call(last_kernel, "last_y", 1, D // 16, keep, came)
        came = lax.ppermute(total, "dp", swap(4))
        total, layer_out = lax.optimization_barrier((total, layer_out))
        own, send = small_call(core_kernel, "cores", 2, D // 32, total, came)
        came = lax.ppermute(send, "seq", pair)
        steering = small_call(owner_kernel, "owner", 1, D // 32, own, came)[0]
    else:
        ones = lax.psum(mark[0, 0], "dp")
        weight = mark[0, 0] / ones - (1.0 - mark[0, 0]) / (sequences - ones)
        whole = lax.dynamic_update_slice_in_dim(jnp.zeros((D, N), F32), weight * reads[0], core * HALF, 0)
        steering = lax.psum_scatter(whole, ("dp", "seq"), scatter_dimension=0, tiled=True)
    return (layer_out, steering)


def solution(mesh):
    return jax.shard_map(
        on_device,
        mesh=mesh,
        in_specs=(
            P("dp", "seq", None),
            P("dp", "seq", None),
            P("dp", "seq", None),
            P(),
            P(),
            P(),
            P(),
            P(),
            P(),
            P("dp"),
            P("dp", None),
        ),
        out_specs=(P("dp", "seq", None), P(("dp", "seq"), None)),
        check_vma=False,
    )
```

time: 70.7 us -> 49.7 us (0.70)
  the two profiles are of different devices: /device:TPU:1 before, /device:TPU:0 now
where the time goes in v2:
time: 49.7 us; the launch traced here: 49.5 us
  starting transfers between devices  20 us (40%)
  Pallas kernels  17.7 us (36%)
  waiting for transfers between devices  10.4 us (21%)
  between operations  1.43 us (3%)
    pallas_call x1, Pallas kernels, on_device(): pl.pallas_call(functools.partial(state_kernel, split=split), out_shape=(s...  7.01 us
    pallas_call x1, Pallas kernels, on_device(): pl.pallas_call(diagonal_kernel, out_shape=(shape((2, n, HALF), F32), shap...  4.12 us
    ppermute x1, waiting for transfers between devices, on_device(): came = lax.ppermute(send, 'seq', [(i, i ^ 2) for i in range(places)])  3.45 us
    ppermute x1, starting transfers between devices, on_device(): quarter = join(tied(mark, later), half, lax.ppermute(half, 'dp', swap(4)))  2.9 us
    pallas_call x1, Pallas kernels, on_device(): pl.pallas_call(finish_kernel, out_shape=shape((1, n, D), BF16), in_specs=...  2.87 us
    ppermute x1, starting transfers between devices, on_device(): edge_a = lax.ppermute(tail, 'seq', one_back)  2.71 us
    ppermute x1, starting transfers between devices, on_device(): came = lax.ppermute(total, 'dp', swap(4))  2.64 us
    ppermute x1, waiting for transfers between devices, on_device(): came_a = lax.ppermute(send_a, 'dp', swap(2))  2.51 us
  transfers between devices with their start and end apart: 18, of which 7 were waited for; matrix products, arithmetic and copies ran while one was open for 0% of the time, Pallas kernels for 20%

profile of v2, /device:TPU:0, one launch (start us, length us, event | category | flops | bytes accessed | tf_op | source)
XLA Modules:
  0.0 49.5 jit_solution(5347223107419892547)
XLA Ops:
  0.6 0.5 %collective-permute-start = (bf16[1,256,2816]{2,1,0:T(8,128)(2,1)}, bf16[1,256,2816]{2,1,0:T(8,128)(2,1)S(1)}, u32[]{:S(2)}, u32[]{:S(2)}) collective-permute-start(bf16[1,256,2816]{2,1,0:T(8,128)(2,1)} %own_ref.1), channel_id=1, source_target_pairs={{0,1},{1,0},{2,3},{3,2},{4,5},{5,4},{6,7},{7,6},{8,9},{9,8},{10,11... | collective-permute-start | bytes 4325384 | tf_op jit(solution)/shard_map/ppermute | solution.py:454
  1.8 1.1 %tail.1 = (bf16[16,3584]{1,0:T(8,128)(2,1)S(1)}, f32[8,128]{1,0:T(8,128)S(1)}, bf16[1,40,256]{2,1,0:T(8,128)(2,1)S(1)}, f32[40,8]{1,0:T(8,128)S(1)}, s32[8,128]{1,0:T(8,128)S(1)}) custom-call(bf16[1,256,2816]{2,1,0:T(8,128)(2,1)} %own_ref.1, bf16[1,40,256]{2,1,0:T(8,128)(2,1)} %bitcast.1, f32[40]{0:T(128)} %bias_hbm.1, f32[40]{0:T(128)} %rate_hbm.1, ...), custom_call_target="tpu_custom_call" | custom-call | tf_op jit(solution)/shard_map/tail/pallas_call | solution.py:456
  2.9 2.7 %collective-permute-start.1 = (bf16[16,3584]{1,0:T(8,128)(2,1)S(1)}, bf16[16,3584]{1,0:T(8,128)(2,1)S(1)}, u32[]{:S(2)}, u32[]{:S(2)}) collective-permute-start(bf16[16,3584]{1,0:T(8,128)(2,1)S(1)} %get-tuple-element.40), channel_id=1, source_target_pairs={{0,3},{1,2},{2,1},{3,0},{4,7},{5,6},{6,5},{7,4},{8,11},{9,10},{10,... | collective-permute-start | bytes 344072 | tf_op jit(solution)/shard_map/ppermute | solution.py:469
  5.6 0.2 collective-permute-start.3
  5.8 1.9 %collective-permute-start.4 = (f32[8,128]{1,0:T(8,128)S(1)}, f32[8,128]{1,0:T(8,128)S(1)}, u32[]{:S(2)}, u32[]{:S(2)}) collective-permute-start(f32[8,128]{1,0:T(8,128)S(1)} %get-tuple-element.49.mark_ref.a_ref), channel_id=1, source_target_pairs={{0,8},{4,12},{8,0},{12,4},{16,24},{20,28},{24,16},{28,20},{1,9},{5... | collective-permute-start | bytes 12296 | tf_op jit(solution)/shard_map/ppermute | solution.py:503
  7.7 1.3 %steps.1 = (bf16[512,128]{1,0:T(8,128)(2,1)S(1)}, bf16[512,128]{1,0:T(8,128)(2,1)S(1)}, bf16[256,128]{1,0:T(8,128)(2,1)S(1)}, bf16[16,128]{1,0:T(8,128)(2,1)S(1)}, f32[8,128]{1,0:T(8,128)}) custom-call(bf16[1,40,256]{2,1,0:T(8,128)(2,1)S(1)} %get-tuple-element.41.own_ref, bf16[1,40,256]{2,1,0:T(8,128)(2,1)S(1)} %collective-permute-done.3.other_ref, ...), custom_call_target="tpu_custom_call" | custom-call | flops 100663296 | bytes 524288 | tf_op jit(solution)/shard_map/steps/pallas_call | solution.py:472
  9.0 0.4 collective-permute-done.4.b_ref.z_mark_ref
  9.4 2.9 %collective-permute-start.5 = (f32[8,128]{1,0:T(8,128)S(1)}, f32[8,128]{1,0:T(8,128)S(1)}, u32[]{:S(2)}, u32[]{:S(2)}) collective-permute-start(f32[8,128]{1,0:T(8,128)S(1)} %join.2.a_ref), channel_id=1, source_target_pairs={{0,16},{4,20},{8,24},{12,28},{16,0},{20,4},{24,8},{28,12},{1,17},{... | collective-permute-start | bytes 12296 | tf_op jit(solution)/shard_map/ppermute | solution.py:505
  12.3 0.5 %later.1.later_ref = bf16[16,128]{1,0:T(8,128)(2,1)S(1)} custom-call(bf16[16,3584]{1,0:T(8,128)(2,1)S(1)} %collective-permute-done.2.same_ref.edge_b_ref, bf16[16,3584]{1,0:T(8,128)(2,1)S(1)} %collective-permute-done.1.cross_ref.edge_a_ref, f32[40,8]{1,0:T(8,128)S(1)} %get-tuple-element.42.columns_ref, s32[8,128]{1,0:T(8,128)S(1)} %get-tuple-element.43.points_ref), custom_call_target="tpu_custom_call" | custom-call | flops 100663296 | bytes 524288 | tf_op jit(solution)/shard_map/later/pallas_call | solution.py:485
  12.9 1.0 %collective-permute-done.5.b_ref = f32[8,128]{1,0:T(8,128)S(1)} collective-permute-done((f32[8,128]{1,0:T(8,128)S(1)}, f32[8,128]{1,0:T(8,128)S(1)}, u32[]{:S(2)}, u32[]{:S(2)}) %collective-permute-start.5) | collective-permute-done | bytes 4128 | tf_op jit(solution)/shard_map/ppermute | solution.py:505
  13.9 0.0 copy-start
  13.9 7.0 %states.1 = (bf16[128,1280]{1,0:T(8,128)(2,1)S(1)}, bf16[128,1280]{1,0:T(8,128)(2,1)S(1)}, bf16[256,1280]{1,0:T(8,128)(2,1)S(1)}, bf16[256,1280]{1,0:T(8,128)(2,...) custom-call(bf16[1,256,2816]{2,1,0:T(8,128)(2,1)} %own_ref.1, ...), custom_call_target="tpu_custom_call" | custom-call | flops 8388608000 | bytes 3145728 | tf_op jit(solution)/shard_map/states/pallas_call | solution.py:509
  20.9 0.1 collective-permute-start.6
  21.0 1.9 %collective-permute-start.7 = (f32[320,128]{1,0:T(8,128)S(1)}, f32[320,128]{1,0:T(8,128)S(1)}, u32[]{:S(2)}, u32[]{:S(2)}) collective-permute-start(f32[320,128]{1,0:T(8,128)S(1)} %get-tuple-element.59), channel_id=1, source_target_pairs={{0,4},{4,0},{8,12},{12,8},{16,20},{20,16},{24,28},{28,24},{1,5},{5... | collective-permute-start | bytes 491528 | tf_op jit(solution)/shard_map/ppermute | solution.py:543
  22.9 0.2 collective-permute-start.9
  23.1 1.9 %collective-permute-start.8 = (f32[320,128]{1,0:T(8,128)S(1)}, f32[320,128]{1,0:T(8,128)S(1)}, u32[]{:S(2)}, u32[]{:S(2)}) collective-permute-start(f32[320,128]{1,0:T(8,128)S(1)} %get-tuple-element.61), channel_id=1, source_target_pairs={{0,8},{4,12},{8,0},{12,4},{16,24},{20,28},{24,16},{28,20},{1,9},{5... | collective-permute-start | bytes 491528 | tf_op jit(solution)/shard_map/ppermute | solution.py:544
  25.0 1.5 %collective-permute-start.13 = (bf16[128,1280]{1,0:T(8,128)(2,1)S(1)}, bf16[128,1280]{1,0:T(8,128)(2,1)S(1)}, u32[]{:S(2)}, u32[]{:S(2)}) collective-permute-start(bf16[128,1280]{1,0:T(8,128)(2,1)S(1)} %get-tuple-element.71), channel_id=1, source_target_pairs={{0,2},{1,3},{2,0},{3,1},{4,6},{5,7},{6,4},{7,5},{8,10},{9,11},{10,... | collective-permute-start | bytes 983048 | tf_op jit(solution)/shard_map/ppermute | solution.py:535
  26.5 4.1 %diagonal.1 = (f32[2,256,1280]{2,1,0:T(8,128)S(1)}, f32[2,256,1280]{2,1,0:T(8,128)S(1)}) custom-call(bf16[256,1280]{1,0:T(8,128)(2,1)S(1)} %get-tuple-element.52.act_own_ref, bf16[256,1280]{1,0:T(8,128)(2,1)S(1)} %collective-permute-done.6.act_other_ref, bf16[256,256]{1,0:T(8,128)(2,1)S(1)} %get-tuple-element.54.bc_ref, ...), custom_call_target="tpu_custom_call" | custom-call | flops 4697620480 | bytes 2621440 | tf_op jit(solution)/shard_map/diagonal/pallas_call | solution.py:546
  30.7 0.1 halves.1
  30.8 0.5 %collective-permute-start.10 = (f32[160,128]{1,0:T(8,128)S(1)}, f32[160,128]{1,0:T(8,128)S(1)}, u32[]{:S(2)}, u32[]{:S(2)}) collective-permute-start(f32[160,128]{1,0:T(8,128)S(1)} %get-tuple-element.64), channel_id=1, source_target_pairs={{0,8},{4,12},{8,0},{12,4},{16,24},{20,28},{24,16},{28,20},{1,9},{5... | collective-permute-start | bytes 245768 | tf_op jit(solution)/shard_map/ppermute | solution.py:561
  31.3 1.5 %collective-permute-start.11 = (f32[160,128]{1,0:T(8,128)S(1)}, f32[160,128]{1,0:T(8,128)S(1)}, u32[]{:S(2)}, u32[]{:S(2)}) collective-permute-start(f32[160,128]{1,0:T(8,128)S(1)} %get-tuple-element.66), channel_id=1, source_target_pairs={{0,4},{4,0},{8,12},{12,8},{16,20},{20,16},{24,28},{28,24},{1,5},{5... | collective-permute-start | bytes 245768 | tf_op jit(solution)/shard_map/ppermute | solution.py:562
  32.8 2.5 %collective-permute-done.10.came_a_ref = f32[160,128]{1,0:T(8,128)S(1)} collective-permute-done((f32[160,128]{1,0:T(8,128)S(1)}, f32[160,128]{1,0:T(8,128)S(1)}, u32[]{:S(2)}, u32[]{:S(2)}) %collective-permute-start.10) | collective-permute-done | bytes 81952 | tf_op jit(solution)/shard_map/ppermute | solution.py:561
  35.3 0.5 collective-permute-done.11.came_b_ref
  35.8 0.1 collective-permute-start.14
  35.9 1.4 %collective-permute-start.12 = (f32[160,128]{1,0:T(8,128)S(1)}, f32[160,128]{1,0:T(8,128)S(1)}, u32[]{:S(2)}, u32[]{:S(2)}) collective-permute-start(f32[160,128]{1,0:T(8,128)S(1)} %get-tuple-element.68), channel_id=1, source_target_pairs={{0,2},{1,3},{2,0},{3,1},{4,6},{5,7},{6,4},{7,5},{8,10},{9,11},{10,... | collective-permute-start | bytes 245768 | tf_op jit(solution)/shard_map/ppermute | solution.py:564
  37.3 3.5 %collective-permute-done.12.came_ref = f32[160,128]{1,0:T(8,128)S(1)} collective-permute-done((f32[160,128]{1,0:T(8,128)S(1)}, f32[160,128]{1,0:T(8,128)S(1)}, u32[]{:S(2)}, u32[]{:S(2)}) %collective-permute-start.12) | collective-permute-done | bytes 81952 | tf_op jit(solution)/shard_map/ppermute | solution.py:564
  40.7 2.6 %collective-permute-start.16 = (f32[160,128]{1,0:T(8,128)S(1)}, f32[160,128]{1,0:T(8,128)S(1)}, u32[]{:S(2)}, u32[]{:S(2)}) collective-permute-start(f32[160,128]{1,0:T(8,128)S(1)} %last_y.1.kept_ref), channel_id=1, source_target_pairs={{0,16},{4,20},{8,24},{12,28},{16,0},{20,4},{24,8},{28,12},{1,17},{... | collective-permute-start | bytes 245768 | tf_op jit(solution)/shard_map/ppermute | solution.py:579
  43.4 2.9 %finish.1 = bf16[1,256,2560]{2,1,0:T(8,128)(2,1)} custom-call(f32[2,256,1280]{2,1,0:T(8,128)S(1)} %get-tuple-element.69.near_ref, f32[2,256,1280]{2,1,0:T(8,128)S(1)} %get-tuple-element.70.far_ref, bf16[256,256]{1,0:T(8,128)(2,1)S(1)} %get-tuple-element.54.bc_ref, bf16[128,1280]{1,0:T(8,128)(2,1)S(1)} %collective-permute-done.13.h_own_ref, ...), custom_call_target="tpu_custom_call" | custom-call | flops 3355443200 | bytes 7864320 | tf_op jit(solution)/shard_map/finish/pallas_call | solution.py:567
  46.3 1.3 %collective-permute-done.16.came_ref = f32[160,128]{1,0:T(8,128)S(1)} collective-permute-done((f32[160,128]{1,0:T(8,128)S(1)}, f32[160,128]{1,0:T(8,128)S(1)}, u32[]{:S(2)}, u32[]{:S(2)}) %collective-permute-start.16) | collective-permute-done | bytes 81952 | tf_op jit(solution)/shard_map/ppermute | solution.py:579
  47.6 0.1 collective-permute-start.17
  47.7 1.2 %collective-permute-done.17.came_ref = f32[80,128]{1,0:T(8,128)S(1)} collective-permute-done((f32[80,128]{1,0:T(8,128)S(1)}, f32[80,128]{1,0:T(8,128)S(1)}, u32[]{:S(2)}, u32[]{:S(2)}) %collective-permute-start.17) | collective-permute-done | bytes 40992 | tf_op jit(solution)/shard_map/ppermute | solution.py:582
  48.9 0.6 %owner.1 = f32[80,128]{1,0:T(8,128)} custom-call(f32[80,128]{1,0:T(8,128)S(1)} %get-tuple-element.76.own_ref, f32[80,128]{1,0:T(8,128)S(1)} %collective-permute-done.17.came_ref), custom_call_target="tpu_custom_call" | custom-call | tf_op jit(solution)/shard_map/owner/pallas_call | solution.py:434
  (23 shorter events, 0.1 us)
Async XLA Ops:
  0.6 5.0 %copy-start.2 = (bf16[1,256,40]{1,2,0:T(8,128)(2,1)S(1)}, bf16[1,256,40]{1,2,0:T(8,128)(2,1)}, u32[]{:S(2)}) copy-start(bf16[1,256,40]{1,2,0:T(8,128)(2,1)} %param.13) | copy-start | bytes 61444
  0.6 13.3 %collective-permute-start = (bf16[1,256,2816]{2,1,0:T(8,128)(2,1)}, bf16[1,256,2816]{2,1,0:T(8,128)(2,1)S(1)}, u32[]{:S(2)}, u32[]{:S(2)}) collective-permute-start(bf16[1,256,2816]{2,1,0:T(8,128)(2,1)} %own_ref.1), channel_id=1, source_target_pairs={{0,1},{1,0},{2,3},{3,2},{4,5},{5,4},{6,7},{7,6},{8,9},{9,8},{10,11... | collective-permute-start | bytes 4325384 | tf_op jit(solution)/shard_map/ppermute | solution.py:454
  2.9 9.4 %collective-permute-start.1 = (bf16[16,3584]{1,0:T(8,128)(2,1)S(1)}, bf16[16,3584]{1,0:T(8,128)(2,1)S(1)}, u32[]{:S(2)}, u32[]{:S(2)}) collective-permute-start(bf16[16,3584]{1,0:T(8,128)(2,1)S(1)} %get-tuple-element.40), channel_id=1, source_target_pairs={{0,3},{1,2},{2,1},{3,0},{4,7},{5,6},{6,5},{7,4},{8,11},{9,10},{10,... | collective-permute-start | bytes 344072 | tf_op jit(solution)/shard_map/ppermute | solution.py:469
  5.6 6.7 %collective-permute-start.2 = (bf16[16,3584]{1,0:T(8,128)(2,1)S(1)}, bf16[16,3584]{1,0:T(8,128)(2,1)S(1)}, u32[]{:S(2)}, u32[]{:S(2)}) collective-permute-start(bf16[16,3584]{1,0:T(8,128)(2,1)S(1)} %get-tuple-element.40), channel_id=1, source_target_pairs={{0,2},{1,3},{2,0},{3,1},{4,6},{5,7},{6,4},{7,5},{8,10},{9,11},{10,... | collective-permute-start | bytes 344072 | tf_op jit(solution)/shard_map/ppermute | solution.py:470
  5.6 2.1 %collective-permute-start.3 = (bf16[1,40,256]{2,1,0:T(8,128)(2,1)S(1)}, bf16[1,40,256]{2,1,0:T(8,128)(2,1)S(1)}, u32[]{:S(2)}, u32[]{:S(2)}) collective-permute-start(bf16[1,40,256]{2,1,0:T(8,128)(2,1)S(1)} %bitcast.2), channel_id=1, source_target_pairs={{0,1},{1,0},{2,3},{3,2},{4,5},{5,4},{6,7},{7,6},{8,9},{9,8},{10,11... | collective-permute-start | bytes 61448 | tf_op jit(solution)/shard_map/ppermute | solution.py:453
  5.8 3.6 %collective-permute-start.4 = (f32[8,128]{1,0:T(8,128)S(1)}, f32[8,128]{1,0:T(8,128)S(1)}, u32[]{:S(2)}, u32[]{:S(2)}) collective-permute-start(f32[8,128]{1,0:T(8,128)S(1)} %get-tuple-element.49.mark_ref.a_ref), channel_id=1, source_target_pairs={{0,8},{4,12},{8,0},{12,4},{16,24},{20,28},{24,16},{28,20},{1,9},{5... | collective-permute-start | bytes 12296 | tf_op jit(solution)/shard_map/ppermute | solution.py:503
  9.4 4.5 %collective-permute-start.5 = (f32[8,128]{1,0:T(8,128)S(1)}, f32[8,128]{1,0:T(8,128)S(1)}, u32[]{:S(2)}, u32[]{:S(2)}) collective-permute-start(f32[8,128]{1,0:T(8,128)S(1)} %join.2.a_ref), channel_id=1, source_target_pairs={{0,16},{4,20},{8,24},{12,28},{16,0},{20,4},{24,8},{28,12},{1,17},{... | collective-permute-start | bytes 12296 | tf_op jit(solution)/shard_map/ppermute | solution.py:505
  13.9 12.6 %copy-start = (bf16[1,256,2560]{2,1,0:T(8,128)(2,1)S(1)}, bf16[1,256,2560]{2,1,0:T(8,128)(2,1)}, u32[]{:S(2)}) copy-start(bf16[1,256,2560]{2,1,0:T(8,128)(2,1)} %gate_ref.1) | copy-start | bytes 3932164
  20.9 5.6 %collective-permute-start.6 = (bf16[256,1280]{1,0:T(8,128)(2,1)S(1)}, bf16[256,1280]{1,0:T(8,128)(2,1)S(1)}, u32[]{:S(2)}, u32[]{:S(2)}) collective-permute-start(bf16[256,1280]{1,0:T(8,128)(2,1)S(1)} %get-tuple-element.53), channel_id=1, source_target_pairs={{0,1},{1,0},{2,3},{3,2},{4,5},{5,4},{6,7},{7,6},{8,9},{9,8},{10,11... | collective-permute-start | bytes 1966088 | tf_op jit(solution)/shard_map/ppermute | solution.py:538
  21.0 9.7 %collective-permute-start.7 = (f32[320,128]{1,0:T(8,128)S(1)}, f32[320,128]{1,0:T(8,128)S(1)}, u32[]{:S(2)}, u32[]{:S(2)}) collective-permute-start(f32[320,128]{1,0:T(8,128)S(1)} %get-tuple-element.59), channel_id=1, source_target_pairs={{0,4},{4,0},{8,12},{12,8},{16,20},{20,16},{24,28},{28,24},{1,5},{5... | collective-permute-start | bytes 491528 | tf_op jit(solution)/shard_map/ppermute | solution.py:543
  22.9 7.8 %collective-permute-start.9 = (f32[8,128]{1,0:T(8,128)S(1)}, f32[8,128]{1,0:T(8,128)S(1)}, u32[]{:S(2)}, u32[]{:S(2)}) collective-permute-start(f32[8,128]{1,0:T(8,128)S(1)} %join.3.sum_ref), channel_id=1, source_target_pairs={{0,4},{4,0},{8,12},{12,8},{16,20},{20,16},{24,28},{28,24},{1,5},{5... | collective-permute-start | bytes 12296 | tf_op jit(solution)/shard_map/ppermute | solution.py:542
  23.1 7.6 %collective-permute-start.8 = (f32[320,128]{1,0:T(8,128)S(1)}, f32[320,128]{1,0:T(8,128)S(1)}, u32[]{:S(2)}, u32[]{:S(2)}) collective-permute-start(f32[320,128]{1,0:T(8,128)S(1)} %get-tuple-element.61), channel_id=1, source_target_pairs={{0,8},{4,12},{8,0},{12,4},{16,24},{20,28},{24,16},{28,20},{1,9},{5... | collective-permute-start | bytes 491528 | tf_op jit(solution)/shard_map/ppermute | solution.py:544
  25.0 10.8 %collective-permute-start.13 = (bf16[128,1280]{1,0:T(8,128)(2,1)S(1)}, bf16[128,1280]{1,0:T(8,128)(2,1)S(1)}, u32[]{:S(2)}, u32[]{:S(2)}) collective-permute-start(bf16[128,1280]{1,0:T(8,128)(2,1)S(1)} %get-tuple-element.71), channel_id=1, source_target_pairs={{0,2},{1,3},{2,0},{3,1},{4,6},{5,7},{6,4},{7,5},{8,10},{9,11},{10,... | collective-permute-start | bytes 983048 | tf_op jit(solution)/shard_map/ppermute | solution.py:535
  26.5 16.8 %copy-start.1 = (f32[2560]{0:T(1024)S(1)}, f32[2560]{0:T(1024)}, u32[]{:S(2)}) copy-start(f32[2560]{0:T(1024)} %gain_hbm.1) | copy-start | bytes 30724
  30.8 4.5 %collective-permute-start.10 = (f32[160,128]{1,0:T(8,128)S(1)}, f32[160,128]{1,0:T(8,128)S(1)}, u32[]{:S(2)}, u32[]{:S(2)}) collective-permute-start(f32[160,128]{1,0:T(8,128)S(1)} %get-tuple-element.64), channel_id=1, source_target_pairs={{0,8},{4,12},{8,0},{12,4},{16,24},{20,28},{24,16},{28,20},{1,9},{5... | collective-permute-start | bytes 245768 | tf_op jit(solution)/shard_map/ppermute | solution.py:561
  31.3 4.4 %collective-permute-start.11 = (f32[160,128]{1,0:T(8,128)S(1)}, f32[160,128]{1,0:T(8,128)S(1)}, u32[]{:S(2)}, u32[]{:S(2)}) collective-permute-start(f32[160,128]{1,0:T(8,128)S(1)} %get-tuple-element.66), channel_id=1, source_target_pairs={{0,4},{4,0},{8,12},{12,8},{16,20},{20,16},{24,28},{28,24},{1,5},{5... | collective-permute-start | bytes 245768 | tf_op jit(solution)/shard_map/ppermute | solution.py:562
  32.8 10.6 %collective-permute-start.15 = (bf16[128,1280]{1,0:T(8,128)(2,1)S(1)}, bf16[128,1280]{1,0:T(8,128)(2,1)S(1)}, u32[]{:S(2)}, u32[]{:S(2)}) collective-permute-start(bf16[128,1280]{1,0:T(8,128)(2,1)S(1)} %get-tuple-element.73.early_own_ref), channel_id=1, source_target_pairs={{0,1},{1,0},{2,3},{3,2},{4,5},{5,4},{6,7},{7,6},{8,9},{9,8},{10,11... | collective-permute-start | bytes 983048 | tf_op jit(solution)/shard_map/ppermute | solution.py:539
  35.8 7.6 %collective-permute-start.14 = (bf16[128,1280]{1,0:T(8,128)(2,1)S(1)}, bf16[128,1280]{1,0:T(8,128)(2,1)S(1)}, u32[]{:S(2)}, u32[]{:S(2)}) collective-permute-start(bf16[128,1280]{1,0:T(8,128)(2,1)S(1)} %collective-permute-done.13.h_own_ref), channel_id=1, source_target_pairs={{0,1},{1,0},{2,3},{3,2},{4,5},{5,4},{6,7},{7,6},{8,9},{9,8},{10,11... | collective-permute-start | bytes 983048 | tf_op jit(solution)/shard_map/ppermute | solution.py:566
  35.9 4.9 %collective-permute-start.12 = (f32[160,128]{1,0:T(8,128)S(1)}, f32[160,128]{1,0:T(8,128)S(1)}, u32[]{:S(2)}, u32[]{:S(2)}) collective-permute-start(f32[160,128]{1,0:T(8,128)S(1)} %get-tuple-element.68), channel_id=1, source_target_pairs={{0,2},{1,3},{2,0},{3,1},{4,6},{5,7},{6,4},{7,5},{8,10},{9,11},{10,... | collective-permute-start | bytes 245768 | tf_op jit(solution)/shard_map/ppermute | solution.py:564
  40.7 6.8 %collective-permute-start.16 = (f32[160,128]{1,0:T(8,128)S(1)}, f32[160,128]{1,0:T(8,128)S(1)}, u32[]{:S(2)}, u32[]{:S(2)}) collective-permute-start(f32[160,128]{1,0:T(8,128)S(1)} %last_y.1.kept_ref), channel_id=1, source_target_pairs={{0,16},{4,20},{8,24},{12,28},{16,0},{20,4},{24,8},{28,12},{1,17},{... | collective-permute-start | bytes 245768 | tf_op jit(solution)/shard_map/ppermute | solution.py:579
  47.6 1.3 %collective-permute-start.17 = (f32[80,128]{1,0:T(8,128)S(1)}, f32[80,128]{1,0:T(8,128)S(1)}, u32[]{:S(2)}, u32[]{:S(2)}) collective-permute-start(f32[80,128]{1,0:T(8,128)S(1)} %get-tuple-element.77), channel_id=1, source_target_pairs={{0,1},{1,0},{2,3},{3,2},{4,5},{5,4},{6,7},{7,6},{8,9},{9,8},{10,11... | collective-permute-start | bytes 122888 | tf_op jit(solution)/shard_map/ppermute | solution.py:582

commit v3 on v2

--- a/solution.py
+++ b/solution.py
@@ -153,10 +153,24 @@
     points_ref[...] = points
 
 
-def steps_kernel(own_ref, other_ref, columns_ref, points_ref, ws_ref, wr_ref, e_ref, rows_ref, small_ref):
+def steps_kernel(
+    own_ref, other_ref, columns_ref, points_ref, xbc_hbm, xbc_other_ref, conv_w_hbm, conv_b_hbm,
+    ws_ref, wr_ref, e_ref, rows_ref, small_ref, x_ref, taps_ref, bias_ref, sems,
+):
     place = lax.axis_index("seq")
     core = lax.rem(place, 2)
     n = own_ref.shape[2]
+    col = pl.multiple_of(core * HALF, 128)
+    copies = []
+    for from_at, to_at, width in ((D, HALF, BC), (col, 0, HALF)):
+        here, there = pl.ds(from_at, width), pl.ds(to_at, width)
+        for source, to in ((xbc_hbm, core), (xbc_other_ref, 1 - core)):
+            copies.append((source.at[0, :, here], x_ref.at[pl.ds(pl.multiple_of(to * n, 16), n), there]))
+        copies.append((conv_w_hbm.at[:, here], taps_ref.at[:, there]))
+        copies.append((conv_b_hbm.at[here], bias_ref.at[0, there]))
+    copies = [pltpu.make_async_copy(source, to, sems.at[i]) for i, (source, to) in enumerate(copies)]
+    for copy in copies:
+        copy.start()
     own = own_ref[0].astype(F32)
     other = other_ref[0].astype(F32)
     bias, rate, skip = columns_ref[:, 0:1], columns_ref[:, 1:2], columns_ref[:, 2:3]
@@ -182,6 +196,8 @@
     rows_ref[...] = pack(beside((decay[0], decay[1], skip, back)))[0:16]
     whole = beside((carry_of(found), jnp.exp(ends[0] + ends[1])))
     small_ref[...] = jnp.concatenate([whole, jnp.zeros((128 - H, 128), F32)], axis=0).T[0:8]
+    for copy in copies:
+        copy.wait()
 
 
 def later_kernel(same_ref, cross_ref, columns_ref, points_ref, later_ref):
@@ -204,39 +220,19 @@
 
 
 def state_kernel(
-    own_ref, other_ref, edge_a_ref, edge_b_ref, ws_ref, wr_ref, rows_ref, later_ref, conv_w_ref, conv_b_ref,
+    x_ref, edge_a_ref, edge_b_ref, ws_ref, wr_ref, rows_ref, later_ref, taps_ref, bias_ref,
     state_ref, early_ref, act_own_ref, act_other_ref, bc_ref, *rest,
     split,
 ):
-    reads = rest[:-6]
-    x_ref, act_ref, taps_ref, bias_ref, read_ref, sems = rest[-6:]
+    reads = rest[:-3]
+    edge_ref, act_ref, read_ref = rest[-3:]
     place = lax.axis_index("seq")
     core = lax.rem(place, 2)
-    n = own_ref.shape[1]
-    col = pl.multiple_of(core * HALF, 128)
-    copies = []
-    for i, (source, to) in enumerate(((own_ref, core), (other_ref, 1 - core))):
-        rows = pl.ds(pl.multiple_of(EDGE + to * n, 16), n)
-        copies.append(pltpu.make_async_copy(source.at[0, :, pl.ds(D, BC)], x_ref.at[rows, pl.ds(HALF, BC)], sems.at[2 * i]))
-        copies.append(pltpu.make_async_copy(source.at[0, :, pl.ds(col, HALF)], x_ref.at[rows, pl.ds(0, HALF)], sems.at[2 * i + 1]))
-    for i, (source, from_at, to_at, width) in enumerate(((conv_w_ref, D, HALF, BC), (conv_w_ref, col, 0, HALF))):
-        copies.append(pltpu.make_async_copy(source.at[:, pl.ds(from_at, width)], taps_ref.at[:, pl.ds(to_at, width)], sems.at[4 + i]))
-    for i, (from_at, to_at, width) in enumerate(((D, HALF, BC), (col, 0, HALF))):
-        copies.append(pltpu.make_async_copy(conv_b_ref.at[pl.ds(from_at, width)], bias_ref.at[0, pl.ds(to_at, width)], sems.at[6 + i]))
-    for i in (0, 2, 4, 6, 1, 3, 5, 7):
-        copies[i].start()
+    n = x_ref.shape[0] // 2
     started = jnp.where(place >= 2, 1.0, 0.0)
     edge = jnp.where(core == 0, edge_a_ref[:, :CH].astype(F32), edge_b_ref[:, :CH].astype(F32)) * started
-    x_ref[0:EDGE, HALF:] = edge[:, D:].astype(BF16)
-
-    @pl.when(core == 0)
-    def _():
-        x_ref[0:EDGE, :HALF] = edge[:, :HALF].astype(BF16)
-
-    @pl.when(core == 1)
-    def _():
-        x_ref[0:EDGE, :HALF] = edge[:, HALF:D].astype(BF16)
-
+    edge_ref[:, HALF:] = edge[:, D:].astype(BF16)
+    edge_ref[:, :HALF] = jnp.where(core == 0, edge[:, :HALF], edge[:, HALF:D]).astype(BF16)
     tile = 128
 
     def convolve(at):
@@ -244,21 +240,19 @@
         taps = taps_ref[:, cols]
         bias = bias_ref[:, cols]
         for t in range(2 * n // tile):
-            seen = x_ref[t * tile : (t + 1) * tile + EDGE, cols].astype(F32)
+            if t == 0:
+                seen = jnp.concatenate([edge_ref[:, cols], x_ref[:tile, cols]], axis=0).astype(F32)
+            else:
+                seen = x_ref[t * tile - EDGE : (t + 1) * tile, cols].astype(F32)
             before = pltpu.roll(seen, 1, 0)
             pair = taps[1:2] * seen + taps[0:1] * before
             total = bias + taps[3:4] * seen[EDGE:] + taps[2:3] * before[EDGE:]
             total += pltpu.roll(pair, 2, 0)[EDGE:]
             act_ref[t * tile : (t + 1) * tile, cols] = silu(total).astype(BF16)
 
-    for i in (0, 2, 4, 6):
-        copies[i].wait()
     convolve(HALF)
     b_turned = act_ref[:, HALF : HALF + N].astype(F32).T.astype(BF16)
-    for i in (1, 3, 5, 7):
-        copies[i].wait()
-
-    @pl.loop(0, HALF // CHUNK)
+    @pl.loop(0, HALF // CHUNK, unroll=True)
     def _(j):
         at = pl.multiple_of(j * CHUNK, CHUNK)
         cols = pl.ds(at, CHUNK)
@@ -312,7 +306,7 @@
     for side, source in enumerate((act_own_ref, act_other_ref)):
         half = core if side == 0 else 1 - core
 
-        @pl.loop(0, HALF // CHUNK)
+        @pl.loop(0, HALF // CHUNK, unroll=True)
         def _(j):
             at = pl.multiple_of(j * CHUNK, CHUNK)
             cols = pl.ds(at, CHUNK)
@@ -327,37 +321,45 @@
             far_ref[side, :, cols] = decay * gate
 
 
-def finish_kernel(near_ref, far_ref, bc_ref, h_own_ref, h_other_ref, early_own_ref, early_other_ref, rows_ref, gain_hbm, out_ref, g_ref, gain_ref, sem):
+def carry_kernel(h_ref, early_ref, rows_ref, keep_ref, send_ref):
     place = lax.axis_index("seq")
-    core = lax.rem(place, 2)
+    first = lax.rem(place, 2) == 0
+    for j in range(HALF // CHUNK):
+        cols = pl.ds(j * CHUNK, CHUNK)
+        spread = spread_matrix(lax.rem(place, 2) * (H // 2) + j * (CHUNK // P_SIZE))
+        chip = jnp.where(place >= 2, h_ref[:, cols].astype(F32), 0.0)
+        middle = dot(rows_ref[...], spread)[0:1] * chip + early_ref[:, cols].astype(F32)
+        keep_ref[:, cols] = jnp.where(first, chip, middle).astype(BF16)
+        send_ref[:, cols] = jnp.where(first, middle, chip).astype(BF16)
+
+
+def finish_kernel(near_ref, far_ref, bc_ref, h_own_ref, h_other_ref, gain_ref, out_hbm, g_ref, out_ref, sems):
+    core = lax.rem(lax.axis_index("seq"), 2)
     n = bc_ref.shape[0]
-    second = core == 1
-    started = place >= 2
-    gain = pltpu.make_async_copy(gain_hbm, gain_ref.at[0], sem)
-    gain.start()
     squares = jnp.zeros((n, CHUNK), F32)
     c_vals = bc_ref[:, N:]
     for side in range(2):
-        half = core if side == 0 else 1 - core
         h_ref = (h_own_ref, h_other_ref)[side]
-        early_ref = (early_own_ref, early_other_ref)[side]
         for j in range(HALF // CHUNK):
             cols = pl.ds(j * CHUNK, CHUNK)
-            spread = spread_matrix(half * (H // 2) + j * (CHUNK // P_SIZE))
-            decay = jnp.where(second, dot(rows_ref[...], spread)[0:1], 1.0)
-            h = jnp.where(started, h_ref[:, cols].astype(F32), 0.0) * decay
-            h += jnp.where(second, early_ref[:, cols].astype(F32), 0.0)
-            g = near_ref[side, :, cols] + far_ref[side, :, cols] * dot(c_vals, h.astype(BF16))
+            g = near_ref[side, :, cols] + far_ref[side, :, cols] * dot(c_vals, h_ref[:, cols])
             g_ref[side, :, cols] = g
             squares += g * g
-    gain.wait()
     scale = lax.rsqrt(jnp.sum(squares, axis=-1, keepdims=True) * (1.0 / D) + 1e-05)
-    for side in range(2):
-        half = core if side == 0 else 1 - core
-        for j in range(HALF // CHUNK):
-            cols = pl.ds(pl.multiple_of(half * HALF + j * CHUNK, CHUNK), CHUNK)
-            g = g_ref[side, :, pl.ds(j * CHUNK, CHUNK)]
-            out_ref[0, :, cols] = (g * scale * gain_ref[:, cols]).astype(BF16)
+    tile = n // 4
+    copies = []
+    for t in range(4):
+        rows = pl.ds(t * tile, tile)
+        for side in range(2):
+            half = core if side == 0 else 1 - core
+            for j in range(HALF // CHUNK):
+                cols = pl.ds(pl.multiple_of(half * HALF + j * CHUNK, CHUNK), CHUNK)
+                g = g_ref[side, rows, pl.ds(j * CHUNK, CHUNK)]
+                out_ref[rows, cols] = (g * scale[t * tile : (t + 1) * tile] * gain_ref[:, cols]).astype(BF16)
+        copies.append(pltpu.make_async_copy(out_ref.at[rows], out_hbm.at[0, rows], sems.at[t]))
+        copies[t].start()
+    for copy in copies:
+        copy.wait()
 
 
 def join_kernel(mark_ref, a_ref, b_ref, out_ref):
@@ -377,7 +379,7 @@
     keep_a_ref, send_a_ref, keep_b_ref, send_b_ref,
     *, sequences,
 ):
-    ones = sum_ref[0:1] + x_mark_ref[0:1]
+    ones = sum_ref[0:1] + z_mark_ref[0:1]
 
     def weight(mark):
         return mark / ones - (1.0 - mark) / (sequences - ones)
@@ -469,17 +471,19 @@
     edge_a = lax.ppermute(tail, "seq", one_back)
     edge_b = lax.ppermute(tail, "seq", two_back)
 
-    ws, wr, e, rows, small = pl.pallas_call(
+    ws, wr, e, rows, small, x, taps, bias = pl.pallas_call(
         steps_kernel,
         out_shape=(
             shape((2 * n, 128), BF16), shape((2 * n, 128), BF16), shape((n, 128), BF16), shape((16, 128), BF16), shape((8, 128), F32),
+            shape((2 * n, SIDE), BF16), shape((KW, SIDE), F32), shape((1, SIDE), F32),
         ),
-        in_specs=[VMEM] * 4,
-        out_specs=(VMEM,) * 5,
+        in_specs=[VMEM] * 4 + [HBM, ANY, HBM, HBM],
+        out_specs=(VMEM,) * 8,
+        scratch_shapes=[pltpu.SemaphoreType.DMA((8,))],
         compiler_params=params(16),
         cost_estimate=cost(2 * 6 * n * n * 128, 8 * n * 256),
         name="steps",
-    )(dt_own, dt_other, columns, points)
+    )(dt_own, dt_other, columns, points, xbc_here, xbc_other, in_hbm(conv_weight), in_hbm(conv_bias))
 
     if chips == 2:
         later = pl.pallas_call(
@@ -490,7 +494,7 @@
             compiler_params=params(16),
             cost_estimate=cost(2 * 6 * n * n * 128, 8 * n * 256),
             name="later",
-        )(edge_b, edge_a, columns, points)
+        )(edge_b, edge_a, tied(columns, ws), points)
     else:
         later = jnp.zeros_like(small)
         for step in range(chips - 1):
@@ -500,10 +504,8 @@
         later = pack(jnp.broadcast_to(later[0, :H, None], (H, 16)))
 
     if split:
-        z_mark = lax.ppermute(mark, "dp", swap(2))
-        half = join(tied(mark, ws), mark, z_mark)
-        quarter = join(tied(mark, later), half, lax.ppermute(half, "dp", swap(4)))
-        later = tied(later, quarter)
+        ones = join(tied(mark, later), mark, lax.ppermute(mark, "dp", swap(4)))
+        later = tied(later, ones)
 
     read_rows = D // 8 if split else HALF
     state, early, act_own, act_other, bc, *reads = pl.pallas_call(
@@ -512,20 +514,13 @@
             shape((N, HALF), BF16), shape((N, HALF), BF16),
             shape((n, HALF), BF16), shape((n, HALF), BF16), shape((n, BC), BF16),
         ) + (shape((read_rows, N), F32),) * (4 if split else 1),
-        in_specs=[HBM, ANY] + [VMEM] * 6 + [HBM, HBM],
+        in_specs=[VMEM] * 9,
         out_specs=(VMEM,) * (9 if split else 6),
-        scratch_shapes=[
-            pltpu.VMEM((EDGE + 2 * n, SIDE), BF16),
-            pltpu.VMEM((2 * n, SIDE), BF16),
-            pltpu.VMEM((KW, SIDE), F32),
-            pltpu.VMEM((1, SIDE), F32),
-            pltpu.VMEM((HALF, N), F32),
-            pltpu.SemaphoreType.DMA((8,)),
-        ],
+        scratch_shapes=[pltpu.VMEM((EDGE, SIDE), BF16), pltpu.VMEM((2 * n, SIDE), BF16), pltpu.VMEM((HALF, N), F32)],
         compiler_params=params(24),
         cost_estimate=cost(50 * n * n * D, 4 * 2 * n * SIDE),
         name="states",
-    )(xbc_here, xbc_other, edge_a, edge_b, ws, wr, rows, later, in_hbm(conv_weight), in_hbm(conv_bias))
+    )(x, edge_a, edge_b, ws, wr, rows, later, taps, bias)
 
     h = state
     for step in range(chips - 1):
@@ -536,12 +531,13 @@
         if chips > 2:
             h = jnp.where(place >= 2, h, jnp.zeros_like(h))
     act_in = lax.ppermute(act_other, "seq", pair)
-    early_in = lax.ppermute(early, "seq", pair)
     if split:
         keep_x, send_x, keep_z, send_z = reads
-        x_mark = lax.ppermute(tied(quarter, send_x), "dp", swap(1))
+        x_mark = lax.ppermute(tied(ones, send_x), "dp", swap(1))
         came_x = lax.ppermute(send_x, "dp", swap(1))
         came_z = lax.ppermute(send_z, "dp", swap(2))
+        ones = join(mark, ones, x_mark)
+        z_mark = lax.ppermute(ones, "dp", swap(2))
 
     near, reach = pl.pallas_call(
         diagonal_kernel,
@@ -556,24 +552,27 @@
         keep_x, near, reach = lax.optimization_barrier((keep_x, near, reach))
         keep_a, send_a, keep_b, send_b = small_call(
             functools.partial(halves_kernel, sequences=float(sequences)), "halves", 4, D // 16,
-            keep_x, came_x, keep_z, came_z, mark, x_mark, z_mark, quarter,
+            keep_x, came_x, keep_z, came_z, mark, x_mark, z_mark, ones,
         )
         came_a = lax.ppermute(send_a, "dp", swap(2))
         came_b = lax.ppermute(send_b, "dp", swap(1))
         keep, send = small_call(join_y_kernel, "join_y", 2, D // 16, keep_a, came_a, keep_b, came_b)
         came = lax.ppermute(send, "seq", [(i, i ^ 2) for i in range(places)])
     h = tied(h, keep) if split else h
-    h_other = lax.ppermute(h, "seq", pair)
+    h_own, h_send = pl.pallas_call(
+        carry_kernel, out_shape=(shape((N, HALF), BF16),) * 2, in_specs=[VMEM] * 3, out_specs=(VMEM,) * 2, compiler_params=params(8), name="carry"
+    )(h, early, rows)
+    h_other = lax.ppermute(h_send, "seq", pair)
     layer_out = pl.pallas_call(
         finish_kernel,
         out_shape=shape((1, n, D), BF16),
-        in_specs=[VMEM] * 8 + [ANY],
-        out_specs=VMEM,
-        scratch_shapes=[pltpu.VMEM((2, n, HALF), F32), pltpu.VMEM((1, D), F32), pltpu.SemaphoreType.DMA(())],
+        in_specs=[VMEM] * 6,
+        out_specs=HBM,
+        scratch_shapes=[pltpu.VMEM((2, n, HALF), F32), pltpu.VMEM((n, D), BF16), pltpu.SemaphoreType.DMA((4,))],
         compiler_params=params(24),
         cost_estimate=cost(20 * n * n * D, 12 * n * D),
         name="finish",
-    )(near, reach, bc, h, h_other, early, early_in, rows, norm_gain)
+    )(near, reach, bc, h_own, h_other, norm_gain[None])
     if split:
         (total,) = small_call(last_kernel, "last_y", 1, D // 16, keep, came)
         came = lax.ppermute(total, "dp", swap(4))

time: 49.7 us -> 45.7 us (0.920)
  Pallas kernels: 17.7 us -> 13.4 us
  waiting for transfers between devices: 10.4 us -> 11.7 us
  starting transfers between devices: 20 us -> 19 us
    pallas_call x1, Pallas kernels: 7.01 us -> 4.68 us  [on_device(): pl.pallas_call(functools.partial(state_kernel, split=split), out_shape=(s...]
    pallas_call x1, Pallas kernels: 4.12 us -> 2.13 us  [on_device(): pl.pallas_call(diagonal_kernel, out_shape=(shape((2, n, HALF), F32), shap...]
    ppermute x1, starting transfers between devices: 1.87 us -> 0.42 us  [on_device(): came_x = lax.ppermute(send_x, 'dp', swap(1))]
    pallas_call x1, Pallas kernels: 2.87 us -> 1.76 us  [on_device(): pl.pallas_call(finish_kernel, out_shape=shape((1, n, D), BF16), in_specs=...]
    ppermute x1, waiting for transfers between devices: 1.32 us -> 2.3 us  [on_device(): came = lax.ppermute(total, 'dp', swap(4))]
    ppermute x1, waiting for transfers between devices: 0.01 us -> 0.91 us  [on_device(): edge_b = lax.ppermute(tail, 'seq', two_back)]
    pallas_call x1, Pallas kernels: 1.29 us -> 2.13 us  [on_device(): pl.pallas_call(steps_kernel, out_shape=(shape((2 * n, 128), BF16), shape(...]
    ppermute x5 -> x4, waiting for transfers between devices: 1.47 us -> 1.02 us  [the longest x1 1.01 us: on_device(): z_mark = lax.ppermute(ones, 'dp', swap(2))]
  transfers between devices with their start and end apart: 18 -> 17, of which waited for: 7 -> 7; matrix products, arithmetic and copies ran while one was open for 0% -> 0% of each run, Pallas kernels for 20% -> 17%
where the time goes in v3:
time: 45.7 us; the launch traced here: 45.5 us
  starting transfers between devices  19 us (42%)
  Pallas kernels  13.4 us (29%)
  waiting for transfers between devices  11.7 us (26%)
  between operations  1.44 us (3%)
    pallas_call x1, Pallas kernels, on_device(): pl.pallas_call(functools.partial(state_kernel, split=split), out_shape=(s...  4.68 us
    ppermute x1, waiting for transfers between devices, on_device(): came = lax.ppermute(send, 'seq', [(i, i ^ 2) for i in range(places)])  3.26 us
    ppermute x1, starting transfers between devices, on_device(): ones = join(tied(mark, later), mark, lax.ppermute(mark, 'dp', swap(4)))  2.9 us
    ppermute x1, starting transfers between devices, on_device(): edge_a = lax.ppermute(tail, 'seq', one_back)  2.71 us
    ppermute x1, starting transfers between devices, on_device(): came = lax.ppermute(total, 'dp', swap(4))  2.65 us
    ppermute x1, waiting for transfers between devices, on_device(): came = lax.ppermute(total, 'dp', swap(4))  2.3 us
    pallas_call x1, Pallas kernels, on_device(): pl.pallas_call(steps_kernel, out_shape=(shape((2 * n, 128), BF16), shape(...  2.13 us
    pallas_call x1, Pallas kernels, on_device(): pl.pallas_call(diagonal_kernel, out_shape=(shape((2, n, HALF), F32), shap...  2.13 us
  transfers between devices with their start and end apart: 17, of which 7 were waited for; matrix products, arithmetic and copies ran while one was open for 0% of the time, Pallas kernels for 17%

profile of v3, /device:TPU:0, one launch (start us, length us, event | category | flops | bytes accessed | tf_op | source)
XLA Modules:
  0.0 45.5 jit_solution(14169998025911783150)
XLA Ops:
  0.6 0.5 %collective-permute-start.1 = (bf16[1,256,2816]{2,1,0:T(8,128)(2,1)}, bf16[1,256,2816]{2,1,0:T(8,128)(2,1)S(1)}, u32[]{:S(2)}, u32[]{:S(2)}) collective-permute-start(bf16[1,256,2816]{2,1,0:T(8,128)(2,1)} %xbc_hbm.3), channel_id=1, source_target_pairs={{0,1},{1,0},{2,3},{3,2},{4,5},{5,4},{6,7},{7,6},{8,9},{9,8},{10,11... | collective-permute-start | bytes 4325384 | tf_op jit(solution)/shard_map/ppermute | solution.py:456
  1.8 1.1 %tail.1 = (bf16[16,3584]{1,0:T(8,128)(2,1)S(1)}, f32[8,128]{1,0:T(8,128)S(1)}, bf16[1,40,256]{2,1,0:T(8,128)(2,1)S(1)}, f32[40,8]{1,0:T(8,128)S(1)}, s32[8,128]{1,0:T(8,128)S(1)}) custom-call(bf16[1,256,2816]{2,1,0:T(8,128)(2,1)} %xbc_hbm.3, bf16[1,40,256]{2,1,0:T(8,128)(2,1)} %bitcast.1, f32[40]{0:T(128)} %bias_hbm.1, f32[40]{0:T(128)} %rate_hbm.1, ...), custom_call_target="tpu_custom_call" | custom-call | tf_op jit(solution)/shard_map/tail/pallas_call | solution.py:458
  2.9 2.7 %collective-permute-start.2 = (bf16[16,3584]{1,0:T(8,128)(2,1)S(1)}, bf16[16,3584]{1,0:T(8,128)(2,1)S(1)}, u32[]{:S(2)}, u32[]{:S(2)}) collective-permute-start(bf16[16,3584]{1,0:T(8,128)(2,1)S(1)} %get-tuple-element.49), channel_id=1, source_target_pairs={{0,3},{1,2},{2,1},{3,0},{4,7},{5,6},{6,5},{7,4},{8,11},{9,10},{10,... | collective-permute-start | bytes 344072 | tf_op jit(solution)/shard_map/ppermute | solution.py:471
  5.6 0.2 collective-permute-start
  5.8 2.9 %collective-permute-start.4 = (f32[8,128]{1,0:T(8,128)S(1)}, f32[8,128]{1,0:T(8,128)S(1)}, u32[]{:S(2)}, u32[]{:S(2)}) collective-permute-start(f32[8,128]{1,0:T(8,128)S(1)} %get-tuple-element.55.mark_ref.a_ref), channel_id=1, source_target_pairs={{0,16},{4,20},{8,24},{12,28},{16,0},{20,4},{24,8},{28,12},{1,17},{... | collective-permute-start | bytes 12296 | tf_op jit(solution)/shard_map/ppermute | solution.py:507
  8.7 2.1 %steps.1 = (bf16[512,128]{1,0:T(8,128)(2,1)S(1)}, bf16[512,128]{1,0:T(8,128)(2,1)S(1)}, bf16[256,128]{1,0:T(8,128)(2,1)S(1)}, bf16[16,128]{1,0:T(8,128)(2,1)S(1)...) custom-call(bf16[1,40,256]{2,1,0:T(8,128)(2,1)S(1)} %get-tuple-element.45.ow, ...), custom_call_target="tpu_custom_call" | custom-call | flops 100663296 | bytes 524288 | tf_op jit(solution)/shard_map/steps/pallas_call | solution.py:474
  10.8 0.9 %collective-permute-done.3.same_ref.edge_b_ref = bf16[16,3584]{1,0:T(8,128)(2,1)S(1)} collective-permute-done((bf16[16,3584]{1,0:T(8,128)(2,1)S(1)}, bf16[16,3584]{1,0:T(8,128)(2,1)S(1)}, u32[]{:S(2)}, u32[]{:S(2)}) %collective-permute-start.3) | collective-permute-done | bytes 114720 | tf_op jit(solution)/shard_map/ppermute | solution.py:472
  11.8 0.5 %later.1.later_ref = bf16[16,128]{1,0:T(8,128)(2,1)S(1)} custom-call(bf16[16,3584]{1,0:T(8,128)(2,1)S(1)} %collective-permute-done.3.same_ref.edge_b_ref, bf16[16,3584]{1,0:T(8,128)(2,1)S(1)} %collective-permute-done.2.cross_ref.edge_a_ref, f32[40,8]{1,0:T(8,128)S(1)} %get-tuple-element.53.columns_ref, s32[8,128]{1,0:T(8,128)S(1)} %get-tuple-element.47.points_ref), custom_call_target="tpu_custom_call" | custom-call | flops 100663296 | bytes 524288 | tf_op jit(solution)/shard_map/later/pallas_call | solution.py:489
  12.3 4.7 %states.1 = (bf16[128,1280]{1,0:T(8,128)(2,1)S(1)}, bf16[128,1280]{1,0:T(8,128)(2,1)S(1)}, bf16[256,1280]{1,0:T(8,128)(2,1)S(1)}, bf16[256,1280]{1,0:T(8,128)(2,...) custom-call(bf16[512,1536]{1,0:T(8,128)(2,1)S(1)} %get-tuple-element, ...), custom_call_target="tpu_custom_call" | custom-call | flops 8388608000 | bytes 3145728 | tf_op jit(solution)/shard_map/states/pallas_call | solution.py:511
  17.0 0.1 collective-permute-start.5
  17.1 1.7 %collective-permute-start.8 = (f32[8,128]{1,0:T(8,128)S(1)}, f32[8,128]{1,0:T(8,128)S(1)}, u32[]{:S(2)}, u32[]{:S(2)}) collective-permute-start(f32[8,128]{1,0:T(8,128)S(1)} %join.2.a_ref), channel_id=1, source_target_pairs={{0,4},{4,0},{8,12},{12,8},{16,20},{20,16},{24,28},{28,24},{1,5},{5... | collective-permute-start | bytes 12296 | tf_op jit(solution)/shard_map/ppermute | solution.py:536
  18.8 0.4 collective-permute-start.6
  19.2 1.7 %collective-permute-start.7 = (f32[320,128]{1,0:T(8,128)S(1)}, f32[320,128]{1,0:T(8,128)S(1)}, u32[]{:S(2)}, u32[]{:S(2)}) collective-permute-start(f32[320,128]{1,0:T(8,128)S(1)} %get-tuple-element.69), channel_id=1, source_target_pairs={{0,8},{4,12},{8,0},{12,4},{16,24},{20,28},{24,16},{28,20},{1,9},{5... | collective-permute-start | bytes 491528 | tf_op jit(solution)/shard_map/ppermute | solution.py:538
  20.9 1.5 %collective-permute-start.13 = (bf16[128,1280]{1,0:T(8,128)(2,1)S(1)}, bf16[128,1280]{1,0:T(8,128)(2,1)S(1)}, u32[]{:S(2)}, u32[]{:S(2)}) collective-permute-start(bf16[128,1280]{1,0:T(8,128)(2,1)S(1)} %get-tuple-element.79), channel_id=1, source_target_pairs={{0,2},{1,3},{2,0},{3,1},{4,6},{5,7},{6,4},{7,5},{8,10},{9,11},{10,... | collective-permute-start | bytes 983048 | tf_op jit(solution)/shard_map/ppermute | solution.py:530
  22.4 0.5 %collective-permute-start.9 = (f32[8,128]{1,0:T(8,128)S(1)}, f32[8,128]{1,0:T(8,128)S(1)}, u32[]{:S(2)}, u32[]{:S(2)}) collective-permute-start(f32[8,128]{1,0:T(8,128)S(1)} %join.3.sum_ref), channel_id=1, source_target_pairs={{0,8},{4,12},{8,0},{12,4},{16,24},{20,28},{24,16},{28,20},{1,9},{5... | collective-permute-start | bytes 12296 | tf_op jit(solution)/shard_map/ppermute | solution.py:540
  22.9 2.1 %diagonal.1 = (f32[2,256,1280]{2,1,0:T(8,128)S(1)}, f32[2,256,1280]{2,1,0:T(8,128)S(1)}) custom-call(bf16[256,1280]{1,0:T(8,128)(2,1)S(1)} %get-tuple-element.60.act_own_ref, bf16[256,1280]{1,0:T(8,128)(2,1)S(1)} %collective-permute-done.5.act_other_ref, bf16[256,256]{1,0:T(8,128)(2,1)S(1)} %get-tuple-element.62.bc_ref, ...), custom_call_target="tpu_custom_call" | custom-call | flops 4697620480 | bytes 2621440 | tf_op jit(solution)/shard_map/diagonal/pallas_call | solution.py:542
  25.1 0.0 copy-start.2
  25.1 1.0 %collective-permute-done.9.z_mark_ref = f32[8,128]{1,0:T(8,128)S(1)} collective-permute-done((f32[8,128]{1,0:T(8,128)S(1)}, f32[8,128]{1,0:T(8,128)S(1)}, u32[]{:S(2)}, u32[]{:S(2)}) %collective-permute-start.9) | collective-permute-done | bytes 4128 | tf_op jit(solution)/shard_map/ppermute | solution.py:540
  26.2 0.9 %collective-permute-start.10 = (f32[160,128]{1,0:T(8,128)S(1)}, f32[160,128]{1,0:T(8,128)S(1)}, u32[]{:S(2)}, u32[]{:S(2)}) collective-permute-start(f32[160,128]{1,0:T(8,128)S(1)} %get-tuple-element.72), channel_id=1, source_target_pairs={{0,8},{4,12},{8,0},{12,4},{16,24},{20,28},{24,16},{28,20},{1,9},{5... | collective-permute-start | bytes 245768 | tf_op jit(solution)/shard_map/ppermute | solution.py:557
  27.1 1.5 %collective-permute-start.11 = (f32[160,128]{1,0:T(8,128)S(1)}, f32[160,128]{1,0:T(8,128)S(1)}, u32[]{:S(2)}, u32[]{:S(2)}) collective-permute-start(f32[160,128]{1,0:T(8,128)S(1)} %get-tuple-element.74), channel_id=1, source_target_pairs={{0,4},{4,0},{8,12},{12,8},{16,20},{20,16},{24,28},{28,24},{1,5},{5... | collective-permute-start | bytes 245768 | tf_op jit(solution)/shard_map/ppermute | solution.py:558
  28.6 2.1 %collective-permute-done.10.came_a_ref = f32[160,128]{1,0:T(8,128)S(1)} collective-permute-done((f32[160,128]{1,0:T(8,128)S(1)}, f32[160,128]{1,0:T(8,128)S(1)}, u32[]{:S(2)}, u32[]{:S(2)}) %collective-permute-start.10) | collective-permute-done | bytes 81952 | tf_op jit(solution)/shard_map/ppermute | solution.py:557
  30.7 0.9 %collective-permute-done.11.came_b_ref = f32[160,128]{1,0:T(8,128)S(1)} collective-permute-done((f32[160,128]{1,0:T(8,128)S(1)}, f32[160,128]{1,0:T(8,128)S(1)}, u32[]{:S(2)}, u32[]{:S(2)}) %collective-permute-start.11) | collective-permute-done | bytes 81952 | tf_op jit(solution)/shard_map/ppermute | solution.py:558
  31.6 0.3 carry.1
  31.9 0.1 collective-permute-start.14
  32.0 1.6 %collective-permute-start.12 = (f32[160,128]{1,0:T(8,128)S(1)}, f32[160,128]{1,0:T(8,128)S(1)}, u32[]{:S(2)}, u32[]{:S(2)}) collective-permute-start(f32[160,128]{1,0:T(8,128)S(1)} %get-tuple-element.76), channel_id=1, source_target_pairs={{0,2},{1,3},{2,0},{3,1},{4,6},{5,7},{6,4},{7,5},{8,10},{9,11},{10,... | collective-permute-start | bytes 245768 | tf_op jit(solution)/shard_map/ppermute | solution.py:560
  33.6 3.3 %collective-permute-done.12.came_ref = f32[160,128]{1,0:T(8,128)S(1)} collective-permute-done((f32[160,128]{1,0:T(8,128)S(1)}, f32[160,128]{1,0:T(8,128)S(1)}, u32[]{:S(2)}, u32[]{:S(2)}) %collective-permute-start.12) | collective-permute-done | bytes 81952 | tf_op jit(solution)/shard_map/ppermute | solution.py:560
  36.9 2.7 %collective-permute-start.15 = (f32[160,128]{1,0:T(8,128)S(1)}, f32[160,128]{1,0:T(8,128)S(1)}, u32[]{:S(2)}, u32[]{:S(2)}) collective-permute-start(f32[160,128]{1,0:T(8,128)S(1)} %last_y.1.kept_ref), channel_id=1, source_target_pairs={{0,16},{4,20},{8,24},{12,28},{16,0},{20,4},{24,8},{28,12},{1,17},{... | collective-permute-start | bytes 245768 | tf_op jit(solution)/shard_map/ppermute | solution.py:578
  39.5 1.8 %finish.1 = bf16[1,256,2560]{2,1,0:T(8,128)(2,1)} custom-call(f32[2,256,1280]{2,1,0:T(8,128)S(1)} %get-tuple-element.77.near_ref, f32[2,256,1280]{2,1,0:T(8,128)S(1)} %get-tuple-element.78.far_ref, bf16[256,256]{1,0:T(8,128)(2,1)S(1)} %get-tuple-element.62.bc_ref, bf16[128,1280]{1,0:T(8,128)(2,1)S(1)} %get-tuple-element.82.h_own_ref, ...), custom_call_target="tpu_custom_call" | custom-call | flops 3355443200 | bytes 7864320 | tf_op jit(solution)/shard_map/finish/pallas_call | solution.py:566
  41.3 2.3 %collective-permute-done.15.came_ref = f32[160,128]{1,0:T(8,128)S(1)} collective-permute-done((f32[160,128]{1,0:T(8,128)S(1)}, f32[160,128]{1,0:T(8,128)S(1)}, u32[]{:S(2)}, u32[]{:S(2)}) %collective-permute-start.15) | collective-permute-done | bytes 81952 | tf_op jit(solution)/shard_map/ppermute | solution.py:578
  43.6 0.1 collective-permute-start.16
  43.7 1.2 %collective-permute-done.16.came_ref = f32[80,128]{1,0:T(8,128)S(1)} collective-permute-done((f32[80,128]{1,0:T(8,128)S(1)}, f32[80,128]{1,0:T(8,128)S(1)}, u32[]{:S(2)}, u32[]{:S(2)}) %collective-permute-start.16) | collective-permute-done | bytes 40992 | tf_op jit(solution)/shard_map/ppermute | solution.py:581
  44.9 0.6 %owner.1 = f32[80,128]{1,0:T(8,128)} custom-call(f32[80,128]{1,0:T(8,128)S(1)} %get-tuple-element.86.own_ref, f32[80,128]{1,0:T(8,128)S(1)} %collective-permute-done.16.came_ref), custom_call_target="tpu_custom_call" | custom-call | tf_op jit(solution)/shard_map/owner/pallas_call | solution.py:436
  (23 shorter events, 0.2 us)
Async XLA Ops:
  0.6 5.0 %copy-start.1 = (bf16[1,256,40]{1,2,0:T(8,128)(2,1)S(1)}, bf16[1,256,40]{1,2,0:T(8,128)(2,1)}, u32[]{:S(2)}) copy-start(bf16[1,256,40]{1,2,0:T(8,128)(2,1)} %param.13) | copy-start | bytes 61444
  0.6 8.1 %collective-permute-start.1 = (bf16[1,256,2816]{2,1,0:T(8,128)(2,1)}, bf16[1,256,2816]{2,1,0:T(8,128)(2,1)S(1)}, u32[]{:S(2)}, u32[]{:S(2)}) collective-permute-start(bf16[1,256,2816]{2,1,0:T(8,128)(2,1)} %xbc_hbm.3), channel_id=1, source_target_pairs={{0,1},{1,0},{2,3},{3,2},{4,5},{5,4},{6,7},{7,6},{8,9},{9,8},{10,11... | collective-permute-start | bytes 4325384 | tf_op jit(solution)/shard_map/ppermute | solution.py:456
  2.9 7.9 %collective-permute-start.2 = (bf16[16,3584]{1,0:T(8,128)(2,1)S(1)}, bf16[16,3584]{1,0:T(8,128)(2,1)S(1)}, u32[]{:S(2)}, u32[]{:S(2)}) collective-permute-start(bf16[16,3584]{1,0:T(8,128)(2,1)S(1)} %get-tuple-element.49), channel_id=1, source_target_pairs={{0,3},{1,2},{2,1},{3,0},{4,7},{5,6},{6,5},{7,4},{8,11},{9,10},{10,... | collective-permute-start | bytes 344072 | tf_op jit(solution)/shard_map/ppermute | solution.py:471
  5.6 6.1 %collective-permute-start.3 = (bf16[16,3584]{1,0:T(8,128)(2,1)S(1)}, bf16[16,3584]{1,0:T(8,128)(2,1)S(1)}, u32[]{:S(2)}, u32[]{:S(2)}) collective-permute-start(bf16[16,3584]{1,0:T(8,128)(2,1)S(1)} %get-tuple-element.49), channel_id=1, source_target_pairs={{0,2},{1,3},{2,0},{3,1},{4,6},{5,7},{6,4},{7,5},{8,10},{9,11},{10,... | collective-permute-start | bytes 344072 | tf_op jit(solution)/shard_map/ppermute | solution.py:472
  5.6 3.1 %collective-permute-start = (bf16[1,40,256]{2,1,0:T(8,128)(2,1)S(1)}, bf16[1,40,256]{2,1,0:T(8,128)(2,1)S(1)}, u32[]{:S(2)}, u32[]{:S(2)}) collective-permute-start(bf16[1,40,256]{2,1,0:T(8,128)(2,1)S(1)} %bitcast.2), channel_id=1, source_target_pairs={{0,1},{1,0},{2,3},{3,2},{4,5},{5,4},{6,7},{7,6},{8,9},{9,8},{10,11... | collective-permute-start | bytes 61448 | tf_op jit(solution)/shard_map/ppermute | solution.py:455
  5.8 6.5 %collective-permute-start.4 = (f32[8,128]{1,0:T(8,128)S(1)}, f32[8,128]{1,0:T(8,128)S(1)}, u32[]{:S(2)}, u32[]{:S(2)}) collective-permute-start(f32[8,128]{1,0:T(8,128)S(1)} %get-tuple-element.55.mark_ref.a_ref), channel_id=1, source_target_pairs={{0,16},{4,20},{8,24},{12,28},{16,0},{20,4},{24,8},{28,12},{1,17},{... | collective-permute-start | bytes 12296 | tf_op jit(solution)/shard_map/ppermute | solution.py:507
  12.3 10.6 %copy-start = (bf16[1,256,2560]{2,1,0:T(8,128)(2,1)S(1)}, bf16[1,256,2560]{2,1,0:T(8,128)(2,1)}, u32[]{:S(2)}) copy-start(bf16[1,256,2560]{2,1,0:T(8,128)(2,1)} %gate_ref.1) | copy-start | bytes 3932164
  17.0 5.9 %collective-permute-start.5 = (bf16[256,1280]{1,0:T(8,128)(2,1)S(1)}, bf16[256,1280]{1,0:T(8,128)(2,1)S(1)}, u32[]{:S(2)}, u32[]{:S(2)}) collective-permute-start(bf16[256,1280]{1,0:T(8,128)(2,1)S(1)} %get-tuple-element.61), channel_id=1, source_target_pairs={{0,1},{1,0},{2,3},{3,2},{4,5},{5,4},{6,7},{7,6},{8,9},{9,8},{10,11... | collective-permute-start | bytes 1966088 | tf_op jit(solution)/shard_map/ppermute | solution.py:533
  17.1 5.3 %collective-permute-start.8 = (f32[8,128]{1,0:T(8,128)S(1)}, f32[8,128]{1,0:T(8,128)S(1)}, u32[]{:S(2)}, u32[]{:S(2)}) collective-permute-start(f32[8,128]{1,0:T(8,128)S(1)} %join.2.a_ref), channel_id=1, source_target_pairs={{0,4},{4,0},{8,12},{12,8},{16,20},{20,16},{24,28},{28,24},{1,5},{5... | collective-permute-start | bytes 12296 | tf_op jit(solution)/shard_map/ppermute | solution.py:536
  18.8 7.3 %collective-permute-start.6 = (f32[320,128]{1,0:T(8,128)S(1)}, f32[320,128]{1,0:T(8,128)S(1)}, u32[]{:S(2)}, u32[]{:S(2)}) collective-permute-start(f32[320,128]{1,0:T(8,128)S(1)} %get-tuple-element.67), channel_id=1, source_target_pairs={{0,4},{4,0},{8,12},{12,8},{16,20},{20,16},{24,28},{28,24},{1,5},{5... | collective-permute-start | bytes 491528 | tf_op jit(solution)/shard_map/ppermute | solution.py:537
  19.2 6.9 %collective-permute-start.7 = (f32[320,128]{1,0:T(8,128)S(1)}, f32[320,128]{1,0:T(8,128)S(1)}, u32[]{:S(2)}, u32[]{:S(2)}) collective-permute-start(f32[320,128]{1,0:T(8,128)S(1)} %get-tuple-element.69), channel_id=1, source_target_pairs={{0,8},{4,12},{8,0},{12,4},{16,24},{20,28},{24,16},{28,20},{1,9},{5... | collective-permute-start | bytes 491528 | tf_op jit(solution)/shard_map/ppermute | solution.py:538
  20.9 10.7 %collective-permute-start.13 = (bf16[128,1280]{1,0:T(8,128)(2,1)S(1)}, bf16[128,1280]{1,0:T(8,128)(2,1)S(1)}, u32[]{:S(2)}, u32[]{:S(2)}) collective-permute-start(bf16[128,1280]{1,0:T(8,128)(2,1)S(1)} %get-tuple-element.79), channel_id=1, source_target_pairs={{0,2},{1,3},{2,0},{3,1},{4,6},{5,7},{6,4},{7,5},{8,10},{9,11},{10,... | collective-permute-start | bytes 983048 | tf_op jit(solution)/shard_map/ppermute | solution.py:530
  22.4 3.7 %collective-permute-start.9 = (f32[8,128]{1,0:T(8,128)S(1)}, f32[8,128]{1,0:T(8,128)S(1)}, u32[]{:S(2)}, u32[]{:S(2)}) collective-permute-start(f32[8,128]{1,0:T(8,128)S(1)} %join.3.sum_ref), channel_id=1, source_target_pairs={{0,8},{4,12},{8,0},{12,4},{16,24},{20,28},{24,16},{28,20},{1,9},{5... | collective-permute-start | bytes 12296 | tf_op jit(solution)/shard_map/ppermute | solution.py:540
  25.1 8.5 %copy-start.2 = (f32[2560]{0:T(1024)S(1)}, f32[2560]{0:T(1024)}, u32[]{:S(2)}) copy-start(f32[2560]{0:T(1024)} %param.19) | copy-start | bytes 30724
  26.2 4.5 %collective-permute-start.10 = (f32[160,128]{1,0:T(8,128)S(1)}, f32[160,128]{1,0:T(8,128)S(1)}, u32[]{:S(2)}, u32[]{:S(2)}) collective-permute-start(f32[160,128]{1,0:T(8,128)S(1)} %get-tuple-element.72), channel_id=1, source_target_pairs={{0,8},{4,12},{8,0},{12,4},{16,24},{20,28},{24,16},{28,20},{1,9},{5... | collective-permute-start | bytes 245768 | tf_op jit(solution)/shard_map/ppermute | solution.py:557
  27.1 4.4 %collective-permute-start.11 = (f32[160,128]{1,0:T(8,128)S(1)}, f32[160,128]{1,0:T(8,128)S(1)}, u32[]{:S(2)}, u32[]{:S(2)}) collective-permute-start(f32[160,128]{1,0:T(8,128)S(1)} %get-tuple-element.74), channel_id=1, source_target_pairs={{0,4},{4,0},{8,12},{12,8},{16,20},{20,16},{24,28},{28,24},{1,5},{5... | collective-permute-start | bytes 245768 | tf_op jit(solution)/shard_map/ppermute | solution.py:558
  31.9 7.6 %collective-permute-start.14 = (bf16[128,1280]{1,0:T(8,128)(2,1)S(1)}, bf16[128,1280]{1,0:T(8,128)(2,1)S(1)}, u32[]{:S(2)}, u32[]{:S(2)}) collective-permute-start(bf16[128,1280]{1,0:T(8,128)(2,1)S(1)} %get-tuple-element.83), channel_id=1, source_target_pairs={{0,1},{1,0},{2,3},{3,2},{4,5},{5,4},{6,7},{7,6},{8,9},{9,8},{10,11... | collective-permute-start | bytes 983048 | tf_op jit(solution)/shard_map/ppermute | solution.py:565
  32.0 4.9 %collective-permute-start.12 = (f32[160,128]{1,0:T(8,128)S(1)}, f32[160,128]{1,0:T(8,128)S(1)}, u32[]{:S(2)}, u32[]{:S(2)}) collective-permute-start(f32[160,128]{1,0:T(8,128)S(1)} %get-tuple-element.76), channel_id=1, source_target_pairs={{0,2},{1,3},{2,0},{3,1},{4,6},{5,7},{6,4},{7,5},{8,10},{9,11},{10,... | collective-permute-start | bytes 245768 | tf_op jit(solution)/shard_map/ppermute | solution.py:560
  36.9 6.7 %collective-permute-start.15 = (f32[160,128]{1,0:T(8,128)S(1)}, f32[160,128]{1,0:T(8,128)S(1)}, u32[]{:S(2)}, u32[]{:S(2)}) collective-permute-start(f32[160,128]{1,0:T(8,128)S(1)} %last_y.1.kept_ref), channel_id=1, source_target_pairs={{0,16},{4,20},{8,24},{12,28},{16,0},{20,4},{24,8},{28,12},{1,17},{... | collective-permute-start | bytes 245768 | tf_op jit(solution)/shard_map/ppermute | solution.py:578
  43.6 1.3 %collective-permute-start.16 = (f32[80,128]{1,0:T(8,128)S(1)}, f32[80,128]{1,0:T(8,128)S(1)}, u32[]{:S(2)}, u32[]{:S(2)}) collective-permute-start(f32[80,128]{1,0:T(8,128)S(1)} %get-tuple-element.87), channel_id=1, source_target_pairs={{0,1},{1,0},{2,3},{3,2},{4,5},{5,4},{6,7},{7,6},{8,9},{9,8},{10,11... | collective-permute-start | bytes 122888 | tf_op jit(solution)/shard_map/ppermute | solution.py:581

commit v4 on v3

--- a/solution.py
+++ b/solution.py
@@ -19,6 +19,7 @@
 CH = D + BC
 CHUNK = 256
 EDGE = 16
+LEAD = 176
 F32 = jnp.float32
 BF16 = jnp.bfloat16
 VMEM = pl.BlockSpec(memory_space=pltpu.VMEM)
@@ -51,7 +52,7 @@
 def pack(w):
     high = w.astype(BF16).astype(F32)
     gap = jnp.zeros((64 - H, w.shape[1]), F32)
-    return jnp.concatenate([high, gap, w - high, gap], axis=0).T.astype(BF16)
+    return jnp.concatenate([high, gap, w - high, gap], axis=0).astype(BF16).T
 
 
 def beside(columns):
@@ -128,23 +129,27 @@
 
 
 def tail_kernel(
-    xbc_hbm, dt_hbm, bias_hbm, rate_hbm, skip_hbm, points_hbm, label_hbm, out_ref, mark_ref, dt_ref, columns_ref, points_ref,
-    bias_ref, rate_ref, skip_ref, spot_ref, label_ref, sems,
+    xbc_hbm, dt_hbm, bias_hbm, rate_hbm, skip_hbm, points_hbm, out_a_ref, out_b_ref, dt_ref, columns_ref, points_ref,
+    rows_ref, bias_ref, rate_ref, skip_ref, spot_ref, sems,
 ):
     n = xbc_hbm.shape[1]
-    width = xbc_hbm.shape[2]
     rows = xbc_hbm.at[0, pl.ds(n - EDGE, EDGE)]
     fetch(
         (
-            (dt_hbm, dt_ref), (rows, out_ref.at[:, pl.ds(0, width)]), (label_hbm, label_ref), (points_hbm, spot_ref),
+            (dt_hbm, dt_ref), (rows, rows_ref), (points_hbm, spot_ref),
             (bias_hbm, bias_ref.at[0]), (rate_hbm, rate_ref.at[0]), (skip_hbm, skip_ref.at[0]),
         ),
         sems,
     )
-    mark_ref[...] = jnp.zeros(mark_ref.shape, F32) + label_ref[0].astype(F32)
-    steps = jnp.concatenate([dt_ref[0].astype(F32), jnp.zeros((-H % EDGE, n), F32)], axis=0).astype(BF16)
-    for i in range(-(-H // EDGE)):
-        out_ref[:, width + i * n : width + (i + 1) * n] = steps[i * EDGE : (i + 1) * EDGE]
+    tail = rows_ref[...].astype(F32)[EDGE - 8 :]
+    steps = jnp.concatenate([dt_ref[0].astype(F32), jnp.zeros((4 * SIDE // 128 - H, n), F32)], axis=0).astype(BF16)
+    upper = lax.broadcasted_iota(jnp.int32, (8, 128), 0) < 4
+    for half, out_ref in enumerate((out_a_ref, out_b_ref)):
+        pieces = [half * HALF + i for i in range(0, HALF, 128)] + [D + i for i in range(0, BC, 128)]
+        pieces = [tail[:, i : i + 128] for i in pieces]
+        stack = [jnp.where(upper, pltpu.roll(pieces[i], 4, 0), pieces[i + 1]) for i in range(0, len(pieces), 2)]
+        out_ref[:, :128] = jnp.concatenate(stack, axis=0).astype(BF16)
+        out_ref[:, 128:] = steps
     columns_ref[...] = turned((bias_ref[...], rate_ref[...], skip_ref[...]))
     spot = lax.broadcasted_iota(jnp.int32, points_ref.shape, 0)
     points = jnp.zeros(points_ref.shape, jnp.int32)
@@ -153,19 +158,23 @@
     points_ref[...] = points
 
 
+def mark_kernel(label_ref, mark_ref):
+    mark_ref[...] = jnp.zeros(mark_ref.shape, F32) + label_ref[0].astype(F32)
+
+
 def steps_kernel(
-    own_ref, other_ref, columns_ref, points_ref, xbc_hbm, xbc_other_ref, conv_w_hbm, conv_b_hbm,
-    ws_ref, wr_ref, e_ref, rows_ref, small_ref, x_ref, taps_ref, bias_ref, sems,
+    own_ref, other_ref, columns_ref, points_ref, xbc_hbm, conv_w_hbm, conv_b_hbm,
+    ws_ref, wr_ref, e_ref, rows_ref, x_ref, taps_ref, bias_ref, *rest,
 ):
     place = lax.axis_index("seq")
     core = lax.rem(place, 2)
     n = own_ref.shape[2]
+    sems = rest[-1]
     col = pl.multiple_of(core * HALF, 128)
     copies = []
     for from_at, to_at, width in ((D, HALF, BC), (col, 0, HALF)):
         here, there = pl.ds(from_at, width), pl.ds(to_at, width)
-        for source, to in ((xbc_hbm, core), (xbc_other_ref, 1 - core)):
-            copies.append((source.at[0, :, here], x_ref.at[pl.ds(pl.multiple_of(to * n, 16), n), there]))
+        copies.append((xbc_hbm.at[0, :, here], x_ref.at[:, there]))
         copies.append((conv_w_hbm.at[:, here], taps_ref.at[:, there]))
         copies.append((conv_b_hbm.at[here], bias_ref.at[0, there]))
     copies = [pltpu.make_async_copy(source, to, sems.at[i]) for i, (source, to) in enumerate(copies)]
@@ -178,8 +187,12 @@
     dts = [step_sizes(jnp.where(first == (block == 0), own, other), bias) for block in range(2)]
     cums = running_sums([-rate * dt for dt in dts])
     ends = [cum[:, n - 1 : n] for cum in cums]
-    for block in range(2):
-        ws_ref[block * n : (block + 1) * n] = pack(dts[block] * jnp.exp(ends[block] - cums[block]))
+
+    def store(ref, values):
+        ref[:n] = pack(jnp.where(first, values[0], values[1]))
+        ref[n:] = pack(jnp.where(first, values[1], values[0]))
+
+    store(ws_ref, [dts[block] * jnp.exp(ends[block] - cums[block]) for block in range(2)])
     total = [cums[0], ends[0] + cums[1]]
     index = lax.broadcasted_iota(jnp.int32, (H, n), 1)
     weight = [jnp.zeros((H, n), F32), jnp.zeros((H, n), F32)]
@@ -188,14 +201,14 @@
         for block in range(2):
             seen = jnp.where(index + block * n <= at, jnp.exp(jnp.minimum(level - total[block], 0.0)), 0.0)
             weight[block] += inside * seen
-    for block in range(2):
-        wr_ref[block * n : (block + 1) * n] = pack(weight[block] * dts[block] * (1.0 / R))
+    store(wr_ref, [weight[block] * dts[block] * (1.0 / R) for block in range(2)])
     e_ref[...] = pack(jnp.exp(jnp.where(first, cums[0], cums[1])))
     decay = [jnp.exp(end) for end in ends]
     back = jnp.exp(-jnp.where(first, ends[0], ends[1]))
     rows_ref[...] = pack(beside((decay[0], decay[1], skip, back)))[0:16]
-    whole = beside((carry_of(found), jnp.exp(ends[0] + ends[1])))
-    small_ref[...] = jnp.concatenate([whole, jnp.zeros((128 - H, 128), F32)], axis=0).T[0:8]
+    if len(rest) > 1:
+        whole = beside((carry_of(found), jnp.exp(ends[0] + ends[1])))
+        rest[0][...] = jnp.concatenate([whole, jnp.zeros((128 - H, 128), F32)], axis=0).T[0:8]
     for copy in copies:
         copy.wait()
 
@@ -203,14 +216,8 @@
 def later_kernel(same_ref, cross_ref, columns_ref, points_ref, later_ref):
     place = lax.axis_index("seq")
     core = lax.rem(place, 2)
-    slabs = -(-H // EDGE)
-    n = (same_ref.shape[1] - CH) // slabs
-
-    def steps_of(ref):
-        slab = [ref[:, CH + i * n : CH + (i + 1) * n].astype(F32) for i in range(slabs)]
-        return jnp.concatenate(slab, axis=0)[:H]
-
-    same, cross = steps_of(same_ref), steps_of(cross_ref)
+    n = same_ref.shape[1] - 128
+    same, cross = same_ref[:, 128:].astype(F32)[:H], cross_ref[:, 128:].astype(F32)[:H]
     bias, rate = columns_ref[:, 0:1], columns_ref[:, 1:2]
     raws = [jnp.where((core == 0) == (block == 0), same, cross) for block in range(2)]
     cums = running_sums([-rate * step_sizes(raw, bias) for raw in raws])
@@ -220,79 +227,93 @@
 
 
 def state_kernel(
-    x_ref, edge_a_ref, edge_b_ref, ws_ref, wr_ref, rows_ref, later_ref, taps_ref, bias_ref,
+    x_ref, other_ref, edge_a_ref, edge_b_ref, ws_ref, wr_ref, rows_ref, later_ref, taps_ref, bias_ref,
     state_ref, early_ref, act_own_ref, act_other_ref, bc_ref, *rest,
     split,
 ):
-    reads = rest[:-3]
-    edge_ref, act_ref, read_ref = rest[-3:]
+    reads = rest[:-2]
+    bc_other_ref, read_ref = rest[-2:]
     place = lax.axis_index("seq")
     core = lax.rem(place, 2)
-    n = x_ref.shape[0] // 2
+    first = core == 0
+    n = x_ref.shape[0]
     started = jnp.where(place >= 2, 1.0, 0.0)
-    edge = jnp.where(core == 0, edge_a_ref[:, :CH].astype(F32), edge_b_ref[:, :CH].astype(F32)) * started
-    edge_ref[:, HALF:] = edge[:, D:].astype(BF16)
-    edge_ref[:, :HALF] = jnp.where(core == 0, edge[:, :HALF], edge[:, HALF:D]).astype(BF16)
+    edge = jnp.where(first, edge_a_ref[:, :128].astype(F32), edge_b_ref[:, :128].astype(F32)) * started
     tile = 128
 
-    def convolve(at):
+    def before(at):
+        pieces = []
+        for i in range(at // 128, (at + CHUNK) // 128):
+            piece = edge[i // 2 * 8 : i // 2 * 8 + 8]
+            pieces.append(pltpu.roll(piece, 4, 0) if i % 2 == 0 else piece)
+        return jnp.concatenate(pieces, axis=1)
+
+    def convolve(at, act_refs, to):
         cols = pl.ds(at, CHUNK)
+        from_cols = pl.ds(D + at - HALF if at >= HALF else pl.multiple_of(core * HALF + at, 128), CHUNK)
         taps = taps_ref[:, cols]
         bias = bias_ref[:, cols]
-        for t in range(2 * n // tile):
-            if t == 0:
-                seen = jnp.concatenate([edge_ref[:, cols], x_ref[:tile, cols]], axis=0).astype(F32)
-            else:
-                seen = x_ref[t * tile - EDGE : (t + 1) * tile, cols].astype(F32)
-            before = pltpu.roll(seen, 1, 0)
-            pair = taps[1:2] * seen + taps[0:1] * before
-            total = bias + taps[3:4] * seen[EDGE:] + taps[2:3] * before[EDGE:]
-            total += pltpu.roll(pair, 2, 0)[EDGE:]
-            act_ref[t * tile : (t + 1) * tile, cols] = silu(total).astype(BF16)
-
-    convolve(HALF)
-    b_turned = act_ref[:, HALF : HALF + N].astype(F32).T.astype(BF16)
-    @pl.loop(0, HALF // CHUNK, unroll=True)
-    def _(j):
-        at = pl.multiple_of(j * CHUNK, CHUNK)
+
+        def rows(side, start, count):
+            return (x_ref[start : start + count, cols] if side == 0 else other_ref[0, start : start + count, from_cols]).astype(F32)
+
+        ends = [rows(side, n - EDGE, EDGE)[EDGE - 8 :] for side in range(2)]
+        chip = before(at)
+        for side, act_ref in enumerate(act_refs):
+            ahead = jnp.where(first == (side == 0), chip, ends[1 - side])
+            for t in range(n // tile):
+                if t == 0:
+                    seen = jnp.concatenate([ahead, rows(side, 0, tile)], axis=0)
+                else:
+                    seen = rows(side, t * tile - EDGE, tile + EDGE)[EDGE - 8 :]
+                last = pltpu.roll(seen, 1, 0)
+                pair = taps[1:2] * seen + taps[0:1] * last
+                total = bias + taps[3:4] * seen[8:] + taps[2:3] * last[8:]
+                total += pltpu.roll(pair, 2, 0)[8:]
+                act_ref[t * tile : (t + 1) * tile, to : to + CHUNK] = silu(total).astype(BF16)
+
+    convolve(HALF, (bc_ref, bc_other_ref), 0)
+    b_turned = [ref[:, :N].T for ref in (bc_ref, bc_other_ref)]
+    both = jnp.concatenate(b_turned, axis=1)
+
+    for j in range(HALF // CHUNK):
+        at = j * CHUNK
         cols = pl.ds(at, CHUNK)
-        convolve(at)
+        convolve(at, (act_own_ref, act_other_ref), at)
         spread = spread_matrix(core * (H // 2) + j * (CHUNK // P_SIZE))
         table = dot(rows_ref[...], spread)
         ahead = dot(later_ref[...], spread)[0:1]
-        act = act_ref[:, cols].astype(F32)
+        act = jnp.concatenate([act_own_ref[:, cols], act_other_ref[:, cols]], axis=0).astype(F32)
         weighted = (act * dot(ws_ref[...], spread)).astype(BF16)
-        early = dot(b_turned[:, :n], weighted[:n])
-        late = dot(b_turned[:, n:], weighted[n:])
-        state = table[1:2] * early + late
-        early_ref[:, cols] = early.astype(BF16)
+        own = dot(b_turned[0], weighted[:n])
+        other = dot(b_turned[1], weighted[n:])
+        state = jnp.where(first, table[1:2], 1.0) * own + jnp.where(first, 1.0, table[1:2]) * other
+        early_ref[:, cols] = jnp.where(first, own, other).astype(BF16)
         state_ref[:, cols] = state.astype(BF16)
         read = act * dot(wr_ref[...], spread)
         high = read.astype(BF16)
         low = (read - high.astype(F32)).astype(BF16)
-        seen = dot(b_turned, high) + dot(b_turned, low) + ahead * state
+        seen = dot(both, high) + dot(both, low) + ahead * state
         read_ref[pl.ds(at, CHUNK)] = seen.T
 
     if split:
-        part = D // 16
+        part = D // 8
         x_bit = lax.rem(lax.axis_index("dp"), 2)
         z_bit = lax.rem(lax.axis_index("dp") // 2, 2)
 
-        def rows(z, x, y):
-            return read_ref[pl.ds(pl.multiple_of((4 * z + 2 * x + y) * part, 8), part)]
-
+        def rows(z, x, start, count):
+            return read_ref[pl.ds(pl.multiple_of((2 * z + x) * part + start, 8), count)]
+
+        rest = part - LEAD
         for q in range(2):
-            here = slice(q * part, (q + 1) * part)
-            reads[0][here] = rows(q, x_bit, 0)
-            reads[1][here] = rows(q, 1 - x_bit, 0)
-            reads[2][here] = rows(z_bit, q, 1)
-            reads[3][here] = rows(1 - z_bit, q, 1)
+            here = slice(q * LEAD, (q + 1) * LEAD)
+            reads[0][here] = rows(q, x_bit, 0, LEAD)
+            reads[1][here] = rows(q, 1 - x_bit, 0, LEAD)
+            here = slice(q * rest, (q + 1) * rest)
+            reads[2][here] = rows(z_bit, q, LEAD, rest)
+            reads[3][here] = rows(1 - z_bit, q, LEAD, rest)
     else:
         reads[0][...] = read_ref[...]
-    mine = pl.ds(pl.multiple_of(core * n, 16), n)
-    act_own_ref[...] = act_ref[mine, :HALF]
-    bc_ref[...] = act_ref[mine, HALF:]
-    act_other_ref[...] = act_ref[pl.ds(pl.multiple_of((1 - core) * n, 16), n), :HALF]
 
 
 def diagonal_kernel(act_own_ref, act_other_ref, bc_ref, ws_ref, e_ref, rows_ref, gate_ref, near_ref, far_ref):
@@ -302,7 +323,7 @@
     row = lax.broadcasted_iota(jnp.int32, (n, n), 0)
     lane = lax.broadcasted_iota(jnp.int32, (n, n), 1)
     masked = jnp.where(row >= lane, scores, 0.0).astype(BF16)
-    ws = ws_ref[pl.ds(pl.multiple_of(core * n, 16), n)]
+    ws = ws_ref[:n]
     for side, source in enumerate((act_own_ref, act_other_ref)):
         half = core if side == 0 else 1 - core
 
@@ -385,7 +406,6 @@
         return mark / ones - (1.0 - mark) / (sequences - ones)
 
     own = weight(mark_ref[1:2])
-    part = keep_a_ref.shape[0]
     place = lax.axis_index("dp")
     x_bit = lax.rem(place, 2)
     z_bit = lax.rem(place // 2, 2)
@@ -395,46 +415,47 @@
     )
     for kept, came, other_mark, bit, keep, send in work:
         other = weight(other_mark[1:2])
+        part = keep.shape[0]
         mine = pl.ds(pl.multiple_of(bit * part, 8), part)
         yours = pl.ds(pl.multiple_of((1 - bit) * part, 8), part)
         send[...] = own * kept[yours] + other * came[yours]
         keep[...] = own * kept[mine] + other * came[mine]
 
 
-def join_y_kernel(keep_a_ref, came_a_ref, keep_b_ref, came_b_ref, keep_ref, send_ref):
-    first = lax.rem(lax.axis_index("seq") // 2, 2) == 0
-    a = keep_a_ref[...] + came_a_ref[...]
-    b = keep_b_ref[...] + came_b_ref[...]
-    keep_ref[...] = jnp.where(first, a, b)
-    send_ref[...] = jnp.where(first, b, a)
-
-
-def last_kernel(kept_ref, came_ref, sum_ref):
-    sum_ref[...] = kept_ref[...] + came_ref[...]
-
-
-def core_kernel(kept_ref, came_ref, own_ref, send_ref):
-    part = own_ref.shape[0]
-    zero = kept_ref[0:part] + came_ref[0:part]
-    one = kept_ref[part:] + came_ref[part:]
-    first = lax.rem(lax.axis_index("seq"), 2) == 0
-    own_ref[...] = jnp.where(first, zero, one)
-    send_ref[...] = jnp.where(first, one, zero)
-
-
-def owner_kernel(own_ref, came_ref, out_ref):
-    z_bit = lax.rem(lax.axis_index("dp") // 4, 2)
-    out_ref[...] = jnp.where(z_bit == lax.rem(lax.axis_index("seq"), 2), own_ref[...], came_ref[...])
+def chunks_kernel(keep_a_ref, came_a_ref, keep_b_ref, came_b_ref, keep_ref, core_ref, same_ref, cross_ref):
+    place = lax.axis_index("seq")
+    part = keep_ref.shape[0]
+    upper = lax.rem(place // 2, 2) == 0
+    first = lax.rem(place, 2) == 0
+    rows = jnp.concatenate([keep_a_ref[...] + came_a_ref[...], keep_b_ref[...] + came_b_ref[...]], axis=0)
+    here = jnp.where(upper, rows[: 2 * part], rows[2 * part :])
+    there = jnp.where(upper, rows[2 * part :], rows[: 2 * part])
+    keep_ref[...] = jnp.where(first, here[:part], here[part:])
+    core_ref[...] = jnp.where(first, here[part:], here[:part])
+    same_ref[...] = jnp.where(first, there[:part], there[part:])
+    cross_ref[...] = jnp.where(first, there[part:], there[:part])
+
+
+def planes_kernel(own_ref, same_ref, core_ref, cross_ref, keep_ref, send_ref):
+    stays = lax.rem(lax.axis_index("dp") // 4, 2) == lax.rem(lax.axis_index("seq"), 2)
+    own = own_ref[...] + same_ref[...]
+    other = core_ref[...] + cross_ref[...]
+    keep_ref[...] = jnp.where(stays, own, other)
+    send_ref[...] = jnp.where(stays, other, own)
+
+
+def sum_kernel(keep_ref, came_ref, out_ref):
+    out_ref[...] = keep_ref[...] + came_ref[...]
 
 
 def swap(k):
     return [(i, i ^ k) for i in range(8)]
 
 
-def small_call(kernel, name, count, rows, *args):
-    part = jax.ShapeDtypeStruct((rows, N), F32)
+def small_call(kernel, name, counts, *args):
+    parts = tuple(jax.ShapeDtypeStruct((rows, N), F32) for rows in counts)
     return pl.pallas_call(
-        kernel, out_shape=(part,) * count, in_specs=[VMEM] * len(args), out_specs=(VMEM,) * count, compiler_params=params(8), name=name
+        kernel, out_shape=parts, in_specs=[VMEM] * len(args), out_specs=(VMEM,) * len(parts), compiler_params=params(8), name=name
     )(*args)
 
 
@@ -455,35 +476,37 @@
     dt_other = lax.ppermute(dt_turned, "seq", pair)
     xbc_other = lax.ppermute(xbc, "seq", pair)
     xbc_here = in_hbm(xbc)
-    tail, mark, dt_own, columns, points = pl.pallas_call(
+    payload = shape((4 * SIDE // 128, 128 + n), BF16)
+    tail_a, tail_b, dt_own, columns, points = pl.pallas_call(
         tail_kernel,
-        out_shape=(
-            shape((EDGE, CH + -(-H // EDGE) * n), BF16), shape((8, N), F32), shape((1, H, n), BF16),
-            shape((H, 8), F32), shape((8, 128), jnp.int32),
-        ),
-        in_specs=[HBM] * 7,
+        out_shape=(payload, payload, shape((1, H, n), BF16), shape((H, 8), F32), shape((8, 128), jnp.int32)),
+        in_specs=[HBM] * 6,
         out_specs=(VMEM,) * 5,
-        scratch_shapes=[pltpu.VMEM((1, H), F32)] * 3
-        + [pltpu.SMEM((1, R), jnp.int32), pltpu.SMEM((1,), jnp.int32), pltpu.SemaphoreType.DMA((7,))],
+        scratch_shapes=[pltpu.VMEM((EDGE, CH), BF16)]
+        + [pltpu.VMEM((1, H), F32)] * 3
+        + [pltpu.SMEM((1, R), jnp.int32), pltpu.SemaphoreType.DMA((6,))],
         compiler_params=params(8),
         name="tail",
-    )(xbc_here, in_hbm(dt_turned), in_hbm(dt_bias), in_hbm(a_rate), in_hbm(d_skip), in_hbm(readout), labels)
-    edge_a = lax.ppermute(tail, "seq", one_back)
-    edge_b = lax.ppermute(tail, "seq", two_back)
-
-    ws, wr, e, rows, small, x, taps, bias = pl.pallas_call(
+    )(xbc_here, in_hbm(dt_turned), in_hbm(dt_bias), in_hbm(a_rate), in_hbm(d_skip), in_hbm(readout))
+    edge_a = lax.ppermute(tail_a, "seq", one_back)
+    edge_b = lax.ppermute(tail_b, "seq", two_back)
+    mark = pl.pallas_call(
+        mark_kernel, out_shape=shape((8, N), F32), in_specs=[SMEM], out_specs=VMEM, compiler_params=params(8), name="mark"
+    )(tied(labels, points))
+
+    ws, wr, e, rows, x, taps, bias, *small = pl.pallas_call(
         steps_kernel,
         out_shape=(
-            shape((2 * n, 128), BF16), shape((2 * n, 128), BF16), shape((n, 128), BF16), shape((16, 128), BF16), shape((8, 128), F32),
-            shape((2 * n, SIDE), BF16), shape((KW, SIDE), F32), shape((1, SIDE), F32),
-        ),
-        in_specs=[VMEM] * 4 + [HBM, ANY, HBM, HBM],
-        out_specs=(VMEM,) * 8,
-        scratch_shapes=[pltpu.SemaphoreType.DMA((8,))],
+            shape((2 * n, 128), BF16), shape((2 * n, 128), BF16), shape((n, 128), BF16), shape((16, 128), BF16),
+            shape((n, SIDE), BF16), shape((KW, SIDE), F32), shape((1, SIDE), F32),
+        ) + ((shape((8, 128), F32),) if chips != 2 else ()),
+        in_specs=[VMEM] * 4 + [HBM] * 3,
+        out_specs=(VMEM,) * (8 if chips != 2 else 7),
+        scratch_shapes=[pltpu.SemaphoreType.DMA((6,))],
         compiler_params=params(16),
         cost_estimate=cost(2 * 6 * n * n * 128, 8 * n * 256),
         name="steps",
-    )(dt_own, dt_other, columns, points, xbc_here, xbc_other, in_hbm(conv_weight), in_hbm(conv_bias))
+    )(dt_own, dt_other, columns, points, xbc_here, in_hbm(conv_weight), in_hbm(conv_bias))
 
     if chips == 2:
         later = pl.pallas_call(
@@ -496,6 +519,7 @@
             name="later",
         )(edge_b, edge_a, tied(columns, ws), points)
     else:
+        small = small[0]
         later = jnp.zeros_like(small)
         for step in range(chips - 1):
             out = small.at[0:1].add(small[1:2] * later[0:1])
@@ -507,20 +531,20 @@
         ones = join(tied(mark, later), mark, lax.ppermute(mark, "dp", swap(4)))
         later = tied(later, ones)
 
-    read_rows = D // 8 if split else HALF
+    read_rows = (2 * LEAD, 2 * LEAD, D // 4 - 2 * LEAD, D // 4 - 2 * LEAD) if split else (HALF,)
     state, early, act_own, act_other, bc, *reads = pl.pallas_call(
         functools.partial(state_kernel, split=split),
         out_shape=(
             shape((N, HALF), BF16), shape((N, HALF), BF16),
             shape((n, HALF), BF16), shape((n, HALF), BF16), shape((n, BC), BF16),
-        ) + (shape((read_rows, N), F32),) * (4 if split else 1),
-        in_specs=[VMEM] * 9,
-        out_specs=(VMEM,) * (9 if split else 6),
-        scratch_shapes=[pltpu.VMEM((EDGE, SIDE), BF16), pltpu.VMEM((2 * n, SIDE), BF16), pltpu.VMEM((HALF, N), F32)],
+        ) + tuple(shape((count, N), F32) for count in read_rows),
+        in_specs=[VMEM] * 10,
+        out_specs=(VMEM,) * (5 + len(read_rows)),
+        scratch_shapes=[pltpu.VMEM((n, BC), BF16), pltpu.VMEM((HALF, N), F32)],
         compiler_params=params(24),
         cost_estimate=cost(50 * n * n * D, 4 * 2 * n * SIDE),
         name="states",
-    )(x, edge_a, edge_b, ws, wr, rows, later, taps, bias)
+    )(x, xbc_other, edge_a, edge_b, ws, wr, rows, later, taps, bias)
 
     h = state
     for step in range(chips - 1):
@@ -551,16 +575,19 @@
     if split:
         keep_x, near, reach = lax.optimization_barrier((keep_x, near, reach))
         keep_a, send_a, keep_b, send_b = small_call(
-            functools.partial(halves_kernel, sequences=float(sequences)), "halves", 4, D // 16,
+            functools.partial(halves_kernel, sequences=float(sequences)), "halves", (LEAD, LEAD, D // 8 - LEAD, D // 8 - LEAD),
             keep_x, came_x, keep_z, came_z, mark, x_mark, z_mark, ones,
         )
         came_a = lax.ppermute(send_a, "dp", swap(2))
         came_b = lax.ppermute(send_b, "dp", swap(1))
-        keep, send = small_call(join_y_kernel, "join_y", 2, D // 16, keep_a, came_a, keep_b, came_b)
-        came = lax.ppermute(send, "seq", [(i, i ^ 2) for i in range(places)])
+        keep, to_core, to_same, to_cross = small_call(chunks_kernel, "chunks", (D // 32,) * 4, keep_a, came_a, keep_b, came_b)
+        from_core = lax.ppermute(to_core, "seq", pair)
+        from_same = lax.ppermute(to_same, "seq", [(i, i ^ 2) for i in range(places)])
+        from_cross = lax.ppermute(to_cross, "seq", [(i, i ^ 3) for i in range(places)])
     h = tied(h, keep) if split else h
     h_own, h_send = pl.pallas_call(
-        carry_kernel, out_shape=(shape((N, HALF), BF16),) * 2, in_specs=[VMEM] * 3, out_specs=(VMEM,) * 2, compiler_params=params(8), name="carry"
+        carry_kernel, out_shape=(shape((N, HALF), BF16),) * 2, in_specs=[VMEM] * 3, out_specs=(VMEM,) * 2, compiler_params=params(8), name="carry",
+        cost_estimate=cost(8 * n * n * D, 4 * N * D),
     )(h, early, rows)
     h_other = lax.ppermute(h_send, "seq", pair)
     layer_out = pl.pallas_call(
@@ -574,12 +601,10 @@
         name="finish",
     )(near, reach, bc, h_own, h_other, norm_gain[None])
     if split:
-        (total,) = small_call(last_kernel, "last_y", 1, D // 16, keep, came)
-        came = lax.ppermute(total, "dp", swap(4))
-        total, layer_out = lax.optimization_barrier((total, layer_out))
-        own, send = small_call(core_kernel, "cores", 2, D // 32, total, came)
-        came = lax.ppermute(send, "seq", pair)
-        steering = small_call(owner_kernel, "owner", 1, D // 32, own, came)[0]
+        keep, send = small_call(planes_kernel, "planes", (D // 32,) * 2, keep, from_same, from_core, from_cross)
+        came = lax.ppermute(send, "dp", swap(4))
+        keep, layer_out = lax.optimization_barrier((keep, layer_out))
+        steering = small_call(sum_kernel, "sum", (D // 32,), keep, came)[0]
     else:
         ones = lax.psum(mark[0, 0], "dp")
         weight = mark[0, 0] / ones - (1.0 - mark[0, 0]) / (sequences - ones)

time: 45.7 us -> 41.9 us (0.917)
  waiting for transfers between devices: 11.7 us -> 8.6 us
  Pallas kernels: 13.4 us -> 12.6 us
    ppermute x5 -> x6, waiting for transfers between devices: 7.68 us -> 4.56 us  [the longest x1 1.85 us: on_device(): lax.ppermute(to_same, 'seq', [(i, i ^ 2) for i in range(places)])]
    ppermute x1, waiting for transfers between devices: 0.88 us -> 2.99 us  [on_device(): came_b = lax.ppermute(send_b, 'dp', swap(1))]
    ppermute x1, waiting for transfers between devices: 2.07 us -> 0.01 us  [on_device(): came_a = lax.ppermute(send_a, 'dp', swap(2))]
    ppermute x5 -> x6, starting transfers between devices: 7.02 us -> 7.2 us  [the longest x1 2.71 us: on_device(): edge_a = lax.ppermute(tail_a, 'seq', one_back)]
  transfers between devices with their start and end apart: 17 -> 18, of which waited for: 7 -> 5; matrix products, arithmetic and copies ran while one was open for 0% -> 0% of each run, Pallas kernels for 17% -> 18%
where the time goes in v4:
time: 41.9 us; the launch traced here: 41.7 us
  starting transfers between devices  19 us (45%)
  Pallas kernels  12.6 us (30%)
  waiting for transfers between devices  8.6 us (21%)
  between operations  1.45 us (3%)
    pallas_call x1, Pallas kernels, on_device(): pl.pallas_call(functools.partial(state_kernel, split=split), out_shape=(s...  4.38 us
    ppermute x1, waiting for transfers between devices, on_device(): came_b = lax.ppermute(send_b, 'dp', swap(1))  2.99 us
    ppermute x1, starting transfers between devices, on_device(): ones = join(tied(mark, later), mark, lax.ppermute(mark, 'dp', swap(4)))  2.97 us
    ppermute x1, starting transfers between devices, on_device(): edge_a = lax.ppermute(tail_a, 'seq', one_back)  2.71 us
    ppermute x1, starting transfers between devices, on_device(): came = lax.ppermute(send, 'dp', swap(4))  2.28 us
    pallas_call x1, Pallas kernels, on_device(): pl.pallas_call(diagonal_kernel, out_shape=(shape((2, n, HALF), F32), shap...  2.13 us
    ppermute x1, waiting for transfers between devices, on_device(): lax.ppermute(to_same, 'seq', [(i, i ^ 2) for i in range(places)])  1.85 us
    pallas_call x1, Pallas kernels, on_device(): pl.pallas_call(finish_kernel, out_shape=shape((1, n, D), BF16), in_specs=...  1.76 us
  transfers between devices with their start and end apart: 18, of which 5 were waited for; matrix products, arithmetic and copies ran while one was open for 0% of the time, Pallas kernels for 18%

profile of v4, /device:TPU:0, one launch (start us, length us, event | category | flops | bytes accessed | tf_op | source)
XLA Modules:
  0.0 41.7 jit_solution(13883409147035478431)
XLA Ops:
  0.6 0.5 %collective-permute-start.1 = (bf16[1,256,2816]{2,1,0:T(8,128)(2,1)}, bf16[1,256,2816]{2,1,0:T(8,128)(2,1)S(1)}, u32[]{:S(2)}, u32[]{:S(2)}) collective-permute-start(bf16[1,256,2816]{2,1,0:T(8,128)(2,1)} %xbc_hbm.3), channel_id=1, source_target_pairs={{0,1},{1,0},{2,3},{3,2},{4,5},{5,4},{6,7},{7,6},{8,9},{9,8},{10,11... | collective-permute-start | bytes 4325384 | tf_op jit(solution)/shard_map/ppermute | solution.py:477
  1.2 1.1 %tail.1 = (bf16[48,384]{1,0:T(8,128)(2,1)S(1)}, bf16[48,384]{1,0:T(8,128)(2,1)S(1)}, bf16[1,40,256]{2,1,0:T(8,128)(2,1)S(1)}, f32[40,8]{1,0:T(8,128)S(1)}, s32[8,128]{1,0:T(8,128)S(1)}) custom-call(bf16[1,256,2816]{2,1,0:T(8,128)(2,1)} %xbc_hbm.3, bf16[1,40,256]{2,1,0:T(8,128)(2,1)} %bitcast.1, f32[40]{0:T(128)} %bias_hbm.1, f32[40]{0:T(128)} %rate_hbm.1, ...), custom_call_target="tpu_custom_call" | custom-call | tf_op jit(solution)/shard_map/tail/pallas_call | solution.py:480
  2.2 2.7 %collective-permute-start.2 = (bf16[48,384]{1,0:T(8,128)(2,1)S(1)}, bf16[48,384]{1,0:T(8,128)(2,1)S(1)}, u32[]{:S(2)}, u32[]{:S(2)}) collective-permute-start(bf16[48,384]{1,0:T(8,128)(2,1)S(1)} %get-tuple-element.52), channel_id=1, source_target_pairs={{0,3},{1,2},{2,1},{3,0},{4,7},{5,6},{6,5},{7,4},{8,11},{9,10},{10,... | collective-permute-start | bytes 110600 | tf_op jit(solution)/shard_map/ppermute | solution.py:491
  4.9 0.2 collective-permute-start
  5.8 3.0 %collective-permute-start.4 = (f32[8,128]{1,0:T(8,128)S(1)}, f32[8,128]{1,0:T(8,128)S(1)}, u32[]{:S(2)}, u32[]{:S(2)}) collective-permute-start(f32[8,128]{1,0:T(8,128)S(1)} %mark.1.mark_ref.a_ref), channel_id=1, source_target_pairs={{0,16},{4,20},{8,24},{12,28},{16,0},{20,4},{24,8},{28,12},{1,17},{... | collective-permute-start | bytes 12296 | tf_op jit(solution)/shard_map/ppermute | solution.py:531
  8.8 1.7 %steps.1 = (bf16[512,128]{1,0:T(8,128)(2,1)S(1)}, bf16[512,128]{1,0:T(8,128)(2,1)S(1)}, bf16[256,128]{1,0:T(8,128)(2,1)S(1)}, bf16[16,128]{1,0:T(8,128)(2,1)S(1)...) custom-call(bf16[1,40,256]{2,1,0:T(8,128)(2,1)S(1)} %get-tuple-element.48.own_ref, ...), custom_call_target="tpu_custom_call" | custom-call | flops 100663296 | bytes 524288 | tf_op jit(solution)/shard_map/steps/pallas_call | solution.py:497
  10.5 0.6 %later.1.later_ref = bf16[16,128]{1,0:T(8,128)(2,1)S(1)} custom-call(bf16[48,384]{1,0:T(8,128)(2,1)S(1)} %collective-permute-done.3.same_ref.edge_b_ref, bf16[48,384]{1,0:T(8,128)(2,1)S(1)} %collective-permute-done.2.cross_ref.edge_a_ref, f32[40,8]{1,0:T(8,128)S(1)} %get-tuple-element.57.columns_ref, s32[8,128]{1,0:T(8,128)S(1)} %get-tuple-element.50.points_ref), custom_call_target="tpu_custom_call" | custom-call | flops 100663296 | bytes 524288 | tf_op jit(solution)/shard_map/later/pallas_call | solution.py:512
  11.1 0.0 copy-start
  11.1 4.4 %states.1 = (bf16[128,1280]{1,0:T(8,128)(2,1)S(1)}, bf16[128,1280]{1,0:T(8,128)(2,1)S(1)}, bf16[256,1280]{1,0:T(8,128)(2,1)S(1)}, bf16[256,1280]{1,0:T(8,128)(2,...) custom-call(bf16[256,1536]{1,0:T(8,128)(2,1)S(1)} %get-tuple-element, ...), custom_call_target="tpu_custom_call" | custom-call | flops 8388608000 | bytes 3145728 | tf_op jit(solution)/shard_map/states/pallas_call | solution.py:535
  15.5 0.3 collective-permute-start.5
  15.8 1.5 %collective-permute-start.8 = (f32[8,128]{1,0:T(8,128)S(1)}, f32[8,128]{1,0:T(8,128)S(1)}, u32[]{:S(2)}, u32[]{:S(2)}) collective-permute-start(f32[8,128]{1,0:T(8,128)S(1)} %join.2.a_ref), channel_id=1, source_target_pairs={{0,4},{4,0},{8,12},{12,8},{16,20},{20,16},{24,28},{28,24},{1,5},{5... | collective-permute-start | bytes 12296 | tf_op jit(solution)/shard_map/ppermute | solution.py:560
  17.3 0.5 %collective-permute-start.6 = (f32[352,128]{1,0:T(8,128)S(1)}, f32[352,128]{1,0:T(8,128)S(1)}, u32[]{:S(2)}, u32[]{:S(2)}) collective-permute-start(f32[352,128]{1,0:T(8,128)S(1)} %get-tuple-element.71), channel_id=1, source_target_pairs={{0,4},{4,0},{8,12},{12,8},{16,20},{20,16},{24,28},{28,24},{1,5},{5... | collective-permute-start | bytes 540680 | tf_op jit(solution)/shard_map/ppermute | solution.py:561
  17.8 1.6 %collective-permute-start.7 = (f32[288,128]{1,0:T(8,128)S(1)}, f32[288,128]{1,0:T(8,128)S(1)}, u32[]{:S(2)}, u32[]{:S(2)}) collective-permute-start(f32[288,128]{1,0:T(8,128)S(1)} %get-tuple-element.73), channel_id=1, source_target_pairs={{0,8},{4,12},{8,0},{12,4},{16,24},{20,28},{24,16},{28,20},{1,9},{5... | collective-permute-start | bytes 442376 | tf_op jit(solution)/shard_map/ppermute | solution.py:562
  19.4 1.5 %collective-permute-start.15 = (bf16[128,1280]{1,0:T(8,128)(2,1)S(1)}, bf16[128,1280]{1,0:T(8,128)(2,1)S(1)}, u32[]{:S(2)}, u32[]{:S(2)}) collective-permute-start(bf16[128,1280]{1,0:T(8,128)(2,1)S(1)} %get-tuple-element.86), channel_id=1, source_target_pairs={{0,2},{1,3},{2,0},{3,1},{4,6},{5,7},{6,4},{7,5},{8,10},{9,11},{10,... | collective-permute-start | bytes 983048 | tf_op jit(solution)/shard_map/ppermute | solution.py:554
  20.9 0.5 %collective-permute-start.9 = (f32[8,128]{1,0:T(8,128)S(1)}, f32[8,128]{1,0:T(8,128)S(1)}, u32[]{:S(2)}, u32[]{:S(2)}) collective-permute-start(f32[8,128]{1,0:T(8,128)S(1)} %join.3.sum_ref), channel_id=1, source_target_pairs={{0,8},{4,12},{8,0},{12,4},{16,24},{20,28},{24,16},{28,20},{1,9},{5... | collective-permute-start | bytes 12296 | tf_op jit(solution)/shard_map/ppermute | solution.py:564
  21.4 2.1 %diagonal.1 = (f32[2,256,1280]{2,1,0:T(8,128)S(1)}, f32[2,256,1280]{2,1,0:T(8,128)S(1)}) custom-call(bf16[256,1280]{1,0:T(8,128)(2,1)S(1)} %get-tuple-element.64.act_own_ref, bf16[256,1280]{1,0:T(8,128)(2,1)S(1)} %collective-permute-done.5.act_other_ref, bf16[256,256]{1,0:T(8,128)(2,1)S(1)} %get-tuple-element.66.bc_ref, ...), custom_call_target="tpu_custom_call" | custom-call | flops 4697620480 | bytes 2621440 | tf_op jit(solution)/shard_map/diagonal/pallas_call | solution.py:566
  23.5 1.0 %collective-permute-done.9.z_mark_ref = f32[8,128]{1,0:T(8,128)S(1)} collective-permute-done((f32[8,128]{1,0:T(8,128)S(1)}, f32[8,128]{1,0:T(8,128)S(1)}, u32[]{:S(2)}, u32[]{:S(2)}) %collective-permute-start.9) | collective-permute-done | bytes 4128 | tf_op jit(solution)/shard_map/ppermute | solution.py:564
  24.6 0.1 halves.1
  24.6 0.8 %collective-permute-start.10 = (f32[176,128]{1,0:T(8,128)S(1)}, f32[176,128]{1,0:T(8,128)S(1)}, u32[]{:S(2)}, u32[]{:S(2)}) collective-permute-start(f32[176,128]{1,0:T(8,128)S(1)} %get-tuple-element.76), channel_id=1, source_target_pairs={{0,8},{4,12},{8,0},{12,4},{16,24},{20,28},{24,16},{28,20},{1,9},{5... | collective-permute-start | bytes 270344 | tf_op jit(solution)/shard_map/ppermute | solution.py:581
  25.4 1.4 %collective-permute-start.11 = (f32[144,128]{1,0:T(8,128)S(1)}, f32[144,128]{1,0:T(8,128)S(1)}, u32[]{:S(2)}, u32[]{:S(2)}) collective-permute-start(f32[144,128]{1,0:T(8,128)S(1)} %get-tuple-element.78), channel_id=1, source_target_pairs={{0,4},{4,0},{8,12},{12,8},{16,20},{20,16},{24,28},{28,24},{1,5},{5... | collective-permute-start | bytes 221192 | tf_op jit(solution)/shard_map/ppermute | solution.py:582
  26.8 3.0 %collective-permute-done.11.came_b_ref = f32[144,128]{1,0:T(8,128)S(1)} collective-permute-done((f32[144,128]{1,0:T(8,128)S(1)}, f32[144,128]{1,0:T(8,128)S(1)}, u32[]{:S(2)}, u32[]{:S(2)}) %collective-permute-start.11) | collective-permute-done | bytes 73760 | tf_op jit(solution)/shard_map/ppermute | solution.py:582
  29.8 0.3 carry.1
  30.1 0.1 collective-permute-start.16
  30.2 1.6 %collective-permute-start.12 = (f32[80,128]{1,0:T(8,128)S(1)}, f32[80,128]{1,0:T(8,128)S(1)}, u32[]{:S(2)}, u32[]{:S(2)}) collective-permute-start(f32[80,128]{1,0:T(8,128)S(1)} %get-tuple-element.80), channel_id=1, source_target_pairs={{0,2},{1,3},{2,0},{3,1},{4,6},{5,7},{6,4},{7,5},{8,10},{9,11},{10,... | collective-permute-start | bytes 122888 | tf_op jit(solution)/shard_map/ppermute | solution.py:585
  31.8 0.2 collective-permute-start.13
  32.0 0.5 %collective-permute-start.14 = (f32[80,128]{1,0:T(8,128)S(1)}, f32[80,128]{1,0:T(8,128)S(1)}, u32[]{:S(2)}, u32[]{:S(2)}) collective-permute-start(f32[80,128]{1,0:T(8,128)S(1)} %get-tuple-element.82), channel_id=1, source_target_pairs={{0,3},{1,2},{2,1},{3,0},{4,7},{5,6},{6,5},{7,4},{8,11},{9,10},{10,... | collective-permute-start | bytes 122888 | tf_op jit(solution)/shard_map/ppermute | solution.py:586
  32.4 1.8 %collective-permute-done.12.same_ref = f32[80,128]{1,0:T(8,128)S(1)} collective-permute-done((f32[80,128]{1,0:T(8,128)S(1)}, f32[80,128]{1,0:T(8,128)S(1)}, u32[]{:S(2)}, u32[]{:S(2)}) %collective-permute-start.12) | collective-permute-done | bytes 40992 | tf_op jit(solution)/shard_map/ppermute | solution.py:585
  34.3 1.1 %collective-permute-done.14.cross_ref = f32[80,128]{1,0:T(8,128)S(1)} collective-permute-done((f32[80,128]{1,0:T(8,128)S(1)}, f32[80,128]{1,0:T(8,128)S(1)}, u32[]{:S(2)}, u32[]{:S(2)}) %collective-permute-start.14) | collective-permute-done | bytes 40992 | tf_op jit(solution)/shard_map/ppermute | solution.py:586
  35.4 2.3 %collective-permute-start.17 = (f32[80,128]{1,0:T(8,128)S(1)}, f32[80,128]{1,0:T(8,128)S(1)}, u32[]{:S(2)}, u32[]{:S(2)}) collective-permute-start(f32[80,128]{1,0:T(8,128)S(1)} %get-tuple-element.93), channel_id=1, source_target_pairs={{0,16},{4,20},{8,24},{12,28},{16,0},{20,4},{24,8},{28,12},{1,17},{... | collective-permute-start | bytes 122888 | tf_op jit(solution)/shard_map/ppermute | solution.py:605
  37.7 1.8 %finish.1 = bf16[1,256,2560]{2,1,0:T(8,128)(2,1)} custom-call(f32[2,256,1280]{2,1,0:T(8,128)S(1)} %get-tuple-element.84.near_ref, f32[2,256,1280]{2,1,0:T(8,128)S(1)} %get-tuple-element.85.far_ref, bf16[256,256]{1,0:T(8,128)(2,1)S(1)} %get-tuple-element.66.bc_ref, bf16[128,1280]{1,0:T(8,128)(2,1)S(1)} %get-tuple-element.89.h_own_ref, ...), custom_call_target="tpu_custom_call" | custom-call | flops 3355443200 | bytes 7864320 | tf_op jit(solution)/shard_map/finish/pallas_call | solution.py:593
  39.5 1.6 %collective-permute-done.17.came_ref = f32[80,128]{1,0:T(8,128)S(1)} collective-permute-done((f32[80,128]{1,0:T(8,128)S(1)}, f32[80,128]{1,0:T(8,128)S(1)}, u32[]{:S(2)}, u32[]{:S(2)}) %collective-permute-start.17) | collective-permute-done | bytes 40992 | tf_op jit(solution)/shard_map/ppermute | solution.py:605
  41.1 0.6 %sum.1 = f32[80,128]{1,0:T(8,128)} custom-call(f32[80,128]{1,0:T(8,128)S(1)} %get-tuple-element.92.keep_ref, f32[80,128]{1,0:T(8,128)S(1)} %collective-permute-done.17.came_ref), custom_call_target="tpu_custom_call" | custom-call | tf_op jit(solution)/shard_map/sum/pallas_call | solution.py:457
  (25 shorter events, 0.1 us)
Async XLA Ops:
  0.6 4.3 %copy-start.1 = (bf16[1,256,40]{1,2,0:T(8,128)(2,1)S(1)}, bf16[1,256,40]{1,2,0:T(8,128)(2,1)}, u32[]{:S(2)}) copy-start(bf16[1,256,40]{1,2,0:T(8,128)(2,1)} %param.13) | copy-start | bytes 61444
  0.6 10.4 %collective-permute-start.1 = (bf16[1,256,2816]{2,1,0:T(8,128)(2,1)}, bf16[1,256,2816]{2,1,0:T(8,128)(2,1)S(1)}, u32[]{:S(2)}, u32[]{:S(2)}) collective-permute-start(bf16[1,256,2816]{2,1,0:T(8,128)(2,1)} %xbc_hbm.3), channel_id=1, source_target_pairs={{0,1},{1,0},{2,3},{3,2},{4,5},{5,4},{6,7},{7,6},{8,9},{9,8},{10,11... | collective-permute-start | bytes 4325384 | tf_op jit(solution)/shard_map/ppermute | solution.py:477
  2.2 8.2 %collective-permute-start.2 = (bf16[48,384]{1,0:T(8,128)(2,1)S(1)}, bf16[48,384]{1,0:T(8,128)(2,1)S(1)}, u32[]{:S(2)}, u32[]{:S(2)}) collective-permute-start(bf16[48,384]{1,0:T(8,128)(2,1)S(1)} %get-tuple-element.52), channel_id=1, source_target_pairs={{0,3},{1,2},{2,1},{3,0},{4,7},{5,6},{6,5},{7,4},{8,11},{9,10},{10,... | collective-permute-start | bytes 110600 | tf_op jit(solution)/shard_map/ppermute | solution.py:491
  4.9 5.5 %collective-permute-start.3 = (bf16[48,384]{1,0:T(8,128)(2,1)S(1)}, bf16[48,384]{1,0:T(8,128)(2,1)S(1)}, u32[]{:S(2)}, u32[]{:S(2)}) collective-permute-start(bf16[48,384]{1,0:T(8,128)(2,1)S(1)} %get-tuple-element.53), channel_id=1, source_target_pairs={{0,2},{1,3},{2,0},{3,1},{4,6},{5,7},{6,4},{7,5},{8,10},{9,11},{10,... | collective-permute-start | bytes 110600 | tf_op jit(solution)/shard_map/ppermute | solution.py:492
  4.9 3.8 %collective-permute-start = (bf16[1,40,256]{2,1,0:T(8,128)(2,1)S(1)}, bf16[1,40,256]{2,1,0:T(8,128)(2,1)S(1)}, u32[]{:S(2)}, u32[]{:S(2)}) collective-permute-start(bf16[1,40,256]{2,1,0:T(8,128)(2,1)S(1)} %bitcast.2), channel_id=1, source_target_pairs={{0,1},{1,0},{2,3},{3,2},{4,5},{5,4},{6,7},{7,6},{8,9},{9,8},{10,11... | collective-permute-start | bytes 61448 | tf_op jit(solution)/shard_map/ppermute | solution.py:476
  5.8 5.3 %collective-permute-start.4 = (f32[8,128]{1,0:T(8,128)S(1)}, f32[8,128]{1,0:T(8,128)S(1)}, u32[]{:S(2)}, u32[]{:S(2)}) collective-permute-start(f32[8,128]{1,0:T(8,128)S(1)} %mark.1.mark_ref.a_ref), channel_id=1, source_target_pairs={{0,16},{4,20},{8,24},{12,28},{16,0},{20,4},{24,8},{28,12},{1,17},{... | collective-permute-start | bytes 12296 | tf_op jit(solution)/shard_map/ppermute | solution.py:531
  11.1 10.3 %copy-start = (bf16[1,256,2560]{2,1,0:T(8,128)(2,1)S(1)}, bf16[1,256,2560]{2,1,0:T(8,128)(2,1)}, u32[]{:S(2)}) copy-start(bf16[1,256,2560]{2,1,0:T(8,128)(2,1)} %gate_ref.1) | copy-start | bytes 3932164
  15.5 5.9 %collective-permute-start.5 = (bf16[256,1280]{1,0:T(8,128)(2,1)S(1)}, bf16[256,1280]{1,0:T(8,128)(2,1)S(1)}, u32[]{:S(2)}, u32[]{:S(2)}) collective-permute-start(bf16[256,1280]{1,0:T(8,128)(2,1)S(1)} %get-tuple-element.65), channel_id=1, source_target_pairs={{0,1},{1,0},{2,3},{3,2},{4,5},{5,4},{6,7},{7,6},{8,9},{9,8},{10,11... | collective-permute-start | bytes 1966088 | tf_op jit(solution)/shard_map/ppermute | solution.py:557
  15.8 5.1 %collective-permute-start.8 = (f32[8,128]{1,0:T(8,128)S(1)}, f32[8,128]{1,0:T(8,128)S(1)}, u32[]{:S(2)}, u32[]{:S(2)}) collective-permute-start(f32[8,128]{1,0:T(8,128)S(1)} %join.2.a_ref), channel_id=1, source_target_pairs={{0,4},{4,0},{8,12},{12,8},{16,20},{20,16},{24,28},{28,24},{1,5},{5... | collective-permute-start | bytes 12296 | tf_op jit(solution)/shard_map/ppermute | solution.py:560
  17.3 7.3 %collective-permute-start.6 = (f32[352,128]{1,0:T(8,128)S(1)}, f32[352,128]{1,0:T(8,128)S(1)}, u32[]{:S(2)}, u32[]{:S(2)}) collective-permute-start(f32[352,128]{1,0:T(8,128)S(1)} %get-tuple-element.71), channel_id=1, source_target_pairs={{0,4},{4,0},{8,12},{12,8},{16,20},{20,16},{24,28},{28,24},{1,5},{5... | collective-permute-start | bytes 540680 | tf_op jit(solution)/shard_map/ppermute | solution.py:561
  17.8 6.8 %collective-permute-start.7 = (f32[288,128]{1,0:T(8,128)S(1)}, f32[288,128]{1,0:T(8,128)S(1)}, u32[]{:S(2)}, u32[]{:S(2)}) collective-permute-start(f32[288,128]{1,0:T(8,128)S(1)} %get-tuple-element.73), channel_id=1, source_target_pairs={{0,8},{4,12},{8,0},{12,4},{16,24},{20,28},{24,16},{28,20},{1,9},{5... | collective-permute-start | bytes 442376 | tf_op jit(solution)/shard_map/ppermute | solution.py:562
  19.4 10.4 %collective-permute-start.15 = (bf16[128,1280]{1,0:T(8,128)(2,1)S(1)}, bf16[128,1280]{1,0:T(8,128)(2,1)S(1)}, u32[]{:S(2)}, u32[]{:S(2)}) collective-permute-start(bf16[128,1280]{1,0:T(8,128)(2,1)S(1)} %get-tuple-element.86), channel_id=1, source_target_pairs={{0,2},{1,3},{2,0},{3,1},{4,6},{5,7},{6,4},{7,5},{8,10},{9,11},{10,... | collective-permute-start | bytes 983048 | tf_op jit(solution)/shard_map/ppermute | solution.py:554
  20.9 3.7 %collective-permute-start.9 = (f32[8,128]{1,0:T(8,128)S(1)}, f32[8,128]{1,0:T(8,128)S(1)}, u32[]{:S(2)}, u32[]{:S(2)}) collective-permute-start(f32[8,128]{1,0:T(8,128)S(1)} %join.3.sum_ref), channel_id=1, source_target_pairs={{0,8},{4,12},{8,0},{12,4},{16,24},{20,28},{24,16},{28,20},{1,9},{5... | collective-permute-start | bytes 12296 | tf_op jit(solution)/shard_map/ppermute | solution.py:564
  24.6 5.1 %collective-permute-start.10 = (f32[176,128]{1,0:T(8,128)S(1)}, f32[176,128]{1,0:T(8,128)S(1)}, u32[]{:S(2)}, u32[]{:S(2)}) collective-permute-start(f32[176,128]{1,0:T(8,128)S(1)} %get-tuple-element.76), channel_id=1, source_target_pairs={{0,8},{4,12},{8,0},{12,4},{16,24},{20,28},{24,16},{28,20},{1,9},{5... | collective-permute-start | bytes 270344 | tf_op jit(solution)/shard_map/ppermute | solution.py:581
  25.4 4.4 %collective-permute-start.11 = (f32[144,128]{1,0:T(8,128)S(1)}, f32[144,128]{1,0:T(8,128)S(1)}, u32[]{:S(2)}, u32[]{:S(2)}) collective-permute-start(f32[144,128]{1,0:T(8,128)S(1)} %get-tuple-element.78), channel_id=1, source_target_pairs={{0,4},{4,0},{8,12},{12,8},{16,20},{20,16},{24,28},{28,24},{1,5},{5... | collective-permute-start | bytes 221192 | tf_op jit(solution)/shard_map/ppermute | solution.py:582
  29.8 2.6 %copy-start.2 = (f32[2560]{0:T(1024)S(1)}, f32[2560]{0:T(1024)}, u32[]{:S(2)}) copy-start(f32[2560]{0:T(1024)} %param.19) | copy-start | bytes 30724
  30.1 7.6 %collective-permute-start.16 = (bf16[128,1280]{1,0:T(8,128)(2,1)S(1)}, bf16[128,1280]{1,0:T(8,128)(2,1)S(1)}, u32[]{:S(2)}, u32[]{:S(2)}) collective-permute-start(bf16[128,1280]{1,0:T(8,128)(2,1)S(1)} %get-tuple-element.90), channel_id=1, source_target_pairs={{0,1},{1,0},{2,3},{3,2},{4,5},{5,4},{6,7},{7,6},{8,9},{9,8},{10,11... | collective-permute-start | bytes 983048 | tf_op jit(solution)/shard_map/ppermute | solution.py:592
  30.2 4.1 %collective-permute-start.12 = (f32[80,128]{1,0:T(8,128)S(1)}, f32[80,128]{1,0:T(8,128)S(1)}, u32[]{:S(2)}, u32[]{:S(2)}) collective-permute-start(f32[80,128]{1,0:T(8,128)S(1)} %get-tuple-element.80), channel_id=1, source_target_pairs={{0,2},{1,3},{2,0},{3,1},{4,6},{5,7},{6,4},{7,5},{8,10},{9,11},{10,... | collective-permute-start | bytes 122888 | tf_op jit(solution)/shard_map/ppermute | solution.py:585
  31.8 2.5 %collective-permute-start.13 = (f32[80,128]{1,0:T(8,128)S(1)}, f32[80,128]{1,0:T(8,128)S(1)}, u32[]{:S(2)}, u32[]{:S(2)}) collective-permute-start(f32[80,128]{1,0:T(8,128)S(1)} %get-tuple-element.81), channel_id=1, source_target_pairs={{0,1},{1,0},{2,3},{3,2},{4,5},{5,4},{6,7},{7,6},{8,9},{9,8},{10,11... | collective-permute-start | bytes 122888 | tf_op jit(solution)/shard_map/ppermute | solution.py:584
  32.0 3.4 %collective-permute-start.14 = (f32[80,128]{1,0:T(8,128)S(1)}, f32[80,128]{1,0:T(8,128)S(1)}, u32[]{:S(2)}, u32[]{:S(2)}) collective-permute-start(f32[80,128]{1,0:T(8,128)S(1)} %get-tuple-element.82), channel_id=1, source_target_pairs={{0,3},{1,2},{2,1},{3,0},{4,7},{5,6},{6,5},{7,4},{8,11},{9,10},{10,... | collective-permute-start | bytes 122888 | tf_op jit(solution)/shard_map/ppermute | solution.py:586
  35.4 5.6 %collective-permute-start.17 = (f32[80,128]{1,0:T(8,128)S(1)}, f32[80,128]{1,0:T(8,128)S(1)}, u32[]{:S(2)}, u32[]{:S(2)}) collective-permute-start(f32[80,128]{1,0:T(8,128)S(1)} %get-tuple-element.93), channel_id=1, source_target_pairs={{0,16},{4,20},{8,24},{12,28},{16,0},{20,4},{24,8},{28,12},{1,17},{... | collective-permute-start | bytes 122888 | tf_op jit(solution)/shard_map/ppermute | solution.py:605

commit v5 on v4

--- a/solution.py
+++ b/solution.py
@@ -53,6 +53,16 @@
     high = w.astype(BF16).astype(F32)
     gap = jnp.zeros((64 - H, w.shape[1]), F32)
     return jnp.concatenate([high, gap, w - high, gap], axis=0).astype(BF16).T
+
+
+def stand(w):
+    return jnp.concatenate([w, jnp.zeros((128 - H, w.shape[1]), F32)], axis=0).T
+
+
+def widen(w, first_head):
+    head = lax.broadcasted_iota(jnp.int32, w.shape, 1) // P_SIZE + first_head
+    picked = [jnp.take_along_axis(w, head + i, axis=1) for i in range(0, CHUNK // P_SIZE, 128 // P_SIZE)]
+    return jnp.concatenate(picked, axis=1)
 
 
 def beside(columns):
@@ -189,8 +199,8 @@
     ends = [cum[:, n - 1 : n] for cum in cums]
 
     def store(ref, values):
-        ref[:n] = pack(jnp.where(first, values[0], values[1]))
-        ref[n:] = pack(jnp.where(first, values[1], values[0]))
+        ref[:n] = stand(jnp.where(first, values[0], values[1]))
+        ref[n:] = stand(jnp.where(first, values[1], values[0]))
 
     store(ws_ref, [dts[block] * jnp.exp(ends[block] - cums[block]) for block in range(2)])
     total = [cums[0], ends[0] + cums[1]]
@@ -202,7 +212,7 @@
             seen = jnp.where(index + block * n <= at, jnp.exp(jnp.minimum(level - total[block], 0.0)), 0.0)
             weight[block] += inside * seen
     store(wr_ref, [weight[block] * dts[block] * (1.0 / R) for block in range(2)])
-    e_ref[...] = pack(jnp.exp(jnp.where(first, cums[0], cums[1])))
+    e_ref[...] = stand(jnp.exp(jnp.where(first, cums[0], cums[1])))
     decay = [jnp.exp(end) for end in ends]
     back = jnp.exp(-jnp.where(first, ends[0], ends[1]))
     rows_ref[...] = pack(beside((decay[0], decay[1], skip, back)))[0:16]
@@ -275,22 +285,24 @@
     convolve(HALF, (bc_ref, bc_other_ref), 0)
     b_turned = [ref[:, :N].T for ref in (bc_ref, bc_other_ref)]
     both = jnp.concatenate(b_turned, axis=1)
+    rows = jnp.concatenate([rows_ref[...], later_ref[...]], axis=0)
 
     for j in range(HALF // CHUNK):
         at = j * CHUNK
         cols = pl.ds(at, CHUNK)
         convolve(at, (act_own_ref, act_other_ref), at)
-        spread = spread_matrix(core * (H // 2) + j * (CHUNK // P_SIZE))
-        table = dot(rows_ref[...], spread)
-        ahead = dot(later_ref[...], spread)[0:1]
+        head = core * (H // 2) + j * (CHUNK // P_SIZE)
+        spread = spread_matrix(head)
+        wide = dot(rows, spread)
+        table, ahead = wide[:16], wide[16:17]
         act = jnp.concatenate([act_own_ref[:, cols], act_other_ref[:, cols]], axis=0).astype(F32)
-        weighted = (act * dot(ws_ref[...], spread)).astype(BF16)
+        weighted = (act * widen(ws_ref[...], head)).astype(BF16)
         own = dot(b_turned[0], weighted[:n])
         other = dot(b_turned[1], weighted[n:])
         state = jnp.where(first, table[1:2], 1.0) * own + jnp.where(first, 1.0, table[1:2]) * other
         early_ref[:, cols] = jnp.where(first, own, other).astype(BF16)
         state_ref[:, cols] = state.astype(BF16)
-        read = act * dot(wr_ref[...], spread)
+        read = act * widen(wr_ref[...], head)
         high = read.astype(BF16)
         low = (read - high.astype(F32)).astype(BF16)
         seen = dot(both, high) + dot(both, low) + ahead * state
@@ -331,11 +343,12 @@
         def _(j):
             at = pl.multiple_of(j * CHUNK, CHUNK)
             cols = pl.ds(at, CHUNK)
-            spread = spread_matrix(half * (H // 2) + j * (CHUNK // P_SIZE))
+            head = half * (H // 2) + j * (CHUNK // P_SIZE)
+            spread = spread_matrix(head)
             act = source[:, cols].astype(F32)
-            weighted = (act * dot(ws, spread)).astype(BF16)
+            weighted = (act * widen(ws, head)).astype(BF16)
             table = dot(rows_ref[...], spread)
-            decay = dot(e_ref[...], spread)
+            decay = widen(e_ref[...], head)
             value = decay * (table[3:4] * dot(masked, weighted)) + table[2:3] * act
             gate = silu(gate_ref[0, :, pl.ds(pl.multiple_of(half * HALF + at, CHUNK), CHUNK)].astype(F32))
             near_ref[side, :, cols] = value * gate
@@ -497,14 +510,14 @@
     ws, wr, e, rows, x, taps, bias, *small = pl.pallas_call(
         steps_kernel,
         out_shape=(
-            shape((2 * n, 128), BF16), shape((2 * n, 128), BF16), shape((n, 128), BF16), shape((16, 128), BF16),
+            shape((2 * n, 128), F32), shape((2 * n, 128), F32), shape((n, 128), F32), shape((16, 128), BF16),
             shape((n, SIDE), BF16), shape((KW, SIDE), F32), shape((1, SIDE), F32),
         ) + ((shape((8, 128), F32),) if chips != 2 else ()),
         in_specs=[VMEM] * 4 + [HBM] * 3,
         out_specs=(VMEM,) * (8 if chips != 2 else 7),
         scratch_shapes=[pltpu.SemaphoreType.DMA((6,))],
         compiler_params=params(16),
-        cost_estimate=cost(2 * 6 * n * n * 128, 8 * n * 256),
+        cost_estimate=cost(30 * n * n * 1024, 8 * n * 256),
         name="steps",
     )(dt_own, dt_other, columns, points, xbc_here, in_hbm(conv_weight), in_hbm(conv_bias))
 
@@ -515,7 +528,7 @@
             in_specs=[VMEM] * 4,
             out_specs=VMEM,
             compiler_params=params(16),
-            cost_estimate=cost(2 * 6 * n * n * 128, 8 * n * 256),
+            cost_estimate=cost(10 * n * n * 1024, 8 * n * 256),
             name="later",
         )(edge_b, edge_a, tied(columns, ws), points)
     else:

time: 41.9 us -> 41.3 us (0.986)
  Pallas kernels: 12.6 us -> 12 us
    pallas_call x1, Pallas kernels: 4.38 us -> 3.74 us  [on_device(): pl.pallas_call(functools.partial(state_kernel, split=split), out_shape=(s...]
where the time goes in v5:
time: 41.3 us; the launch traced here: 41.1 us
  starting transfers between devices  18.8 us (46%)
  Pallas kernels  12 us (29%)
  waiting for transfers between devices  8.83 us (21%)
  between operations  1.45 us (4%)
    pallas_call x1, Pallas kernels, on_device(): pl.pallas_call(functools.partial(state_kernel, split=split), out_shape=(s...  3.74 us
    ppermute x1, waiting for transfers between devices, on_device(): came_b = lax.ppermute(send_b, 'dp', swap(1))  3.21 us
    ppermute x1, starting transfers between devices, on_device(): ones = join(tied(mark, later), mark, lax.ppermute(mark, 'dp', swap(4)))  2.77 us
    ppermute x1, starting transfers between devices, on_device(): edge_a = lax.ppermute(tail_a, 'seq', one_back)  2.69 us
    ppermute x1, starting transfers between devices, on_device(): came = lax.ppermute(send, 'dp', swap(4))  2.24 us
    pallas_call x1, Pallas kernels, on_device(): pl.pallas_call(diagonal_kernel, out_shape=(shape((2, n, HALF), F32), shap...  2.06 us
    ppermute x1, waiting for transfers between devices, on_device(): lax.ppermute(to_same, 'seq', [(i, i ^ 2) for i in range(places)])  1.85 us
    pallas_call x1, Pallas kernels, on_device(): pl.pallas_call(finish_kernel, out_shape=shape((1, n, D), BF16), in_specs=...  1.76 us
  transfers between devices with their start and end apart: 18, of which 5 were waited for; matrix products, arithmetic and copies ran while one was open for 0% of the time, Pallas kernels for 18%

profile of v5, /device:TPU:0, one launch (start us, length us, event | category | flops | bytes accessed | tf_op | source)
XLA Modules:
  0.0 41.1 jit_solution(17216489245016413991)
XLA Ops:
  0.6 0.5 %collective-permute-start.1 = (bf16[1,256,2816]{2,1,0:T(8,128)(2,1)}, bf16[1,256,2816]{2,1,0:T(8,128)(2,1)S(1)}, u32[]{:S(2)}, u32[]{:S(2)}) collective-permute-start(bf16[1,256,2816]{2,1,0:T(8,128)(2,1)} %xbc_hbm.3), channel_id=1, source_target_pairs={{0,1},{1,0},{2,3},{3,2},{4,5},{5,4},{6,7},{7,6},{8,9},{9,8},{10,11... | collective-permute-start | bytes 4325384 | tf_op jit(solution)/shard_map/ppermute | solution.py:490
  1.1 0.1 collective-permute-start
  1.2 1.1 %tail.1 = (bf16[48,384]{1,0:T(8,128)(2,1)S(1)}, bf16[48,384]{1,0:T(8,128)(2,1)S(1)}, bf16[1,40,256]{2,1,0:T(8,128)(2,1)S(1)}, f32[40,8]{1,0:T(8,128)S(1)}, s32[8,128]{1,0:T(8,128)S(1)}) custom-call(bf16[1,256,2816]{2,1,0:T(8,128)(2,1)} %xbc_hbm.3, bf16[1,40,256]{2,1,0:T(8,128)(2,1)} %bitcast.2, f32[40]{0:T(128)} %bias_hbm.1, f32[40]{0:T(128)} %rate_hbm.1, ...), custom_call_target="tpu_custom_call" | custom-call | tf_op jit(solution)/shard_map/tail/pallas_call | solution.py:493
  2.3 2.7 %collective-permute-start.2 = (bf16[48,384]{1,0:T(8,128)(2,1)S(1)}, bf16[48,384]{1,0:T(8,128)(2,1)S(1)}, u32[]{:S(2)}, u32[]{:S(2)}) collective-permute-start(bf16[48,384]{1,0:T(8,128)(2,1)S(1)} %get-tuple-element.52), channel_id=1, source_target_pairs={{0,3},{1,2},{2,1},{3,0},{4,7},{5,6},{6,5},{7,4},{8,11},{9,10},{10,... | collective-permute-start | bytes 110600 | tf_op jit(solution)/shard_map/ppermute | solution.py:504
  5.0 0.4 collective-permute-start.3
  6.0 2.8 %collective-permute-start.4 = (f32[8,128]{1,0:T(8,128)S(1)}, f32[8,128]{1,0:T(8,128)S(1)}, u32[]{:S(2)}, u32[]{:S(2)}) collective-permute-start(f32[8,128]{1,0:T(8,128)S(1)} %mark.1.mark_ref.a_ref), channel_id=1, source_target_pairs={{0,16},{4,20},{8,24},{12,28},{16,0},{20,4},{24,8},{28,12},{1,17},{... | collective-permute-start | bytes 12296 | tf_op jit(solution)/shard_map/ppermute | solution.py:544
  8.8 1.7 %steps.1 = (f32[512,128]{1,0:T(8,128)S(1)}, f32[512,128]{1,0:T(8,128)S(1)}, f32[256,128]{1,0:T(8,128)S(1)}, bf16[16,128]{1,0:T(8,128)(2,1)S(1)}, bf16[256,1536]{...) custom-call(bf16[1,40,256]{2,1,0:T(8,128)(2,1)S(1)} %get-tuple-element.48.own_ref, ...), custom_call_target="tpu_custom_call" | custom-call | flops 2013265920 | bytes 524288 | tf_op jit(solution)/shard_map/steps/pallas_call | solution.py:510
  10.6 0.6 %later.1.later_ref = bf16[16,128]{1,0:T(8,128)(2,1)S(1)} custom-call(bf16[48,384]{1,0:T(8,128)(2,1)S(1)} %collective-permute-done.3.same_ref.edge_b_ref, bf16[48,384]{1,0:T(8,128)(2,1)S(1)} %collective-permute-done.2.cross_ref.edge_a_ref, f32[40,8]{1,0:T(8,128)S(1)} %get-tuple-element.57.columns_ref, s32[8,128]{1,0:T(8,128)S(1)} %get-tuple-element.50.points_ref), custom_call_target="tpu_custom_call" | custom-call | flops 671088640 | bytes 524288 | tf_op jit(solution)/shard_map/later/pallas_call | solution.py:525
  11.2 3.7 %states.1 = (bf16[128,1280]{1,0:T(8,128)(2,1)S(1)}, bf16[128,1280]{1,0:T(8,128)(2,1)S(1)}, bf16[256,1280]{1,0:T(8,128)(2,1)S(1)}, bf16[256,1280]{1,0:T(8,128)(2,...) custom-call(bf16[256,1536]{1,0:T(8,128)(2,1)S(1)} %get-tuple-element, ...), custom_call_target="tpu_custom_call" | custom-call | flops 8388608000 | bytes 3145728 | tf_op jit(solution)/shard_map/states/pallas_call | solution.py:548
  14.9 0.1 collective-permute-start.5
  15.0 1.6 %collective-permute-start.8 = (f32[8,128]{1,0:T(8,128)S(1)}, f32[8,128]{1,0:T(8,128)S(1)}, u32[]{:S(2)}, u32[]{:S(2)}) collective-permute-start(f32[8,128]{1,0:T(8,128)S(1)} %join.2.a_ref), channel_id=1, source_target_pairs={{0,4},{4,0},{8,12},{12,8},{16,20},{20,16},{24,28},{28,24},{1,5},{5... | collective-permute-start | bytes 12296 | tf_op jit(solution)/shard_map/ppermute | solution.py:573
  16.6 0.5 %collective-permute-start.6 = (f32[352,128]{1,0:T(8,128)S(1)}, f32[352,128]{1,0:T(8,128)S(1)}, u32[]{:S(2)}, u32[]{:S(2)}) collective-permute-start(f32[352,128]{1,0:T(8,128)S(1)} %get-tuple-element.71), channel_id=1, source_target_pairs={{0,4},{4,0},{8,12},{12,8},{16,20},{20,16},{24,28},{28,24},{1,5},{5... | collective-permute-start | bytes 540680 | tf_op jit(solution)/shard_map/ppermute | solution.py:574
  17.1 1.6 %collective-permute-start.7 = (f32[288,128]{1,0:T(8,128)S(1)}, f32[288,128]{1,0:T(8,128)S(1)}, u32[]{:S(2)}, u32[]{:S(2)}) collective-permute-start(f32[288,128]{1,0:T(8,128)S(1)} %get-tuple-element.73), channel_id=1, source_target_pairs={{0,8},{4,12},{8,0},{12,4},{16,24},{20,28},{24,16},{28,20},{1,9},{5... | collective-permute-start | bytes 442376 | tf_op jit(solution)/shard_map/ppermute | solution.py:575
  18.7 1.5 %collective-permute-start.15 = (bf16[128,1280]{1,0:T(8,128)(2,1)S(1)}, bf16[128,1280]{1,0:T(8,128)(2,1)S(1)}, u32[]{:S(2)}, u32[]{:S(2)}) collective-permute-start(bf16[128,1280]{1,0:T(8,128)(2,1)S(1)} %get-tuple-element.86), channel_id=1, source_target_pairs={{0,2},{1,3},{2,0},{3,1},{4,6},{5,7},{6,4},{7,5},{8,10},{9,11},{10,... | collective-permute-start | bytes 983048 | tf_op jit(solution)/shard_map/ppermute | solution.py:567
  20.2 0.5 %collective-permute-start.9 = (f32[8,128]{1,0:T(8,128)S(1)}, f32[8,128]{1,0:T(8,128)S(1)}, u32[]{:S(2)}, u32[]{:S(2)}) collective-permute-start(f32[8,128]{1,0:T(8,128)S(1)} %join.3.sum_ref), channel_id=1, source_target_pairs={{0,8},{4,12},{8,0},{12,4},{16,24},{20,28},{24,16},{28,20},{1,9},{5... | collective-permute-start | bytes 12296 | tf_op jit(solution)/shard_map/ppermute | solution.py:577
  20.7 2.1 %diagonal.1 = (f32[2,256,1280]{2,1,0:T(8,128)S(1)}, f32[2,256,1280]{2,1,0:T(8,128)S(1)}) custom-call(bf16[256,1280]{1,0:T(8,128)(2,1)S(1)} %get-tuple-element.64.act_own_ref, bf16[256,1280]{1,0:T(8,128)(2,1)S(1)} %collective-permute-done.5.act_other_ref, bf16[256,256]{1,0:T(8,128)(2,1)S(1)} %get-tuple-element.66.bc_ref, ...), custom_call_target="tpu_custom_call" | custom-call | flops 4697620480 | bytes 2621440 | tf_op jit(solution)/shard_map/diagonal/pallas_call | solution.py:579
  22.8 1.1 %collective-permute-done.9.z_mark_ref = f32[8,128]{1,0:T(8,128)S(1)} collective-permute-done((f32[8,128]{1,0:T(8,128)S(1)}, f32[8,128]{1,0:T(8,128)S(1)}, u32[]{:S(2)}, u32[]{:S(2)}) %collective-permute-start.9) | collective-permute-done | bytes 4128 | tf_op jit(solution)/shard_map/ppermute | solution.py:577
  23.9 0.1 halves.1
  23.9 0.9 %collective-permute-start.10 = (f32[176,128]{1,0:T(8,128)S(1)}, f32[176,128]{1,0:T(8,128)S(1)}, u32[]{:S(2)}, u32[]{:S(2)}) collective-permute-start(f32[176,128]{1,0:T(8,128)S(1)} %get-tuple-element.76), channel_id=1, source_target_pairs={{0,8},{4,12},{8,0},{12,4},{16,24},{20,28},{24,16},{28,20},{1,9},{5... | collective-permute-start | bytes 270344 | tf_op jit(solution)/shard_map/ppermute | solution.py:594
  24.9 1.1 %collective-permute-start.11 = (f32[144,128]{1,0:T(8,128)S(1)}, f32[144,128]{1,0:T(8,128)S(1)}, u32[]{:S(2)}, u32[]{:S(2)}) collective-permute-start(f32[144,128]{1,0:T(8,128)S(1)} %get-tuple-element.78), channel_id=1, source_target_pairs={{0,4},{4,0},{8,12},{12,8},{16,20},{20,16},{24,28},{28,24},{1,5},{5... | collective-permute-start | bytes 221192 | tf_op jit(solution)/shard_map/ppermute | solution.py:595
  26.0 3.2 %collective-permute-done.11.came_b_ref = f32[144,128]{1,0:T(8,128)S(1)} collective-permute-done((f32[144,128]{1,0:T(8,128)S(1)}, f32[144,128]{1,0:T(8,128)S(1)}, u32[]{:S(2)}, u32[]{:S(2)}) %collective-permute-start.11) | collective-permute-done | bytes 73760 | tf_op jit(solution)/shard_map/ppermute | solution.py:595
  29.3 0.3 carry.1
  29.6 0.1 collective-permute-start.16
  29.7 1.6 %collective-permute-start.12 = (f32[80,128]{1,0:T(8,128)S(1)}, f32[80,128]{1,0:T(8,128)S(1)}, u32[]{:S(2)}, u32[]{:S(2)}) collective-permute-start(f32[80,128]{1,0:T(8,128)S(1)} %get-tuple-element.80), channel_id=1, source_target_pairs={{0,2},{1,3},{2,0},{3,1},{4,6},{5,7},{6,4},{7,5},{8,10},{9,11},{10,... | collective-permute-start | bytes 122888 | tf_op jit(solution)/shard_map/ppermute | solution.py:598
  31.3 0.2 collective-permute-start.13
  31.4 0.5 %collective-permute-start.14 = (f32[80,128]{1,0:T(8,128)S(1)}, f32[80,128]{1,0:T(8,128)S(1)}, u32[]{:S(2)}, u32[]{:S(2)}) collective-permute-start(f32[80,128]{1,0:T(8,128)S(1)} %get-tuple-element.82), channel_id=1, source_target_pairs={{0,3},{1,2},{2,1},{3,0},{4,7},{5,6},{6,5},{7,4},{8,11},{9,10},{10,... | collective-permute-start | bytes 122888 | tf_op jit(solution)/shard_map/ppermute | solution.py:599
  31.9 1.8 %collective-permute-done.12.same_ref = f32[80,128]{1,0:T(8,128)S(1)} collective-permute-done((f32[80,128]{1,0:T(8,128)S(1)}, f32[80,128]{1,0:T(8,128)S(1)}, u32[]{:S(2)}, u32[]{:S(2)}) %collective-permute-start.12) | collective-permute-done | bytes 40992 | tf_op jit(solution)/shard_map/ppermute | solution.py:598
  33.8 1.1 %collective-permute-done.14.cross_ref = f32[80,128]{1,0:T(8,128)S(1)} collective-permute-done((f32[80,128]{1,0:T(8,128)S(1)}, f32[80,128]{1,0:T(8,128)S(1)}, u32[]{:S(2)}, u32[]{:S(2)}) %collective-permute-start.14) | collective-permute-done | bytes 40992 | tf_op jit(solution)/shard_map/ppermute | solution.py:599
  34.9 2.2 %collective-permute-start.17 = (f32[80,128]{1,0:T(8,128)S(1)}, f32[80,128]{1,0:T(8,128)S(1)}, u32[]{:S(2)}, u32[]{:S(2)}) collective-permute-start(f32[80,128]{1,0:T(8,128)S(1)} %get-tuple-element.93), channel_id=1, source_target_pairs={{0,16},{4,20},{8,24},{12,28},{16,0},{20,4},{24,8},{28,12},{1,17},{... | collective-permute-start | bytes 122888 | tf_op jit(solution)/shard_map/ppermute | solution.py:618
  37.1 1.8 %finish.1 = bf16[1,256,2560]{2,1,0:T(8,128)(2,1)} custom-call(f32[2,256,1280]{2,1,0:T(8,128)S(1)} %get-tuple-element.84.near_ref, f32[2,256,1280]{2,1,0:T(8,128)S(1)} %get-tuple-element.85.far_ref, bf16[256,256]{1,0:T(8,128)(2,1)S(1)} %get-tuple-element.66.bc_ref, bf16[128,1280]{1,0:T(8,128)(2,1)S(1)} %get-tuple-element.89.h_own_ref, ...), custom_call_target="tpu_custom_call" | custom-call | flops 3355443200 | bytes 7864320 | tf_op jit(solution)/shard_map/finish/pallas_call | solution.py:606
  38.9 1.5 %collective-permute-done.17.came_ref = f32[80,128]{1,0:T(8,128)S(1)} collective-permute-done((f32[80,128]{1,0:T(8,128)S(1)}, f32[80,128]{1,0:T(8,128)S(1)}, u32[]{:S(2)}, u32[]{:S(2)}) %collective-permute-start.17) | collective-permute-done | bytes 40992 | tf_op jit(solution)/shard_map/ppermute | solution.py:618
  40.4 0.6 %sum.1 = f32[80,128]{1,0:T(8,128)} custom-call(f32[80,128]{1,0:T(8,128)S(1)} %get-tuple-element.92.keep_ref, f32[80,128]{1,0:T(8,128)S(1)} %collective-permute-done.17.came_ref), custom_call_target="tpu_custom_call" | custom-call | tf_op jit(solution)/shard_map/sum/pallas_call | solution.py:470
  (23 shorter events, 0.1 us)
Async XLA Ops:
  0.6 10.5 %collective-permute-start.1 = (bf16[1,256,2816]{2,1,0:T(8,128)(2,1)}, bf16[1,256,2816]{2,1,0:T(8,128)(2,1)S(1)}, u32[]{:S(2)}, u32[]{:S(2)}) collective-permute-start(bf16[1,256,2816]{2,1,0:T(8,128)(2,1)} %xbc_hbm.3), channel_id=1, source_target_pairs={{0,1},{1,0},{2,3},{3,2},{4,5},{5,4},{6,7},{7,6},{8,9},{9,8},{10,11... | collective-permute-start | bytes 4325384 | tf_op jit(solution)/shard_map/ppermute | solution.py:490
  1.1 7.7 %collective-permute-start = (bf16[1,40,256]{2,1,0:T(8,128)(2,1)}, bf16[1,40,256]{2,1,0:T(8,128)(2,1)S(1)}, u32[]{:S(2)}, u32[]{:S(2)}) collective-permute-start(bf16[1,40,256]{2,1,0:T(8,128)(2,1)} %bitcast.1), channel_id=1, source_target_pairs={{0,1},{1,0},{2,3},{3,2},{4,5},{5,4},{6,7},{7,6},{8,9},{9,8},{10,11... | collective-permute-start | bytes 61448 | tf_op jit(solution)/shard_map/ppermute | solution.py:489
  2.3 8.3 %collective-permute-start.2 = (bf16[48,384]{1,0:T(8,128)(2,1)S(1)}, bf16[48,384]{1,0:T(8,128)(2,1)S(1)}, u32[]{:S(2)}, u32[]{:S(2)}) collective-permute-start(bf16[48,384]{1,0:T(8,128)(2,1)S(1)} %get-tuple-element.52), channel_id=1, source_target_pairs={{0,3},{1,2},{2,1},{3,0},{4,7},{5,6},{6,5},{7,4},{8,11},{9,10},{10,... | collective-permute-start | bytes 110600 | tf_op jit(solution)/shard_map/ppermute | solution.py:504
  5.0 5.6 %collective-permute-start.3 = (bf16[48,384]{1,0:T(8,128)(2,1)S(1)}, bf16[48,384]{1,0:T(8,128)(2,1)S(1)}, u32[]{:S(2)}, u32[]{:S(2)}) collective-permute-start(bf16[48,384]{1,0:T(8,128)(2,1)S(1)} %get-tuple-element.53), channel_id=1, source_target_pairs={{0,2},{1,3},{2,0},{3,1},{4,6},{5,7},{6,4},{7,5},{8,10},{9,11},{10,... | collective-permute-start | bytes 110600 | tf_op jit(solution)/shard_map/ppermute | solution.py:505
  6.0 5.1 %collective-permute-start.4 = (f32[8,128]{1,0:T(8,128)S(1)}, f32[8,128]{1,0:T(8,128)S(1)}, u32[]{:S(2)}, u32[]{:S(2)}) collective-permute-start(f32[8,128]{1,0:T(8,128)S(1)} %mark.1.mark_ref.a_ref), channel_id=1, source_target_pairs={{0,16},{4,20},{8,24},{12,28},{16,0},{20,4},{24,8},{28,12},{1,17},{... | collective-permute-start | bytes 12296 | tf_op jit(solution)/shard_map/ppermute | solution.py:544
  11.2 9.5 %copy-start = (bf16[1,256,2560]{2,1,0:T(8,128)(2,1)S(1)}, bf16[1,256,2560]{2,1,0:T(8,128)(2,1)}, u32[]{:S(2)}) copy-start(bf16[1,256,2560]{2,1,0:T(8,128)(2,1)} %gate_ref.1) | copy-start | bytes 3932164
  14.9 5.8 %collective-permute-start.5 = (bf16[256,1280]{1,0:T(8,128)(2,1)S(1)}, bf16[256,1280]{1,0:T(8,128)(2,1)S(1)}, u32[]{:S(2)}, u32[]{:S(2)}) collective-permute-start(bf16[256,1280]{1,0:T(8,128)(2,1)S(1)} %get-tuple-element.65), channel_id=1, source_target_pairs={{0,1},{1,0},{2,3},{3,2},{4,5},{5,4},{6,7},{7,6},{8,9},{9,8},{10,11... | collective-permute-start | bytes 1966088 | tf_op jit(solution)/shard_map/ppermute | solution.py:570
  15.0 5.2 %collective-permute-start.8 = (f32[8,128]{1,0:T(8,128)S(1)}, f32[8,128]{1,0:T(8,128)S(1)}, u32[]{:S(2)}, u32[]{:S(2)}) collective-permute-start(f32[8,128]{1,0:T(8,128)S(1)} %join.2.a_ref), channel_id=1, source_target_pairs={{0,4},{4,0},{8,12},{12,8},{16,20},{20,16},{24,28},{28,24},{1,5},{5... | collective-permute-start | bytes 12296 | tf_op jit(solution)/shard_map/ppermute | solution.py:573
  16.6 7.3 %collective-permute-start.6 = (f32[352,128]{1,0:T(8,128)S(1)}, f32[352,128]{1,0:T(8,128)S(1)}, u32[]{:S(2)}, u32[]{:S(2)}) collective-permute-start(f32[352,128]{1,0:T(8,128)S(1)} %get-tuple-element.71), channel_id=1, source_target_pairs={{0,4},{4,0},{8,12},{12,8},{16,20},{20,16},{24,28},{28,24},{1,5},{5... | collective-permute-start | bytes 540680 | tf_op jit(solution)/shard_map/ppermute | solution.py:574
  17.1 6.8 %collective-permute-start.7 = (f32[288,128]{1,0:T(8,128)S(1)}, f32[288,128]{1,0:T(8,128)S(1)}, u32[]{:S(2)}, u32[]{:S(2)}) collective-permute-start(f32[288,128]{1,0:T(8,128)S(1)} %get-tuple-element.73), channel_id=1, source_target_pairs={{0,8},{4,12},{8,0},{12,4},{16,24},{20,28},{24,16},{28,20},{1,9},{5... | collective-permute-start | bytes 442376 | tf_op jit(solution)/shard_map/ppermute | solution.py:575
  18.7 10.6 %collective-permute-start.15 = (bf16[128,1280]{1,0:T(8,128)(2,1)S(1)}, bf16[128,1280]{1,0:T(8,128)(2,1)S(1)}, u32[]{:S(2)}, u32[]{:S(2)}) collective-permute-start(bf16[128,1280]{1,0:T(8,128)(2,1)S(1)} %get-tuple-element.86), channel_id=1, source_target_pairs={{0,2},{1,3},{2,0},{3,1},{4,6},{5,7},{6,4},{7,5},{8,10},{9,11},{10,... | collective-permute-start | bytes 983048 | tf_op jit(solution)/shard_map/ppermute | solution.py:567
  20.2 3.7 %collective-permute-start.9 = (f32[8,128]{1,0:T(8,128)S(1)}, f32[8,128]{1,0:T(8,128)S(1)}, u32[]{:S(2)}, u32[]{:S(2)}) collective-permute-start(f32[8,128]{1,0:T(8,128)S(1)} %join.3.sum_ref), channel_id=1, source_target_pairs={{0,8},{4,12},{8,0},{12,4},{16,24},{20,28},{24,16},{28,20},{1,9},{5... | collective-permute-start | bytes 12296 | tf_op jit(solution)/shard_map/ppermute | solution.py:577
  23.9 5.3 %collective-permute-start.10 = (f32[176,128]{1,0:T(8,128)S(1)}, f32[176,128]{1,0:T(8,128)S(1)}, u32[]{:S(2)}, u32[]{:S(2)}) collective-permute-start(f32[176,128]{1,0:T(8,128)S(1)} %get-tuple-element.76), channel_id=1, source_target_pairs={{0,8},{4,12},{8,0},{12,4},{16,24},{20,28},{24,16},{28,20},{1,9},{5... | collective-permute-start | bytes 270344 | tf_op jit(solution)/shard_map/ppermute | solution.py:594
  24.9 4.4 %collective-permute-start.11 = (f32[144,128]{1,0:T(8,128)S(1)}, f32[144,128]{1,0:T(8,128)S(1)}, u32[]{:S(2)}, u32[]{:S(2)}) collective-permute-start(f32[144,128]{1,0:T(8,128)S(1)} %get-tuple-element.78), channel_id=1, source_target_pairs={{0,4},{4,0},{8,12},{12,8},{16,20},{20,16},{24,28},{28,24},{1,5},{5... | collective-permute-start | bytes 221192 | tf_op jit(solution)/shard_map/ppermute | solution.py:595
  29.3 2.6 %copy-start.1 = (f32[2560]{0:T(1024)S(1)}, f32[2560]{0:T(1024)}, u32[]{:S(2)}) copy-start(f32[2560]{0:T(1024)} %param.19) | copy-start | bytes 30724
  29.6 7.5 %collective-permute-start.16 = (bf16[128,1280]{1,0:T(8,128)(2,1)S(1)}, bf16[128,1280]{1,0:T(8,128)(2,1)S(1)}, u32[]{:S(2)}, u32[]{:S(2)}) collective-permute-start(bf16[128,1280]{1,0:T(8,128)(2,1)S(1)} %get-tuple-element.90), channel_id=1, source_target_pairs={{0,1},{1,0},{2,3},{3,2},{4,5},{5,4},{6,7},{7,6},{8,9},{9,8},{10,11... | collective-permute-start | bytes 983048 | tf_op jit(solution)/shard_map/ppermute | solution.py:605
  29.7 4.1 %collective-permute-start.12 = (f32[80,128]{1,0:T(8,128)S(1)}, f32[80,128]{1,0:T(8,128)S(1)}, u32[]{:S(2)}, u32[]{:S(2)}) collective-permute-start(f32[80,128]{1,0:T(8,128)S(1)} %get-tuple-element.80), channel_id=1, source_target_pairs={{0,2},{1,3},{2,0},{3,1},{4,6},{5,7},{6,4},{7,5},{8,10},{9,11},{10,... | collective-permute-start | bytes 122888 | tf_op jit(solution)/shard_map/ppermute | solution.py:598
  31.3 2.5 %collective-permute-start.13 = (f32[80,128]{1,0:T(8,128)S(1)}, f32[80,128]{1,0:T(8,128)S(1)}, u32[]{:S(2)}, u32[]{:S(2)}) collective-permute-start(f32[80,128]{1,0:T(8,128)S(1)} %get-tuple-element.81), channel_id=1, source_target_pairs={{0,1},{1,0},{2,3},{3,2},{4,5},{5,4},{6,7},{7,6},{8,9},{9,8},{10,11... | collective-permute-start | bytes 122888 | tf_op jit(solution)/shard_map/ppermute | solution.py:597
  31.4 3.4 %collective-permute-start.14 = (f32[80,128]{1,0:T(8,128)S(1)}, f32[80,128]{1,0:T(8,128)S(1)}, u32[]{:S(2)}, u32[]{:S(2)}) collective-permute-start(f32[80,128]{1,0:T(8,128)S(1)} %get-tuple-element.82), channel_id=1, source_target_pairs={{0,3},{1,2},{2,1},{3,0},{4,7},{5,6},{6,5},{7,4},{8,11},{9,10},{10,... | collective-permute-start | bytes 122888 | tf_op jit(solution)/shard_map/ppermute | solution.py:599
  34.9 5.5 %collective-permute-start.17 = (f32[80,128]{1,0:T(8,128)S(1)}, f32[80,128]{1,0:T(8,128)S(1)}, u32[]{:S(2)}, u32[]{:S(2)}) collective-permute-start(f32[80,128]{1,0:T(8,128)S(1)} %get-tuple-element.93), channel_id=1, source_target_pairs={{0,16},{4,20},{8,24},{12,28},{16,0},{20,4},{24,8},{28,12},{1,17},{... | collective-permute-start | bytes 122888 | tf_op jit(solution)/shard_map/ppermute | solution.py:618

commit v6 on v5

--- a/solution.py
+++ b/solution.py
@@ -19,7 +19,7 @@
 CH = D + BC
 CHUNK = 256
 EDGE = 16
-LEAD = 176
+LEAD = 192
 F32 = jnp.float32
 BF16 = jnp.bfloat16
 VMEM = pl.BlockSpec(memory_space=pltpu.VMEM)
@@ -237,7 +237,7 @@
 
 
 def state_kernel(
-    x_ref, other_ref, edge_a_ref, edge_b_ref, ws_ref, wr_ref, rows_ref, later_ref, taps_ref, bias_ref,
+    x_ref, other_ref, edge_a_ref, edge_b_ref, ws_ref, wr_ref, rows_ref, later_ref, taps_ref, bias_ref, mark_ref,
     state_ref, early_ref, act_own_ref, act_other_ref, bc_ref, *rest,
     split,
 ):
@@ -324,6 +324,8 @@
             here = slice(q * rest, (q + 1) * rest)
             reads[2][here] = rows(z_bit, q, LEAD, rest)
             reads[3][here] = rows(1 - z_bit, q, LEAD, rest)
+        reads[1][2 * LEAD :] = mark_ref[...]
+        reads[3][2 * rest :] = mark_ref[...]
     else:
         reads[0][...] = read_ref[...]
 
@@ -409,11 +411,13 @@
 
 
 def halves_kernel(
-    kept_x_ref, came_x_ref, kept_z_ref, came_z_ref, mark_ref, x_mark_ref, z_mark_ref, sum_ref,
+    kept_x_ref, came_x_ref, kept_z_ref, came_z_ref, mark_ref, across_ref,
     keep_a_ref, send_a_ref, keep_b_ref, send_b_ref,
     *, sequences,
 ):
-    ones = sum_ref[0:1] + z_mark_ref[0:1]
+    x_mark_ref = came_x_ref.at[kept_x_ref.shape[0] :]
+    z_mark_ref = came_z_ref.at[kept_z_ref.shape[0] :]
+    ones = (mark_ref[0:1] + x_mark_ref[0:1]) + (z_mark_ref[0:1] + across_ref[0:1])
 
     def weight(mark):
         return mark / ones - (1.0 - mark) / (sequences - ones)
@@ -542,22 +546,23 @@
 
     if split:
         ones = join(tied(mark, later), mark, lax.ppermute(mark, "dp", swap(4)))
-        later = tied(later, ones)
-
-    read_rows = (2 * LEAD, 2 * LEAD, D // 4 - 2 * LEAD, D // 4 - 2 * LEAD) if split else (HALF,)
+    else:
+        ones = mark
+
+    read_rows = (2 * LEAD, 2 * LEAD + 8, D // 4 - 2 * LEAD, D // 4 - 2 * LEAD + 8) if split else (HALF,)
     state, early, act_own, act_other, bc, *reads = pl.pallas_call(
         functools.partial(state_kernel, split=split),
         out_shape=(
             shape((N, HALF), BF16), shape((N, HALF), BF16),
             shape((n, HALF), BF16), shape((n, HALF), BF16), shape((n, BC), BF16),
         ) + tuple(shape((count, N), F32) for count in read_rows),
-        in_specs=[VMEM] * 10,
+        in_specs=[VMEM] * 11,
         out_specs=(VMEM,) * (5 + len(read_rows)),
         scratch_shapes=[pltpu.VMEM((n, BC), BF16), pltpu.VMEM((HALF, N), F32)],
         compiler_params=params(24),
         cost_estimate=cost(50 * n * n * D, 4 * 2 * n * SIDE),
         name="states",
-    )(x, xbc_other, edge_a, edge_b, ws, wr, rows, later, taps, bias)
+    )(x, xbc_other, edge_a, edge_b, ws, wr, rows, later, taps, bias, ones)
 
     h = state
     for step in range(chips - 1):
@@ -570,33 +575,42 @@
     act_in = lax.ppermute(act_other, "seq", pair)
     if split:
         keep_x, send_x, keep_z, send_z = reads
-        x_mark = lax.ppermute(tied(ones, send_x), "dp", swap(1))
         came_x = lax.ppermute(send_x, "dp", swap(1))
         came_z = lax.ppermute(send_z, "dp", swap(2))
-        ones = join(mark, ones, x_mark)
-        z_mark = lax.ppermute(ones, "dp", swap(2))
-
-    near, reach = pl.pallas_call(
-        diagonal_kernel,
-        out_shape=(shape((2, n, HALF), F32), shape((2, n, HALF), F32)),
-        in_specs=[VMEM] * 7,
-        out_specs=(VMEM, VMEM),
-        compiler_params=params(24),
-        cost_estimate=cost(28 * n * n * D, 4 * n * D),
-        name="diagonal",
-    )(act_own, act_in, bc, ws, e, rows, gate_input)
+        across = lax.ppermute(tied(ones, send_x), "dp", swap(3))
+
     if split:
-        keep_x, near, reach = lax.optimization_barrier((keep_x, near, reach))
         keep_a, send_a, keep_b, send_b = small_call(
             functools.partial(halves_kernel, sequences=float(sequences)), "halves", (LEAD, LEAD, D // 8 - LEAD, D // 8 - LEAD),
-            keep_x, came_x, keep_z, came_z, mark, x_mark, z_mark, ones,
+            keep_x, came_x, keep_z, came_z, ones, across,
         )
         came_a = lax.ppermute(send_a, "dp", swap(2))
         came_b = lax.ppermute(send_b, "dp", swap(1))
+        act_in = tied(act_in, keep_a)
+        near, reach = pl.pallas_call(
+            diagonal_kernel,
+            out_shape=(shape((2, n, HALF), F32), shape((2, n, HALF), F32)),
+            in_specs=[VMEM] * 7,
+            out_specs=(VMEM, VMEM),
+            compiler_params=params(24),
+            cost_estimate=cost(28 * n * n * D, 4 * n * D),
+            name="diagonal",
+        )(act_own, act_in, bc, ws, e, rows, gate_input)
+        keep_b, near, reach = lax.optimization_barrier((keep_b, near, reach))
         keep, to_core, to_same, to_cross = small_call(chunks_kernel, "chunks", (D // 32,) * 4, keep_a, came_a, keep_b, came_b)
         from_core = lax.ppermute(to_core, "seq", pair)
         from_same = lax.ppermute(to_same, "seq", [(i, i ^ 2) for i in range(places)])
         from_cross = lax.ppermute(to_cross, "seq", [(i, i ^ 3) for i in range(places)])
+    else:
+        near, reach = pl.pallas_call(
+            diagonal_kernel,
+            out_shape=(shape((2, n, HALF), F32), shape((2, n, HALF), F32)),
+            in_specs=[VMEM] * 7,
+            out_specs=(VMEM, VMEM),
+            compiler_params=params(24),
+            cost_estimate=cost(28 * n * n * D, 4 * n * D),
+            name="diagonal",
+        )(act_own, act_in, bc, ws, e, rows, gate_input)
     h = tied(h, keep) if split else h
     h_own, h_send = pl.pallas_call(
         carry_kernel, out_shape=(shape((N, HALF), BF16),) * 2, in_specs=[VMEM] * 3, out_specs=(VMEM,) * 2, compiler_params=params(8), name="carry",

time: 41.3 us -> 40.6 us (0.983)
  waiting for transfers between devices: 8.83 us -> 7.89 us
    ppermute x1, waiting for transfers between devices: 3.21 us -> 0.67 us  [on_device(): came_b = lax.ppermute(send_b, 'dp', swap(1))]
    ppermute x2 -> x1, starting transfers between devices: 2.06 us -> 0.42 us  [on_device(): across = lax.ppermute(tied(ones, send_x), 'dp', swap(3))]
    ppermute x2 -> x1, waiting for transfers between devices: 1.09 us -> 2.57 us  [on_device(): across = lax.ppermute(tied(ones, send_x), 'dp', swap(3))]
    ppermute x1, starting transfers between devices: 0.53 us -> 1.56 us  [on_device(): came_x = lax.ppermute(send_x, 'dp', swap(1))]
    ppermute x1, starting transfers between devices: 0.95 us -> 1.49 us  [on_device(): came_a = lax.ppermute(send_a, 'dp', swap(2))]
  transfers between devices with their start and end apart: 18 -> 17, of which waited for: 5 -> 5; matrix products, arithmetic and copies ran while one was open for 0% -> 0% of each run, Pallas kernels for 18% -> 18%
where the time goes in v6:
time: 40.6 us; the launch traced here: 40.5 us
  starting transfers between devices  19.1 us (47%)
  Pallas kernels  12 us (30%)
  waiting for transfers between devices  7.89 us (19%)
  between operations  1.45 us (4%)
    pallas_call x1, Pallas kernels, on_device(): pl.pallas_call(functools.partial(state_kernel, split=split), out_shape=(s...  3.8 us
    ppermute x1, starting transfers between devices, on_device(): ones = join(tied(mark, later), mark, lax.ppermute(mark, 'dp', swap(4)))  2.77 us
    ppermute x1, starting transfers between devices, on_device(): edge_a = lax.ppermute(tail_a, 'seq', one_back)  2.69 us
    ppermute x1, waiting for transfers between devices, on_device(): across = lax.ppermute(tied(ones, send_x), 'dp', swap(3))  2.57 us
    ppermute x1, starting transfers between devices, on_device(): came = lax.ppermute(send, 'dp', swap(4))  2.24 us
    pallas_call x1, Pallas kernels, on_device(): pl.pallas_call(diagonal_kernel, out_shape=(shape((2, n, HALF), F32), shap...  2.09 us
    ppermute x1, waiting for transfers between devices, on_device(): lax.ppermute(to_same, 'seq', [(i, i ^ 2) for i in range(places)])  1.85 us
    pallas_call x1, Pallas kernels, on_device(): pl.pallas_call(finish_kernel, out_shape=shape((1, n, D), BF16), in_specs=...  1.75 us
  transfers between devices with their start and end apart: 17, of which 5 were waited for; matrix products, arithmetic and copies ran while one was open for 0% of the time, Pallas kernels for 18%

profile of v6, /device:TPU:0, one launch (start us, length us, event | category | flops | bytes accessed | tf_op | source)
XLA Modules:
  0.0 40.5 jit_solution(13186919961345956062)
XLA Ops:
  0.6 0.5 %collective-permute-start.1 = (bf16[1,256,2816]{2,1,0:T(8,128)(2,1)}, bf16[1,256,2816]{2,1,0:T(8,128)(2,1)S(1)}, u32[]{:S(2)}, u32[]{:S(2)}) collective-permute-start(bf16[1,256,2816]{2,1,0:T(8,128)(2,1)} %xbc_hbm.3), channel_id=1, source_target_pairs={{0,1},{1,0},{2,3},{3,2},{4,5},{5,4},{6,7},{7,6},{8,9},{9,8},{10,11... | collective-permute-start | bytes 4325384 | tf_op jit(solution)/shard_map/ppermute | solution.py:494
  1.1 0.1 collective-permute-start
  1.2 1.1 %tail.1 = (bf16[48,384]{1,0:T(8,128)(2,1)S(1)}, bf16[48,384]{1,0:T(8,128)(2,1)S(1)}, bf16[1,40,256]{2,1,0:T(8,128)(2,1)S(1)}, f32[40,8]{1,0:T(8,128)S(1)}, s32[8,128]{1,0:T(8,128)S(1)}) custom-call(bf16[1,256,2816]{2,1,0:T(8,128)(2,1)} %xbc_hbm.3, bf16[1,40,256]{2,1,0:T(8,128)(2,1)} %bitcast.2, f32[40]{0:T(128)} %bias_hbm.1, f32[40]{0:T(128)} %rate_hbm.1, ...), custom_call_target="tpu_custom_call" | custom-call | tf_op jit(solution)/shard_map/tail/pallas_call | solution.py:497
  2.3 2.7 %collective-permute-start.2 = (bf16[48,384]{1,0:T(8,128)(2,1)S(1)}, bf16[48,384]{1,0:T(8,128)(2,1)S(1)}, u32[]{:S(2)}, u32[]{:S(2)}) collective-permute-start(bf16[48,384]{1,0:T(8,128)(2,1)S(1)} %get-tuple-element.52), channel_id=1, source_target_pairs={{0,3},{1,2},{2,1},{3,0},{4,7},{5,6},{6,5},{7,4},{8,11},{9,10},{10,... | collective-permute-start | bytes 110600 | tf_op jit(solution)/shard_map/ppermute | solution.py:508
  5.0 0.4 collective-permute-start.3
  6.0 2.8 %collective-permute-start.4 = (f32[8,128]{1,0:T(8,128)S(1)}, f32[8,128]{1,0:T(8,128)S(1)}, u32[]{:S(2)}, u32[]{:S(2)}) collective-permute-start(f32[8,128]{1,0:T(8,128)S(1)} %mark.1.mark_ref.a_ref), channel_id=1, source_target_pairs={{0,16},{4,20},{8,24},{12,28},{16,0},{20,4},{24,8},{28,12},{1,17},{... | collective-permute-start | bytes 12296 | tf_op jit(solution)/shard_map/ppermute | solution.py:548
  8.8 1.7 %steps.1 = (f32[512,128]{1,0:T(8,128)S(1)}, f32[512,128]{1,0:T(8,128)S(1)}, f32[256,128]{1,0:T(8,128)S(1)}, bf16[16,128]{1,0:T(8,128)(2,1)S(1)}, bf16[256,1536]{...) custom-call(bf16[1,40,256]{2,1,0:T(8,128)(2,1)S(1)} %get-tuple-element.48.own_ref, ...), custom_call_target="tpu_custom_call" | custom-call | flops 2013265920 | bytes 524288 | tf_op jit(solution)/shard_map/steps/pallas_call | solution.py:514
  10.6 0.6 %later.1.later_ref = bf16[16,128]{1,0:T(8,128)(2,1)S(1)} custom-call(bf16[48,384]{1,0:T(8,128)(2,1)S(1)} %collective-permute-done.3.same_ref.edge_b_ref, bf16[48,384]{1,0:T(8,128)(2,1)S(1)} %collective-permute-done.2.cross_ref.edge_a_ref, f32[40,8]{1,0:T(8,128)S(1)} %get-tuple-element.57.columns_ref, s32[8,128]{1,0:T(8,128)S(1)} %get-tuple-element.50.points_ref), custom_call_target="tpu_custom_call" | custom-call | flops 671088640 | bytes 524288 | tf_op jit(solution)/shard_map/later/pallas_call | solution.py:529
  11.2 0.0 copy-start
  11.2 3.8 %states.1 = (bf16[128,1280]{1,0:T(8,128)(2,1)S(1)}, bf16[128,1280]{1,0:T(8,128)(2,1)S(1)}, bf16[256,1280]{1,0:T(8,128)(2,1)S(1)}, bf16[256,1280]{1,0:T(8,128)(2,...) custom-call(bf16[256,1536]{1,0:T(8,128)(2,1)S(1)} %get-tuple-element, ...), custom_call_target="tpu_custom_call" | custom-call | flops 8388608000 | bytes 3145728 | tf_op jit(solution)/shard_map/states/pallas_call | solution.py:553
  15.0 0.1 collective-permute-start.9
  15.1 1.6 %collective-permute-start.5 = (f32[392,128]{1,0:T(8,128)S(1)}, f32[392,128]{1,0:T(8,128)S(1)}, u32[]{:S(2)}, u32[]{:S(2)}) collective-permute-start(f32[392,128]{1,0:T(8,128)S(1)} %get-tuple-element.63), channel_id=1, source_target_pairs={{0,4},{4,0},{8,12},{12,8},{16,20},{20,16},{24,28},{28,24},{1,5},{5... | collective-permute-start | bytes 602120 | tf_op jit(solution)/shard_map/ppermute | solution.py:578
  16.6 1.6 %collective-permute-start.6 = (f32[264,128]{1,0:T(8,128)S(1)}, f32[264,128]{1,0:T(8,128)S(1)}, u32[]{:S(2)}, u32[]{:S(2)}) collective-permute-start(f32[264,128]{1,0:T(8,128)S(1)} %get-tuple-element.65), channel_id=1, source_target_pairs={{0,8},{4,12},{8,0},{12,4},{16,24},{20,28},{24,16},{28,20},{1,9},{5... | collective-permute-start | bytes 405512 | tf_op jit(solution)/shard_map/ppermute | solution.py:579
  18.2 0.4 %collective-permute-start.7 = (f32[8,128]{1,0:T(8,128)S(1)}, f32[8,128]{1,0:T(8,128)S(1)}, u32[]{:S(2)}, u32[]{:S(2)}) collective-permute-start(f32[8,128]{1,0:T(8,128)S(1)} %join.1.mark_ref), channel_id=1, source_target_pairs={{0,12},{4,8},{8,4},{12,0},{16,28},{20,24},{24,20},{28,16},{1,13},{... | collective-permute-start | bytes 12296 | tf_op jit(solution)/shard_map/ppermute | solution.py:580
  18.6 1.5 %collective-permute-start.14 = (bf16[128,1280]{1,0:T(8,128)(2,1)S(1)}, bf16[128,1280]{1,0:T(8,128)(2,1)S(1)}, u32[]{:S(2)}, u32[]{:S(2)}) collective-permute-start(bf16[128,1280]{1,0:T(8,128)(2,1)S(1)} %get-tuple-element.86), channel_id=1, source_target_pairs={{0,2},{1,3},{2,0},{3,1},{4,6},{5,7},{6,4},{7,5},{8,10},{9,11},{10,... | collective-permute-start | bytes 983048 | tf_op jit(solution)/shard_map/ppermute | solution.py:572
  20.1 2.6 %collective-permute-done.7.across_ref = f32[8,128]{1,0:T(8,128)S(1)} collective-permute-done((f32[8,128]{1,0:T(8,128)S(1)}, f32[8,128]{1,0:T(8,128)S(1)}, u32[]{:S(2)}, u32[]{:S(2)}) %collective-permute-start.7) | collective-permute-done | bytes 4128 | tf_op jit(solution)/shard_map/ppermute | solution.py:580
  22.7 0.1 halves.1
  22.8 1.5 %collective-permute-start.8 = (f32[192,128]{1,0:T(8,128)S(1)}, f32[192,128]{1,0:T(8,128)S(1)}, u32[]{:S(2)}, u32[]{:S(2)}) collective-permute-start(f32[192,128]{1,0:T(8,128)S(1)} %get-tuple-element.68), channel_id=1, source_target_pairs={{0,8},{4,12},{8,0},{12,4},{16,24},{20,28},{24,16},{28,20},{1,9},{5... | collective-permute-start | bytes 294920 | tf_op jit(solution)/shard_map/ppermute | solution.py:587
  24.2 1.5 %collective-permute-start.10 = (f32[128,128]{1,0:T(8,128)S(1)}, f32[128,128]{1,0:T(8,128)S(1)}, u32[]{:S(2)}, u32[]{:S(2)}) collective-permute-start(f32[128,128]{1,0:T(8,128)S(1)} %get-tuple-element.78), channel_id=1, source_target_pairs={{0,4},{4,0},{8,12},{12,8},{16,20},{20,16},{24,28},{28,24},{1,5},{5... | collective-permute-start | bytes 196616 | tf_op jit(solution)/shard_map/ppermute | solution.py:588
  25.7 2.1 %diagonal.1 = (f32[2,256,1280]{2,1,0:T(8,128)S(1)}, f32[2,256,1280]{2,1,0:T(8,128)S(1)}) custom-call(bf16[256,1280]{1,0:T(8,128)(2,1)S(1)} %get-tuple-element.70.act_own_ref, bf16[256,1280]{1,0:T(8,128)(2,1)S(1)} %collective-permute-done.9.act_other_ref, bf16[256,256]{1,0:T(8,128)(2,1)S(1)} %get-tuple-element.73.bc_ref, ...), custom_call_target="tpu_custom_call" | custom-call | flops 4697620480 | bytes 2621440 | tf_op jit(solution)/shard_map/diagonal/pallas_call | solution.py:590
  27.8 0.7 %collective-permute-done.10.came_b_ref = f32[128,128]{1,0:T(8,128)S(1)} collective-permute-done((f32[128,128]{1,0:T(8,128)S(1)}, f32[128,128]{1,0:T(8,128)S(1)}, u32[]{:S(2)}, u32[]{:S(2)}) %collective-permute-start.10) | collective-permute-done | bytes 65568 | tf_op jit(solution)/shard_map/ppermute | solution.py:588
  28.6 0.3 carry.1
  28.9 0.1 collective-permute-start.15
  29.0 1.6 %collective-permute-start.11 = (f32[80,128]{1,0:T(8,128)S(1)}, f32[80,128]{1,0:T(8,128)S(1)}, u32[]{:S(2)}, u32[]{:S(2)}) collective-permute-start(f32[80,128]{1,0:T(8,128)S(1)} %get-tuple-element.80), channel_id=1, source_target_pairs={{0,2},{1,3},{2,0},{3,1},{4,6},{5,7},{6,4},{7,5},{8,10},{9,11},{10,... | collective-permute-start | bytes 122888 | tf_op jit(solution)/shard_map/ppermute | solution.py:602
  30.6 0.2 collective-permute-start.12
  30.7 0.5 %collective-permute-start.13 = (f32[80,128]{1,0:T(8,128)S(1)}, f32[80,128]{1,0:T(8,128)S(1)}, u32[]{:S(2)}, u32[]{:S(2)}) collective-permute-start(f32[80,128]{1,0:T(8,128)S(1)} %get-tuple-element.82), channel_id=1, source_target_pairs={{0,3},{1,2},{2,1},{3,0},{4,7},{5,6},{6,5},{7,4},{8,11},{9,10},{10,... | collective-permute-start | bytes 122888 | tf_op jit(solution)/shard_map/ppermute | solution.py:603
  31.2 1.8 %collective-permute-done.11.same_ref = f32[80,128]{1,0:T(8,128)S(1)} collective-permute-done((f32[80,128]{1,0:T(8,128)S(1)}, f32[80,128]{1,0:T(8,128)S(1)}, u32[]{:S(2)}, u32[]{:S(2)}) %collective-permute-start.11) | collective-permute-done | bytes 40992 | tf_op jit(solution)/shard_map/ppermute | solution.py:602
  33.0 1.1 %collective-permute-done.13.cross_ref = f32[80,128]{1,0:T(8,128)S(1)} collective-permute-done((f32[80,128]{1,0:T(8,128)S(1)}, f32[80,128]{1,0:T(8,128)S(1)}, u32[]{:S(2)}, u32[]{:S(2)}) %collective-permute-start.13) | collective-permute-done | bytes 40992 | tf_op jit(solution)/shard_map/ppermute | solution.py:603
  34.2 2.2 %collective-permute-start.16 = (f32[80,128]{1,0:T(8,128)S(1)}, f32[80,128]{1,0:T(8,128)S(1)}, u32[]{:S(2)}, u32[]{:S(2)}) collective-permute-start(f32[80,128]{1,0:T(8,128)S(1)} %get-tuple-element.93), channel_id=1, source_target_pairs={{0,16},{4,20},{8,24},{12,28},{16,0},{20,4},{24,8},{28,12},{1,17},{... | collective-permute-start | bytes 122888 | tf_op jit(solution)/shard_map/ppermute | solution.py:632
  36.4 1.7 %finish.1 = bf16[1,256,2560]{2,1,0:T(8,128)(2,1)} custom-call(f32[2,256,1280]{2,1,0:T(8,128)S(1)} %get-tuple-element.84.near_ref, f32[2,256,1280]{2,1,0:T(8,128)S(1)} %get-tuple-element.85.far_ref, bf16[256,256]{1,0:T(8,128)(2,1)S(1)} %get-tuple-element.73.bc_ref, bf16[128,1280]{1,0:T(8,128)(2,1)S(1)} %get-tuple-element.89.h_own_ref, ...), custom_call_target="tpu_custom_call" | custom-call | flops 3355443200 | bytes 7864320 | tf_op jit(solution)/shard_map/finish/pallas_call | solution.py:620
  38.2 1.7 %collective-permute-done.16.came_ref = f32[80,128]{1,0:T(8,128)S(1)} collective-permute-done((f32[80,128]{1,0:T(8,128)S(1)}, f32[80,128]{1,0:T(8,128)S(1)}, u32[]{:S(2)}, u32[]{:S(2)}) %collective-permute-start.16) | collective-permute-done | bytes 40992 | tf_op jit(solution)/shard_map/ppermute | solution.py:632
  39.8 0.6 %sum.1 = f32[80,128]{1,0:T(8,128)} custom-call(f32[80,128]{1,0:T(8,128)S(1)} %get-tuple-element.92.keep_ref, f32[80,128]{1,0:T(8,128)S(1)} %collective-permute-done.16.came_ref), custom_call_target="tpu_custom_call" | custom-call | tf_op jit(solution)/shard_map/sum/pallas_call | solution.py:474
  (20 shorter events, 0.1 us)
Async XLA Ops:
  0.6 10.5 %collective-permute-start.1 = (bf16[1,256,2816]{2,1,0:T(8,128)(2,1)}, bf16[1,256,2816]{2,1,0:T(8,128)(2,1)S(1)}, u32[]{:S(2)}, u32[]{:S(2)}) collective-permute-start(bf16[1,256,2816]{2,1,0:T(8,128)(2,1)} %xbc_hbm.3), channel_id=1, source_target_pairs={{0,1},{1,0},{2,3},{3,2},{4,5},{5,4},{6,7},{7,6},{8,9},{9,8},{10,11... | collective-permute-start | bytes 4325384 | tf_op jit(solution)/shard_map/ppermute | solution.py:494
  1.1 7.7 %collective-permute-start = (bf16[1,40,256]{2,1,0:T(8,128)(2,1)}, bf16[1,40,256]{2,1,0:T(8,128)(2,1)S(1)}, u32[]{:S(2)}, u32[]{:S(2)}) collective-permute-start(bf16[1,40,256]{2,1,0:T(8,128)(2,1)} %bitcast.1), channel_id=1, source_target_pairs={{0,1},{1,0},{2,3},{3,2},{4,5},{5,4},{6,7},{7,6},{8,9},{9,8},{10,11... | collective-permute-start | bytes 61448 | tf_op jit(solution)/shard_map/ppermute | solution.py:493
  2.3 8.3 %collective-permute-start.2 = (bf16[48,384]{1,0:T(8,128)(2,1)S(1)}, bf16[48,384]{1,0:T(8,128)(2,1)S(1)}, u32[]{:S(2)}, u32[]{:S(2)}) collective-permute-start(bf16[48,384]{1,0:T(8,128)(2,1)S(1)} %get-tuple-element.52), channel_id=1, source_target_pairs={{0,3},{1,2},{2,1},{3,0},{4,7},{5,6},{6,5},{7,4},{8,11},{9,10},{10,... | collective-permute-start | bytes 110600 | tf_op jit(solution)/shard_map/ppermute | solution.py:508
  5.0 5.6 %collective-permute-start.3 = (bf16[48,384]{1,0:T(8,128)(2,1)S(1)}, bf16[48,384]{1,0:T(8,128)(2,1)S(1)}, u32[]{:S(2)}, u32[]{:S(2)}) collective-permute-start(bf16[48,384]{1,0:T(8,128)(2,1)S(1)} %get-tuple-element.53), channel_id=1, source_target_pairs={{0,2},{1,3},{2,0},{3,1},{4,6},{5,7},{6,4},{7,5},{8,10},{9,11},{10,... | collective-permute-start | bytes 110600 | tf_op jit(solution)/shard_map/ppermute | solution.py:509
  6.0 5.1 %collective-permute-start.4 = (f32[8,128]{1,0:T(8,128)S(1)}, f32[8,128]{1,0:T(8,128)S(1)}, u32[]{:S(2)}, u32[]{:S(2)}) collective-permute-start(f32[8,128]{1,0:T(8,128)S(1)} %mark.1.mark_ref.a_ref), channel_id=1, source_target_pairs={{0,16},{4,20},{8,24},{12,28},{16,0},{20,4},{24,8},{28,12},{1,17},{... | collective-permute-start | bytes 12296 | tf_op jit(solution)/shard_map/ppermute | solution.py:548
  11.2 14.6 %copy-start = (bf16[1,256,2560]{2,1,0:T(8,128)(2,1)S(1)}, bf16[1,256,2560]{2,1,0:T(8,128)(2,1)}, u32[]{:S(2)}) copy-start(bf16[1,256,2560]{2,1,0:T(8,128)(2,1)} %gate_ref.1) | copy-start | bytes 3932164
  15.0 10.8 %collective-permute-start.9 = (bf16[256,1280]{1,0:T(8,128)(2,1)S(1)}, bf16[256,1280]{1,0:T(8,128)(2,1)S(1)}, u32[]{:S(2)}, u32[]{:S(2)}) collective-permute-start(bf16[256,1280]{1,0:T(8,128)(2,1)S(1)} %get-tuple-element.71), channel_id=1, source_target_pairs={{0,1},{1,0},{2,3},{3,2},{4,5},{5,4},{6,7},{7,6},{8,9},{9,8},{10,11... | collective-permute-start | bytes 1966088 | tf_op jit(solution)/shard_map/ppermute | solution.py:575
  15.1 7.6 %collective-permute-start.5 = (f32[392,128]{1,0:T(8,128)S(1)}, f32[392,128]{1,0:T(8,128)S(1)}, u32[]{:S(2)}, u32[]{:S(2)}) collective-permute-start(f32[392,128]{1,0:T(8,128)S(1)} %get-tuple-element.63), channel_id=1, source_target_pairs={{0,4},{4,0},{8,12},{12,8},{16,20},{20,16},{24,28},{28,24},{1,5},{5... | collective-permute-start | bytes 602120 | tf_op jit(solution)/shard_map/ppermute | solution.py:578
  16.6 6.1 %collective-permute-start.6 = (f32[264,128]{1,0:T(8,128)S(1)}, f32[264,128]{1,0:T(8,128)S(1)}, u32[]{:S(2)}, u32[]{:S(2)}) collective-permute-start(f32[264,128]{1,0:T(8,128)S(1)} %get-tuple-element.65), channel_id=1, source_target_pairs={{0,8},{4,12},{8,0},{12,4},{16,24},{20,28},{24,16},{28,20},{1,9},{5... | collective-permute-start | bytes 405512 | tf_op jit(solution)/shard_map/ppermute | solution.py:579
  18.2 4.5 %collective-permute-start.7 = (f32[8,128]{1,0:T(8,128)S(1)}, f32[8,128]{1,0:T(8,128)S(1)}, u32[]{:S(2)}, u32[]{:S(2)}) collective-permute-start(f32[8,128]{1,0:T(8,128)S(1)} %join.1.mark_ref), channel_id=1, source_target_pairs={{0,12},{4,8},{8,4},{12,0},{16,28},{20,24},{24,20},{28,16},{1,13},{... | collective-permute-start | bytes 12296 | tf_op jit(solution)/shard_map/ppermute | solution.py:580
  18.6 9.9 %collective-permute-start.14 = (bf16[128,1280]{1,0:T(8,128)(2,1)S(1)}, bf16[128,1280]{1,0:T(8,128)(2,1)S(1)}, u32[]{:S(2)}, u32[]{:S(2)}) collective-permute-start(bf16[128,1280]{1,0:T(8,128)(2,1)S(1)} %get-tuple-element.86), channel_id=1, source_target_pairs={{0,2},{1,3},{2,0},{3,1},{4,6},{5,7},{6,4},{7,5},{8,10},{9,11},{10,... | collective-permute-start | bytes 983048 | tf_op jit(solution)/shard_map/ppermute | solution.py:572
  22.8 5.8 %collective-permute-start.8 = (f32[192,128]{1,0:T(8,128)S(1)}, f32[192,128]{1,0:T(8,128)S(1)}, u32[]{:S(2)}, u32[]{:S(2)}) collective-permute-start(f32[192,128]{1,0:T(8,128)S(1)} %get-tuple-element.68), channel_id=1, source_target_pairs={{0,8},{4,12},{8,0},{12,4},{16,24},{20,28},{24,16},{28,20},{1,9},{5... | collective-permute-start | bytes 294920 | tf_op jit(solution)/shard_map/ppermute | solution.py:587
  24.2 4.3 %collective-permute-start.10 = (f32[128,128]{1,0:T(8,128)S(1)}, f32[128,128]{1,0:T(8,128)S(1)}, u32[]{:S(2)}, u32[]{:S(2)}) collective-permute-start(f32[128,128]{1,0:T(8,128)S(1)} %get-tuple-element.78), channel_id=1, source_target_pairs={{0,4},{4,0},{8,12},{12,8},{16,20},{20,16},{24,28},{28,24},{1,5},{5... | collective-permute-start | bytes 196616 | tf_op jit(solution)/shard_map/ppermute | solution.py:588
  28.6 2.6 %copy-start.1 = (f32[2560]{0:T(1024)S(1)}, f32[2560]{0:T(1024)}, u32[]{:S(2)}) copy-start(f32[2560]{0:T(1024)} %param.19) | copy-start | bytes 30724
  28.9 7.5 %collective-permute-start.15 = (bf16[128,1280]{1,0:T(8,128)(2,1)S(1)}, bf16[128,1280]{1,0:T(8,128)(2,1)S(1)}, u32[]{:S(2)}, u32[]{:S(2)}) collective-permute-start(bf16[128,1280]{1,0:T(8,128)(2,1)S(1)} %get-tuple-element.90), channel_id=1, source_target_pairs={{0,1},{1,0},{2,3},{3,2},{4,5},{5,4},{6,7},{7,6},{8,9},{9,8},{10,11... | collective-permute-start | bytes 983048 | tf_op jit(solution)/shard_map/ppermute | solution.py:619
  29.0 4.1 %collective-permute-start.11 = (f32[80,128]{1,0:T(8,128)S(1)}, f32[80,128]{1,0:T(8,128)S(1)}, u32[]{:S(2)}, u32[]{:S(2)}) collective-permute-start(f32[80,128]{1,0:T(8,128)S(1)} %get-tuple-element.80), channel_id=1, source_target_pairs={{0,2},{1,3},{2,0},{3,1},{4,6},{5,7},{6,4},{7,5},{8,10},{9,11},{10,... | collective-permute-start | bytes 122888 | tf_op jit(solution)/shard_map/ppermute | solution.py:602
  30.6 2.5 %collective-permute-start.12 = (f32[80,128]{1,0:T(8,128)S(1)}, f32[80,128]{1,0:T(8,128)S(1)}, u32[]{:S(2)}, u32[]{:S(2)}) collective-permute-start(f32[80,128]{1,0:T(8,128)S(1)} %get-tuple-element.81), channel_id=1, source_target_pairs={{0,1},{1,0},{2,3},{3,2},{4,5},{5,4},{6,7},{7,6},{8,9},{9,8},{10,11... | collective-permute-start | bytes 122888 | tf_op jit(solution)/shard_map/ppermute | solution.py:601
  30.7 3.4 %collective-permute-start.13 = (f32[80,128]{1,0:T(8,128)S(1)}, f32[80,128]{1,0:T(8,128)S(1)}, u32[]{:S(2)}, u32[]{:S(2)}) collective-permute-start(f32[80,128]{1,0:T(8,128)S(1)} %get-tuple-element.82), channel_id=1, source_target_pairs={{0,3},{1,2},{2,1},{3,0},{4,7},{5,6},{6,5},{7,4},{8,11},{9,10},{10,... | collective-permute-start | bytes 122888 | tf_op jit(solution)/shard_map/ppermute | solution.py:603
  34.2 5.7 %collective-permute-start.16 = (f32[80,128]{1,0:T(8,128)S(1)}, f32[80,128]{1,0:T(8,128)S(1)}, u32[]{:S(2)}, u32[]{:S(2)}) collective-permute-start(f32[80,128]{1,0:T(8,128)S(1)} %get-tuple-element.93), channel_id=1, source_target_pairs={{0,16},{4,20},{8,24},{12,28},{16,0},{20,4},{24,8},{28,12},{1,17},{... | collective-permute-start | bytes 122888 | tf_op jit(solution)/shard_map/ppermute | solution.py:632

commit v7 on v6

--- a/solution.py
+++ b/solution.py
@@ -296,16 +296,19 @@
         wide = dot(rows, spread)
         table, ahead = wide[:16], wide[16:17]
         act = jnp.concatenate([act_own_ref[:, cols], act_other_ref[:, cols]], axis=0).astype(F32)
-        weighted = (act * widen(ws_ref[...], head)).astype(BF16)
+        scaled = act * widen(ws_ref[...], head)
+        weighted = scaled.astype(BF16)
         own = dot(b_turned[0], weighted[:n])
         other = dot(b_turned[1], weighted[n:])
-        state = jnp.where(first, table[1:2], 1.0) * own + jnp.where(first, 1.0, table[1:2]) * other
+        to_end = [jnp.where(first, table[1:2], 1.0), jnp.where(first, 1.0, table[1:2])]
+        state = to_end[0] * own + to_end[1] * other
         early_ref[:, cols] = jnp.where(first, own, other).astype(BF16)
         state_ref[:, cols] = state.astype(BF16)
-        read = act * widen(wr_ref[...], head)
+        beyond = jnp.concatenate([(ahead * to_end[0]) * scaled[:n], (ahead * to_end[1]) * scaled[n:]], axis=0)
+        read = act * widen(wr_ref[...], head) + beyond
         high = read.astype(BF16)
         low = (read - high.astype(F32)).astype(BF16)
-        seen = dot(both, high) + dot(both, low) + ahead * state
+        seen = dot(both, high) + dot(both, low)
         read_ref[pl.ds(at, CHUNK)] = seen.T
 
     if split:
@@ -542,7 +545,10 @@
             out = small.at[0:1].add(small[1:2] * later[0:1])
             later = lax.ppermute(out, "seq", [(i, (i - 2) % places) for i in range(places)])
             later = jnp.where(place < places - 2, later, 0.0)
-        later = pack(jnp.broadcast_to(later[0, :H, None], (H, 16)))
+        high = lax.reduce_precision(later[0, :H], 8, 7)
+        gap = jnp.zeros(64 - H, F32)
+        packed = jnp.concatenate([high, gap, later[0, :H] - high, gap])
+        later = jnp.broadcast_to(packed, (16, 128)).astype(BF16)
 
     if split:
         ones = join(tied(mark, later), mark, lax.ppermute(mark, "dp", swap(4)))

time: 40.6 us -> 40.9 us (level)
  no operation moved by 1% of the time
where the time goes in v7:
time: 40.9 us; the launch traced here: 40.7 us
  starting transfers between devices  19.1 us (47%)
  Pallas kernels  12.3 us (30%)
  waiting for transfers between devices  7.88 us (19%)
  between operations  1.45 us (4%)
    pallas_call x1, Pallas kernels, on_device(): pl.pallas_call(functools.partial(state_kernel, split=split), out_shape=(s...  4.03 us
    ppermute x1, starting transfers between devices, on_device(): ones = join(tied(mark, later), mark, lax.ppermute(mark, 'dp', swap(4)))  2.77 us
    ppermute x1, starting transfers between devices, on_device(): edge_a = lax.ppermute(tail_a, 'seq', one_back)  2.69 us
    ppermute x1, waiting for transfers between devices, on_device(): across = lax.ppermute(tied(ones, send_x), 'dp', swap(3))  2.56 us
    ppermute x1, starting transfers between devices, on_device(): came = lax.ppermute(send, 'dp', swap(4))  2.24 us
    pallas_call x1, Pallas kernels, on_device(): pl.pallas_call(diagonal_kernel, out_shape=(shape((2, n, HALF), F32), shap...  2.09 us
    ppermute x1, waiting for transfers between devices, on_device(): lax.ppermute(to_same, 'seq', [(i, i ^ 2) for i in range(places)])  1.85 us
    pallas_call x1, Pallas kernels, on_device(): pl.pallas_call(finish_kernel, out_shape=shape((1, n, D), BF16), in_specs=...  1.75 us
  transfers between devices with their start and end apart: 17, of which 5 were waited for; matrix products, arithmetic and copies ran while one was open for 0% of the time, Pallas kernels for 18%

profile of v7, /device:TPU:0, one launch (start us, length us, event | category | flops | bytes accessed | tf_op | source)
XLA Modules:
  0.0 40.7 jit_solution(16349618113681329940)
XLA Ops:
  0.6 0.5 %collective-permute-start.1 = (bf16[1,256,2816]{2,1,0:T(8,128)(2,1)}, bf16[1,256,2816]{2,1,0:T(8,128)(2,1)S(1)}, u32[]{:S(2)}, u32[]{:S(2)}) collective-permute-start(bf16[1,256,2816]{2,1,0:T(8,128)(2,1)} %xbc_hbm.3), channel_id=1, source_target_pairs={{0,1},{1,0},{2,3},{3,2},{4,5},{5,4},{6,7},{7,6},{8,9},{9,8},{10,11... | collective-permute-start | bytes 4325384 | tf_op jit(solution)/shard_map/ppermute | solution.py:497
  1.1 0.1 collective-permute-start
  1.2 1.1 %tail.1 = (bf16[48,384]{1,0:T(8,128)(2,1)S(1)}, bf16[48,384]{1,0:T(8,128)(2,1)S(1)}, bf16[1,40,256]{2,1,0:T(8,128)(2,1)S(1)}, f32[40,8]{1,0:T(8,128)S(1)}, s32[8,128]{1,0:T(8,128)S(1)}) custom-call(bf16[1,256,2816]{2,1,0:T(8,128)(2,1)} %xbc_hbm.3, bf16[1,40,256]{2,1,0:T(8,128)(2,1)} %bitcast.2, f32[40]{0:T(128)} %bias_hbm.1, f32[40]{0:T(128)} %rate_hbm.1, ...), custom_call_target="tpu_custom_call" | custom-call | tf_op jit(solution)/shard_map/tail/pallas_call | solution.py:500
  2.3 2.7 %collective-permute-start.2 = (bf16[48,384]{1,0:T(8,128)(2,1)S(1)}, bf16[48,384]{1,0:T(8,128)(2,1)S(1)}, u32[]{:S(2)}, u32[]{:S(2)}) collective-permute-start(bf16[48,384]{1,0:T(8,128)(2,1)S(1)} %get-tuple-element.52), channel_id=1, source_target_pairs={{0,3},{1,2},{2,1},{3,0},{4,7},{5,6},{6,5},{7,4},{8,11},{9,10},{10,... | collective-permute-start | bytes 110600 | tf_op jit(solution)/shard_map/ppermute | solution.py:511
  5.0 0.4 collective-permute-start.3
  6.0 2.8 %collective-permute-start.4 = (f32[8,128]{1,0:T(8,128)S(1)}, f32[8,128]{1,0:T(8,128)S(1)}, u32[]{:S(2)}, u32[]{:S(2)}) collective-permute-start(f32[8,128]{1,0:T(8,128)S(1)} %mark.1.mark_ref.a_ref), channel_id=1, source_target_pairs={{0,16},{4,20},{8,24},{12,28},{16,0},{20,4},{24,8},{28,12},{1,17},{... | collective-permute-start | bytes 12296 | tf_op jit(solution)/shard_map/ppermute | solution.py:554
  8.8 1.7 %steps.1 = (f32[512,128]{1,0:T(8,128)S(1)}, f32[512,128]{1,0:T(8,128)S(1)}, f32[256,128]{1,0:T(8,128)S(1)}, bf16[16,128]{1,0:T(8,128)(2,1)S(1)}, bf16[256,1536]{...) custom-call(bf16[1,40,256]{2,1,0:T(8,128)(2,1)S(1)} %get-tuple-element.48.own_ref, ...), custom_call_target="tpu_custom_call" | custom-call | flops 2013265920 | bytes 524288 | tf_op jit(solution)/shard_map/steps/pallas_call | solution.py:517
  10.6 0.6 %later.1.later_ref = bf16[16,128]{1,0:T(8,128)(2,1)S(1)} custom-call(bf16[48,384]{1,0:T(8,128)(2,1)S(1)} %collective-permute-done.3.same_ref.edge_b_ref, bf16[48,384]{1,0:T(8,128)(2,1)S(1)} %collective-permute-done.2.cross_ref.edge_a_ref, f32[40,8]{1,0:T(8,128)S(1)} %get-tuple-element.57.columns_ref, s32[8,128]{1,0:T(8,128)S(1)} %get-tuple-element.50.points_ref), custom_call_target="tpu_custom_call" | custom-call | flops 671088640 | bytes 524288 | tf_op jit(solution)/shard_map/later/pallas_call | solution.py:532
  11.2 0.0 copy-start
  11.2 4.0 %states.1 = (bf16[128,1280]{1,0:T(8,128)(2,1)S(1)}, bf16[128,1280]{1,0:T(8,128)(2,1)S(1)}, bf16[256,1280]{1,0:T(8,128)(2,1)S(1)}, bf16[256,1280]{1,0:T(8,128)(2,...) custom-call(bf16[256,1536]{1,0:T(8,128)(2,1)S(1)} %get-tuple-element, ...), custom_call_target="tpu_custom_call" | custom-call | flops 8388608000 | bytes 3145728 | tf_op jit(solution)/shard_map/states/pallas_call | solution.py:559
  15.2 0.1 collective-permute-start.9
  15.3 1.6 %collective-permute-start.5 = (f32[392,128]{1,0:T(8,128)S(1)}, f32[392,128]{1,0:T(8,128)S(1)}, u32[]{:S(2)}, u32[]{:S(2)}) collective-permute-start(f32[392,128]{1,0:T(8,128)S(1)} %get-tuple-element.63), channel_id=1, source_target_pairs={{0,4},{4,0},{8,12},{12,8},{16,20},{20,16},{24,28},{28,24},{1,5},{5... | collective-permute-start | bytes 602120 | tf_op jit(solution)/shard_map/ppermute | solution.py:584
  16.8 1.6 %collective-permute-start.6 = (f32[264,128]{1,0:T(8,128)S(1)}, f32[264,128]{1,0:T(8,128)S(1)}, u32[]{:S(2)}, u32[]{:S(2)}) collective-permute-start(f32[264,128]{1,0:T(8,128)S(1)} %get-tuple-element.65), channel_id=1, source_target_pairs={{0,8},{4,12},{8,0},{12,4},{16,24},{20,28},{24,16},{28,20},{1,9},{5... | collective-permute-start | bytes 405512 | tf_op jit(solution)/shard_map/ppermute | solution.py:585
  18.4 0.4 %collective-permute-start.7 = (f32[8,128]{1,0:T(8,128)S(1)}, f32[8,128]{1,0:T(8,128)S(1)}, u32[]{:S(2)}, u32[]{:S(2)}) collective-permute-start(f32[8,128]{1,0:T(8,128)S(1)} %join.1.mark_ref), channel_id=1, source_target_pairs={{0,12},{4,8},{8,4},{12,0},{16,28},{20,24},{24,20},{28,16},{1,13},{... | collective-permute-start | bytes 12296 | tf_op jit(solution)/shard_map/ppermute | solution.py:586
  18.8 1.5 %collective-permute-start.14 = (bf16[128,1280]{1,0:T(8,128)(2,1)S(1)}, bf16[128,1280]{1,0:T(8,128)(2,1)S(1)}, u32[]{:S(2)}, u32[]{:S(2)}) collective-permute-start(bf16[128,1280]{1,0:T(8,128)(2,1)S(1)} %get-tuple-element.86), channel_id=1, source_target_pairs={{0,2},{1,3},{2,0},{3,1},{4,6},{5,7},{6,4},{7,5},{8,10},{9,11},{10,... | collective-permute-start | bytes 983048 | tf_op jit(solution)/shard_map/ppermute | solution.py:578
  20.4 2.6 %collective-permute-done.7.across_ref = f32[8,128]{1,0:T(8,128)S(1)} collective-permute-done((f32[8,128]{1,0:T(8,128)S(1)}, f32[8,128]{1,0:T(8,128)S(1)}, u32[]{:S(2)}, u32[]{:S(2)}) %collective-permute-start.7) | collective-permute-done | bytes 4128 | tf_op jit(solution)/shard_map/ppermute | solution.py:586
  22.9 0.1 halves.1
  23.0 1.5 %collective-permute-start.8 = (f32[192,128]{1,0:T(8,128)S(1)}, f32[192,128]{1,0:T(8,128)S(1)}, u32[]{:S(2)}, u32[]{:S(2)}) collective-permute-start(f32[192,128]{1,0:T(8,128)S(1)} %get-tuple-element.68), channel_id=1, source_target_pairs={{0,8},{4,12},{8,0},{12,4},{16,24},{20,28},{24,16},{28,20},{1,9},{5... | collective-permute-start | bytes 294920 | tf_op jit(solution)/shard_map/ppermute | solution.py:593
  24.5 1.5 %collective-permute-start.10 = (f32[128,128]{1,0:T(8,128)S(1)}, f32[128,128]{1,0:T(8,128)S(1)}, u32[]{:S(2)}, u32[]{:S(2)}) collective-permute-start(f32[128,128]{1,0:T(8,128)S(1)} %get-tuple-element.78), channel_id=1, source_target_pairs={{0,4},{4,0},{8,12},{12,8},{16,20},{20,16},{24,28},{28,24},{1,5},{5... | collective-permute-start | bytes 196616 | tf_op jit(solution)/shard_map/ppermute | solution.py:594
  26.0 2.1 %diagonal.1 = (f32[2,256,1280]{2,1,0:T(8,128)S(1)}, f32[2,256,1280]{2,1,0:T(8,128)S(1)}) custom-call(bf16[256,1280]{1,0:T(8,128)(2,1)S(1)} %get-tuple-element.70.act_own_ref, bf16[256,1280]{1,0:T(8,128)(2,1)S(1)} %collective-permute-done.9.act_other_ref, bf16[256,256]{1,0:T(8,128)(2,1)S(1)} %get-tuple-element.73.bc_ref, ...), custom_call_target="tpu_custom_call" | custom-call | flops 4697620480 | bytes 2621440 | tf_op jit(solution)/shard_map/diagonal/pallas_call | solution.py:596
  28.1 0.7 %collective-permute-done.10.came_b_ref = f32[128,128]{1,0:T(8,128)S(1)} collective-permute-done((f32[128,128]{1,0:T(8,128)S(1)}, f32[128,128]{1,0:T(8,128)S(1)}, u32[]{:S(2)}, u32[]{:S(2)}) %collective-permute-start.10) | collective-permute-done | bytes 65568 | tf_op jit(solution)/shard_map/ppermute | solution.py:594
  28.8 0.3 carry.1
  29.1 0.1 collective-permute-start.15
  29.2 1.6 %collective-permute-start.11 = (f32[80,128]{1,0:T(8,128)S(1)}, f32[80,128]{1,0:T(8,128)S(1)}, u32[]{:S(2)}, u32[]{:S(2)}) collective-permute-start(f32[80,128]{1,0:T(8,128)S(1)} %get-tuple-element.80), channel_id=1, source_target_pairs={{0,2},{1,3},{2,0},{3,1},{4,6},{5,7},{6,4},{7,5},{8,10},{9,11},{10,... | collective-permute-start | bytes 122888 | tf_op jit(solution)/shard_map/ppermute | solution.py:608
  30.8 0.2 collective-permute-start.12
  31.0 0.5 %collective-permute-start.13 = (f32[80,128]{1,0:T(8,128)S(1)}, f32[80,128]{1,0:T(8,128)S(1)}, u32[]{:S(2)}, u32[]{:S(2)}) collective-permute-start(f32[80,128]{1,0:T(8,128)S(1)} %get-tuple-element.82), channel_id=1, source_target_pairs={{0,3},{1,2},{2,1},{3,0},{4,7},{5,6},{6,5},{7,4},{8,11},{9,10},{10,... | collective-permute-start | bytes 122888 | tf_op jit(solution)/shard_map/ppermute | solution.py:609
  31.4 1.8 %collective-permute-done.11.same_ref = f32[80,128]{1,0:T(8,128)S(1)} collective-permute-done((f32[80,128]{1,0:T(8,128)S(1)}, f32[80,128]{1,0:T(8,128)S(1)}, u32[]{:S(2)}, u32[]{:S(2)}) %collective-permute-start.11) | collective-permute-done | bytes 40992 | tf_op jit(solution)/shard_map/ppermute | solution.py:608
  33.3 1.1 %collective-permute-done.13.cross_ref = f32[80,128]{1,0:T(8,128)S(1)} collective-permute-done((f32[80,128]{1,0:T(8,128)S(1)}, f32[80,128]{1,0:T(8,128)S(1)}, u32[]{:S(2)}, u32[]{:S(2)}) %collective-permute-start.13) | collective-permute-done | bytes 40992 | tf_op jit(solution)/shard_map/ppermute | solution.py:609
  34.4 2.2 %collective-permute-start.16 = (f32[80,128]{1,0:T(8,128)S(1)}, f32[80,128]{1,0:T(8,128)S(1)}, u32[]{:S(2)}, u32[]{:S(2)}) collective-permute-start(f32[80,128]{1,0:T(8,128)S(1)} %get-tuple-element.93), channel_id=1, source_target_pairs={{0,16},{4,20},{8,24},{12,28},{16,0},{20,4},{24,8},{28,12},{1,17},{... | collective-permute-start | bytes 122888 | tf_op jit(solution)/shard_map/ppermute | solution.py:638
  36.7 1.7 %finish.1 = bf16[1,256,2560]{2,1,0:T(8,128)(2,1)} custom-call(f32[2,256,1280]{2,1,0:T(8,128)S(1)} %get-tuple-element.84.near_ref, f32[2,256,1280]{2,1,0:T(8,128)S(1)} %get-tuple-element.85.far_ref, bf16[256,256]{1,0:T(8,128)(2,1)S(1)} %get-tuple-element.73.bc_ref, bf16[128,1280]{1,0:T(8,128)(2,1)S(1)} %get-tuple-element.89.h_own_ref, ...), custom_call_target="tpu_custom_call" | custom-call | flops 3355443200 | bytes 7864320 | tf_op jit(solution)/shard_map/finish/pallas_call | solution.py:626
  38.4 1.7 %collective-permute-done.16.came_ref = f32[80,128]{1,0:T(8,128)S(1)} collective-permute-done((f32[80,128]{1,0:T(8,128)S(1)}, f32[80,128]{1,0:T(8,128)S(1)}, u32[]{:S(2)}, u32[]{:S(2)}) %collective-permute-start.16) | collective-permute-done | bytes 40992 | tf_op jit(solution)/shard_map/ppermute | solution.py:638
  40.1 0.6 %sum.1 = f32[80,128]{1,0:T(8,128)} custom-call(f32[80,128]{1,0:T(8,128)S(1)} %get-tuple-element.92.keep_ref, f32[80,128]{1,0:T(8,128)S(1)} %collective-permute-done.16.came_ref), custom_call_target="tpu_custom_call" | custom-call | tf_op jit(solution)/shard_map/sum/pallas_call | solution.py:477
  (20 shorter events, 0.1 us)
Async XLA Ops:
  0.6 10.5 %collective-permute-start.1 = (bf16[1,256,2816]{2,1,0:T(8,128)(2,1)}, bf16[1,256,2816]{2,1,0:T(8,128)(2,1)S(1)}, u32[]{:S(2)}, u32[]{:S(2)}) collective-permute-start(bf16[1,256,2816]{2,1,0:T(8,128)(2,1)} %xbc_hbm.3), channel_id=1, source_target_pairs={{0,1},{1,0},{2,3},{3,2},{4,5},{5,4},{6,7},{7,6},{8,9},{9,8},{10,11... | collective-permute-start | bytes 4325384 | tf_op jit(solution)/shard_map/ppermute | solution.py:497
  1.1 7.7 %collective-permute-start = (bf16[1,40,256]{2,1,0:T(8,128)(2,1)}, bf16[1,40,256]{2,1,0:T(8,128)(2,1)S(1)}, u32[]{:S(2)}, u32[]{:S(2)}) collective-permute-start(bf16[1,40,256]{2,1,0:T(8,128)(2,1)} %bitcast.1), channel_id=1, source_target_pairs={{0,1},{1,0},{2,3},{3,2},{4,5},{5,4},{6,7},{7,6},{8,9},{9,8},{10,11... | collective-permute-start | bytes 61448 | tf_op jit(solution)/shard_map/ppermute | solution.py:496
  2.3 8.3 %collective-permute-start.2 = (bf16[48,384]{1,0:T(8,128)(2,1)S(1)}, bf16[48,384]{1,0:T(8,128)(2,1)S(1)}, u32[]{:S(2)}, u32[]{:S(2)}) collective-permute-start(bf16[48,384]{1,0:T(8,128)(2,1)S(1)} %get-tuple-element.52), channel_id=1, source_target_pairs={{0,3},{1,2},{2,1},{3,0},{4,7},{5,6},{6,5},{7,4},{8,11},{9,10},{10,... | collective-permute-start | bytes 110600 | tf_op jit(solution)/shard_map/ppermute | solution.py:511
  5.0 5.6 %collective-permute-start.3 = (bf16[48,384]{1,0:T(8,128)(2,1)S(1)}, bf16[48,384]{1,0:T(8,128)(2,1)S(1)}, u32[]{:S(2)}, u32[]{:S(2)}) collective-permute-start(bf16[48,384]{1,0:T(8,128)(2,1)S(1)} %get-tuple-element.53), channel_id=1, source_target_pairs={{0,2},{1,3},{2,0},{3,1},{4,6},{5,7},{6,4},{7,5},{8,10},{9,11},{10,... | collective-permute-start | bytes 110600 | tf_op jit(solution)/shard_map/ppermute | solution.py:512
  6.0 5.1 %collective-permute-start.4 = (f32[8,128]{1,0:T(8,128)S(1)}, f32[8,128]{1,0:T(8,128)S(1)}, u32[]{:S(2)}, u32[]{:S(2)}) collective-permute-start(f32[8,128]{1,0:T(8,128)S(1)} %mark.1.mark_ref.a_ref), channel_id=1, source_target_pairs={{0,16},{4,20},{8,24},{12,28},{16,0},{20,4},{24,8},{28,12},{1,17},{... | collective-permute-start | bytes 12296 | tf_op jit(solution)/shard_map/ppermute | solution.py:554
  11.2 14.8 %copy-start = (bf16[1,256,2560]{2,1,0:T(8,128)(2,1)S(1)}, bf16[1,256,2560]{2,1,0:T(8,128)(2,1)}, u32[]{:S(2)}) copy-start(bf16[1,256,2560]{2,1,0:T(8,128)(2,1)} %gate_ref.1) | copy-start | bytes 3932164
  15.2 10.8 %collective-permute-start.9 = (bf16[256,1280]{1,0:T(8,128)(2,1)S(1)}, bf16[256,1280]{1,0:T(8,128)(2,1)S(1)}, u32[]{:S(2)}, u32[]{:S(2)}) collective-permute-start(bf16[256,1280]{1,0:T(8,128)(2,1)S(1)} %get-tuple-element.71), channel_id=1, source_target_pairs={{0,1},{1,0},{2,3},{3,2},{4,5},{5,4},{6,7},{7,6},{8,9},{9,8},{10,11... | collective-permute-start | bytes 1966088 | tf_op jit(solution)/shard_map/ppermute | solution.py:581
  15.3 7.6 %collective-permute-start.5 = (f32[392,128]{1,0:T(8,128)S(1)}, f32[392,128]{1,0:T(8,128)S(1)}, u32[]{:S(2)}, u32[]{:S(2)}) collective-permute-start(f32[392,128]{1,0:T(8,128)S(1)} %get-tuple-element.63), channel_id=1, source_target_pairs={{0,4},{4,0},{8,12},{12,8},{16,20},{20,16},{24,28},{28,24},{1,5},{5... | collective-permute-start | bytes 602120 | tf_op jit(solution)/shard_map/ppermute | solution.py:584
  16.8 6.1 %collective-permute-start.6 = (f32[264,128]{1,0:T(8,128)S(1)}, f32[264,128]{1,0:T(8,128)S(1)}, u32[]{:S(2)}, u32[]{:S(2)}) collective-permute-start(f32[264,128]{1,0:T(8,128)S(1)} %get-tuple-element.65), channel_id=1, source_target_pairs={{0,8},{4,12},{8,0},{12,4},{16,24},{20,28},{24,16},{28,20},{1,9},{5... | collective-permute-start | bytes 405512 | tf_op jit(solution)/shard_map/ppermute | solution.py:585
  18.4 4.5 %collective-permute-start.7 = (f32[8,128]{1,0:T(8,128)S(1)}, f32[8,128]{1,0:T(8,128)S(1)}, u32[]{:S(2)}, u32[]{:S(2)}) collective-permute-start(f32[8,128]{1,0:T(8,128)S(1)} %join.1.mark_ref), channel_id=1, source_target_pairs={{0,12},{4,8},{8,4},{12,0},{16,28},{20,24},{24,20},{28,16},{1,13},{... | collective-permute-start | bytes 12296 | tf_op jit(solution)/shard_map/ppermute | solution.py:586
  18.8 9.9 %collective-permute-start.14 = (bf16[128,1280]{1,0:T(8,128)(2,1)S(1)}, bf16[128,1280]{1,0:T(8,128)(2,1)S(1)}, u32[]{:S(2)}, u32[]{:S(2)}) collective-permute-start(bf16[128,1280]{1,0:T(8,128)(2,1)S(1)} %get-tuple-element.86), channel_id=1, source_target_pairs={{0,2},{1,3},{2,0},{3,1},{4,6},{5,7},{6,4},{7,5},{8,10},{9,11},{10,... | collective-permute-start | bytes 983048 | tf_op jit(solution)/shard_map/ppermute | solution.py:578
  23.0 5.8 %collective-permute-start.8 = (f32[192,128]{1,0:T(8,128)S(1)}, f32[192,128]{1,0:T(8,128)S(1)}, u32[]{:S(2)}, u32[]{:S(2)}) collective-permute-start(f32[192,128]{1,0:T(8,128)S(1)} %get-tuple-element.68), channel_id=1, source_target_pairs={{0,8},{4,12},{8,0},{12,4},{16,24},{20,28},{24,16},{28,20},{1,9},{5... | collective-permute-start | bytes 294920 | tf_op jit(solution)/shard_map/ppermute | solution.py:593
  24.5 4.3 %collective-permute-start.10 = (f32[128,128]{1,0:T(8,128)S(1)}, f32[128,128]{1,0:T(8,128)S(1)}, u32[]{:S(2)}, u32[]{:S(2)}) collective-permute-start(f32[128,128]{1,0:T(8,128)S(1)} %get-tuple-element.78), channel_id=1, source_target_pairs={{0,4},{4,0},{8,12},{12,8},{16,20},{20,16},{24,28},{28,24},{1,5},{5... | collective-permute-start | bytes 196616 | tf_op jit(solution)/shard_map/ppermute | solution.py:594
  28.8 2.6 %copy-start.1 = (f32[2560]{0:T(1024)S(1)}, f32[2560]{0:T(1024)}, u32[]{:S(2)}) copy-start(f32[2560]{0:T(1024)} %param.19) | copy-start | bytes 30724
  29.1 7.5 %collective-permute-start.15 = (bf16[128,1280]{1,0:T(8,128)(2,1)S(1)}, bf16[128,1280]{1,0:T(8,128)(2,1)S(1)}, u32[]{:S(2)}, u32[]{:S(2)}) collective-permute-start(bf16[128,1280]{1,0:T(8,128)(2,1)S(1)} %get-tuple-element.90), channel_id=1, source_target_pairs={{0,1},{1,0},{2,3},{3,2},{4,5},{5,4},{6,7},{7,6},{8,9},{9,8},{10,11... | collective-permute-start | bytes 983048 | tf_op jit(solution)/shard_map/ppermute | solution.py:625
  29.2 4.1 %collective-permute-start.11 = (f32[80,128]{1,0:T(8,128)S(1)}, f32[80,128]{1,0:T(8,128)S(1)}, u32[]{:S(2)}, u32[]{:S(2)}) collective-permute-start(f32[80,128]{1,0:T(8,128)S(1)} %get-tuple-element.80), channel_id=1, source_target_pairs={{0,2},{1,3},{2,0},{3,1},{4,6},{5,7},{6,4},{7,5},{8,10},{9,11},{10,... | collective-permute-start | bytes 122888 | tf_op jit(solution)/shard_map/ppermute | solution.py:608
  30.8 2.5 %collective-permute-start.12 = (f32[80,128]{1,0:T(8,128)S(1)}, f32[80,128]{1,0:T(8,128)S(1)}, u32[]{:S(2)}, u32[]{:S(2)}) collective-permute-start(f32[80,128]{1,0:T(8,128)S(1)} %get-tuple-element.81), channel_id=1, source_target_pairs={{0,1},{1,0},{2,3},{3,2},{4,5},{5,4},{6,7},{7,6},{8,9},{9,8},{10,11... | collective-permute-start | bytes 122888 | tf_op jit(solution)/shard_map/ppermute | solution.py:607
  31.0 3.4 %collective-permute-start.13 = (f32[80,128]{1,0:T(8,128)S(1)}, f32[80,128]{1,0:T(8,128)S(1)}, u32[]{:S(2)}, u32[]{:S(2)}) collective-permute-start(f32[80,128]{1,0:T(8,128)S(1)} %get-tuple-element.82), channel_id=1, source_target_pairs={{0,3},{1,2},{2,1},{3,0},{4,7},{5,6},{6,5},{7,4},{8,11},{9,10},{10,... | collective-permute-start | bytes 122888 | tf_op jit(solution)/shard_map/ppermute | solution.py:609
  34.4 5.7 %collective-permute-start.16 = (f32[80,128]{1,0:T(8,128)S(1)}, f32[80,128]{1,0:T(8,128)S(1)}, u32[]{:S(2)}, u32[]{:S(2)}) collective-permute-start(f32[80,128]{1,0:T(8,128)S(1)} %get-tuple-element.93), channel_id=1, source_target_pairs={{0,16},{4,20},{8,24},{12,28},{16,0},{20,4},{24,8},{28,12},{1,17},{... | collective-permute-start | bytes 122888 | tf_op jit(solution)/shard_map/ppermute | solution.py:638

commit v8 on v7

--- a/solution.py
+++ b/solution.py
@@ -139,11 +139,18 @@
 
 
 def tail_kernel(
-    xbc_hbm, dt_hbm, bias_hbm, rate_hbm, skip_hbm, points_hbm, out_a_ref, out_b_ref, dt_ref, columns_ref, points_ref,
+    xbc_hbm, dt_hbm, bias_hbm, rate_hbm, skip_hbm, points_hbm, out_a_ref, out_b_ref, dt_ref, columns_ref, points_ref, x_ref,
     rows_ref, bias_ref, rate_ref, skip_ref, spot_ref, sems,
 ):
     n = xbc_hbm.shape[1]
     rows = xbc_hbm.at[0, pl.ds(n - EDGE, EDGE)]
+    col = pl.multiple_of(lax.rem(lax.axis_index("seq"), 2) * HALF, 128)
+    inputs = [
+        pltpu.make_async_copy(xbc_hbm.at[0, :, pl.ds(from_at, width)], x_ref.at[:, pl.ds(to_at, width)], sems.at[6 + i])
+        for i, (from_at, to_at, width) in enumerate(((D, HALF, BC), (col, 0, HALF)))
+    ]
+    for copy in inputs:
+        copy.start()
     fetch(
         (
             (dt_hbm, dt_ref), (rows, rows_ref), (points_hbm, spot_ref),
@@ -166,6 +173,8 @@
     for r in range(R):
         points = jnp.where(spot == r, spot_ref[0, r], points)
     points_ref[...] = points
+    for copy in inputs:
+        copy.wait()
 
 
 def mark_kernel(label_ref, mark_ref):
@@ -173,8 +182,8 @@
 
 
 def steps_kernel(
-    own_ref, other_ref, columns_ref, points_ref, xbc_hbm, conv_w_hbm, conv_b_hbm,
-    ws_ref, wr_ref, e_ref, rows_ref, x_ref, taps_ref, bias_ref, *rest,
+    own_ref, other_ref, columns_ref, points_ref, conv_w_hbm, conv_b_hbm,
+    ws_ref, wr_ref, e_ref, rows_ref, taps_ref, bias_ref, *rest,
 ):
     place = lax.axis_index("seq")
     core = lax.rem(place, 2)
@@ -184,7 +193,6 @@
     copies = []
     for from_at, to_at, width in ((D, HALF, BC), (col, 0, HALF)):
         here, there = pl.ds(from_at, width), pl.ds(to_at, width)
-        copies.append((xbc_hbm.at[0, :, here], x_ref.at[:, there]))
         copies.append((conv_w_hbm.at[:, here], taps_ref.at[:, there]))
         copies.append((conv_b_hbm.at[here], bias_ref.at[0, there]))
     copies = [pltpu.make_async_copy(source, to, sems.at[i]) for i, (source, to) in enumerate(copies)]
@@ -497,14 +505,14 @@
     xbc_other = lax.ppermute(xbc, "seq", pair)
     xbc_here = in_hbm(xbc)
     payload = shape((4 * SIDE // 128, 128 + n), BF16)
-    tail_a, tail_b, dt_own, columns, points = pl.pallas_call(
+    tail_a, tail_b, dt_own, columns, points, x = pl.pallas_call(
         tail_kernel,
-        out_shape=(payload, payload, shape((1, H, n), BF16), shape((H, 8), F32), shape((8, 128), jnp.int32)),
+        out_shape=(payload, payload, shape((1, H, n), BF16), shape((H, 8), F32), shape((8, 128), jnp.int32), shape((n, SIDE), BF16)),
         in_specs=[HBM] * 6,
-        out_specs=(VMEM,) * 5,
+        out_specs=(VMEM,) * 6,
         scratch_shapes=[pltpu.VMEM((EDGE, CH), BF16)]
         + [pltpu.VMEM((1, H), F32)] * 3
-        + [pltpu.SMEM((1, R), jnp.int32), pltpu.SemaphoreType.DMA((6,))],
+        + [pltpu.SMEM((1, R), jnp.int32), pltpu.SemaphoreType.DMA((8,))],
         compiler_params=params(8),
         name="tail",
     )(xbc_here, in_hbm(dt_turned), in_hbm(dt_bias), in_hbm(a_rate), in_hbm(d_skip), in_hbm(readout))
@@ -514,19 +522,19 @@
         mark_kernel, out_shape=shape((8, N), F32), in_specs=[SMEM], out_specs=VMEM, compiler_params=params(8), name="mark"
     )(tied(labels, points))
 
-    ws, wr, e, rows, x, taps, bias, *small = pl.pallas_call(
+    ws, wr, e, rows, taps, bias, *small = pl.pallas_call(
         steps_kernel,
         out_shape=(
             shape((2 * n, 128), F32), shape((2 * n, 128), F32), shape((n, 128), F32), shape((16, 128), BF16),
-            shape((n, SIDE), BF16), shape((KW, SIDE), F32), shape((1, SIDE), F32),
+            shape((KW, SIDE), F32), shape((1, SIDE), F32),
         ) + ((shape((8, 128), F32),) if chips != 2 else ()),
-        in_specs=[VMEM] * 4 + [HBM] * 3,
-        out_specs=(VMEM,) * (8 if chips != 2 else 7),
-        scratch_shapes=[pltpu.SemaphoreType.DMA((6,))],
+        in_specs=[VMEM] * 4 + [HBM] * 2,
+        out_specs=(VMEM,) * (7 if chips != 2 else 6),
+        scratch_shapes=[pltpu.SemaphoreType.DMA((4,))],
         compiler_params=params(16),
         cost_estimate=cost(30 * n * n * 1024, 8 * n * 256),
         name="steps",
-    )(dt_own, dt_other, columns, points, xbc_here, in_hbm(conv_weight), in_hbm(conv_bias))
+    )(dt_own, dt_other, columns, points, in_hbm(conv_weight), in_hbm(conv_bias))
 
     if chips == 2:
         later = pl.pallas_call(

time: 40.9 us -> 40.8 us (level)
  no operation moved by 1% of the time
where the time goes in v8:
time: 40.8 us; the launch traced here: 40.6 us
  starting transfers between devices  19.5 us (48%)
  Pallas kernels  12.1 us (30%)
  waiting for transfers between devices  7.49 us (18%)
  between operations  1.45 us (4%)
    pallas_call x1, Pallas kernels, on_device(): pl.pallas_call(functools.partial(state_kernel, split=split), out_shape=(s...  4.02 us
    ppermute x1, starting transfers between devices, on_device(): ones = join(tied(mark, later), mark, lax.ppermute(mark, 'dp', swap(4)))  2.76 us
    ppermute x1, starting transfers between devices, on_device(): edge_a = lax.ppermute(tail_a, 'seq', one_back)  2.69 us
    ppermute x1, starting transfers between devices, on_device(): came = lax.ppermute(send, 'dp', swap(4))  2.63 us
    ppermute x1, waiting for transfers between devices, on_device(): across = lax.ppermute(tied(ones, send_x), 'dp', swap(3))  2.56 us
    pallas_call x1, Pallas kernels, on_device(): pl.pallas_call(diagonal_kernel, out_shape=(shape((2, n, HALF), F32), shap...  2.09 us
    ppermute x1, waiting for transfers between devices, on_device(): lax.ppermute(to_same, 'seq', [(i, i ^ 2) for i in range(places)])  1.85 us
    pallas_call x1, Pallas kernels, on_device(): pl.pallas_call(finish_kernel, out_shape=shape((1, n, D), BF16), in_specs=...  1.75 us
  transfers between devices with their start and end apart: 17, of which 5 were waited for; matrix products, arithmetic and copies ran while one was open for 0% of the time, Pallas kernels for 18%

profile of v8, /device:TPU:0, one launch (start us, length us, event | category | flops | bytes accessed | tf_op | source)
XLA Modules:
  0.0 40.6 jit_solution(7633276986514794376)
XLA Ops:
  0.6 0.5 %collective-permute-start = (bf16[1,256,2816]{2,1,0:T(8,128)(2,1)}, bf16[1,256,2816]{2,1,0:T(8,128)(2,1)S(1)}, u32[]{:S(2)}, u32[]{:S(2)}) collective-permute-start(bf16[1,256,2816]{2,1,0:T(8,128)(2,1)} %xbc_hbm.1), channel_id=1, source_target_pairs={{0,1},{1,0},{2,3},{3,2},{4,5},{5,4},{6,7},{7,6},{8,9},{9,8},{10,11... | collective-permute-start | bytes 4325384 | tf_op jit(solution)/shard_map/ppermute | solution.py:505
  1.1 0.1 collective-permute-start.3
  1.2 1.3 %tail.1 = (bf16[48,384]{1,0:T(8,128)(2,1)S(1)}, bf16[48,384]{1,0:T(8,128)(2,1)S(1)}, bf16[1,40,256]{2,1,0:T(8,128)(2,1)S(1)}, f32[40,8]{1,0:T(8,128)S(1)}, s32[8...) custom-call(bf16[1,256,2816]{2,1,0:T(8,128)(2,1)} %xbc_hbm.1, bf16[1,40,256]{2,1,0:T(8,128)(2,1)} %bitcast.2, f32[40]{0:T(128)} %bias_hbm.1, ...), custom_call_target="tpu_custom_call" | custom-call | tf_op jit(solution)/shard_map/tail/pallas_call | solution.py:508
  2.6 2.7 %collective-permute-start.1 = (bf16[48,384]{1,0:T(8,128)(2,1)S(1)}, bf16[48,384]{1,0:T(8,128)(2,1)S(1)}, u32[]{:S(2)}, u32[]{:S(2)}) collective-permute-start(bf16[48,384]{1,0:T(8,128)(2,1)S(1)} %get-tuple-element.49), channel_id=1, source_target_pairs={{0,3},{1,2},{2,1},{3,0},{4,7},{5,6},{6,5},{7,4},{8,11},{9,10},{10,... | collective-permute-start | bytes 110600 | tf_op jit(solution)/shard_map/ppermute | solution.py:519
  5.3 0.4 collective-permute-start.2
  6.3 2.8 %collective-permute-start.4 = (f32[8,128]{1,0:T(8,128)S(1)}, f32[8,128]{1,0:T(8,128)S(1)}, u32[]{:S(2)}, u32[]{:S(2)}) collective-permute-start(f32[8,128]{1,0:T(8,128)S(1)} %mark.1.mark_ref.a_ref), channel_id=1, source_target_pairs={{0,16},{4,20},{8,24},{12,28},{16,0},{20,4},{24,8},{28,12},{1,17},{... | collective-permute-start | bytes 12296 | tf_op jit(solution)/shard_map/ppermute | solution.py:562
  9.1 1.3 %steps.1 = (f32[512,128]{1,0:T(8,128)S(1)}, f32[512,128]{1,0:T(8,128)S(1)}, f32[256,128]{1,0:T(8,128)S(1)}, bf16[16,128]{1,0:T(8,128)(2,1)S(1)}, f32[4,1536]{1,0:T(4,128)S(1)}, /*index=5*/f32[1,1536]{1,0:T(1,128)S(1)}) custom-call(bf16[1,40,256]{2,1,0:T(8,128)(2,1)S(1)} %get-tuple-element.51.own_ref, ...), custom_call_target="tpu_custom_call" | custom-call | flops 2013265920 | bytes 524288 | tf_op jit(solution)/shard_map/steps/pallas_call | solution.py:525
  10.5 0.6 %later.1.later_ref = bf16[16,128]{1,0:T(8,128)(2,1)S(1)} custom-call(bf16[48,384]{1,0:T(8,128)(2,1)S(1)} %collective-permute-done.2.same_ref.edge_b_ref, bf16[48,384]{1,0:T(8,128)(2,1)S(1)} %collective-permute-done.1.cross_ref.edge_a_ref, f32[40,8]{1,0:T(8,128)S(1)} %get-tuple-element.57.columns_ref, s32[8,128]{1,0:T(8,128)S(1)} %get-tuple-element.53.points_ref), custom_call_target="tpu_custom_call" | custom-call | flops 671088640 | bytes 524288 | tf_op jit(solution)/shard_map/later/pallas_call | solution.py:540
  11.1 4.0 %states.1 = (bf16[128,1280]{1,0:T(8,128)(2,1)S(1)}, bf16[128,1280]{1,0:T(8,128)(2,1)S(1)}, bf16[256,1280]{1,0:T(8,128)(2,1)S(1)}, bf16[256,1280]{1,0:T(8,128)(2,...) custom-call(bf16[256,1536]{1,0:T(8,128)(2,1)S(1)} %get-tuple-element, ...), custom_call_target="tpu_custom_call" | custom-call | flops 8388608000 | bytes 3145728 | tf_op jit(solution)/shard_map/states/pallas_call | solution.py:567
  15.1 0.1 collective-permute-start.9
  15.2 1.6 %collective-permute-start.5 = (f32[392,128]{1,0:T(8,128)S(1)}, f32[392,128]{1,0:T(8,128)S(1)}, u32[]{:S(2)}, u32[]{:S(2)}) collective-permute-start(f32[392,128]{1,0:T(8,128)S(1)} %get-tuple-element.63), channel_id=1, source_target_pairs={{0,4},{4,0},{8,12},{12,8},{16,20},{20,16},{24,28},{28,24},{1,5},{5... | collective-permute-start | bytes 602120 | tf_op jit(solution)/shard_map/ppermute | solution.py:592
  16.7 1.6 %collective-permute-start.6 = (f32[264,128]{1,0:T(8,128)S(1)}, f32[264,128]{1,0:T(8,128)S(1)}, u32[]{:S(2)}, u32[]{:S(2)}) collective-permute-start(f32[264,128]{1,0:T(8,128)S(1)} %get-tuple-element.65), channel_id=1, source_target_pairs={{0,8},{4,12},{8,0},{12,4},{16,24},{20,28},{24,16},{28,20},{1,9},{5... | collective-permute-start | bytes 405512 | tf_op jit(solution)/shard_map/ppermute | solution.py:593
  18.3 0.4 %collective-permute-start.7 = (f32[8,128]{1,0:T(8,128)S(1)}, f32[8,128]{1,0:T(8,128)S(1)}, u32[]{:S(2)}, u32[]{:S(2)}) collective-permute-start(f32[8,128]{1,0:T(8,128)S(1)} %join.1.mark_ref), channel_id=1, source_target_pairs={{0,12},{4,8},{8,4},{12,0},{16,28},{20,24},{24,20},{28,16},{1,13},{... | collective-permute-start | bytes 12296 | tf_op jit(solution)/shard_map/ppermute | solution.py:594
  18.7 1.5 %collective-permute-start.14 = (bf16[128,1280]{1,0:T(8,128)(2,1)S(1)}, bf16[128,1280]{1,0:T(8,128)(2,1)S(1)}, u32[]{:S(2)}, u32[]{:S(2)}) collective-permute-start(bf16[128,1280]{1,0:T(8,128)(2,1)S(1)} %get-tuple-element.86), channel_id=1, source_target_pairs={{0,2},{1,3},{2,0},{3,1},{4,6},{5,7},{6,4},{7,5},{8,10},{9,11},{10,... | collective-permute-start | bytes 983048 | tf_op jit(solution)/shard_map/ppermute | solution.py:586
  20.2 2.6 %collective-permute-done.7.across_ref = f32[8,128]{1,0:T(8,128)S(1)} collective-permute-done((f32[8,128]{1,0:T(8,128)S(1)}, f32[8,128]{1,0:T(8,128)S(1)}, u32[]{:S(2)}, u32[]{:S(2)}) %collective-permute-start.7) | collective-permute-done | bytes 4128 | tf_op jit(solution)/shard_map/ppermute | solution.py:594
  22.8 0.1 halves.1
  22.9 1.5 %collective-permute-start.8 = (f32[192,128]{1,0:T(8,128)S(1)}, f32[192,128]{1,0:T(8,128)S(1)}, u32[]{:S(2)}, u32[]{:S(2)}) collective-permute-start(f32[192,128]{1,0:T(8,128)S(1)} %get-tuple-element.68), channel_id=1, source_target_pairs={{0,8},{4,12},{8,0},{12,4},{16,24},{20,28},{24,16},{28,20},{1,9},{5... | collective-permute-start | bytes 294920 | tf_op jit(solution)/shard_map/ppermute | solution.py:601
  24.4 1.5 %collective-permute-start.10 = (f32[128,128]{1,0:T(8,128)S(1)}, f32[128,128]{1,0:T(8,128)S(1)}, u32[]{:S(2)}, u32[]{:S(2)}) collective-permute-start(f32[128,128]{1,0:T(8,128)S(1)} %get-tuple-element.78), channel_id=1, source_target_pairs={{0,4},{4,0},{8,12},{12,8},{16,20},{20,16},{24,28},{28,24},{1,5},{5... | collective-permute-start | bytes 196616 | tf_op jit(solution)/shard_map/ppermute | solution.py:602
  25.9 2.1 %diagonal.1 = (f32[2,256,1280]{2,1,0:T(8,128)S(1)}, f32[2,256,1280]{2,1,0:T(8,128)S(1)}) custom-call(bf16[256,1280]{1,0:T(8,128)(2,1)S(1)} %get-tuple-element.70.act_own_ref, bf16[256,1280]{1,0:T(8,128)(2,1)S(1)} %collective-permute-done.9.act_other_ref, bf16[256,256]{1,0:T(8,128)(2,1)S(1)} %get-tuple-element.73.bc_ref, ...), custom_call_target="tpu_custom_call" | custom-call | flops 4697620480 | bytes 2621440 | tf_op jit(solution)/shard_map/diagonal/pallas_call | solution.py:604
  28.0 0.7 %collective-permute-done.10.came_b_ref = f32[128,128]{1,0:T(8,128)S(1)} collective-permute-done((f32[128,128]{1,0:T(8,128)S(1)}, f32[128,128]{1,0:T(8,128)S(1)}, u32[]{:S(2)}, u32[]{:S(2)}) %collective-permute-start.10) | collective-permute-done | bytes 65568 | tf_op jit(solution)/shard_map/ppermute | solution.py:602
  28.7 0.0 copy-start.1
  28.7 0.3 carry.1
  29.0 0.1 collective-permute-start.15
  29.1 1.6 %collective-permute-start.11 = (f32[80,128]{1,0:T(8,128)S(1)}, f32[80,128]{1,0:T(8,128)S(1)}, u32[]{:S(2)}, u32[]{:S(2)}) collective-permute-start(f32[80,128]{1,0:T(8,128)S(1)} %get-tuple-element.80), channel_id=1, source_target_pairs={{0,2},{1,3},{2,0},{3,1},{4,6},{5,7},{6,4},{7,5},{8,10},{9,11},{10,... | collective-permute-start | bytes 122888 | tf_op jit(solution)/shard_map/ppermute | solution.py:616
  30.7 0.2 collective-permute-start.12
  30.8 0.5 %collective-permute-start.13 = (f32[80,128]{1,0:T(8,128)S(1)}, f32[80,128]{1,0:T(8,128)S(1)}, u32[]{:S(2)}, u32[]{:S(2)}) collective-permute-start(f32[80,128]{1,0:T(8,128)S(1)} %get-tuple-element.82), channel_id=1, source_target_pairs={{0,3},{1,2},{2,1},{3,0},{4,7},{5,6},{6,5},{7,4},{8,11},{9,10},{10,... | collective-permute-start | bytes 122888 | tf_op jit(solution)/shard_map/ppermute | solution.py:617
  31.3 1.8 %collective-permute-done.11.same_ref = f32[80,128]{1,0:T(8,128)S(1)} collective-permute-done((f32[80,128]{1,0:T(8,128)S(1)}, f32[80,128]{1,0:T(8,128)S(1)}, u32[]{:S(2)}, u32[]{:S(2)}) %collective-permute-start.11) | collective-permute-done | bytes 40992 | tf_op jit(solution)/shard_map/ppermute | solution.py:616
  33.2 1.1 %collective-permute-done.13.cross_ref = f32[80,128]{1,0:T(8,128)S(1)} collective-permute-done((f32[80,128]{1,0:T(8,128)S(1)}, f32[80,128]{1,0:T(8,128)S(1)}, u32[]{:S(2)}, u32[]{:S(2)}) %collective-permute-start.13) | collective-permute-done | bytes 40992 | tf_op jit(solution)/shard_map/ppermute | solution.py:617
  34.3 2.6 %collective-permute-start.16 = (f32[80,128]{1,0:T(8,128)S(1)}, f32[80,128]{1,0:T(8,128)S(1)}, u32[]{:S(2)}, u32[]{:S(2)}) collective-permute-start(f32[80,128]{1,0:T(8,128)S(1)} %get-tuple-element.93), channel_id=1, source_target_pairs={{0,16},{4,20},{8,24},{12,28},{16,0},{20,4},{24,8},{28,12},{1,17},{... | collective-permute-start | bytes 122888 | tf_op jit(solution)/shard_map/ppermute | solution.py:646
  36.9 1.7 %finish.1 = bf16[1,256,2560]{2,1,0:T(8,128)(2,1)} custom-call(f32[2,256,1280]{2,1,0:T(8,128)S(1)} %get-tuple-element.84.near_ref, f32[2,256,1280]{2,1,0:T(8,128)S(1)} %get-tuple-element.85.far_ref, bf16[256,256]{1,0:T(8,128)(2,1)S(1)} %get-tuple-element.73.bc_ref, bf16[128,1280]{1,0:T(8,128)(2,1)S(1)} %get-tuple-element.89.h_own_ref, ...), custom_call_target="tpu_custom_call" | custom-call | flops 3355443200 | bytes 7864320 | tf_op jit(solution)/shard_map/finish/pallas_call | solution.py:634
  38.7 1.3 %collective-permute-done.16.came_ref = f32[80,128]{1,0:T(8,128)S(1)} collective-permute-done((f32[80,128]{1,0:T(8,128)S(1)}, f32[80,128]{1,0:T(8,128)S(1)}, u32[]{:S(2)}, u32[]{:S(2)}) %collective-permute-start.16) | collective-permute-done | bytes 40992 | tf_op jit(solution)/shard_map/ppermute | solution.py:646
  39.9 0.6 %sum.1 = f32[80,128]{1,0:T(8,128)} custom-call(f32[80,128]{1,0:T(8,128)S(1)} %get-tuple-element.92.keep_ref, f32[80,128]{1,0:T(8,128)S(1)} %collective-permute-done.16.came_ref), custom_call_target="tpu_custom_call" | custom-call | tf_op jit(solution)/shard_map/sum/pallas_call | solution.py:485
  (20 shorter events, 0.1 us)
Async XLA Ops:
  0.6 10.4 %collective-permute-start = (bf16[1,256,2816]{2,1,0:T(8,128)(2,1)}, bf16[1,256,2816]{2,1,0:T(8,128)(2,1)S(1)}, u32[]{:S(2)}, u32[]{:S(2)}) collective-permute-start(bf16[1,256,2816]{2,1,0:T(8,128)(2,1)} %xbc_hbm.1), channel_id=1, source_target_pairs={{0,1},{1,0},{2,3},{3,2},{4,5},{5,4},{6,7},{7,6},{8,9},{9,8},{10,11... | collective-permute-start | bytes 4325384 | tf_op jit(solution)/shard_map/ppermute | solution.py:505
  1.1 8.0 %collective-permute-start.3 = (bf16[1,40,256]{2,1,0:T(8,128)(2,1)}, bf16[1,40,256]{2,1,0:T(8,128)(2,1)S(1)}, u32[]{:S(2)}, u32[]{:S(2)}) collective-permute-start(bf16[1,40,256]{2,1,0:T(8,128)(2,1)} %bitcast.1), channel_id=1, source_target_pairs={{0,1},{1,0},{2,3},{3,2},{4,5},{5,4},{6,7},{7,6},{8,9},{9,8},{10,11... | collective-permute-start | bytes 61448 | tf_op jit(solution)/shard_map/ppermute | solution.py:504
  2.6 7.9 %collective-permute-start.1 = (bf16[48,384]{1,0:T(8,128)(2,1)S(1)}, bf16[48,384]{1,0:T(8,128)(2,1)S(1)}, u32[]{:S(2)}, u32[]{:S(2)}) collective-permute-start(bf16[48,384]{1,0:T(8,128)(2,1)S(1)} %get-tuple-element.49), channel_id=1, source_target_pairs={{0,3},{1,2},{2,1},{3,0},{4,7},{5,6},{6,5},{7,4},{8,11},{9,10},{10,... | collective-permute-start | bytes 110600 | tf_op jit(solution)/shard_map/ppermute | solution.py:519
  5.3 5.2 %collective-permute-start.2 = (bf16[48,384]{1,0:T(8,128)(2,1)S(1)}, bf16[48,384]{1,0:T(8,128)(2,1)S(1)}, u32[]{:S(2)}, u32[]{:S(2)}) collective-permute-start(bf16[48,384]{1,0:T(8,128)(2,1)S(1)} %get-tuple-element.50), channel_id=1, source_target_pairs={{0,2},{1,3},{2,0},{3,1},{4,6},{5,7},{6,4},{7,5},{8,10},{9,11},{10,... | collective-permute-start | bytes 110600 | tf_op jit(solution)/shard_map/ppermute | solution.py:520
  6.3 4.7 %collective-permute-start.4 = (f32[8,128]{1,0:T(8,128)S(1)}, f32[8,128]{1,0:T(8,128)S(1)}, u32[]{:S(2)}, u32[]{:S(2)}) collective-permute-start(f32[8,128]{1,0:T(8,128)S(1)} %mark.1.mark_ref.a_ref), channel_id=1, source_target_pairs={{0,16},{4,20},{8,24},{12,28},{16,0},{20,4},{24,8},{28,12},{1,17},{... | collective-permute-start | bytes 12296 | tf_op jit(solution)/shard_map/ppermute | solution.py:562
  11.1 14.8 %copy-start = (bf16[1,256,2560]{2,1,0:T(8,128)(2,1)S(1)}, bf16[1,256,2560]{2,1,0:T(8,128)(2,1)}, u32[]{:S(2)}) copy-start(bf16[1,256,2560]{2,1,0:T(8,128)(2,1)} %gate_ref.1) | copy-start | bytes 3932164
  15.1 10.8 %collective-permute-start.9 = (bf16[256,1280]{1,0:T(8,128)(2,1)S(1)}, bf16[256,1280]{1,0:T(8,128)(2,1)S(1)}, u32[]{:S(2)}, u32[]{:S(2)}) collective-permute-start(bf16[256,1280]{1,0:T(8,128)(2,1)S(1)} %get-tuple-element.71), channel_id=1, source_target_pairs={{0,1},{1,0},{2,3},{3,2},{4,5},{5,4},{6,7},{7,6},{8,9},{9,8},{10,11... | collective-permute-start | bytes 1966088 | tf_op jit(solution)/shard_map/ppermute | solution.py:589
  15.2 7.6 %collective-permute-start.5 = (f32[392,128]{1,0:T(8,128)S(1)}, f32[392,128]{1,0:T(8,128)S(1)}, u32[]{:S(2)}, u32[]{:S(2)}) collective-permute-start(f32[392,128]{1,0:T(8,128)S(1)} %get-tuple-element.63), channel_id=1, source_target_pairs={{0,4},{4,0},{8,12},{12,8},{16,20},{20,16},{24,28},{28,24},{1,5},{5... | collective-permute-start | bytes 602120 | tf_op jit(solution)/shard_map/ppermute | solution.py:592
  16.7 6.1 %collective-permute-start.6 = (f32[264,128]{1,0:T(8,128)S(1)}, f32[264,128]{1,0:T(8,128)S(1)}, u32[]{:S(2)}, u32[]{:S(2)}) collective-permute-start(f32[264,128]{1,0:T(8,128)S(1)} %get-tuple-element.65), channel_id=1, source_target_pairs={{0,8},{4,12},{8,0},{12,4},{16,24},{20,28},{24,16},{28,20},{1,9},{5... | collective-permute-start | bytes 405512 | tf_op jit(solution)/shard_map/ppermute | solution.py:593
  18.3 4.5 %collective-permute-start.7 = (f32[8,128]{1,0:T(8,128)S(1)}, f32[8,128]{1,0:T(8,128)S(1)}, u32[]{:S(2)}, u32[]{:S(2)}) collective-permute-start(f32[8,128]{1,0:T(8,128)S(1)} %join.1.mark_ref), channel_id=1, source_target_pairs={{0,12},{4,8},{8,4},{12,0},{16,28},{20,24},{24,20},{28,16},{1,13},{... | collective-permute-start | bytes 12296 | tf_op jit(solution)/shard_map/ppermute | solution.py:594
  18.7 9.9 %collective-permute-start.14 = (bf16[128,1280]{1,0:T(8,128)(2,1)S(1)}, bf16[128,1280]{1,0:T(8,128)(2,1)S(1)}, u32[]{:S(2)}, u32[]{:S(2)}) collective-permute-start(bf16[128,1280]{1,0:T(8,128)(2,1)S(1)} %get-tuple-element.86), channel_id=1, source_target_pairs={{0,2},{1,3},{2,0},{3,1},{4,6},{5,7},{6,4},{7,5},{8,10},{9,11},{10,... | collective-permute-start | bytes 983048 | tf_op jit(solution)/shard_map/ppermute | solution.py:586
  22.9 5.8 %collective-permute-start.8 = (f32[192,128]{1,0:T(8,128)S(1)}, f32[192,128]{1,0:T(8,128)S(1)}, u32[]{:S(2)}, u32[]{:S(2)}) collective-permute-start(f32[192,128]{1,0:T(8,128)S(1)} %get-tuple-element.68), channel_id=1, source_target_pairs={{0,8},{4,12},{8,0},{12,4},{16,24},{20,28},{24,16},{28,20},{1,9},{5... | collective-permute-start | bytes 294920 | tf_op jit(solution)/shard_map/ppermute | solution.py:601
  24.4 4.3 %collective-permute-start.10 = (f32[128,128]{1,0:T(8,128)S(1)}, f32[128,128]{1,0:T(8,128)S(1)}, u32[]{:S(2)}, u32[]{:S(2)}) collective-permute-start(f32[128,128]{1,0:T(8,128)S(1)} %get-tuple-element.78), channel_id=1, source_target_pairs={{0,4},{4,0},{8,12},{12,8},{16,20},{20,16},{24,28},{28,24},{1,5},{5... | collective-permute-start | bytes 196616 | tf_op jit(solution)/shard_map/ppermute | solution.py:602
  28.7 2.6 %copy-start.1 = (f32[2560]{0:T(1024)S(1)}, f32[2560]{0:T(1024)}, u32[]{:S(2)}) copy-start(f32[2560]{0:T(1024)} %param.19) | copy-start | bytes 30724
  29.0 7.9 %collective-permute-start.15 = (bf16[128,1280]{1,0:T(8,128)(2,1)S(1)}, bf16[128,1280]{1,0:T(8,128)(2,1)S(1)}, u32[]{:S(2)}, u32[]{:S(2)}) collective-permute-start(bf16[128,1280]{1,0:T(8,128)(2,1)S(1)} %get-tuple-element.90), channel_id=1, source_target_pairs={{0,1},{1,0},{2,3},{3,2},{4,5},{5,4},{6,7},{7,6},{8,9},{9,8},{10,11... | collective-permute-start | bytes 983048 | tf_op jit(solution)/shard_map/ppermute | solution.py:633
  29.1 4.1 %collective-permute-start.11 = (f32[80,128]{1,0:T(8,128)S(1)}, f32[80,128]{1,0:T(8,128)S(1)}, u32[]{:S(2)}, u32[]{:S(2)}) collective-permute-start(f32[80,128]{1,0:T(8,128)S(1)} %get-tuple-element.80), channel_id=1, source_target_pairs={{0,2},{1,3},{2,0},{3,1},{4,6},{5,7},{6,4},{7,5},{8,10},{9,11},{10,... | collective-permute-start | bytes 122888 | tf_op jit(solution)/shard_map/ppermute | solution.py:616
  30.7 2.5 %collective-permute-start.12 = (f32[80,128]{1,0:T(8,128)S(1)}, f32[80,128]{1,0:T(8,128)S(1)}, u32[]{:S(2)}, u32[]{:S(2)}) collective-permute-start(f32[80,128]{1,0:T(8,128)S(1)} %get-tuple-element.81), channel_id=1, source_target_pairs={{0,1},{1,0},{2,3},{3,2},{4,5},{5,4},{6,7},{7,6},{8,9},{9,8},{10,11... | collective-permute-start | bytes 122888 | tf_op jit(solution)/shard_map/ppermute | solution.py:615
  30.8 3.4 %collective-permute-start.13 = (f32[80,128]{1,0:T(8,128)S(1)}, f32[80,128]{1,0:T(8,128)S(1)}, u32[]{:S(2)}, u32[]{:S(2)}) collective-permute-start(f32[80,128]{1,0:T(8,128)S(1)} %get-tuple-element.82), channel_id=1, source_target_pairs={{0,3},{1,2},{2,1},{3,0},{4,7},{5,6},{6,5},{7,4},{8,11},{9,10},{10,... | collective-permute-start | bytes 122888 | tf_op jit(solution)/shard_map/ppermute | solution.py:617
  34.3 5.7 %collective-permute-start.16 = (f32[80,128]{1,0:T(8,128)S(1)}, f32[80,128]{1,0:T(8,128)S(1)}, u32[]{:S(2)}, u32[]{:S(2)}) collective-permute-start(f32[80,128]{1,0:T(8,128)S(1)} %get-tuple-element.93), channel_id=1, source_target_pairs={{0,16},{4,20},{8,24},{12,28},{16,0},{20,4},{24,8},{28,12},{1,17},{... | collective-permute-start | bytes 122888 | tf_op jit(solution)/shard_map/ppermute | solution.py:646

commit v9 on v8

--- a/solution.py
+++ b/solution.py
@@ -594,13 +594,6 @@
         across = lax.ppermute(tied(ones, send_x), "dp", swap(3))
 
     if split:
-        keep_a, send_a, keep_b, send_b = small_call(
-            functools.partial(halves_kernel, sequences=float(sequences)), "halves", (LEAD, LEAD, D // 8 - LEAD, D // 8 - LEAD),
-            keep_x, came_x, keep_z, came_z, ones, across,
-        )
-        came_a = lax.ppermute(send_a, "dp", swap(2))
-        came_b = lax.ppermute(send_b, "dp", swap(1))
-        act_in = tied(act_in, keep_a)
         near, reach = pl.pallas_call(
             diagonal_kernel,
             out_shape=(shape((2, n, HALF), F32), shape((2, n, HALF), F32)),
@@ -610,7 +603,13 @@
             cost_estimate=cost(28 * n * n * D, 4 * n * D),
             name="diagonal",
         )(act_own, act_in, bc, ws, e, rows, gate_input)
-        keep_b, near, reach = lax.optimization_barrier((keep_b, near, reach))
+        keep_x, near, reach = lax.optimization_barrier((keep_x, near, reach))
+        keep_a, send_a, keep_b, send_b = small_call(
+            functools.partial(halves_kernel, sequences=float(sequences)), "halves", (LEAD, LEAD, D // 8 - LEAD, D // 8 - LEAD),
+            keep_x, came_x, keep_z, came_z, ones, across,
+        )
+        came_a = lax.ppermute(send_a, "dp", swap(2))
+        came_b = lax.ppermute(send_b, "dp", swap(1))
         keep, to_core, to_same, to_cross = small_call(chunks_kernel, "chunks", (D // 32,) * 4, keep_a, came_a, keep_b, came_b)
         from_core = lax.ppermute(to_core, "seq", pair)
         from_same = lax.ppermute(to_same, "seq", [(i, i ^ 2) for i in range(places)])

time: 40.8 us -> 40.6 us (level)
  starting transfers between devices: 19.5 us -> 18.6 us
  waiting for transfers between devices: 7.49 us -> 8.03 us
    ppermute x1, waiting for transfers between devices: 2.56 us -> 0.01 us  [on_device(): across = lax.ppermute(tied(ones, send_x), 'dp', swap(3))]
    ppermute x1, waiting for transfers between devices: 0.67 us -> 2.78 us  [on_device(): came_b = lax.ppermute(send_b, 'dp', swap(1))]
    ppermute x1, waiting for transfers between devices: 0.01 us -> 1.25 us  [on_device(): came_z = lax.ppermute(send_z, 'dp', swap(2))]
    ppermute x1, starting transfers between devices: 1.58 us -> 0.45 us  [on_device(): came_z = lax.ppermute(send_z, 'dp', swap(2))]
    ppermute x1, starting transfers between devices: 0.42 us -> 1.55 us  [on_device(): across = lax.ppermute(tied(ones, send_x), 'dp', swap(3))]
    ppermute x1, starting transfers between devices: 1.49 us -> 0.65 us  [on_device(): came_a = lax.ppermute(send_a, 'dp', swap(2))]
where the time goes in v9:
time: 40.6 us; the launch traced here: 40.4 us
  starting transfers between devices  18.6 us (46%)
  Pallas kernels  12.2 us (30%)
  waiting for transfers between devices  8.03 us (20%)
  between operations  1.45 us (4%)
    pallas_call x1, Pallas kernels, on_device(): pl.pallas_call(functools.partial(state_kernel, split=split), out_shape=(s...  4.06 us
    ppermute x1, waiting for transfers between devices, on_device(): came_b = lax.ppermute(send_b, 'dp', swap(1))  2.78 us
    ppermute x1, starting transfers between devices, on_device(): ones = join(tied(mark, later), mark, lax.ppermute(mark, 'dp', swap(4)))  2.76 us
    ppermute x1, starting transfers between devices, on_device(): edge_a = lax.ppermute(tail_a, 'seq', one_back)  2.69 us
    ppermute x1, starting transfers between devices, on_device(): came = lax.ppermute(send, 'dp', swap(4))  2.63 us
    pallas_call x1, Pallas kernels, on_device(): pl.pallas_call(diagonal_kernel, out_shape=(shape((2, n, HALF), F32), shap...  2.14 us
    ppermute x1, waiting for transfers between devices, on_device(): lax.ppermute(to_same, 'seq', [(i, i ^ 2) for i in range(places)])  1.85 us
    pallas_call x1, Pallas kernels, on_device(): pl.pallas_call(finish_kernel, out_shape=shape((1, n, D), BF16), in_specs=...  1.75 us
  transfers between devices with their start and end apart: 17, of which 5 were waited for; matrix products, arithmetic and copies ran while one was open for 0% of the time, Pallas kernels for 18%

profile of v9, /device:TPU:0, one launch (start us, length us, event | category | flops | bytes accessed | tf_op | source)
XLA Modules:
  0.0 40.4 jit_solution(3104105746237421985)
XLA Ops:
  0.6 0.5 %collective-permute-start = (bf16[1,256,2816]{2,1,0:T(8,128)(2,1)}, bf16[1,256,2816]{2,1,0:T(8,128)(2,1)S(1)}, u32[]{:S(2)}, u32[]{:S(2)}) collective-permute-start(bf16[1,256,2816]{2,1,0:T(8,128)(2,1)} %xbc_hbm.1), channel_id=1, source_target_pairs={{0,1},{1,0},{2,3},{3,2},{4,5},{5,4},{6,7},{7,6},{8,9},{9,8},{10,11... | collective-permute-start | bytes 4325384 | tf_op jit(solution)/shard_map/ppermute | solution.py:505
  1.1 0.1 collective-permute-start.3
  1.2 1.3 %tail.1 = (bf16[48,384]{1,0:T(8,128)(2,1)S(1)}, bf16[48,384]{1,0:T(8,128)(2,1)S(1)}, bf16[1,40,256]{2,1,0:T(8,128)(2,1)S(1)}, f32[40,8]{1,0:T(8,128)S(1)}, s32[8...) custom-call(bf16[1,256,2816]{2,1,0:T(8,128)(2,1)} %xbc_hbm.1, bf16[1,40,256]{2,1,0:T(8,128)(2,1)} %bitcast.2, f32[40]{0:T(128)} %bias_hbm.1, ...), custom_call_target="tpu_custom_call" | custom-call | tf_op jit(solution)/shard_map/tail/pallas_call | solution.py:508
  2.6 2.7 %collective-permute-start.1 = (bf16[48,384]{1,0:T(8,128)(2,1)S(1)}, bf16[48,384]{1,0:T(8,128)(2,1)S(1)}, u32[]{:S(2)}, u32[]{:S(2)}) collective-permute-start(bf16[48,384]{1,0:T(8,128)(2,1)S(1)} %get-tuple-element.48), channel_id=1, source_target_pairs={{0,3},{1,2},{2,1},{3,0},{4,7},{5,6},{6,5},{7,4},{8,11},{9,10},{10,... | collective-permute-start | bytes 110600 | tf_op jit(solution)/shard_map/ppermute | solution.py:519
  5.3 0.4 collective-permute-start.2
  6.3 2.8 %collective-permute-start.4 = (f32[8,128]{1,0:T(8,128)S(1)}, f32[8,128]{1,0:T(8,128)S(1)}, u32[]{:S(2)}, u32[]{:S(2)}) collective-permute-start(f32[8,128]{1,0:T(8,128)S(1)} %mark.1.mark_ref.a_ref), channel_id=1, source_target_pairs={{0,16},{4,20},{8,24},{12,28},{16,0},{20,4},{24,8},{28,12},{1,17},{... | collective-permute-start | bytes 12296 | tf_op jit(solution)/shard_map/ppermute | solution.py:562
  9.1 1.3 %steps.1 = (f32[512,128]{1,0:T(8,128)S(1)}, f32[512,128]{1,0:T(8,128)S(1)}, f32[256,128]{1,0:T(8,128)S(1)}, bf16[16,128]{1,0:T(8,128)(2,1)S(1)}, f32[4,1536]{1,0:T(4,128)S(1)}, /*index=5*/f32[1,1536]{1,0:T(1,128)S(1)}) custom-call(bf16[1,40,256]{2,1,0:T(8,128)(2,1)S(1)} %get-tuple-element.50.own_ref, ...), custom_call_target="tpu_custom_call" | custom-call | flops 2013265920 | bytes 524288 | tf_op jit(solution)/shard_map/steps/pallas_call | solution.py:525
  10.5 0.6 %later.1.later_ref = bf16[16,128]{1,0:T(8,128)(2,1)S(1)} custom-call(bf16[48,384]{1,0:T(8,128)(2,1)S(1)} %collective-permute-done.2.same_ref.edge_b_ref, bf16[48,384]{1,0:T(8,128)(2,1)S(1)} %collective-permute-done.1.cross_ref.edge_a_ref, f32[40,8]{1,0:T(8,128)S(1)} %get-tuple-element.56.columns_ref, s32[8,128]{1,0:T(8,128)S(1)} %get-tuple-element.52.points_ref), custom_call_target="tpu_custom_call" | custom-call | flops 671088640 | bytes 524288 | tf_op jit(solution)/shard_map/later/pallas_call | solution.py:540
  11.1 0.0 copy-start
  11.1 4.1 %states.1 = (bf16[128,1280]{1,0:T(8,128)(2,1)S(1)}, bf16[128,1280]{1,0:T(8,128)(2,1)S(1)}, bf16[256,1280]{1,0:T(8,128)(2,1)S(1)}, bf16[256,1280]{1,0:T(8,128)(2,...) custom-call(bf16[256,1536]{1,0:T(8,128)(2,1)S(1)} %get-tuple-element, ...), custom_call_target="tpu_custom_call" | custom-call | flops 8388608000 | bytes 3145728 | tf_op jit(solution)/shard_map/states/pallas_call | solution.py:567
  15.1 0.1 collective-permute-start.5
  15.2 1.6 %collective-permute-start.6 = (f32[392,128]{1,0:T(8,128)S(1)}, f32[392,128]{1,0:T(8,128)S(1)}, u32[]{:S(2)}, u32[]{:S(2)}) collective-permute-start(f32[392,128]{1,0:T(8,128)S(1)} %get-tuple-element.69), channel_id=1, source_target_pairs={{0,4},{4,0},{8,12},{12,8},{16,20},{20,16},{24,28},{28,24},{1,5},{5... | collective-permute-start | bytes 602120 | tf_op jit(solution)/shard_map/ppermute | solution.py:592
  16.8 1.6 %collective-permute-start.8 = (f32[8,128]{1,0:T(8,128)S(1)}, f32[8,128]{1,0:T(8,128)S(1)}, u32[]{:S(2)}, u32[]{:S(2)}) collective-permute-start(f32[8,128]{1,0:T(8,128)S(1)} %join.1.mark_ref), channel_id=1, source_target_pairs={{0,12},{4,8},{8,4},{12,0},{16,28},{20,24},{24,20},{28,16},{1,13},{... | collective-permute-start | bytes 12296 | tf_op jit(solution)/shard_map/ppermute | solution.py:594
  18.3 0.4 %collective-permute-start.7 = (f32[264,128]{1,0:T(8,128)S(1)}, f32[264,128]{1,0:T(8,128)S(1)}, u32[]{:S(2)}, u32[]{:S(2)}) collective-permute-start(f32[264,128]{1,0:T(8,128)S(1)} %get-tuple-element.71), channel_id=1, source_target_pairs={{0,8},{4,12},{8,0},{12,4},{16,24},{20,28},{24,16},{28,20},{1,9},{5... | collective-permute-start | bytes 405512 | tf_op jit(solution)/shard_map/ppermute | solution.py:593
  18.8 1.5 %collective-permute-start.14 = (bf16[128,1280]{1,0:T(8,128)(2,1)S(1)}, bf16[128,1280]{1,0:T(8,128)(2,1)S(1)}, u32[]{:S(2)}, u32[]{:S(2)}) collective-permute-start(bf16[128,1280]{1,0:T(8,128)(2,1)S(1)} %get-tuple-element.84), channel_id=1, source_target_pairs={{0,2},{1,3},{2,0},{3,1},{4,6},{5,7},{6,4},{7,5},{8,10},{9,11},{10,... | collective-permute-start | bytes 983048 | tf_op jit(solution)/shard_map/ppermute | solution.py:586
  20.3 2.1 %diagonal.1 = (f32[2,256,1280]{2,1,0:T(8,128)S(1)}, f32[2,256,1280]{2,1,0:T(8,128)S(1)}) custom-call(bf16[256,1280]{1,0:T(8,128)(2,1)S(1)} %get-tuple-element.62.act_own_ref, bf16[256,1280]{1,0:T(8,128)(2,1)S(1)} %collective-permute-done.5.act_other_ref, bf16[256,256]{1,0:T(8,128)(2,1)S(1)} %get-tuple-element.64.bc_ref, ...), custom_call_target="tpu_custom_call" | custom-call | flops 4697620480 | bytes 2621440 | tf_op jit(solution)/shard_map/diagonal/pallas_call | solution.py:597
  22.4 1.2 %collective-permute-done.7.came_z_ref = f32[264,128]{1,0:T(8,128)S(1)} collective-permute-done((f32[264,128]{1,0:T(8,128)S(1)}, f32[264,128]{1,0:T(8,128)S(1)}, u32[]{:S(2)}, u32[]{:S(2)}) %collective-permute-start.7) | collective-permute-done | bytes 135200 | tf_op jit(solution)/shard_map/ppermute | solution.py:593
  23.7 0.1 halves.1
  23.8 0.7 %collective-permute-start.9 = (f32[192,128]{1,0:T(8,128)S(1)}, f32[192,128]{1,0:T(8,128)S(1)}, u32[]{:S(2)}, u32[]{:S(2)}) collective-permute-start(f32[192,128]{1,0:T(8,128)S(1)} %get-tuple-element.74), channel_id=1, source_target_pairs={{0,8},{4,12},{8,0},{12,4},{16,24},{20,28},{24,16},{28,20},{1,9},{5... | collective-permute-start | bytes 294920 | tf_op jit(solution)/shard_map/ppermute | solution.py:611
  24.4 1.5 %collective-permute-start.10 = (f32[128,128]{1,0:T(8,128)S(1)}, f32[128,128]{1,0:T(8,128)S(1)}, u32[]{:S(2)}, u32[]{:S(2)}) collective-permute-start(f32[128,128]{1,0:T(8,128)S(1)} %get-tuple-element.76), channel_id=1, source_target_pairs={{0,4},{4,0},{8,12},{12,8},{16,20},{20,16},{24,28},{28,24},{1,5},{5... | collective-permute-start | bytes 196616 | tf_op jit(solution)/shard_map/ppermute | solution.py:612
  25.9 2.8 %collective-permute-done.10.came_b_ref = f32[128,128]{1,0:T(8,128)S(1)} collective-permute-done((f32[128,128]{1,0:T(8,128)S(1)}, f32[128,128]{1,0:T(8,128)S(1)}, u32[]{:S(2)}, u32[]{:S(2)}) %collective-permute-start.10) | collective-permute-done | bytes 65568 | tf_op jit(solution)/shard_map/ppermute | solution.py:612
  28.7 0.3 carry.1
  29.0 0.1 collective-permute-start.15
  29.1 1.6 %collective-permute-start.11 = (f32[80,128]{1,0:T(8,128)S(1)}, f32[80,128]{1,0:T(8,128)S(1)}, u32[]{:S(2)}, u32[]{:S(2)}) collective-permute-start(f32[80,128]{1,0:T(8,128)S(1)} %get-tuple-element.78), channel_id=1, source_target_pairs={{0,2},{1,3},{2,0},{3,1},{4,6},{5,7},{6,4},{7,5},{8,10},{9,11},{10,... | collective-permute-start | bytes 122888 | tf_op jit(solution)/shard_map/ppermute | solution.py:615
  30.7 0.2 collective-permute-start.12
  30.9 0.5 %collective-permute-start.13 = (f32[80,128]{1,0:T(8,128)S(1)}, f32[80,128]{1,0:T(8,128)S(1)}, u32[]{:S(2)}, u32[]{:S(2)}) collective-permute-start(f32[80,128]{1,0:T(8,128)S(1)} %get-tuple-element.80), channel_id=1, source_target_pairs={{0,3},{1,2},{2,1},{3,0},{4,7},{5,6},{6,5},{7,4},{8,11},{9,10},{10,... | collective-permute-start | bytes 122888 | tf_op jit(solution)/shard_map/ppermute | solution.py:616
  31.3 1.8 %collective-permute-done.11.same_ref = f32[80,128]{1,0:T(8,128)S(1)} collective-permute-done((f32[80,128]{1,0:T(8,128)S(1)}, f32[80,128]{1,0:T(8,128)S(1)}, u32[]{:S(2)}, u32[]{:S(2)}) %collective-permute-start.11) | collective-permute-done | bytes 40992 | tf_op jit(solution)/shard_map/ppermute | solution.py:615
  33.2 1.1 %collective-permute-done.13.cross_ref = f32[80,128]{1,0:T(8,128)S(1)} collective-permute-done((f32[80,128]{1,0:T(8,128)S(1)}, f32[80,128]{1,0:T(8,128)S(1)}, u32[]{:S(2)}, u32[]{:S(2)}) %collective-permute-start.13) | collective-permute-done | bytes 40992 | tf_op jit(solution)/shard_map/ppermute | solution.py:616
  34.3 2.6 %collective-permute-start.16 = (f32[80,128]{1,0:T(8,128)S(1)}, f32[80,128]{1,0:T(8,128)S(1)}, u32[]{:S(2)}, u32[]{:S(2)}) collective-permute-start(f32[80,128]{1,0:T(8,128)S(1)} %get-tuple-element.91), channel_id=1, source_target_pairs={{0,16},{4,20},{8,24},{12,28},{16,0},{20,4},{24,8},{28,12},{1,17},{... | collective-permute-start | bytes 122888 | tf_op jit(solution)/shard_map/ppermute | solution.py:645
  37.0 1.7 %finish.1 = bf16[1,256,2560]{2,1,0:T(8,128)(2,1)} custom-call(f32[2,256,1280]{2,1,0:T(8,128)S(1)} %get-tuple-element.82.near_ref, f32[2,256,1280]{2,1,0:T(8,128)S(1)} %get-tuple-element.83.far_ref, bf16[256,256]{1,0:T(8,128)(2,1)S(1)} %get-tuple-element.64.bc_ref, bf16[128,1280]{1,0:T(8,128)(2,1)S(1)} %get-tuple-element.87.h_own_ref, ...), custom_call_target="tpu_custom_call" | custom-call | flops 3355443200 | bytes 7864320 | tf_op jit(solution)/shard_map/finish/pallas_call | solution.py:633
  38.7 1.0 %collective-permute-done.16.came_ref = f32[80,128]{1,0:T(8,128)S(1)} collective-permute-done((f32[80,128]{1,0:T(8,128)S(1)}, f32[80,128]{1,0:T(8,128)S(1)}, u32[]{:S(2)}, u32[]{:S(2)}) %collective-permute-start.16) | collective-permute-done | bytes 40992 | tf_op jit(solution)/shard_map/ppermute | solution.py:645
  39.7 0.6 %sum.1 = f32[80,128]{1,0:T(8,128)} custom-call(f32[80,128]{1,0:T(8,128)S(1)} %get-tuple-element.90.keep_ref, f32[80,128]{1,0:T(8,128)S(1)} %collective-permute-done.16.came_ref), custom_call_target="tpu_custom_call" | custom-call | tf_op jit(solution)/shard_map/sum/pallas_call | solution.py:485
  (20 shorter events, 0.1 us)
Async XLA Ops:
  0.6 10.4 %collective-permute-start = (bf16[1,256,2816]{2,1,0:T(8,128)(2,1)}, bf16[1,256,2816]{2,1,0:T(8,128)(2,1)S(1)}, u32[]{:S(2)}, u32[]{:S(2)}) collective-permute-start(bf16[1,256,2816]{2,1,0:T(8,128)(2,1)} %xbc_hbm.1), channel_id=1, source_target_pairs={{0,1},{1,0},{2,3},{3,2},{4,5},{5,4},{6,7},{7,6},{8,9},{9,8},{10,11... | collective-permute-start | bytes 4325384 | tf_op jit(solution)/shard_map/ppermute | solution.py:505
  1.1 8.0 %collective-permute-start.3 = (bf16[1,40,256]{2,1,0:T(8,128)(2,1)}, bf16[1,40,256]{2,1,0:T(8,128)(2,1)S(1)}, u32[]{:S(2)}, u32[]{:S(2)}) collective-permute-start(bf16[1,40,256]{2,1,0:T(8,128)(2,1)} %bitcast.1), channel_id=1, source_target_pairs={{0,1},{1,0},{2,3},{3,2},{4,5},{5,4},{6,7},{7,6},{8,9},{9,8},{10,11... | collective-permute-start | bytes 61448 | tf_op jit(solution)/shard_map/ppermute | solution.py:504
  2.6 7.9 %collective-permute-start.1 = (bf16[48,384]{1,0:T(8,128)(2,1)S(1)}, bf16[48,384]{1,0:T(8,128)(2,1)S(1)}, u32[]{:S(2)}, u32[]{:S(2)}) collective-permute-start(bf16[48,384]{1,0:T(8,128)(2,1)S(1)} %get-tuple-element.48), channel_id=1, source_target_pairs={{0,3},{1,2},{2,1},{3,0},{4,7},{5,6},{6,5},{7,4},{8,11},{9,10},{10,... | collective-permute-start | bytes 110600 | tf_op jit(solution)/shard_map/ppermute | solution.py:519
  5.3 5.2 %collective-permute-start.2 = (bf16[48,384]{1,0:T(8,128)(2,1)S(1)}, bf16[48,384]{1,0:T(8,128)(2,1)S(1)}, u32[]{:S(2)}, u32[]{:S(2)}) collective-permute-start(bf16[48,384]{1,0:T(8,128)(2,1)S(1)} %get-tuple-element.49), channel_id=1, source_target_pairs={{0,2},{1,3},{2,0},{3,1},{4,6},{5,7},{6,4},{7,5},{8,10},{9,11},{10,... | collective-permute-start | bytes 110600 | tf_op jit(solution)/shard_map/ppermute | solution.py:520
  6.3 4.7 %collective-permute-start.4 = (f32[8,128]{1,0:T(8,128)S(1)}, f32[8,128]{1,0:T(8,128)S(1)}, u32[]{:S(2)}, u32[]{:S(2)}) collective-permute-start(f32[8,128]{1,0:T(8,128)S(1)} %mark.1.mark_ref.a_ref), channel_id=1, source_target_pairs={{0,16},{4,20},{8,24},{12,28},{16,0},{20,4},{24,8},{28,12},{1,17},{... | collective-permute-start | bytes 12296 | tf_op jit(solution)/shard_map/ppermute | solution.py:562
  11.1 9.2 %copy-start = (bf16[1,256,2560]{2,1,0:T(8,128)(2,1)S(1)}, bf16[1,256,2560]{2,1,0:T(8,128)(2,1)}, u32[]{:S(2)}) copy-start(bf16[1,256,2560]{2,1,0:T(8,128)(2,1)} %gate_ref.1) | copy-start | bytes 3932164
  15.1 5.2 %collective-permute-start.5 = (bf16[256,1280]{1,0:T(8,128)(2,1)S(1)}, bf16[256,1280]{1,0:T(8,128)(2,1)S(1)}, u32[]{:S(2)}, u32[]{:S(2)}) collective-permute-start(bf16[256,1280]{1,0:T(8,128)(2,1)S(1)} %get-tuple-element.63), channel_id=1, source_target_pairs={{0,1},{1,0},{2,3},{3,2},{4,5},{5,4},{6,7},{7,6},{8,9},{9,8},{10,11... | collective-permute-start | bytes 1966088 | tf_op jit(solution)/shard_map/ppermute | solution.py:589
  15.2 8.5 %collective-permute-start.6 = (f32[392,128]{1,0:T(8,128)S(1)}, f32[392,128]{1,0:T(8,128)S(1)}, u32[]{:S(2)}, u32[]{:S(2)}) collective-permute-start(f32[392,128]{1,0:T(8,128)S(1)} %get-tuple-element.69), channel_id=1, source_target_pairs={{0,4},{4,0},{8,12},{12,8},{16,20},{20,16},{24,28},{28,24},{1,5},{5... | collective-permute-start | bytes 602120 | tf_op jit(solution)/shard_map/ppermute | solution.py:592
  16.8 5.7 %collective-permute-start.8 = (f32[8,128]{1,0:T(8,128)S(1)}, f32[8,128]{1,0:T(8,128)S(1)}, u32[]{:S(2)}, u32[]{:S(2)}) collective-permute-start(f32[8,128]{1,0:T(8,128)S(1)} %join.1.mark_ref), channel_id=1, source_target_pairs={{0,12},{4,8},{8,4},{12,0},{16,28},{20,24},{24,20},{28,16},{1,13},{... | collective-permute-start | bytes 12296 | tf_op jit(solution)/shard_map/ppermute | solution.py:594
  18.3 5.4 %collective-permute-start.7 = (f32[264,128]{1,0:T(8,128)S(1)}, f32[264,128]{1,0:T(8,128)S(1)}, u32[]{:S(2)}, u32[]{:S(2)}) collective-permute-start(f32[264,128]{1,0:T(8,128)S(1)} %get-tuple-element.71), channel_id=1, source_target_pairs={{0,8},{4,12},{8,0},{12,4},{16,24},{20,28},{24,16},{28,20},{1,9},{5... | collective-permute-start | bytes 405512 | tf_op jit(solution)/shard_map/ppermute | solution.py:593
  18.8 9.9 %collective-permute-start.14 = (bf16[128,1280]{1,0:T(8,128)(2,1)S(1)}, bf16[128,1280]{1,0:T(8,128)(2,1)S(1)}, u32[]{:S(2)}, u32[]{:S(2)}) collective-permute-start(bf16[128,1280]{1,0:T(8,128)(2,1)S(1)} %get-tuple-element.84), channel_id=1, source_target_pairs={{0,2},{1,3},{2,0},{3,1},{4,6},{5,7},{6,4},{7,5},{8,10},{9,11},{10,... | collective-permute-start | bytes 983048 | tf_op jit(solution)/shard_map/ppermute | solution.py:586
  23.8 4.9 %collective-permute-start.9 = (f32[192,128]{1,0:T(8,128)S(1)}, f32[192,128]{1,0:T(8,128)S(1)}, u32[]{:S(2)}, u32[]{:S(2)}) collective-permute-start(f32[192,128]{1,0:T(8,128)S(1)} %get-tuple-element.74), channel_id=1, source_target_pairs={{0,8},{4,12},{8,0},{12,4},{16,24},{20,28},{24,16},{28,20},{1,9},{5... | collective-permute-start | bytes 294920 | tf_op jit(solution)/shard_map/ppermute | solution.py:611
  24.4 4.3 %collective-permute-start.10 = (f32[128,128]{1,0:T(8,128)S(1)}, f32[128,128]{1,0:T(8,128)S(1)}, u32[]{:S(2)}, u32[]{:S(2)}) collective-permute-start(f32[128,128]{1,0:T(8,128)S(1)} %get-tuple-element.76), channel_id=1, source_target_pairs={{0,4},{4,0},{8,12},{12,8},{16,20},{20,16},{24,28},{28,24},{1,5},{5... | collective-permute-start | bytes 196616 | tf_op jit(solution)/shard_map/ppermute | solution.py:612
  28.7 2.6 %copy-start.1 = (f32[2560]{0:T(1024)S(1)}, f32[2560]{0:T(1024)}, u32[]{:S(2)}) copy-start(f32[2560]{0:T(1024)} %param.19) | copy-start | bytes 30724
  29.0 7.9 %collective-permute-start.15 = (bf16[128,1280]{1,0:T(8,128)(2,1)S(1)}, bf16[128,1280]{1,0:T(8,128)(2,1)S(1)}, u32[]{:S(2)}, u32[]{:S(2)}) collective-permute-start(bf16[128,1280]{1,0:T(8,128)(2,1)S(1)} %get-tuple-element.88), channel_id=1, source_target_pairs={{0,1},{1,0},{2,3},{3,2},{4,5},{5,4},{6,7},{7,6},{8,9},{9,8},{10,11... | collective-permute-start | bytes 983048 | tf_op jit(solution)/shard_map/ppermute | solution.py:632
  29.1 4.1 %collective-permute-start.11 = (f32[80,128]{1,0:T(8,128)S(1)}, f32[80,128]{1,0:T(8,128)S(1)}, u32[]{:S(2)}, u32[]{:S(2)}) collective-permute-start(f32[80,128]{1,0:T(8,128)S(1)} %get-tuple-element.78), channel_id=1, source_target_pairs={{0,2},{1,3},{2,0},{3,1},{4,6},{5,7},{6,4},{7,5},{8,10},{9,11},{10,... | collective-permute-start | bytes 122888 | tf_op jit(solution)/shard_map/ppermute | solution.py:615
  30.7 2.5 %collective-permute-start.12 = (f32[80,128]{1,0:T(8,128)S(1)}, f32[80,128]{1,0:T(8,128)S(1)}, u32[]{:S(2)}, u32[]{:S(2)}) collective-permute-start(f32[80,128]{1,0:T(8,128)S(1)} %get-tuple-element.79), channel_id=1, source_target_pairs={{0,1},{1,0},{2,3},{3,2},{4,5},{5,4},{6,7},{7,6},{8,9},{9,8},{10,11... | collective-permute-start | bytes 122888 | tf_op jit(solution)/shard_map/ppermute | solution.py:614
  30.9 3.4 %collective-permute-start.13 = (f32[80,128]{1,0:T(8,128)S(1)}, f32[80,128]{1,0:T(8,128)S(1)}, u32[]{:S(2)}, u32[]{:S(2)}) collective-permute-start(f32[80,128]{1,0:T(8,128)S(1)} %get-tuple-element.80), channel_id=1, source_target_pairs={{0,3},{1,2},{2,1},{3,0},{4,7},{5,6},{6,5},{7,4},{8,11},{9,10},{10,... | collective-permute-start | bytes 122888 | tf_op jit(solution)/shard_map/ppermute | solution.py:616
  34.3 5.4 %collective-permute-start.16 = (f32[80,128]{1,0:T(8,128)S(1)}, f32[80,128]{1,0:T(8,128)S(1)}, u32[]{:S(2)}, u32[]{:S(2)}) collective-permute-start(f32[80,128]{1,0:T(8,128)S(1)} %get-tuple-element.91), channel_id=1, source_target_pairs={{0,16},{4,20},{8,24},{12,28},{16,0},{20,4},{24,8},{28,12},{1,17},{... | collective-permute-start | bytes 122888 | tf_op jit(solution)/shard_map/ppermute | solution.py:645

commit v10 on v9

--- a/solution.py
+++ b/solution.py
@@ -19,7 +19,7 @@
 CH = D + BC
 CHUNK = 256
 EDGE = 16
-LEAD = 192
+LEAD = 184
 F32 = jnp.float32
 BF16 = jnp.bfloat16
 VMEM = pl.BlockSpec(memory_space=pltpu.VMEM)

time: 40.6 us -> 40.3 us (level)
    ppermute x1, waiting for transfers between devices: 1.02 us -> 0.61 us  [on_device(): came = lax.ppermute(send, 'dp', swap(4))]
where the time goes in v10:
time: 40.3 us; the launch traced here: 40.1 us
  starting transfers between devices  18.5 us (46%)
  Pallas kernels  12.2 us (30%)
  waiting for transfers between devices  7.88 us (20%)
  between operations  1.45 us (4%)
    pallas_call x1, Pallas kernels, on_device(): pl.pallas_call(functools.partial(state_kernel, split=split), out_shape=(s...  4.06 us
    ppermute x1, waiting for transfers between devices, on_device(): came_b = lax.ppermute(send_b, 'dp', swap(1))  2.82 us
    ppermute x1, starting transfers between devices, on_device(): ones = join(tied(mark, later), mark, lax.ppermute(mark, 'dp', swap(4)))  2.76 us
    ppermute x1, starting transfers between devices, on_device(): edge_a = lax.ppermute(tail_a, 'seq', one_back)  2.69 us
    ppermute x1, starting transfers between devices, on_device(): came = lax.ppermute(send, 'dp', swap(4))  2.63 us
    pallas_call x1, Pallas kernels, on_device(): pl.pallas_call(diagonal_kernel, out_shape=(shape((2, n, HALF), F32), shap...  2.09 us
    ppermute x1, waiting for transfers between devices, on_device(): lax.ppermute(to_same, 'seq', [(i, i ^ 2) for i in range(places)])  1.85 us
    pallas_call x1, Pallas kernels, on_device(): pl.pallas_call(finish_kernel, out_shape=shape((1, n, D), BF16), in_specs=...  1.73 us
  transfers between devices with their start and end apart: 17, of which 5 were waited for; matrix products, arithmetic and copies ran while one was open for 0% of the time, Pallas kernels for 18%

profile of v10, /device:TPU:0, one launch (start us, length us, event | category | flops | bytes accessed | tf_op | source)
XLA Modules:
  0.0 40.1 jit_solution(3408216701653442059)
XLA Ops:
  0.6 0.5 %collective-permute-start = (bf16[1,256,2816]{2,1,0:T(8,128)(2,1)}, bf16[1,256,2816]{2,1,0:T(8,128)(2,1)S(1)}, u32[]{:S(2)}, u32[]{:S(2)}) collective-permute-start(bf16[1,256,2816]{2,1,0:T(8,128)(2,1)} %xbc_hbm.1), channel_id=1, source_target_pairs={{0,1},{1,0},{2,3},{3,2},{4,5},{5,4},{6,7},{7,6},{8,9},{9,8},{10,11... | collective-permute-start | bytes 4325384 | tf_op jit(solution)/shard_map/ppermute | solution.py:505
  1.1 0.1 collective-permute-start.3
  1.2 1.3 %tail.1 = (bf16[48,384]{1,0:T(8,128)(2,1)S(1)}, bf16[48,384]{1,0:T(8,128)(2,1)S(1)}, bf16[1,40,256]{2,1,0:T(8,128)(2,1)S(1)}, f32[40,8]{1,0:T(8,128)S(1)}, s32[8...) custom-call(bf16[1,256,2816]{2,1,0:T(8,128)(2,1)} %xbc_hbm.1, bf16[1,40,256]{2,1,0:T(8,128)(2,1)} %bitcast.2, f32[40]{0:T(128)} %bias_hbm.1, ...), custom_call_target="tpu_custom_call" | custom-call | tf_op jit(solution)/shard_map/tail/pallas_call | solution.py:508
  2.6 2.7 %collective-permute-start.1 = (bf16[48,384]{1,0:T(8,128)(2,1)S(1)}, bf16[48,384]{1,0:T(8,128)(2,1)S(1)}, u32[]{:S(2)}, u32[]{:S(2)}) collective-permute-start(bf16[48,384]{1,0:T(8,128)(2,1)S(1)} %get-tuple-element.48), channel_id=1, source_target_pairs={{0,3},{1,2},{2,1},{3,0},{4,7},{5,6},{6,5},{7,4},{8,11},{9,10},{10,... | collective-permute-start | bytes 110600 | tf_op jit(solution)/shard_map/ppermute | solution.py:519
  5.3 0.4 collective-permute-start.2
  6.3 2.8 %collective-permute-start.4 = (f32[8,128]{1,0:T(8,128)S(1)}, f32[8,128]{1,0:T(8,128)S(1)}, u32[]{:S(2)}, u32[]{:S(2)}) collective-permute-start(f32[8,128]{1,0:T(8,128)S(1)} %mark.1.mark_ref.a_ref), channel_id=1, source_target_pairs={{0,16},{4,20},{8,24},{12,28},{16,0},{20,4},{24,8},{28,12},{1,17},{... | collective-permute-start | bytes 12296 | tf_op jit(solution)/shard_map/ppermute | solution.py:562
  9.1 1.3 %steps.1 = (f32[512,128]{1,0:T(8,128)S(1)}, f32[512,128]{1,0:T(8,128)S(1)}, f32[256,128]{1,0:T(8,128)S(1)}, bf16[16,128]{1,0:T(8,128)(2,1)S(1)}, f32[4,1536]{1,0:T(4,128)S(1)}, /*index=5*/f32[1,1536]{1,0:T(1,128)S(1)}) custom-call(bf16[1,40,256]{2,1,0:T(8,128)(2,1)S(1)} %get-tuple-element.50.own_ref, ...), custom_call_target="tpu_custom_call" | custom-call | flops 2013265920 | bytes 524288 | tf_op jit(solution)/shard_map/steps/pallas_call | solution.py:525
  10.5 0.6 %later.1.later_ref = bf16[16,128]{1,0:T(8,128)(2,1)S(1)} custom-call(bf16[48,384]{1,0:T(8,128)(2,1)S(1)} %collective-permute-done.2.same_ref.edge_b_ref, bf16[48,384]{1,0:T(8,128)(2,1)S(1)} %collective-permute-done.1.cross_ref.edge_a_ref, f32[40,8]{1,0:T(8,128)S(1)} %get-tuple-element.56.columns_ref, s32[8,128]{1,0:T(8,128)S(1)} %get-tuple-element.52.points_ref), custom_call_target="tpu_custom_call" | custom-call | flops 671088640 | bytes 524288 | tf_op jit(solution)/shard_map/later/pallas_call | solution.py:540
  11.1 0.0 copy-start
  11.1 4.1 %states.1 = (bf16[128,1280]{1,0:T(8,128)(2,1)S(1)}, bf16[128,1280]{1,0:T(8,128)(2,1)S(1)}, bf16[256,1280]{1,0:T(8,128)(2,1)S(1)}, bf16[256,1280]{1,0:T(8,128)(2,...) custom-call(bf16[256,1536]{1,0:T(8,128)(2,1)S(1)} %get-tuple-element, ...), custom_call_target="tpu_custom_call" | custom-call | flops 8388608000 | bytes 3145728 | tf_op jit(solution)/shard_map/states/pallas_call | solution.py:567
  15.1 0.1 collective-permute-start.5
  15.2 1.6 %collective-permute-start.6 = (f32[376,128]{1,0:T(8,128)S(1)}, f32[376,128]{1,0:T(8,128)S(1)}, u32[]{:S(2)}, u32[]{:S(2)}) collective-permute-start(f32[376,128]{1,0:T(8,128)S(1)} %get-tuple-element.69), channel_id=1, source_target_pairs={{0,4},{4,0},{8,12},{12,8},{16,20},{20,16},{24,28},{28,24},{1,5},{5... | collective-permute-start | bytes 577544 | tf_op jit(solution)/shard_map/ppermute | solution.py:592
  16.8 1.6 %collective-permute-start.8 = (f32[8,128]{1,0:T(8,128)S(1)}, f32[8,128]{1,0:T(8,128)S(1)}, u32[]{:S(2)}, u32[]{:S(2)}) collective-permute-start(f32[8,128]{1,0:T(8,128)S(1)} %join.1.mark_ref), channel_id=1, source_target_pairs={{0,12},{4,8},{8,4},{12,0},{16,28},{20,24},{24,20},{28,16},{1,13},{... | collective-permute-start | bytes 12296 | tf_op jit(solution)/shard_map/ppermute | solution.py:594
  18.3 0.4 %collective-permute-start.7 = (f32[280,128]{1,0:T(8,128)S(1)}, f32[280,128]{1,0:T(8,128)S(1)}, u32[]{:S(2)}, u32[]{:S(2)}) collective-permute-start(f32[280,128]{1,0:T(8,128)S(1)} %get-tuple-element.71), channel_id=1, source_target_pairs={{0,8},{4,12},{8,0},{12,4},{16,24},{20,28},{24,16},{28,20},{1,9},{5... | collective-permute-start | bytes 430088 | tf_op jit(solution)/shard_map/ppermute | solution.py:593
  18.8 1.5 %collective-permute-start.14 = (bf16[128,1280]{1,0:T(8,128)(2,1)S(1)}, bf16[128,1280]{1,0:T(8,128)(2,1)S(1)}, u32[]{:S(2)}, u32[]{:S(2)}) collective-permute-start(bf16[128,1280]{1,0:T(8,128)(2,1)S(1)} %get-tuple-element.84), channel_id=1, source_target_pairs={{0,2},{1,3},{2,0},{3,1},{4,6},{5,7},{6,4},{7,5},{8,10},{9,11},{10,... | collective-permute-start | bytes 983048 | tf_op jit(solution)/shard_map/ppermute | solution.py:586
  20.3 2.1 %diagonal.1 = (f32[2,256,1280]{2,1,0:T(8,128)S(1)}, f32[2,256,1280]{2,1,0:T(8,128)S(1)}) custom-call(bf16[256,1280]{1,0:T(8,128)(2,1)S(1)} %get-tuple-element.62.act_own_ref, bf16[256,1280]{1,0:T(8,128)(2,1)S(1)} %collective-permute-done.5.act_other_ref, bf16[256,256]{1,0:T(8,128)(2,1)S(1)} %get-tuple-element.64.bc_ref, ...), custom_call_target="tpu_custom_call" | custom-call | flops 4697620480 | bytes 2621440 | tf_op jit(solution)/shard_map/diagonal/pallas_call | solution.py:597
  22.4 1.5 %collective-permute-done.7.came_z_ref = f32[280,128]{1,0:T(8,128)S(1)} collective-permute-done((f32[280,128]{1,0:T(8,128)S(1)}, f32[280,128]{1,0:T(8,128)S(1)}, u32[]{:S(2)}, u32[]{:S(2)}) %collective-permute-start.7) | collective-permute-done | bytes 143392 | tf_op jit(solution)/shard_map/ppermute | solution.py:593
  23.9 0.1 halves.1
  23.9 0.6 %collective-permute-start.9 = (f32[184,128]{1,0:T(8,128)S(1)}, f32[184,128]{1,0:T(8,128)S(1)}, u32[]{:S(2)}, u32[]{:S(2)}) collective-permute-start(f32[184,128]{1,0:T(8,128)S(1)} %get-tuple-element.74), channel_id=1, source_target_pairs={{0,8},{4,12},{8,0},{12,4},{16,24},{20,28},{24,16},{28,20},{1,9},{5... | collective-permute-start | bytes 282632 | tf_op jit(solution)/shard_map/ppermute | solution.py:611
  24.5 1.5 %collective-permute-start.10 = (f32[136,128]{1,0:T(8,128)S(1)}, f32[136,128]{1,0:T(8,128)S(1)}, u32[]{:S(2)}, u32[]{:S(2)}) collective-permute-start(f32[136,128]{1,0:T(8,128)S(1)} %get-tuple-element.76), channel_id=1, source_target_pairs={{0,4},{4,0},{8,12},{12,8},{16,20},{20,16},{24,28},{28,24},{1,5},{5... | collective-permute-start | bytes 208904 | tf_op jit(solution)/shard_map/ppermute | solution.py:612
  26.0 2.8 %collective-permute-done.10.came_b_ref = f32[136,128]{1,0:T(8,128)S(1)} collective-permute-done((f32[136,128]{1,0:T(8,128)S(1)}, f32[136,128]{1,0:T(8,128)S(1)}, u32[]{:S(2)}, u32[]{:S(2)}) %collective-permute-start.10) | collective-permute-done | bytes 69664 | tf_op jit(solution)/shard_map/ppermute | solution.py:612
  28.9 0.3 carry.1
  29.2 0.1 collective-permute-start.15
  29.3 1.6 %collective-permute-start.11 = (f32[80,128]{1,0:T(8,128)S(1)}, f32[80,128]{1,0:T(8,128)S(1)}, u32[]{:S(2)}, u32[]{:S(2)}) collective-permute-start(f32[80,128]{1,0:T(8,128)S(1)} %get-tuple-element.78), channel_id=1, source_target_pairs={{0,2},{1,3},{2,0},{3,1},{4,6},{5,7},{6,4},{7,5},{8,10},{9,11},{10,... | collective-permute-start | bytes 122888 | tf_op jit(solution)/shard_map/ppermute | solution.py:615
  30.9 0.2 collective-permute-start.12
  31.0 0.5 %collective-permute-start.13 = (f32[80,128]{1,0:T(8,128)S(1)}, f32[80,128]{1,0:T(8,128)S(1)}, u32[]{:S(2)}, u32[]{:S(2)}) collective-permute-start(f32[80,128]{1,0:T(8,128)S(1)} %get-tuple-element.80), channel_id=1, source_target_pairs={{0,3},{1,2},{2,1},{3,0},{4,7},{5,6},{6,5},{7,4},{8,11},{9,10},{10,... | collective-permute-start | bytes 122888 | tf_op jit(solution)/shard_map/ppermute | solution.py:616
  31.5 1.8 %collective-permute-done.11.same_ref = f32[80,128]{1,0:T(8,128)S(1)} collective-permute-done((f32[80,128]{1,0:T(8,128)S(1)}, f32[80,128]{1,0:T(8,128)S(1)}, u32[]{:S(2)}, u32[]{:S(2)}) %collective-permute-start.11) | collective-permute-done | bytes 40992 | tf_op jit(solution)/shard_map/ppermute | solution.py:615
  33.3 1.1 %collective-permute-done.13.cross_ref = f32[80,128]{1,0:T(8,128)S(1)} collective-permute-done((f32[80,128]{1,0:T(8,128)S(1)}, f32[80,128]{1,0:T(8,128)S(1)}, u32[]{:S(2)}, u32[]{:S(2)}) %collective-permute-start.13) | collective-permute-done | bytes 40992 | tf_op jit(solution)/shard_map/ppermute | solution.py:616
  34.5 2.6 %collective-permute-start.16 = (f32[80,128]{1,0:T(8,128)S(1)}, f32[80,128]{1,0:T(8,128)S(1)}, u32[]{:S(2)}, u32[]{:S(2)}) collective-permute-start(f32[80,128]{1,0:T(8,128)S(1)} %get-tuple-element.91), channel_id=1, source_target_pairs={{0,16},{4,20},{8,24},{12,28},{16,0},{20,4},{24,8},{28,12},{1,17},{... | collective-permute-start | bytes 122888 | tf_op jit(solution)/shard_map/ppermute | solution.py:645
  37.1 1.7 %finish.1 = bf16[1,256,2560]{2,1,0:T(8,128)(2,1)} custom-call(f32[2,256,1280]{2,1,0:T(8,128)S(1)} %get-tuple-element.82.near_ref, f32[2,256,1280]{2,1,0:T(8,128)S(1)} %get-tuple-element.83.far_ref, bf16[256,256]{1,0:T(8,128)(2,1)S(1)} %get-tuple-element.64.bc_ref, bf16[128,1280]{1,0:T(8,128)(2,1)S(1)} %get-tuple-element.87.h_own_ref, ...), custom_call_target="tpu_custom_call" | custom-call | flops 3355443200 | bytes 7864320 | tf_op jit(solution)/shard_map/finish/pallas_call | solution.py:633
  38.8 0.6 %collective-permute-done.16.came_ref = f32[80,128]{1,0:T(8,128)S(1)} collective-permute-done((f32[80,128]{1,0:T(8,128)S(1)}, f32[80,128]{1,0:T(8,128)S(1)}, u32[]{:S(2)}, u32[]{:S(2)}) %collective-permute-start.16) | collective-permute-done | bytes 40992 | tf_op jit(solution)/shard_map/ppermute | solution.py:645
  39.5 0.6 %sum.1 = f32[80,128]{1,0:T(8,128)} custom-call(f32[80,128]{1,0:T(8,128)S(1)} %get-tuple-element.90.keep_ref, f32[80,128]{1,0:T(8,128)S(1)} %collective-permute-done.16.came_ref), custom_call_target="tpu_custom_call" | custom-call | tf_op jit(solution)/shard_map/sum/pallas_call | solution.py:485
  (20 shorter events, 0.1 us)
Async XLA Ops:
  0.6 10.4 %collective-permute-start = (bf16[1,256,2816]{2,1,0:T(8,128)(2,1)}, bf16[1,256,2816]{2,1,0:T(8,128)(2,1)S(1)}, u32[]{:S(2)}, u32[]{:S(2)}) collective-permute-start(bf16[1,256,2816]{2,1,0:T(8,128)(2,1)} %xbc_hbm.1), channel_id=1, source_target_pairs={{0,1},{1,0},{2,3},{3,2},{4,5},{5,4},{6,7},{7,6},{8,9},{9,8},{10,11... | collective-permute-start | bytes 4325384 | tf_op jit(solution)/shard_map/ppermute | solution.py:505
  1.1 8.0 %collective-permute-start.3 = (bf16[1,40,256]{2,1,0:T(8,128)(2,1)}, bf16[1,40,256]{2,1,0:T(8,128)(2,1)S(1)}, u32[]{:S(2)}, u32[]{:S(2)}) collective-permute-start(bf16[1,40,256]{2,1,0:T(8,128)(2,1)} %bitcast.1), channel_id=1, source_target_pairs={{0,1},{1,0},{2,3},{3,2},{4,5},{5,4},{6,7},{7,6},{8,9},{9,8},{10,11... | collective-permute-start | bytes 61448 | tf_op jit(solution)/shard_map/ppermute | solution.py:504
  2.6 7.9 %collective-permute-start.1 = (bf16[48,384]{1,0:T(8,128)(2,1)S(1)}, bf16[48,384]{1,0:T(8,128)(2,1)S(1)}, u32[]{:S(2)}, u32[]{:S(2)}) collective-permute-start(bf16[48,384]{1,0:T(8,128)(2,1)S(1)} %get-tuple-element.48), channel_id=1, source_target_pairs={{0,3},{1,2},{2,1},{3,0},{4,7},{5,6},{6,5},{7,4},{8,11},{9,10},{10,... | collective-permute-start | bytes 110600 | tf_op jit(solution)/shard_map/ppermute | solution.py:519
  5.3 5.2 %collective-permute-start.2 = (bf16[48,384]{1,0:T(8,128)(2,1)S(1)}, bf16[48,384]{1,0:T(8,128)(2,1)S(1)}, u32[]{:S(2)}, u32[]{:S(2)}) collective-permute-start(bf16[48,384]{1,0:T(8,128)(2,1)S(1)} %get-tuple-element.49), channel_id=1, source_target_pairs={{0,2},{1,3},{2,0},{3,1},{4,6},{5,7},{6,4},{7,5},{8,10},{9,11},{10,... | collective-permute-start | bytes 110600 | tf_op jit(solution)/shard_map/ppermute | solution.py:520
  6.3 4.7 %collective-permute-start.4 = (f32[8,128]{1,0:T(8,128)S(1)}, f32[8,128]{1,0:T(8,128)S(1)}, u32[]{:S(2)}, u32[]{:S(2)}) collective-permute-start(f32[8,128]{1,0:T(8,128)S(1)} %mark.1.mark_ref.a_ref), channel_id=1, source_target_pairs={{0,16},{4,20},{8,24},{12,28},{16,0},{20,4},{24,8},{28,12},{1,17},{... | collective-permute-start | bytes 12296 | tf_op jit(solution)/shard_map/ppermute | solution.py:562
  11.1 9.2 %copy-start = (bf16[1,256,2560]{2,1,0:T(8,128)(2,1)S(1)}, bf16[1,256,2560]{2,1,0:T(8,128)(2,1)}, u32[]{:S(2)}) copy-start(bf16[1,256,2560]{2,1,0:T(8,128)(2,1)} %gate_ref.1) | copy-start | bytes 3932164
  15.1 5.2 %collective-permute-start.5 = (bf16[256,1280]{1,0:T(8,128)(2,1)S(1)}, bf16[256,1280]{1,0:T(8,128)(2,1)S(1)}, u32[]{:S(2)}, u32[]{:S(2)}) collective-permute-start(bf16[256,1280]{1,0:T(8,128)(2,1)S(1)} %get-tuple-element.63), channel_id=1, source_target_pairs={{0,1},{1,0},{2,3},{3,2},{4,5},{5,4},{6,7},{7,6},{8,9},{9,8},{10,11... | collective-permute-start | bytes 1966088 | tf_op jit(solution)/shard_map/ppermute | solution.py:589
  15.2 8.7 %collective-permute-start.6 = (f32[376,128]{1,0:T(8,128)S(1)}, f32[376,128]{1,0:T(8,128)S(1)}, u32[]{:S(2)}, u32[]{:S(2)}) collective-permute-start(f32[376,128]{1,0:T(8,128)S(1)} %get-tuple-element.69), channel_id=1, source_target_pairs={{0,4},{4,0},{8,12},{12,8},{16,20},{20,16},{24,28},{28,24},{1,5},{5... | collective-permute-start | bytes 577544 | tf_op jit(solution)/shard_map/ppermute | solution.py:592
  16.8 5.6 %collective-permute-start.8 = (f32[8,128]{1,0:T(8,128)S(1)}, f32[8,128]{1,0:T(8,128)S(1)}, u32[]{:S(2)}, u32[]{:S(2)}) collective-permute-start(f32[8,128]{1,0:T(8,128)S(1)} %join.1.mark_ref), channel_id=1, source_target_pairs={{0,12},{4,8},{8,4},{12,0},{16,28},{20,24},{24,20},{28,16},{1,13},{... | collective-permute-start | bytes 12296 | tf_op jit(solution)/shard_map/ppermute | solution.py:594
  18.3 5.6 %collective-permute-start.7 = (f32[280,128]{1,0:T(8,128)S(1)}, f32[280,128]{1,0:T(8,128)S(1)}, u32[]{:S(2)}, u32[]{:S(2)}) collective-permute-start(f32[280,128]{1,0:T(8,128)S(1)} %get-tuple-element.71), channel_id=1, source_target_pairs={{0,8},{4,12},{8,0},{12,4},{16,24},{20,28},{24,16},{28,20},{1,9},{5... | collective-permute-start | bytes 430088 | tf_op jit(solution)/shard_map/ppermute | solution.py:593
  18.8 10.1 %collective-permute-start.14 = (bf16[128,1280]{1,0:T(8,128)(2,1)S(1)}, bf16[128,1280]{1,0:T(8,128)(2,1)S(1)}, u32[]{:S(2)}, u32[]{:S(2)}) collective-permute-start(bf16[128,1280]{1,0:T(8,128)(2,1)S(1)} %get-tuple-element.84), channel_id=1, source_target_pairs={{0,2},{1,3},{2,0},{3,1},{4,6},{5,7},{6,4},{7,5},{8,10},{9,11},{10,... | collective-permute-start | bytes 983048 | tf_op jit(solution)/shard_map/ppermute | solution.py:586
  23.9 4.9 %collective-permute-start.9 = (f32[184,128]{1,0:T(8,128)S(1)}, f32[184,128]{1,0:T(8,128)S(1)}, u32[]{:S(2)}, u32[]{:S(2)}) collective-permute-start(f32[184,128]{1,0:T(8,128)S(1)} %get-tuple-element.74), channel_id=1, source_target_pairs={{0,8},{4,12},{8,0},{12,4},{16,24},{20,28},{24,16},{28,20},{1,9},{5... | collective-permute-start | bytes 282632 | tf_op jit(solution)/shard_map/ppermute | solution.py:611
  24.5 4.3 %collective-permute-start.10 = (f32[136,128]{1,0:T(8,128)S(1)}, f32[136,128]{1,0:T(8,128)S(1)}, u32[]{:S(2)}, u32[]{:S(2)}) collective-permute-start(f32[136,128]{1,0:T(8,128)S(1)} %get-tuple-element.76), channel_id=1, source_target_pairs={{0,4},{4,0},{8,12},{12,8},{16,20},{20,16},{24,28},{28,24},{1,5},{5... | collective-permute-start | bytes 208904 | tf_op jit(solution)/shard_map/ppermute | solution.py:612
  28.9 2.6 %copy-start.1 = (f32[2560]{0:T(1024)S(1)}, f32[2560]{0:T(1024)}, u32[]{:S(2)}) copy-start(f32[2560]{0:T(1024)} %param.19) | copy-start | bytes 30724
  29.2 7.9 %collective-permute-start.15 = (bf16[128,1280]{1,0:T(8,128)(2,1)S(1)}, bf16[128,1280]{1,0:T(8,128)(2,1)S(1)}, u32[]{:S(2)}, u32[]{:S(2)}) collective-permute-start(bf16[128,1280]{1,0:T(8,128)(2,1)S(1)} %get-tuple-element.88), channel_id=1, source_target_pairs={{0,1},{1,0},{2,3},{3,2},{4,5},{5,4},{6,7},{7,6},{8,9},{9,8},{10,11... | collective-permute-start | bytes 983048 | tf_op jit(solution)/shard_map/ppermute | solution.py:632
  29.3 4.1 %collective-permute-start.11 = (f32[80,128]{1,0:T(8,128)S(1)}, f32[80,128]{1,0:T(8,128)S(1)}, u32[]{:S(2)}, u32[]{:S(2)}) collective-permute-start(f32[80,128]{1,0:T(8,128)S(1)} %get-tuple-element.78), channel_id=1, source_target_pairs={{0,2},{1,3},{2,0},{3,1},{4,6},{5,7},{6,4},{7,5},{8,10},{9,11},{10,... | collective-permute-start | bytes 122888 | tf_op jit(solution)/shard_map/ppermute | solution.py:615
  30.9 2.5 %collective-permute-start.12 = (f32[80,128]{1,0:T(8,128)S(1)}, f32[80,128]{1,0:T(8,128)S(1)}, u32[]{:S(2)}, u32[]{:S(2)}) collective-permute-start(f32[80,128]{1,0:T(8,128)S(1)} %get-tuple-element.79), channel_id=1, source_target_pairs={{0,1},{1,0},{2,3},{3,2},{4,5},{5,4},{6,7},{7,6},{8,9},{9,8},{10,11... | collective-permute-start | bytes 122888 | tf_op jit(solution)/shard_map/ppermute | solution.py:614
  31.0 3.4 %collective-permute-start.13 = (f32[80,128]{1,0:T(8,128)S(1)}, f32[80,128]{1,0:T(8,128)S(1)}, u32[]{:S(2)}, u32[]{:S(2)}) collective-permute-start(f32[80,128]{1,0:T(8,128)S(1)} %get-tuple-element.80), channel_id=1, source_target_pairs={{0,3},{1,2},{2,1},{3,0},{4,7},{5,6},{6,5},{7,4},{8,11},{9,10},{10,... | collective-permute-start | bytes 122888 | tf_op jit(solution)/shard_map/ppermute | solution.py:616
  34.5 5.0 %collective-permute-start.16 = (f32[80,128]{1,0:T(8,128)S(1)}, f32[80,128]{1,0:T(8,128)S(1)}, u32[]{:S(2)}, u32[]{:S(2)}) collective-permute-start(f32[80,128]{1,0:T(8,128)S(1)} %get-tuple-element.91), channel_id=1, source_target_pairs={{0,16},{4,20},{8,24},{12,28},{16,0},{20,4},{24,8},{28,12},{1,17},{... | collective-permute-start | bytes 122888 | tf_op jit(solution)/shard_map/ppermute | solution.py:645
